TPU v7x, 32 devices: a whole 2x2x4 slice. The times are simulated.
32 devices in a mesh: dp: 8 (over y, x, core), mp: 4 (over z).
Axes of the slice: x: 2, y: 2, z: 4, core: 2. Of those that a mesh axis runs over, the one named last changes fastest.
Arguments:
- hr_in: bfloat16 [8, 48, 48, 1536], P('dp', 'mp'), may hold values from -6 to 6
- low_in: bfloat16 [8, 576, 1024], P('dp', 'mp'), may hold values from -6 to 6
- valid: int32 [8, 48, 48], P('dp', 'mp'), may hold values from 0 to 1, as said below
- conv_w: bfloat16 [7, 7, 1536], replicated, may hold values from -0.875 to 0.875
- hr_gain: bfloat16 [1536], replicated, may hold values from 0.099609375 to 1.8984375
- cn_up: bfloat16 [1536, 6144], P(None, 'mp'), may hold values from -0.15625 to 0.15625
- cn_down: bfloat16 [6144, 1536], P('mp'), may hold values from -0.078125 to 0.078125
- ad_gate: bfloat16 [1024, 1024], P(None, 'mp'), may hold values from -0.1875 to 0.1875
- ad_high: bfloat16 [1536, 1024], P(None, 'mp'), may hold values from -0.15625 to 0.15625
- ad_out: bfloat16 [1024, 1024], P('mp'), may hold values from -0.1875 to 0.1875
- ln1_gain: bfloat16 [1024], replicated, may hold values from 0.099609375 to 1.8984375
- w_qkv: bfloat16 [3, 1024, 1024], P(None, None, 'mp'), may hold values from -0.1875 to 0.1875
- w_proj: bfloat16 [1024, 1024], P('mp'), may hold values from -0.75 to 0.75
- ln2_gain: bfloat16 [1024], replicated, may hold values from 0.099609375 to 1.8984375
- w_up: bfloat16 [1024, 4096], P(None, 'mp'), may hold values from -0.1875 to 0.1875
- w_down: bfloat16 [4096, 1024], P('mp'), may hold values from -0.09375 to 0.09375
- cot_low: bfloat16 [8, 576, 1024], P('dp', 'mp'), may hold values from -6 to 6
- cot_hr: bfloat16 [8, 48, 48, 1536], P('dp', 'mp'), may hold values from -6 to 6
Outputs:
- low_out: float32 [8, 576, 1024], P('dp', 'mp')
- hr_out: float32 [8, 48, 48, 1536], P('dp', 'mp')
- d_low_in: float32 [8, 576, 1024], P('dp', 'mp')
- d_hr_in: float32 [8, 48, 48, 1536], P('dp', 'mp')
- g_conv: float32 [7, 7, 1536], replicated
- g_hr_gain: float32 [1536], replicated
- g_cn_up: float32 [1536, 6144], P('dp', 'mp')
- g_cn_down: float32 [6144, 1536], P('mp', 'dp')
- g_ad_gate: float32 [1024, 1024], P('dp', 'mp')
- g_ad_high: float32 [1536, 1024], P('dp', 'mp')
- g_ad_out: float32 [1024, 1024], P('mp', 'dp')
- g_ln1: float32 [1024], replicated
- g_qkv: float32 [3, 1024, 1024], P(None, 'dp', 'mp')
- g_proj: float32 [1024, 1024], P('mp', 'dp')
- g_ln2: float32 [1024], replicated
- g_up: float32 [1024, 4096], P('dp', 'mp')
- g_down: float32 [4096, 1024], P('mp', 'dp')
Inputs may be any that keep to these rules, and one draw needn't show every extreme that they name: `valid`: for each item the cells of rows below s and columns below w are 1 and the others 0, with s one half, two thirds or all of 48 and w from s // 2 to s; in every aligned block of 2 items one item has s = 48.
All inputs are finite; a program needn't handle non-finite values.
Results may differ from a plain program's by a relative error of at most 0.034.
Values may be sent and summed in bfloat16 or wider, within the bound.
A program may use at most 256 MiB of HBM per device.

v0:
```python
import jax
import jax.numpy as jnp
from jax import lax
from jax.sharding import PartitionSpec as P

HEAD = 64


def for_sending(value):
    return jax.tree.map(lambda a: a.astype(jnp.bfloat16) if a.dtype == jnp.float32 else a, value)


def extended(value, sides, width):
    for axis, dim in sides:
        devices, length = (lax.axis_size(axis), value.shape[dim])
        up = [(i, (i + 1) % devices) for i in range(devices - 1)]
        down = [(j, i) for i, j in up]
        last = lax.slice_in_dim(value, length - width, length, axis=dim)
        first = lax.slice_in_dim(value, 0, width, axis=dim)
        before = lax.ppermute(last, axis, up)
        after = lax.ppermute(first, axis, down)
        value = jnp.concatenate([before, value, after], axis=dim)
    return value


def layer_norm(values, gain):
    centre = jnp.mean(values, -1, keepdims=True)
    centred = values - centre
    variance = jnp.mean(centred * centred, -1, keepdims=True)
    return centred * lax.rsqrt(variance + 1e-06) * gain


def spread(values):
    return jax.tree.map(
        lambda part, own: part.astype(own.dtype),
        lax.all_gather(for_sending(values), "mp", axis=1, tiled=True),
        values,
    )


def collect(values):
    return jax.tree.map(
        lambda part: part.astype(jnp.float32),
        lax.psum_scatter(for_sending(values), "mp", scatter_dimension=1, tiled=True),
    )


def per_device(
    hr_in,
    low_in,
    valid,
    conv_w,
    hr_gain,
    cn_up,
    cn_down,
    ad_gate,
    ad_high,
    ad_out,
    ln1_gain,
    w_qkv,
    w_proj,
    ln2_gain,
    w_up,
    w_down,
    cot_low,
    cot_hr,
):
    item_count, row_count, col_count, chan_count = hr_in.shape
    plane_mask = valid.astype(jnp.float32)
    cell_mask = plane_mask[..., None]
    masked = hr_in * valid.astype(jnp.bfloat16)[..., None]
    bordered = extended(masked, (("mp", 1),), 3)
    framed = jnp.pad(bordered, ((0, 0), (0, 0), (3, 3), (0, 0)))
    kernel = conv_w.astype(jnp.float32)
    conv_out = jnp.zeros(hr_in.shape, jnp.float32)
    for row_off in range(7):
        for col_off in range(7):
            conv_out = (
                conv_out
                + framed[:, row_off : row_off + row_count, col_off : col_off + col_count]
                * kernel[row_off, col_off]
            )
    conv_out = conv_out * cell_mask
    hr_gainf = hr_gain.astype(jnp.float32)
    normed = layer_norm(conv_out, hr_gainf).astype(jnp.bfloat16)
    normed_all = spread(normed)
    hidden_pre = jnp.einsum("igjc,ch->igjh", normed_all, cn_up, preferred_element_type=jnp.float32)
    hidden_act = jax.nn.gelu(hidden_pre).astype(jnp.bfloat16)
    branch = collect(
        jnp.einsum("igjh,hc->igjc", hidden_act, cn_down, preferred_element_type=jnp.float32)
    )
    hr_out = (masked.astype(jnp.float32) + branch) * cell_mask
    half_rows, half_cols = (row_count // 2, col_count // 2)
    block_sum = hr_out.reshape(item_count, half_rows, 2, half_cols, 2, chan_count).sum(axis=(2, 4))
    counts = plane_mask.reshape(item_count, half_rows, 2, half_cols, 2).sum(axis=(2, 4))
    divisor = jnp.maximum(counts, 1.0)[..., None]
    pooled = (
        (block_sum / divisor)
        .astype(jnp.bfloat16)
        .reshape(item_count, half_rows * half_cols, chan_count)
    )
    low_all, pooled_all = spread((low_in, pooled))
    gate_pre = jnp.einsum("itd,dh->ith", low_all, ad_gate, preferred_element_type=jnp.float32)
    high_pre = jnp.einsum("itc,ch->ith", pooled_all, ad_high, preferred_element_type=jnp.float32)
    gate_vals = jax.nn.sigmoid(gate_pre)
    merging = (high_pre * gate_vals).astype(jnp.bfloat16)
    merged_rows = low_in.astype(jnp.float32) + collect(
        jnp.einsum("ith,hd->itd", merging, ad_out, preferred_element_type=jnp.float32)
    )
    ln1f = ln1_gain.astype(jnp.float32)
    first_norm = layer_norm(merged_rows, ln1f).astype(jnp.bfloat16)
    first_all = spread(first_norm)
    token_count = first_all.shape[1]
    heads_local = w_qkv.shape[2] // HEAD
    stacked = jnp.einsum(
        "itd,kdh->kith", first_all, w_qkv, preferred_element_type=jnp.float32
    ).astype(jnp.bfloat16)
    stacked = stacked.reshape(3, item_count, token_count, heads_local, HEAD)
    query_heads, key_heads, value_heads = (stacked[0], stacked[1], stacked[2])
    score_scale = HEAD ** (-0.5)
    scores = (
        jnp.einsum("iqne,ikne->inqk", query_heads, key_heads, preferred_element_type=jnp.float32)
        * score_scale
    )
    row_max = jnp.max(scores, -1, keepdims=True)
    log_total = jnp.log(jnp.sum(jnp.exp(scores - row_max), -1, keepdims=True)) + row_max
    attn_probs = jnp.exp(scores - log_total).astype(jnp.bfloat16)
    attended = jnp.einsum(
        "inqk,ikne->iqne", attn_probs, value_heads, preferred_element_type=jnp.float32
    )
    attended = attended.astype(jnp.bfloat16).reshape(item_count, token_count, heads_local * HEAD)
    residual = merged_rows + collect(
        jnp.einsum("itm,md->itd", attended, w_proj, preferred_element_type=jnp.float32)
    )
    ln2f = ln2_gain.astype(jnp.float32)
    second_norm = layer_norm(residual, ln2f).astype(jnp.bfloat16)
    second_all = spread(second_norm)
    up_pre = jnp.einsum("itd,df->itf", second_all, w_up, preferred_element_type=jnp.float32)
    up_act = jax.nn.gelu(up_pre).astype(jnp.bfloat16)
    low_out = residual + collect(
        jnp.einsum("itf,fd->itd", up_act, w_down, preferred_element_type=jnp.float32)
    )
    d_out_all = spread(cot_low)
    g_down = jnp.einsum("itf,itd->fd", up_act, d_out_all, preferred_element_type=jnp.float32)
    d_upact = jnp.einsum("itd,fd->itf", d_out_all, w_down, preferred_element_type=jnp.float32)
    d_uppre = jax.vjp(jax.nn.gelu, up_pre)[1](d_upact)[0].astype(jnp.bfloat16)
    g_up = jnp.einsum("itd,itf->df", second_all, d_uppre, preferred_element_type=jnp.float32)
    d_second = collect(jnp.einsum("itf,df->itd", d_uppre, w_up, preferred_element_type=jnp.float32))
    d_res_norm, g_ln2 = jax.vjp(layer_norm, residual, ln2f)[1](d_second)
    d_res = cot_low.astype(jnp.float32) + d_res_norm
    d_attn_all = spread(d_res.astype(jnp.bfloat16))
    g_proj = jnp.einsum("itm,itd->md", attended, d_attn_all, preferred_element_type=jnp.float32)
    d_att = jnp.einsum(
        "itd,md->itm", d_attn_all, w_proj, preferred_element_type=jnp.float32
    ).astype(jnp.bfloat16)
    d_att = d_att.reshape(item_count, token_count, heads_local, HEAD)
    scores_again = (
        jnp.einsum("iqne,ikne->inqk", query_heads, key_heads, preferred_element_type=jnp.float32)
        * score_scale
    )
    probs_full = jnp.exp(scores_again - log_total)
    d_value = jnp.einsum(
        "inqk,iqne->ikne",
        probs_full.astype(jnp.bfloat16),
        d_att,
        preferred_element_type=jnp.float32,
    ).astype(jnp.bfloat16)
    d_probs = jnp.einsum("iqne,ikne->inqk", d_att, value_heads, preferred_element_type=jnp.float32)
    d_scores = (probs_full * (d_probs - jnp.sum(d_probs * probs_full, -1, keepdims=True))).astype(
        jnp.bfloat16
    )
    d_query = (
        jnp.einsum("inqk,ikne->iqne", d_scores, key_heads, preferred_element_type=jnp.float32)
        * score_scale
    ).astype(jnp.bfloat16)
    d_key = (
        jnp.einsum("inqk,iqne->ikne", d_scores, query_heads, preferred_element_type=jnp.float32)
        * score_scale
    ).astype(jnp.bfloat16)
    d_stacked = jnp.stack([d_query, d_key, d_value]).reshape(
        3, item_count, token_count, heads_local * HEAD
    )
    g_qkv = jnp.einsum("itd,kith->kdh", first_all, d_stacked, preferred_element_type=jnp.float32)
    d_first = collect(
        jnp.einsum("kith,kdh->itd", d_stacked, w_qkv, preferred_element_type=jnp.float32)
    )
    d_merged_norm, g_ln1 = jax.vjp(layer_norm, merged_rows, ln1f)[1](d_first)
    d_merged = d_res + d_merged_norm
    d_merging_all = spread(d_merged.astype(jnp.bfloat16))
    g_ad_out = jnp.einsum("ith,itd->hd", merging, d_merging_all, preferred_element_type=jnp.float32)
    d_merging = jnp.einsum("itd,hd->ith", d_merging_all, ad_out, preferred_element_type=jnp.float32)
    d_high = (d_merging * gate_vals).astype(jnp.bfloat16)
    d_gate = (d_merging * high_pre * gate_vals * (1.0 - gate_vals)).astype(jnp.bfloat16)
    g_ad_high = jnp.einsum("itc,ith->ch", pooled_all, d_high, preferred_element_type=jnp.float32)
    g_ad_gate = jnp.einsum("itd,ith->dh", low_all, d_gate, preferred_element_type=jnp.float32)
    d_pooled, d_low = collect(
        (
            jnp.einsum("ith,ch->itc", d_high, ad_high, preferred_element_type=jnp.float32),
            jnp.einsum("ith,dh->itd", d_gate, ad_gate, preferred_element_type=jnp.float32),
        )
    )
    d_low_in = d_merged + d_low
    d_block = d_pooled.reshape(item_count, half_rows, half_cols, chan_count) / divisor
    d_block = d_block.reshape(item_count, half_rows, 1, half_cols, 1, chan_count)
    d_map = cot_hr.astype(jnp.float32) + jnp.broadcast_to(
        d_block, (item_count, half_rows, 2, half_cols, 2, chan_count)
    ).reshape(hr_in.shape)
    d_branch = d_map * cell_mask
    d_branch_all = spread(d_branch.astype(jnp.bfloat16))
    hidden_again = jnp.einsum(
        "igjc,ch->igjh", normed_all, cn_up, preferred_element_type=jnp.float32
    )
    act_again = jax.nn.gelu(hidden_again).astype(jnp.bfloat16)
    g_cn_down = jnp.einsum(
        "igjh,igjc->hc", act_again, d_branch_all, preferred_element_type=jnp.float32
    )
    d_act = jnp.einsum("igjc,hc->igjh", d_branch_all, cn_down, preferred_element_type=jnp.float32)
    d_hidden = jax.vjp(jax.nn.gelu, hidden_again)[1](d_act)[0].astype(jnp.bfloat16)
    g_cn_up = jnp.einsum("igjc,igjh->ch", normed_all, d_hidden, preferred_element_type=jnp.float32)
    d_normed = collect(
        jnp.einsum("igjh,ch->igjc", d_hidden, cn_up, preferred_element_type=jnp.float32)
    )
    d_conv, g_hr_gain = jax.vjp(layer_norm, conv_out, hr_gainf)[1](d_normed)
    d_conv = d_conv * cell_mask
    d_bordered = extended(d_conv.astype(jnp.bfloat16), (("mp", 1),), 3).astype(d_conv.dtype)
    d_framed = jnp.pad(d_bordered, ((0, 0), (0, 0), (3, 3), (0, 0)))
    d_conv_in = jnp.zeros(hr_in.shape, jnp.float32)
    kernel_terms = []
    for row_off in range(7):
        for col_off in range(7):
            d_conv_in = (
                d_conv_in
                + d_framed[
                    :, 6 - row_off : 6 - row_off + row_count, 6 - col_off : 6 - col_off + col_count
                ]
                * kernel[row_off, col_off]
            )
            window = framed[:, row_off : row_off + row_count, col_off : col_off + col_count]
            kernel_terms.append(jnp.sum(window * d_conv, axis=(0, 1, 2)))
    g_conv = jnp.stack(kernel_terms).reshape(7, 7, chan_count)
    d_hr_in = (d_branch + d_conv_in) * cell_mask
    g_conv, g_hr_gain, g_ln1, g_ln2 = lax.psum((g_conv, g_hr_gain, g_ln1, g_ln2), ("dp", "mp"))
    g_cn_up, g_ad_gate, g_ad_high, g_up = (
        lax.psum_scatter(g_cn_up, "dp", scatter_dimension=0, tiled=True),
        lax.psum_scatter(g_ad_gate, "dp", scatter_dimension=0, tiled=True),
        lax.psum_scatter(g_ad_high, "dp", scatter_dimension=0, tiled=True),
        lax.psum_scatter(g_up, "dp", scatter_dimension=0, tiled=True),
    )
    g_cn_down, g_ad_out, g_qkv, g_proj, g_down = (
        lax.psum_scatter(g_cn_down, "dp", scatter_dimension=1, tiled=True),
        lax.psum_scatter(g_ad_out, "dp", scatter_dimension=1, tiled=True),
        lax.psum_scatter(g_qkv, "dp", scatter_dimension=1, tiled=True),
        lax.psum_scatter(g_proj, "dp", scatter_dimension=1, tiled=True),
        lax.psum_scatter(g_down, "dp", scatter_dimension=1, tiled=True),
    )
    return (
        low_out,
        hr_out,
        d_low_in,
        d_hr_in,
        g_conv,
        g_hr_gain,
        g_cn_up,
        g_cn_down,
        g_ad_gate,
        g_ad_high,
        g_ad_out,
        g_ln1,
        g_qkv,
        g_proj,
        g_ln2,
        g_up,
        g_down,
    )


def solution(mesh):
    return jax.shard_map(
        per_device,
        mesh=mesh,
        in_specs=(
            P("dp", "mp", None, None),
            P("dp", "mp", None),
            P("dp", "mp", None),
            P(),
            P(),
            P(None, "mp"),
            P("mp", None),
            P(None, "mp"),
            P(None, "mp"),
            P("mp", None),
            P(),
            P(None, None, "mp"),
            P("mp", None),
            P(),
            P(None, "mp"),
            P("mp", None),
            P("dp", "mp", None),
            P("dp", "mp", None, None),
        ),
        out_specs=(
            P("dp", "mp", None),
            P("dp", "mp", None, None),
            P("dp", "mp", None),
            P("dp", "mp", None, None),
            P(),
            P(),
            P("dp", "mp"),
            P("mp", "dp"),
            P("dp", "mp"),
            P("dp", "mp"),
            P("mp", "dp"),
            P(),
            P(None, "dp", "mp"),
            P("mp", "dp"),
            P(),
            P("dp", "mp"),
            P("mp", "dp"),
        ),
        check_vma=False,
    )
```

profile of v0, /device:TPU:0, one launch (start us, length us, event | category | flops | bytes accessed | tf_op | source)
XLA Modules:
  0.0 1750.1 jit_solution(8830346861084776844)
XLA Ops:
  9.9 5.0 collective-permute-start
  18.0 6.3 collective-permute-done
  24.2 4.1 collective-permute-done.1
  29.8 42.0 %fusion.296 = (f32[12,48]{1,0:T(8,128)S(1)}, f32[1,12,48,1536]{3,2,1,0:T(8,128)S(1)}) fusion(f32[12,48]{1,0:T(8,128)S(1)} %bitcast.198, f32[1536]{0:T(1024)S(1)} %get-tuple-element.127, bf16[1,18,54,1536]{3,2,1,0:T(8,128)(2,1)S(1)} %fusion.217, f32[1536]{0:T(1024)S(1)} %get-tuple-element.128, f32[1536]{0:T(1024)} %get-tuple-element.129, ...), kind=kLoop, calls=%fused_computation.580 | loop fusion | flops 136248768 | bytes 80816640 | tf_op jit(solution)/shard_map/reduce_sum | solution.py:27
  76.6 128.3 %all-gather.10.cloned.1.call-done = bf16[1,48,48,1536]{3,2,0,1:T(8,128)(2,1)} async-done(((bf16[1,12,48,1536]{3,2,0,1:T(8,128)(2,1)}), bf16[1,48,48,1536]{3,2,0,1:T(8,128)(2,1)}) %all-gather.10.cloned.1.call-update) | async-done | bytes 7077904 | tf_op jit(solution)/shard_map/all_gather | solution.py:36
  204.9 14.8 fusion.10
  219.7 5.0 copy-done.137
  224.7 16.1 convert_bitcast_fusion.1
  242.0 120.8 %reduce-scatter.19.cloned.1.call-done = bf16[1,12,48,1536]{3,2,1,0:T(8,128)(2,1)} async-done(((bf16[1,48,48,1536]{3,2,1,0:T(8,128)(2,1)}), bf16[1,12,48,1536]{3,2,1,0:T(8,128)(2,1)}) %reduce-scatter.19.cloned.1.call-update) | async-done | bytes 1769488 | tf_op jit(solution)/shard_map/reduce_scatter | solution.py:44
  362.7 4.5 fusion.121
  367.2 5.3 reshape.741
  372.5 4.6 reduce_sum.676
  378.1 17.2 all-gather.14.cloned.1.call-done
  397.1 39.6 %all-gather.12.cloned.1.call-done = bf16[1,576,1536]{2,1,0:T(8,128)(2,1)} async-done(((bf16[1,144,1536]{2,1,0:T(8,128)(2,1)}), bf16[1,576,1536]{2,1,0:T(8,128)(2,1)}) %all-gather.12.cloned.1.call-update) | async-done | bytes 1769488 | tf_op jit(solution)/shard_map/all_gather | solution.py:36
  442.6 27.7 %reduce-scatter.21.cloned.1.call-done = bf16[1,144,1024]{2,1,0:T(8,128)(2,1)} async-done(((bf16[1,576,1024]{2,1,0:T(8,128)(2,1)}), bf16[1,144,1024]{2,1,0:T(8,128)(2,1)}) %reduce-scatter.21.cloned.1.call-update) | async-done | bytes 294928 | tf_op jit(solution)/shard_map/reduce_scatter | solution.py:44
  474.5 29.3 %all-gather.16.cloned.1.call-done = bf16[1,576,1024]{2,1,0:T(8,128)(2,1)} async-done(((bf16[1,144,1024]{2,1,0:T(8,128)(2,1)}), bf16[1,576,1024]{2,1,0:T(8,128)(2,1)}) %all-gather.16.cloned.1.call-update) | async-done | bytes 1179664 | tf_op jit(solution)/shard_map/all_gather | solution.py:36
  514.9 28.4 %reduce-scatter.23.cloned.1.call-done = bf16[1,144,1024]{2,1,0:T(8,128)(2,1)} async-done(((bf16[1,576,1024]{2,1,0:T(8,128)(2,1)}), bf16[1,144,1024]{2,1,0:T(8,128)(2,1)}) %reduce-scatter.23.cloned.1.call-update) | async-done | bytes 294928 | tf_op jit(solution)/shard_map/reduce_scatter | solution.py:44
  546.4 28.5 %all-gather.18.cloned.1.call-done = bf16[1,576,1024]{2,1,0:T(8,128)(2,1)} async-done(((bf16[1,144,1024]{2,1,0:T(8,128)(2,1)}), bf16[1,576,1024]{2,1,0:T(8,128)(2,1)}) %all-gather.18.cloned.1.call-update) | async-done | bytes 1179664 | tf_op jit(solution)/shard_map/all_gather | solution.py:36
  579.1 27.0 %all-gather.20.cloned.1.call-done = bf16[1,576,1024]{2,1,0:T(8,128)(2,1)} async-done(((bf16[1,144,1024]{2,1,0:T(8,128)(2,1)}), bf16[1,576,1024]{2,1,0:T(8,128)(2,1)}) %all-gather.20.cloned.1.call-update) | async-done | bytes 1179664 | tf_op jit(solution)/shard_map/all_gather | solution.py:36
  606.1 5.3 fusion.225
  615.1 4.9 fusion.237
  620.1 23.2 %reduce-scatter.27.cloned.1.call-done = bf16[1,144,1024]{2,1,0:T(8,128)(2,1)} async-done(((bf16[1,576,1024]{2,1,0:T(8,128)(2,1)}), bf16[1,144,1024]{2,1,0:T(8,128)(2,1)}) %reduce-scatter.27.cloned.1.call-update) | async-done | bytes 294928 | tf_op jit(solution)/shard_map/reduce_scatter | solution.py:44
  645.2 29.0 %reduce-scatter.25.cloned.1.call-done = bf16[1,144,1024]{2,1,0:T(8,128)(2,1)} async-done(((bf16[1,576,1024]{2,1,0:T(8,128)(2,1)}), bf16[1,144,1024]{2,1,0:T(8,128)(2,1)}) %reduce-scatter.25.cloned.1.call-update) | async-done | bytes 294928 | tf_op jit(solution)/shard_map/reduce_scatter | solution.py:44
  677.2 29.3 %all-gather.22.cloned.1.call-done = bf16[1,576,1024]{2,1,0:T(8,128)(2,1)} async-done(((bf16[1,144,1024]{2,1,0:T(8,128)(2,1)}), bf16[1,576,1024]{2,1,0:T(8,128)(2,1)}) %all-gather.22.cloned.1.call-update) | async-done | bytes 1179664 | tf_op jit(solution)/shard_map/all_gather | solution.py:36
  712.5 4.4 multiply_reduce_fusion
  725.3 28.4 %reduce-scatter.29.cloned.1.call-done = bf16[1,144,1024]{2,1,0:T(8,128)(2,1)} async-done(((bf16[1,576,1024]{2,1,0:T(8,128)(2,1)}), bf16[1,144,1024]{2,1,0:T(8,128)(2,1)}) %reduce-scatter.29.cloned.1.call-update) | async-done | bytes 294928 | tf_op jit(solution)/shard_map/reduce_scatter | solution.py:44
  759.4 29.2 %all-gather.24.cloned.1.call-done = bf16[1,576,1024]{2,1,0:T(8,128)(2,1)} async-done(((bf16[1,144,1024]{2,1,0:T(8,128)(2,1)}), bf16[1,576,1024]{2,1,0:T(8,128)(2,1)}) %all-gather.24.cloned.1.call-update) | async-done | bytes 1179664 | tf_op jit(solution)/shard_map/all_gather | solution.py:36
  792.6 37.6 %reduce-scatter.33.cloned.1.call-done = bf16[1,144,1536]{2,1,0:T(8,128)(2,1)} async-done(((bf16[1,576,1536]{2,1,0:T(8,128)(2,1)}), bf16[1,144,1536]{2,1,0:T(8,128)(2,1)}) %reduce-scatter.33.cloned.1.call-update) | async-done | bytes 442384 | tf_op jit(solution)/shard_map/reduce_scatter | solution.py:44
  834.4 5.6 broadcast_in_dim.21
  843.8 4.5 convolution_bitcast_fusion.2
  852.1 119.1 %all-gather.26.cloned.1.call-done = bf16[1,48,48,1536]{3,2,0,1:T(8,128)(2,1)} async-done(((bf16[1,12,48,1536]{3,2,0,1:T(8,128)(2,1)}), bf16[1,48,48,1536]{3,2,0,1:T(8,128)(2,1)}) %all-gather.26.cloned.1.call-update) | async-done | bytes 7077904 | tf_op jit(solution)/shard_map/all_gather | solution.py:36
  971.2 24.7 %fusion.6 = bf16[48,48,1536]{2,1,0:T(8,128)(2,1)S(1)} fusion(f32[48,48,1536]{2,1,0:T(8,128)} %copy-done.137, bf16[1,48,48,1536]{3,2,0,1:T(8,128)(2,1)} %all-gather.26.cloned.1.call-done, bf16[1536,1536]{1,0:T(8,128)(2,1)} %param.24), kind=kOutput, calls=%fused_computation.8 | convolution fusion | flops 10942414848 | bytes 33030144 | tf_op jit(solution)/shard_map/igjc,hc->igjh/dot_general | solution.py:217
  998.8 15.6 convert_bitcast_fusion
  1017.6 5.7 fusion.257
  1034.8 19.6 %convolution_bitcast_fusion = f32[1536,1536]{0,1:T(8,128)} fusion(bf16[1,48,48,1536]{3,2,0,1:T(8,128)(2,1)} %all-gather.26.cloned.1.call-done, f32[48,48,1536]{2,1,0:T(8,128)} %copy-done.137), kind=kOutput, calls=%fused_computation.54 | convolution fusion | flops 10903486464 | bytes 30670848 | tf_op jit(solution)/shard_map/igjh,igjc->hc/dot_general | solution.py:214
  1054.7 17.3 convolution_bitcast_fusion.1
  1075.7 14.8 reduce-scatter.31.cloned.1.call-done
  1092.3 122.5 %reduce-scatter.35.cloned.1.call-done = bf16[1,12,48,1536]{3,2,1,0:T(8,128)(2,1)} async-done(((bf16[1,48,48,1536]{3,2,1,0:T(8,128)(2,1)}), bf16[1,12,48,1536]{3,2,1,0:T(8,128)(2,1)}) %reduce-scatter.35.cloned.1.call-update) | async-done | bytes 1769488 | tf_op jit(solution)/shard_map/reduce_scatter | solution.py:44
  1221.8 10.6 fusion.119
  1232.4 8.9 fusion.98
  1241.5 4.2 collective-permute-start.2
  1254.5 42.0 %all-reduce.2 = (f32[1536]{0:T(1024)}, f32[1024]{0:T(1024)}, f32[1024]{0:T(1024)}) all-reduce(f32[1536]{0:T(1024)S(1)} %get-tuple-element.116, f32[1024]{0:T(1024)S(1)} %copy-done.128, f32[1024]{0:T(1024)S(1)} %copy-done.127), channel_id=1, replica_groups=mesh['dp'=8,'mp'=4] {'dp','mp'}, use_global_device_ids=true, to_apply=%region_77.78 | all-reduce | flops 3584 | bytes 28672 | tf_op jit(solution)/shard_map/psum | solution.py:242
  1301.1 79.7 %fusion.211 = f32[1,12,48,1536]{3,2,1,0:T(8,128)} fusion(f32[1,18,48,1536]{3,2,1,0:T(8,128)} %maximum_convert_fusion, f32[1,12,48,1536]{3,2,1,0:T(8,128)} %broadcast_in_dim.21, bf16[1,12,48,1536]{3,2,1,0:T(8,128)(2,1)} %param.35, f32[12,48]{1,0:T(8,128)S(1)} %bitcast.202, f32[1536]{0:T(1024)S(1)} %copy-done.123, f32[1536]{0:T(1024)S(1)} %copy-done.125, ...), kind=kLoop, calls=%fused_computation.369 | loop fusion | flops 90243072 | bytes 39264512 | tf_op jit(solution)/shard_map/mul | solution.py:241
  1380.8 25.4 %reduce-scatter.45.cloned.1.call-done = f32[256,128]{1,0:T(8,128)} async-done(((f32[256,1024]{1,0:T(8,128)}), f32[256,128]{1,0:T(8,128)}) %reduce-scatter.45.cloned.1.call-update) | async-done | bytes 131088 | tf_op jit(solution)/shard_map/reduce_scatter | solution.py:251
  1406.3 42.4 %reduce-scatter.43.cloned.1.call-done = f32[192,256]{1,0:T(8,128)} async-done(((f32[1536,256]{1,0:T(8,128)}), f32[192,256]{1,0:T(8,128)}) %reduce-scatter.43.cloned.1.call-update) | async-done | bytes 196624 | tf_op jit(solution)/shard_map/reduce_scatter | solution.py:246
  1448.6 80.4 %reduce-scatter.39.cloned.1.call-done = f32[1536,192]{0,1:T(8,128)} async-done(((f32[1536,1536]{0,1:T(8,128)}), f32[1536,192]{0,1:T(8,128)}) %reduce-scatter.39.cloned.1.call-update) | async-done | bytes 1179664 | tf_op jit(solution)/shard_map/reduce_scatter | solution.py:250
  1529.1 80.4 %reduce-scatter.37.cloned.1.call-done = f32[192,1536]{1,0:T(8,128)} async-done(((f32[1536,1536]{1,0:T(8,128)}), f32[192,1536]{1,0:T(8,128)}) %reduce-scatter.37.cloned.1.call-update) | async-done | bytes 1179664 | tf_op jit(solution)/shard_map/reduce_scatter | solution.py:244
  1609.5 131.6 %all-reduce.5.cloned.1.call-done = f32[7,7,1536]{2,1,0:T(8,128)} async-done(((f32[7,7,1536]{2,1,0:T(8,128)}), f32[7,7,1536]{2,1,0:T(8,128)}) %all-reduce.5.cloned.1.call-update) | async-done | bytes 301072 | tf_op jit(solution)/shard_map/psum | solution.py:242
  (487 shorter events, 132.1 us)
Async XLA Ops:
  7.2 567.7 %copy-start = (bf16[1024,1024]{1,0:T(8,128)(2,1)S(1)}, bf16[1024,1024]{1,0:T(8,128)(2,1)}, u32[]{:S(2)}) copy-start(bf16[1024,1024]{1,0:T(8,128)(2,1)} %param.32) | copy-start | bytes 6291460
  7.2 197.7 %all-gather.10.cloned.1.call-start = ((), (), s32[]{:S(2)}) async-start(), calls=%async_computation.18 | async-start | bytes 8847360 | tf_op jit(solution)/shard_map/all_gather | solution.py:36
  9.9 14.3 collective-permute-start
  14.9 13.5 collective-permute-start.1
  16.2 57.5 %copy-start.53 = (f32[1536]{0:T(1024)}, f32[1536]{0:T(1024)S(1)}, u32[]{:S(2)}) copy-start(f32[1536]{0:T(1024)S(1)} %convert_element_type.494) | copy-start | bytes 18436
  16.4 55.4 %copy-start.60 = (f32[1536]{0:T(1024)}, f32[1536]{0:T(1024)S(1)}, u32[]{:S(2)}) copy-start(f32[1536]{0:T(1024)S(1)} %get-tuple-element.164) | copy-start | bytes 18436
  16.4 55.4 %copy-start.62 = (f32[1536]{0:T(1024)}, f32[1536]{0:T(1024)S(1)}, u32[]{:S(2)}) copy-start(f32[1536]{0:T(1024)S(1)} %get-tuple-element.165) | copy-start | bytes 18436
  16.5 55.4 %copy-start.64 = (f32[1536]{0:T(1024)}, f32[1536]{0:T(1024)S(1)}, u32[]{:S(2)}) copy-start(f32[1536]{0:T(1024)S(1)} %get-tuple-element.166) | copy-start | bytes 18436
  16.5 55.4 %copy-start.66 = (f32[1536]{0:T(1024)}, f32[1536]{0:T(1024)S(1)}, u32[]{:S(2)}) copy-start(f32[1536]{0:T(1024)S(1)} %get-tuple-element.167) | copy-start | bytes 18436
  76.3 286.4 %reduce-scatter.19.cloned.1.call-start = ((), (), s32[]{:S(2)}) async-start(), calls=%async_computation.19 | async-start | bytes 8847360 | tf_op jit(solution)/shard_map/reduce_scatter | solution.py:44
  240.8 154.5 %all-gather.14.cloned.1.call-start = ((), (), s32[]{:S(2)}) async-start(), calls=%async_computation.21 | async-start | bytes 1474560 | tf_op jit(solution)/shard_map/all_gather | solution.py:36
  241.6 195.2 %all-gather.12.cloned.1.call-start = ((), (), s32[]{:S(2)}) async-start(), calls=%async_computation.20 | async-start | bytes 2211840 | tf_op jit(solution)/shard_map/all_gather | solution.py:36
  378.1 92.2 %reduce-scatter.21.cloned.1.call-start = ((), (), s32[]{:S(2)}) async-start(), calls=%async_computation.22 | async-start | bytes 1474560 | tf_op jit(solution)/shard_map/reduce_scatter | solution.py:44
  397.1 73.2 %copy-start.9 = (bf16[1,144,1024]{2,1,0:T(8,128)(2,1)S(1)}, bf16[1,144,1024]{2,1,0:T(8,128)(2,1)}, u32[]{:S(2)}) copy-start(bf16[1,144,1024]{2,1,0:T(8,128)(2,1)} %param.19) | copy-start | bytes 884740
  442.1 61.7 %all-gather.16.cloned.1.call-start = ((), (), s32[]{:S(2)}) async-start(), calls=%async_computation.23 | async-start | bytes 1474560 | tf_op jit(solution)/shard_map/all_gather | solution.py:36
  474.5 68.9 %reduce-scatter.23.cloned.1.call-start = ((), (), s32[]{:S(2)}) async-start(), calls=%async_computation.24 | async-start | bytes 1474560 | tf_op jit(solution)/shard_map/reduce_scatter | solution.py:44
  514.9 60.1 %all-gather.18.cloned.1.call-start = ((), (), s32[]{:S(2)}) async-start(), calls=%async_computation.25 | async-start | bytes 1474560 | tf_op jit(solution)/shard_map/all_gather | solution.py:36
  545.6 60.5 %all-gather.20.cloned.1.call-start = ((), (), s32[]{:S(2)}) async-start(), calls=%async_computation.27 | async-start | bytes 1474560 | tf_op jit(solution)/shard_map/all_gather | solution.py:36
  546.4 97.0 %reduce-scatter.27.cloned.1.call-start = ((), (), s32[]{:S(2)}) async-start(), calls=%async_computation.28 | async-start | bytes 1474560 | tf_op jit(solution)/shard_map/reduce_scatter | solution.py:44
  614.9 59.3 %reduce-scatter.25.cloned.1.call-start = ((), (), s32[]{:S(2)}) async-start(), calls=%async_computation.26 | async-start | bytes 1474560 | tf_op jit(solution)/shard_map/reduce_scatter | solution.py:44
  620.0 56.2 %copy-start.35 = (bf16[1,144,1024]{2,1,0:T(8,128)(2,1)S(1)}, bf16[1,144,1024]{2,1,0:T(8,128)(2,1)}, u32[]{:S(2)}) copy-start(bf16[1,144,1024]{2,1,0:T(8,128)(2,1)} %param.34) | copy-start | bytes 884740
  620.0 86.4 %copy-start.42 = (bf16[256,1024]{1,0:T(8,128)(2,1)S(1)}, bf16[256,1024]{1,0:T(8,128)(2,1)}, u32[]{:S(2)}) copy-start(bf16[256,1024]{1,0:T(8,128)(2,1)} %param.30) | copy-start | bytes 1572868
  620.1 86.4 %all-gather.22.cloned.1.call-start = ((), (), s32[]{:S(2)}) async-start(), calls=%async_computation.29 | async-start | bytes 1474560 | tf_op jit(solution)/shard_map/all_gather | solution.py:36
  677.1 76.6 %reduce-scatter.29.cloned.1.call-start = ((), (), s32[]{:S(2)}) async-start(), calls=%async_computation.30 | async-start | bytes 1474560 | tf_op jit(solution)/shard_map/reduce_scatter | solution.py:44
  725.2 63.4 %copy-start.18 = (f32[576,256]{1,0:T(8,128)S(1)}, f32[576,256]{1,0:T(8,128)}, u32[]{:S(2)}) copy-start(f32[576,256]{1,0:T(8,128)} %copy-done.17) | copy-start | bytes 1769476
  725.2 63.4 %copy-start.19 = (f32[576,256]{1,0:T(8,128)S(1)}, f32[576,256]{1,0:T(8,128)}, u32[]{:S(2)}) copy-start(f32[576,256]{1,0:T(8,128)} %get-tuple-element.201) | copy-start | bytes 1769476
  725.3 63.4 %all-gather.24.cloned.1.call-start = ((), (), s32[]{:S(2)}) async-start(), calls=%async_computation.31 | async-start | bytes 1474560 | tf_op jit(solution)/shard_map/all_gather | solution.py:36
  759.4 70.8 %reduce-scatter.33.cloned.1.call-start = ((), (), s32[]{:S(2)}) async-start(), calls=%async_computation.33 | async-start | bytes 2211840 | tf_op jit(solution)/shard_map/reduce_scatter | solution.py:44
  792.5 178.7 %all-gather.26.cloned.1.call-start = ((), (), s32[]{:S(2)}) async-start(), calls=%async_computation.34 | async-start | bytes 8847360 | tf_op jit(solution)/shard_map/all_gather | solution.py:36
  843.7 228.3 %reduce-scatter.47.cloned.1.call-start = ((), (), s32[]{:S(2)}) async-start(), calls=%async_computation.42 | async-start | bytes 3538944 | tf_op jit(solution)/shard_map/reduce_scatter | solution.py:252
  848.3 225.8 %reduce-scatter.41.cloned.1.call-start = ((), (), s32[]{:S(2)}) async-start(), calls=%async_computation.39 | async-start | bytes 1179648 | tf_op jit(solution)/shard_map/reduce_scatter | solution.py:245
  850.0 240.5 %reduce-scatter.31.cloned.1.call-start = ((), (), s32[]{:S(2)}) async-start(), calls=%async_computation.32 | async-start | bytes 1474560 | tf_op jit(solution)/shard_map/reduce_scatter | solution.py:44
  851.7 363.2 %reduce-scatter.35.cloned.1.call-start = ((), (), s32[]{:S(2)}) async-start(), calls=%async_computation.35 | async-start | bytes 8847360 | tf_op jit(solution)/shard_map/reduce_scatter | solution.py:44
  1014.4 366.4 %reduce-scatter.49.cloned.1.call-start = ((), (), s32[]{:S(2)}) async-start(), calls=%async_computation.43 | async-start | bytes 1179648 | tf_op jit(solution)/shard_map/reduce_scatter | solution.py:253
  1017.4 363.4 %reduce-scatter.53.cloned.1.call-start = ((), (), s32[]{:S(2)}) async-start(), calls=%async_computation.45 | async-start | bytes 4718592 | tf_op jit(solution)/shard_map/reduce_scatter | solution.py:254
  1023.3 357.5 %reduce-scatter.51.cloned.1.call-start = ((), (), s32[]{:S(2)}) async-start(), calls=%async_computation.44 | async-start | bytes 4718592 | tf_op jit(solution)/shard_map/reduce_scatter | solution.py:247
  1028.7 377.5 %reduce-scatter.45.cloned.1.call-start = ((), (), s32[]{:S(2)}) async-start(), calls=%async_computation.41 | async-start | bytes 1179648 | tf_op jit(solution)/shard_map/reduce_scatter | solution.py:251
  1031.7 417.0 %reduce-scatter.43.cloned.1.call-start = ((), (), s32[]{:S(2)}) async-start(), calls=%async_computation.40 | async-start | bytes 1769472 | tf_op jit(solution)/shard_map/reduce_scatter | solution.py:246
  1034.7 494.3 %reduce-scatter.39.cloned.1.call-start = ((), (), s32[]{:S(2)}) async-start(), calls=%async_computation.38 | async-start | bytes 10616832 | tf_op jit(solution)/shard_map/reduce_scatter | solution.py:250
  1054.5 555.1 %reduce-scatter.37.cloned.1.call-start = ((), (), s32[]{:S(2)}) async-start(), calls=%async_computation.37 | async-start | bytes 10616832 | tf_op jit(solution)/shard_map/reduce_scatter | solution.py:244
  1072.0 142.9 %copy-start.46 = (f32[12,48]{1,0:T(8,128)S(1)}, f32[12,48]{1,0:T(8,128)}, u32[]{:S(2)}) copy-start(f32[12,48]{1,0:T(8,128)} %copy-done.45) | copy-start | bytes 6916
  1072.0 142.9 %copy-start.54 = (f32[1536]{0:T(1024)S(1)}, f32[1536]{0:T(1024)}, u32[]{:S(2)}) copy-start(f32[1536]{0:T(1024)} %copy-done.53) | copy-start | bytes 18436
  1072.0 669.1 %all-reduce.5.cloned.1.call-start = ((), (), s32[]{:S(2)}) async-start(), calls=%async_computation.36 | async-start | bytes 688128 | tf_op jit(solution)/shard_map/psum | solution.py:242
  1074.1 144.2 %copy-start.59 = (f32[12,48]{1,0:T(8,128)S(1)}, f32[12,48]{1,0:T(8,128)}, u32[]{:S(2)}) copy-start(f32[12,48]{1,0:T(8,128)} %copy-done.58) | copy-start | bytes 6916
  1074.1 144.2 %copy-start.57 = (f32[12,48]{1,0:T(8,128)S(1)}, f32[12,48]{1,0:T(8,128)}, u32[]{:S(2)}) copy-start(f32[12,48]{1,0:T(8,128)} %copy-done.56) | copy-start | bytes 6916
  1241.5 55.3 %collective-permute-start.2 = (bf16[1,3,48,1536]{3,2,1,0:T(8,128)(2,1)S(1)}, bf16[1,3,48,1536]{3,2,1,0:T(8,128)(2,1)}, u32[]{:S(2)}, u32[]{:S(2)}) collective-permute-start(bf16[1,3,48,1536]{3,2,1,0:T(8,128)(2,1)S(1)} %get-tuple-element.188), channel_id=1, source_target_pairs={{0,1},{1,2},{2,3},{4,5},{5,6},{6,7},{8,9},{9,10},{10,11},{12,13},{... | collective-permute-start | bytes 1327112 | tf_op jit(solution)/shard_map/ppermute | solution.py:20
  1245.6 51.2 %collective-permute-start.3 = (bf16[1,3,48,1536]{3,2,1,0:T(8,128)(2,1)S(1)}, bf16[1,3,48,1536]{3,2,1,0:T(8,128)(2,1)}, u32[]{:S(2)}, u32[]{:S(2)}) collective-permute-start(bf16[1,3,48,1536]{3,2,1,0:T(8,128)(2,1)S(1)} %get-tuple-element.189), channel_id=1, source_target_pairs={{1,0},{2,1},{3,2},{5,4},{6,5},{7,6},{9,8},{10,9},{11,10},{13,12},{... | collective-permute-start | bytes 1327112 | tf_op jit(solution)/shard_map/ppermute | solution.py:21
  1301.1 441.8 %copy-start.1 = (bf16[1024,1024]{1,0:T(8,128)(2,1)S(1)}, bf16[1024,1024]{1,0:T(8,128)(2,1)}, u32[]{:S(2)}) copy-start(bf16[1024,1024]{1,0:T(8,128)(2,1)} %param.32) | copy-start | bytes 6291460
  (124 other events, 2407.4 us)
Sparse Core Ops, SparseCore 0:
  76.4 128.4 all-gather.9
  240.9 121.7 reduce-scatter.18
  364.3 30.9 all-gather.13
  397.3 39.4 all-gather.11
  442.2 28.0 reduce-scatter.20
  474.6 29.1 all-gather.15
  515.0 28.2 reduce-scatter.22
  545.8 29.1 all-gather.17
  576.5 29.5 all-gather.19
  615.0 28.2 reduce-scatter.26
  646.2 27.8 reduce-scatter.24
  677.3 29.1 all-gather.21
  725.4 28.2 reduce-scatter.28
  759.5 29.1 all-gather.23
  792.6 37.5 reduce-scatter.32
  843.8 127.2 all-gather.25
  975.4 44.4 reduce-scatter.46
  1022.9 36.0 reduce-scatter.40
  1061.3 29.1 reduce-scatter.30
  1092.6 122.1 reduce-scatter.34
  1218.6 36.4 reduce-scatter.48
  1259.1 51.8 reduce-scatter.52
  1315.3 51.2 reduce-scatter.50
  1370.2 35.9 reduce-scatter.44
  1410.1 38.4 reduce-scatter.42
  1452.6 76.4 reduce-scatter.38
  1533.0 76.4 reduce-scatter.36
  1615.4 125.6 all-reduce.4
where the time goes:
time: 1760 us; the launch traced here: 1750 us
  waiting for transfers between devices  1250 us (71%)
  other arithmetic  200 us (11%)
  matrix products  180 us (10%)
  local copies, waits for them, and re-layouts  44.2 us (3%)
  blocking collectives  42 us (2%)
    all_gather x9, waiting for transfers between devices, spread(): lax.all_gather(for_sending(values), 'mp', axis=1, tiled=True)  448 us
    reduce_scatter x9, waiting for transfers between devices, collect(): lax.psum_scatter(for_sending(values), 'mp', scatter_dimension=1, tiled=True)  432 us
    psum x1, waiting for transfers between devices, per_device(): lax.psum((g_conv, g_hr_gain, g_ln1, g_ln2), ('dp', 'mp'))  132 us
    reduce_scatter x1, waiting for transfers between devices, per_device(): lax.psum_scatter(g_cn_down, 'dp', scatter_dimension=1, tiled=True)  80.4 us
    reduce_scatter x1, waiting for transfers between devices, per_device(): lax.psum_scatter(g_cn_up, 'dp', scatter_dimension=0, tiled=True)  80.4 us
    mul x1, other arithmetic, per_device(): d_hr_in = (d_branch + d_conv_in) * cell_mask  79.7 us
    reduce_sum x3, other arithmetic, layer_norm(): centre = jnp.mean(values, -1, keepdims=True)  44.3 us
    reduce_scatter x1, waiting for transfers between devices, per_device(): lax.psum_scatter(g_ad_high, 'dp', scatter_dimension=0, tiled=True)  42.4 us
  transfers between devices with their start and end apart: 32, of which 25 were waited for; matrix products, arithmetic and copies ran while one was open for 14% of the time, Pallas kernels for 0%

commit v1 on v0

--- a/solution.py
+++ b/solution.py
@@ -1,9 +1,440 @@
 import jax
 import jax.numpy as jnp
 from jax import lax
+from jax.experimental import pallas as pl
+from jax.experimental.pallas import tpu as pltpu
 from jax.sharding import PartitionSpec as P
 
 HEAD = 64
+LANES = 128
+EDGE = 8
+CHUNKS = 6
+TILE = 512
+MIB = 1024 * 1024
+MESH = pl.DeviceIdType.MESH
+BF = jnp.bfloat16
+F32 = jnp.float32
+
+def gelu_parts(x):
+    c = 0.7978845608028654
+    x2 = x * x
+    t = jnp.tanh(c * x * (1.0 + 0.044715 * x2))
+    half = 0.5 * (1.0 + t)
+    slope = half + 0.5 * x * (1.0 - t * t) * (c * (1.0 + 3 * 0.044715 * x2))
+    return x * half, slope
+
+
+def gelu(x):
+    c = 0.7978845608028654
+    t = jnp.tanh(c * x * (1.0 + 0.044715 * (x * x)))
+    return 0.5 * x * (1.0 + t)
+
+
+def chain_exchange(n, chunks, lag, own_hbm, gathered, partial, travel, compute, result_hbm,
+                   sems, prepare, arrived):
+    ag_send, ag_recv, rs_send, rs_recv, local_sem = sems
+    d = lax.axis_index("mp")
+    has_left, has_right = d > 0, d < n - 1
+
+    barrier = pltpu.get_barrier_semaphore()
+
+    @pl.when(has_left)
+    def _():
+        pl.semaphore_signal(barrier, inc=1, device_id={"mp": d - 1}, device_id_type=MESH)
+
+    @pl.when(has_right)
+    def _():
+        pl.semaphore_signal(barrier, inc=1, device_id={"mp": d + 1}, device_id_type=MESH)
+
+    load = pltpu.make_async_copy(own_hbm, gathered.at[d], local_sem)
+    load.start()
+
+    pl.semaphore_wait(barrier, has_left.astype(jnp.int32) + has_right.astype(jnp.int32))
+    load.wait()
+
+    def ag(way, s, j):
+        return pltpu.make_async_remote_copy(
+            src_ref=gathered.at[s, j], dst_ref=gathered.at[s, j],
+            send_sem=ag_send.at[way, s, j], recv_sem=ag_recv.at[s, j],
+            device_id={"mp": d + 1 - 2 * way}, device_id_type=MESH)
+
+    def rs(way, s, j):
+        there = d + 1 - 2 * way
+        slot = jnp.where((s == there) & (way == 0), n, s)
+        return pltpu.make_async_remote_copy(
+            src_ref=travel.at[s, j], dst_ref=travel.at[slot, j],
+            send_sem=rs_send.at[s, j], recv_sem=rs_recv.at[slot, j],
+            device_id={"mp": there}, device_id_type=MESH)
+
+    def rs_wait(slot, j):
+        pltpu.make_async_copy(travel.at[slot, j], travel.at[slot, j], rs_recv.at[slot, j]).wait()
+
+    def first(j, _):
+        @pl.when(has_right)
+        def _():
+            ag(0, d, j).start()
+
+        @pl.when(has_left)
+        def _():
+            ag(1, d, j).start()
+        return 0
+    lax.fori_loop(0, chunks, first, 0)
+
+    def step(g, _):
+        k, j = g // chunks, lax.rem(g, chunks)
+
+        @pl.when(g < n * chunks)
+        def _():
+            def side(way, _):
+                s = d - k + 2 * k * way
+                ok = (s >= 0) & (s < n) & ((k > 0) | (way == 0))
+
+                @pl.when(ok)
+                def _():
+                    prepare(s, j)
+
+                    @pl.when(k > 0)
+                    def _():
+                        pltpu.make_async_copy(gathered.at[s, j], gathered.at[s, j], ag_recv.at[s, j]).wait()
+
+                        @pl.when((way == 0) & has_right)
+                        def _():
+                            ag(0, s, j).start()
+
+                        @pl.when((way == 1) & has_left)
+                        def _():
+                            ag(1, s, j).start()
+                    arrived(s, j)
+                    compute(s, j)
+                return 0
+            lax.fori_loop(0, 2, side, 0)
+
+        q = g - (n - 1 - d) * lag
+        ql = jnp.clip(q, 0, n * chunks - 1)
+        s, jj = n - 1 - ql // chunks, lax.rem(ql, chunks)
+
+        @pl.when((q >= 0) & (q < n * chunks) & (s <= d) & (has_right | (s < d)))
+        def _():
+            @pl.when(has_right)
+            def _():
+                rs_wait(s, jj)
+
+                @pl.when(s < d)
+                def _():
+                    travel[s, jj] = (partial[s, jj].astype(F32) + travel[s, jj].astype(F32)).astype(BF)
+
+                @pl.when(s == d)
+                def _():
+                    partial[s, jj] = (partial[s, jj].astype(F32) + travel[s, jj].astype(F32)).astype(partial.dtype)
+
+            @pl.when(d == n - 1)
+            def _():
+                travel[s, jj] = partial[s, jj].astype(BF)
+
+            @pl.when(s < d)
+            def _():
+                rs(1, s, jj).start()
+
+        q2 = g - d * lag
+        qr = jnp.clip(q2, 0, n * chunks - 1)
+        s2, j2 = qr // chunks, lax.rem(qr, chunks)
+
+        @pl.when((q2 >= 0) & (q2 < n * chunks) & (s2 >= d) & (has_left | (s2 > d)))
+        def _():
+            @pl.when(has_left)
+            def _():
+                slot = jnp.where(s2 == d, n, s2)
+                rs_wait(slot, j2)
+
+                @pl.when(s2 > d)
+                def _():
+                    travel[s2, j2] = (partial[s2, j2].astype(F32) + travel[s2, j2].astype(F32)).astype(BF)
+
+                @pl.when(s2 == d)
+                def _():
+                    partial[s2, j2] = (partial[s2, j2].astype(F32) + travel[n, j2].astype(F32)).astype(partial.dtype)
+
+            @pl.when(d == 0)
+            def _():
+                travel[s2, j2] = partial[s2, j2].astype(BF)
+
+            @pl.when(s2 > d)
+            def _():
+                rs(0, s2, j2).start()
+        return 0
+
+    lax.fori_loop(0, n * chunks + (n - 1) * lag, step, 0)
+
+    store = pltpu.make_async_copy(partial.at[d], result_hbm, local_sem)
+    store.start()
+
+    def drain(i, _):
+        s, j = i // chunks, lax.rem(i, chunks)
+
+        @pl.when(has_right & (s <= d))
+        def _():
+            ag(0, s, j).wait_send()
+
+        @pl.when(has_left & (s >= d))
+        def _():
+            ag(1, s, j).wait_send()
+
+        @pl.when(s < d)
+        def _():
+            rs(1, s, j).wait_send()
+
+        @pl.when(s > d)
+        def _():
+            rs(0, s, j).wait_send()
+        return 0
+    lax.fori_loop(0, n * chunks, drain, 0)
+    store.wait()
+
+
+def chain_sems(n, chunks):
+    dma = pltpu.SemaphoreType.DMA
+    return [dma((2, n, chunks)), dma((n, chunks)), dma((n, chunks)), dma((n + 1, chunks)), dma]
+
+
+def chunk_buffers(n, rows, c, kept):
+    return [
+        pltpu.VMEM((n, CHUNKS, rows, c), BF),
+        pltpu.VMEM((n, CHUNKS, rows, c), kept),
+        pltpu.VMEM((n + 1, CHUNKS, rows, c), BF),
+    ]
+
+
+def columns(i):
+    return pl.ds(pl.multiple_of(i * TILE, TILE), TILE)
+
+
+def drain_copies(n, copy):
+    def one(i, _):
+        copy(i // CHUNKS, lax.rem(i, CHUNKS)).wait()
+        return 0
+
+    lax.fori_loop(0, n * CHUNKS, one, 0)
+
+
+def big_forward(x, w_up, w_down, n):
+    t, c = x.shape
+    h = w_up.shape[1]
+    rows = t // CHUNKS
+
+    def kernel(
+        x_ref, wu, wd, out, x_all, act_all, slope_all,
+        gathered, partial, travel, act, slope, copied, stored, *sems
+    ):
+        def x_copy(s, j):
+            return pltpu.make_async_copy(gathered.at[s, j], x_all.at[s, j], copied.at[s, j])
+
+        def prepare(s, j):
+            pass
+
+        def arrived(s, j):
+            x_copy(s, j).start()
+
+        def compute(s, j):
+            block = gathered.at[s, j]
+
+            def up(i, _):
+                pre = jnp.dot(block[...], wu[:, columns(i)], preferred_element_type=F32)
+                value, rate = gelu_parts(pre)
+                act[:, columns(i)] = value.astype(BF)
+                slope[:, columns(i)] = rate.astype(BF)
+                return 0
+
+            lax.fori_loop(0, h // TILE, up, 0)
+            keep_act = pltpu.make_async_copy(act, act_all.at[s, j], stored.at[0])
+            keep_slope = pltpu.make_async_copy(slope, slope_all.at[s, j], stored.at[1])
+            keep_act.start()
+            keep_slope.start()
+
+            def down(i, _):
+                partial[s, j, :, columns(i)] = jnp.dot(
+                    act[...], wd[:, columns(i)], preferred_element_type=F32
+                )
+                return 0
+
+            lax.fori_loop(0, c // TILE, down, 0)
+            keep_act.wait()
+            keep_slope.wait()
+
+        chain_exchange(
+            n, CHUNKS, 1, x_ref, gathered, partial, travel, compute, out, sems, prepare, arrived
+        )
+        drain_copies(n, x_copy)
+
+    whole = pl.BlockSpec(memory_space=pl.ANY)
+    local = pl.BlockSpec(memory_space=pltpu.VMEM)
+    out, x_all, act_all, slope_all = pl.pallas_call(
+        kernel,
+        out_shape=(
+            jax.ShapeDtypeStruct((CHUNKS, rows, c), F32),
+            jax.ShapeDtypeStruct((n, CHUNKS, rows, c), BF),
+            jax.ShapeDtypeStruct((n, CHUNKS, rows, h), BF),
+            jax.ShapeDtypeStruct((n, CHUNKS, rows, h), BF),
+        ),
+        in_specs=[whole, local, local],
+        out_specs=(whole,) * 4,
+        scratch_shapes=chunk_buffers(n, rows, c, F32)
+        + [pltpu.VMEM((rows, h), BF)] * 2
+        + [pltpu.SemaphoreType.DMA((n, CHUNKS)), pltpu.SemaphoreType.DMA((2,))]
+        + chain_sems(n, CHUNKS),
+        compiler_params=pltpu.CompilerParams(
+            collective_id=0, has_side_effects=True, vmem_limit_bytes=60 * MIB
+        ),
+        cost_estimate=pl.CostEstimate(
+            flops=4 * n * t * c * h, bytes_accessed=8 * n * t * c, transcendentals=n * t * h
+        ),
+    )(x.reshape(CHUNKS, rows, c), w_up, w_down)
+    return (
+        out.reshape(t, c),
+        x_all.reshape(n * t, c),
+        act_all.reshape(n * t, h),
+        slope_all.reshape(n * t, h),
+    )
+
+
+def big_backward(d, slope_all, w_up, w_down, n):
+    t, c = d.shape
+    h = w_up.shape[1]
+    rows = t // CHUNKS
+
+    def kernel(
+        d_ref, slopes, wu, wd, out, d_all, h_all,
+        gathered, partial, travel, slope, grad, copied, stored, *sems
+    ):
+        def d_copy(s, j):
+            return pltpu.make_async_copy(gathered.at[s, j], d_all.at[s, j], copied.at[s, j])
+
+        def slope_copy(s, j):
+            return pltpu.make_async_copy(slopes.at[s, j], slope, stored.at[0])
+
+        def prepare(s, j):
+            slope_copy(s, j).start()
+
+        def arrived(s, j):
+            d_copy(s, j).start()
+
+        def compute(s, j):
+            block = gathered.at[s, j]
+            slope_copy(s, j).wait()
+
+            def up(i, _):
+                back = lax.dot_general(
+                    block[...], wd[columns(i), :], (((1,), (1,)), ((), ())), preferred_element_type=F32
+                )
+                grad[:, columns(i)] = (back * slope[:, columns(i)].astype(F32)).astype(BF)
+                return 0
+
+            lax.fori_loop(0, h // TILE, up, 0)
+            keep = pltpu.make_async_copy(grad, h_all.at[s, j], stored.at[1])
+            keep.start()
+
+            def down(i, _):
+                partial[s, j, :, columns(i)] = lax.dot_general(
+                    grad[...], wu[columns(i), :], (((1,), (1,)), ((), ())), preferred_element_type=F32
+                )
+                return 0
+
+            lax.fori_loop(0, c // TILE, down, 0)
+            keep.wait()
+
+        chain_exchange(
+            n, CHUNKS, 1, d_ref, gathered, partial, travel, compute, out, sems, prepare, arrived
+        )
+        drain_copies(n, d_copy)
+
+    whole = pl.BlockSpec(memory_space=pl.ANY)
+    local = pl.BlockSpec(memory_space=pltpu.VMEM)
+    out, d_all, h_all = pl.pallas_call(
+        kernel,
+        out_shape=(
+            jax.ShapeDtypeStruct((CHUNKS, rows, c), F32),
+            jax.ShapeDtypeStruct((n, CHUNKS, rows, c), BF),
+            jax.ShapeDtypeStruct((n, CHUNKS, rows, h), BF),
+        ),
+        in_specs=[whole, whole, local, local],
+        out_specs=(whole,) * 3,
+        scratch_shapes=chunk_buffers(n, rows, c, F32)
+        + [pltpu.VMEM((rows, h), BF)] * 2
+        + [pltpu.SemaphoreType.DMA((n, CHUNKS)), pltpu.SemaphoreType.DMA((2,))]
+        + chain_sems(n, CHUNKS),
+        compiler_params=pltpu.CompilerParams(
+            collective_id=1, has_side_effects=True, vmem_limit_bytes=60 * MIB
+        ),
+        cost_estimate=pl.CostEstimate(
+            flops=4 * n * t * c * h, bytes_accessed=8 * n * t * c, transcendentals=0
+        ),
+    )(d.reshape(CHUNKS, rows, c), slope_all.reshape(n, CHUNKS, rows, h), w_up, w_down)
+    return out.reshape(t, c), d_all.reshape(n * t, c), h_all.reshape(n * t, h)
+
+
+def frame(dst, src):
+    rows, cols, _ = src.shape
+    dst[:, :EDGE] = jnp.zeros((rows, EDGE, LANES), F32)
+    dst[:, EDGE + cols:] = jnp.zeros((rows, EDGE, LANES), F32)
+    dst[:, EDGE:EDGE + cols] = src[...].astype(F32)
+
+
+def correlate(out, framed, taps, size, flip, group):
+    rows, cols, _ = out.shape
+    reach = size // 2
+    def some(r, _):
+        acc = jnp.zeros((group, cols, LANES), F32)
+        for a in range(size):
+            for b in range(size):
+                tap = (size - 1 - a) * size + size - 1 - b if flip else a * size + b
+                acc = acc + framed[pl.ds(r * group + a, group), pl.ds(EDGE - reach + b, cols), :] * taps[tap]
+        out[pl.ds(r * group, group)] = acc
+        return 0
+    lax.fori_loop(0, rows // group, some, 0)
+
+
+def conv_forward(x, w, size, group=2):
+    high, cols, c = x.shape
+    rows = high - size + 1
+    def kernel(x_ref, w_ref, out, framed):
+        frame(framed, x_ref)
+        correlate(out, framed, w_ref, size, False, group)
+    return pl.pallas_call(
+        kernel, grid=(c // LANES,),
+        out_shape=jax.ShapeDtypeStruct((rows, cols, c), F32),
+        in_specs=[pl.BlockSpec((high, cols, LANES), lambda i: (0, 0, i)), pl.BlockSpec((size * size, 1, LANES), lambda i: (0, 0, i))],
+        out_specs=pl.BlockSpec((rows, cols, LANES), lambda i: (0, 0, i)),
+        scratch_shapes=[pltpu.VMEM((high, cols + 2 * EDGE, LANES), F32)],
+        compiler_params=pltpu.CompilerParams(vmem_limit_bytes=32 << 20),
+    )(x, w)
+
+
+def conv_backward(d, x, w, size, group=2, bgroup=2):
+    high, cols, c = x.shape
+    rows = high - size + 1
+    reach = size // 2
+    def kernel(d_ref, x_ref, w_ref, out, g, dframed, xframed):
+        frame(dframed, d_ref)
+        frame(xframed, x_ref)
+        correlate(out, dframed, w_ref, size, True, group)
+        for a in range(size):
+            def some(r, accs):
+                dv = dframed[pl.ds(reach + r * bgroup, bgroup), EDGE:EDGE + cols]
+                new = []
+                for b in range(size):
+                    prod = dv * xframed[pl.ds(r * bgroup + a, bgroup), pl.ds(EDGE - reach + b, cols), :]
+                    new.append(accs[b] + jnp.sum(prod.reshape(-1, 8, LANES), axis=0))
+                return tuple(new)
+            accs = lax.fori_loop(0, rows // bgroup, some, tuple(jnp.zeros((8, LANES), F32) for _ in range(size)))
+            for b in range(size):
+                g[a * size + b] = jnp.sum(accs[b], axis=0, keepdims=True)
+    return pl.pallas_call(
+        kernel, grid=(c // LANES,),
+        out_shape=(jax.ShapeDtypeStruct((rows, cols, c), F32), jax.ShapeDtypeStruct((size * size, 1, c), F32)),
+        in_specs=[pl.BlockSpec((high, cols, LANES), lambda i: (0, 0, i))] * 2 + [pl.BlockSpec((size * size, 1, LANES), lambda i: (0, 0, i))],
+        out_specs=(pl.BlockSpec((rows, cols, LANES), lambda i: (0, 0, i)), pl.BlockSpec((size * size, 1, LANES), lambda i: (0, 0, i))),
+        scratch_shapes=[pltpu.VMEM((high, cols + 2 * EDGE, LANES), F32)] * 2,
+        compiler_params=pltpu.CompilerParams(vmem_limit_bytes=32 << 20),
+    )(d, x, w)
 
 
 def for_sending(value):
@@ -70,25 +501,17 @@
     cell_mask = plane_mask[..., None]
     masked = hr_in * valid.astype(jnp.bfloat16)[..., None]
     bordered = extended(masked, (("mp", 1),), 3)
-    framed = jnp.pad(bordered, ((0, 0), (0, 0), (3, 3), (0, 0)))
-    kernel = conv_w.astype(jnp.float32)
-    conv_out = jnp.zeros(hr_in.shape, jnp.float32)
-    for row_off in range(7):
-        for col_off in range(7):
-            conv_out = (
-                conv_out
-                + framed[:, row_off : row_off + row_count, col_off : col_off + col_count]
-                * kernel[row_off, col_off]
-            )
+    size = conv_w.shape[0]
+    taps = conv_w.astype(F32).reshape(size * size, 1, chan_count)
+    conv_out = conv_forward(bordered[0], taps, size)[None]
     conv_out = conv_out * cell_mask
     hr_gainf = hr_gain.astype(jnp.float32)
     normed = layer_norm(conv_out, hr_gainf).astype(jnp.bfloat16)
-    normed_all = spread(normed)
-    hidden_pre = jnp.einsum("igjc,ch->igjh", normed_all, cn_up, preferred_element_type=jnp.float32)
-    hidden_act = jax.nn.gelu(hidden_pre).astype(jnp.bfloat16)
-    branch = collect(
-        jnp.einsum("igjh,hc->igjc", hidden_act, cn_down, preferred_element_type=jnp.float32)
-    )
+    shards = lax.axis_size("mp")
+    branch, normed_all, hidden_act, hidden_slope = big_forward(
+        normed.reshape(row_count * col_count, chan_count), cn_up, cn_down, shards
+    )
+    branch = branch.reshape(hr_in.shape)
     hr_out = (masked.astype(jnp.float32) + branch) * cell_mask
     half_rows, half_cols = (row_count // 2, col_count // 2)
     block_sum = hr_out.reshape(item_count, half_rows, 2, half_cols, 2, chan_count).sum(axis=(2, 4))
@@ -206,52 +629,39 @@
         d_block, (item_count, half_rows, 2, half_cols, 2, chan_count)
     ).reshape(hr_in.shape)
     d_branch = d_map * cell_mask
-    d_branch_all = spread(d_branch.astype(jnp.bfloat16))
-    hidden_again = jnp.einsum(
-        "igjc,ch->igjh", normed_all, cn_up, preferred_element_type=jnp.float32
-    )
-    act_again = jax.nn.gelu(hidden_again).astype(jnp.bfloat16)
-    g_cn_down = jnp.einsum(
-        "igjh,igjc->hc", act_again, d_branch_all, preferred_element_type=jnp.float32
-    )
-    d_act = jnp.einsum("igjc,hc->igjh", d_branch_all, cn_down, preferred_element_type=jnp.float32)
-    d_hidden = jax.vjp(jax.nn.gelu, hidden_again)[1](d_act)[0].astype(jnp.bfloat16)
-    g_cn_up = jnp.einsum("igjc,igjh->ch", normed_all, d_hidden, preferred_element_type=jnp.float32)
-    d_normed = collect(
-        jnp.einsum("igjh,ch->igjc", d_hidden, cn_up, preferred_element_type=jnp.float32)
-    )
+    d_normed, d_branch_all, d_hidden = big_backward(
+        d_branch.astype(BF).reshape(row_count * col_count, chan_count),
+        hidden_slope, cn_up, cn_down, shards,
+    )
+    d_normed = d_normed.reshape(hr_in.shape)
+    g_cn_down = jnp.einsum("th,tc->hc", hidden_act, d_branch_all, preferred_element_type=F32).astype(BF)
+    g_cn_up = jnp.einsum("tc,th->ch", normed_all, d_hidden, preferred_element_type=F32).astype(BF)
     d_conv, g_hr_gain = jax.vjp(layer_norm, conv_out, hr_gainf)[1](d_normed)
     d_conv = d_conv * cell_mask
-    d_bordered = extended(d_conv.astype(jnp.bfloat16), (("mp", 1),), 3).astype(d_conv.dtype)
-    d_framed = jnp.pad(d_bordered, ((0, 0), (0, 0), (3, 3), (0, 0)))
-    d_conv_in = jnp.zeros(hr_in.shape, jnp.float32)
-    kernel_terms = []
-    for row_off in range(7):
-        for col_off in range(7):
-            d_conv_in = (
-                d_conv_in
-                + d_framed[
-                    :, 6 - row_off : 6 - row_off + row_count, 6 - col_off : 6 - col_off + col_count
-                ]
-                * kernel[row_off, col_off]
-            )
-            window = framed[:, row_off : row_off + row_count, col_off : col_off + col_count]
-            kernel_terms.append(jnp.sum(window * d_conv, axis=(0, 1, 2)))
-    g_conv = jnp.stack(kernel_terms).reshape(7, 7, chan_count)
+    d_bordered = extended(d_conv.astype(BF), (("mp", 1),), 3)
+    d_conv_in, g_conv = conv_backward(d_bordered[0], bordered[0], taps, size)
+    g_conv = g_conv.reshape(conv_w.shape)
     d_hr_in = (d_branch + d_conv_in) * cell_mask
-    g_conv, g_hr_gain, g_ln1, g_ln2 = lax.psum((g_conv, g_hr_gain, g_ln1, g_ln2), ("dp", "mp"))
+    small = (g_conv, g_hr_gain, g_ln1, g_ln2)
+    packed = jnp.concatenate([g.reshape(-1) for g in small])
+    packed = lax.psum(lax.psum(packed, "mp"), "dp")
+    parts, at = [], 0
+    for g in small:
+        parts.append(packed[at : at + g.size].reshape(g.shape))
+        at += g.size
+    g_conv, g_hr_gain, g_ln1, g_ln2 = parts
     g_cn_up, g_ad_gate, g_ad_high, g_up = (
-        lax.psum_scatter(g_cn_up, "dp", scatter_dimension=0, tiled=True),
-        lax.psum_scatter(g_ad_gate, "dp", scatter_dimension=0, tiled=True),
-        lax.psum_scatter(g_ad_high, "dp", scatter_dimension=0, tiled=True),
-        lax.psum_scatter(g_up, "dp", scatter_dimension=0, tiled=True),
+        lax.psum_scatter(g_cn_up.astype(BF), "dp", scatter_dimension=0, tiled=True).astype(F32),
+        lax.psum_scatter(g_ad_gate.astype(BF), "dp", scatter_dimension=0, tiled=True).astype(F32),
+        lax.psum_scatter(g_ad_high.astype(BF), "dp", scatter_dimension=0, tiled=True).astype(F32),
+        lax.psum_scatter(g_up.astype(BF), "dp", scatter_dimension=0, tiled=True).astype(F32),
     )
     g_cn_down, g_ad_out, g_qkv, g_proj, g_down = (
-        lax.psum_scatter(g_cn_down, "dp", scatter_dimension=1, tiled=True),
-        lax.psum_scatter(g_ad_out, "dp", scatter_dimension=1, tiled=True),
-        lax.psum_scatter(g_qkv, "dp", scatter_dimension=1, tiled=True),
-        lax.psum_scatter(g_proj, "dp", scatter_dimension=1, tiled=True),
-        lax.psum_scatter(g_down, "dp", scatter_dimension=1, tiled=True),
+        lax.psum_scatter(g_cn_down.astype(BF), "dp", scatter_dimension=1, tiled=True).astype(F32),
+        lax.psum_scatter(g_ad_out.astype(BF), "dp", scatter_dimension=1, tiled=True).astype(F32),
+        lax.psum_scatter(g_qkv.astype(BF), "dp", scatter_dimension=1, tiled=True).astype(F32),
+        lax.psum_scatter(g_proj.astype(BF), "dp", scatter_dimension=1, tiled=True).astype(F32),
+        lax.psum_scatter(g_down.astype(BF), "dp", scatter_dimension=1, tiled=True).astype(F32),
     )
     return (
         low_out,

time: 1760 us -> 1500 us (0.85)
  waiting for transfers between devices: 1250 us -> 809 us
  Pallas kernels: 0 us -> 428 us
  other arithmetic: 200 us -> 68.5 us
  matrix products: 180 us -> 107 us
  blocking collectives: 42 us -> 0 us
    pallas_call x0 -> x4, Pallas kernels: none -> 428 us  [the longest x1 194 us: big_backward(): pl.pallas_call(kernel, out_shape=(jax.ShapeDtypeStruct((CHUNKS, rows, c),...]
    all_gather x9 -> x7, waiting for transfers between devices: 448 us -> 183 us  [spread(): lax.all_gather(for_sending(values), 'mp', axis=1, tiled=True)]
    reduce_scatter x9 -> x7, waiting for transfers between devices: 432 us -> 205 us  [collect(): lax.psum_scatter(for_sending(values), 'mp', scatter_dimension=1, tiled=True)]
    unnamed x28 -> x30, waiting for transfers between devices: 1.79 us -> 160 us
    psum x1 -> x2, waiting for transfers between devices: 132 us -> 54.3 us  [per_device(): packed = lax.psum(lax.psum(packed, 'mp'), 'dp')]
    dot_general x6 -> x2, matrix products: 108 us -> 33.2 us  [the longest x1 16.7 us: per_device(): jnp.einsum('tc,th->ch', normed_all, d_hidden, preferred_element_type=F32)]
    mul x1, other arithmetic: 79.7 us -> 6.49 us  [per_device(): d_hr_in = (d_branch + d_conv_in) * cell_mask]
    reduce_scatter x9 -> x4, waiting for transfers between devices: 229 us -> 187 us  [the longest x1 55.5 us: per_device(): lax.psum_scatter(g_cn_up.astype(BF), 'dp', scatter_dimension=0, tiled=True)]
  transfers between devices with their start and end apart: 32 -> 29, of which waited for: 25 -> 28; matrix products, arithmetic and copies ran while one was open for 14% -> 8% of each run, Pallas kernels for 0% -> 13%
where the time goes in v1:
time: 1500 us; the launch traced here: 1490 us
  waiting for transfers between devices  809 us (54%)
  Pallas kernels  428 us (29%)
  matrix products  107 us (7%)
  other arithmetic  68.5 us (5%)
  local copies, waits for them, and re-layouts  51.9 us (3%)
  between operations  15.5 us (1%)
    reduce_scatter x7, waiting for transfers between devices, collect(): lax.psum_scatter(for_sending(values), 'mp', scatter_dimension=1, tiled=True)  205 us
    pallas_call x1, Pallas kernels, big_backward(): pl.pallas_call(kernel, out_shape=(jax.ShapeDtypeStruct((CHUNKS, rows, c),...  194 us
    all_gather x7, waiting for transfers between devices, spread(): lax.all_gather(for_sending(values), 'mp', axis=1, tiled=True)  183 us
    pallas_call x1, Pallas kernels, big_forward(): pl.pallas_call(kernel, out_shape=(jax.ShapeDtypeStruct((CHUNKS, rows, c),...  179 us
    unnamed x30, waiting for transfers between devices  160 us
    reduce_scatter x1, waiting for transfers between devices, per_device(): lax.psum_scatter(g_cn_up.astype(BF), 'dp', scatter_dimension=0, tiled=True)  55.5 us
    psum x2, waiting for transfers between devices, per_device(): packed = lax.psum(lax.psum(packed, 'mp'), 'dp')  54.3 us
    reduce_scatter x1, waiting for transfers between devices, per_device(): lax.psum_scatter(g_cn_down.astype(BF), 'dp', scatter_dimension=1, tiled=T...  52.4 us
  transfers between devices with their start and end apart: 29, of which 28 were waited for; matrix products, arithmetic and copies ran while one was open for 8% of the time, Pallas kernels for 13%

profile of v1, /device:TPU:0, one launch (start us, length us, event | category | flops | bytes accessed | tf_op | source)
XLA Modules:
  0.0 1492.2 jit_solution(800177717877694587)
XLA Ops:
  11.9 5.7 collective-permute-start
  19.8 6.8 collective-permute-done
  26.6 4.7 collective-permute-done.1
  33.2 17.6 %shard_map.305 = f32[12,48,1536]{2,1,0:T(8,128)S(1)} custom-call(bf16[18,48,1536]{2,1,0:T(8,128)(2,1)S(1)} %maximum_bitcast_fusion.x_ref, f32[49,1,1536]{2,1,0:T(1,128)S(1)} %reshape.557.w_ref), custom_call_target="tpu_custom_call" | custom-call | tf_op jit(solution)/shard_map/pallas_call | solution.py:401
  54.5 179.4 %shard_map.306 = (f32[6,96,1536]{2,1,0:T(8,128)}, bf16[4,6,96,1536]{3,2,1,0:T(8,128)(2,1)}, bf16[4,6,96,1536]{3,2,1,0:T(8,128)(2,1)}, bf16[4,6,96,1536]{3,2,1,0:T(8,128)(2,1)}) custom-call(bf16[6,96,1536]{2,1,0:T(8,128)(2,1)} %bitcast.208, bf16[1536,1536]{1,0:T(8,128)(2,1)} %wu.3, bf16[1536,1536]{1,0:T(8,128)(2,1)} %wd.3), custom_call_target="tpu_custom_call" | custom-call | flops 21743271936 | bytes 28311552 | tf_op jit(solution)/shard_map/pallas_call | solution.py:270
  233.9 4.9 add_multiply_fusion.1
  238.8 5.3 reshape.538
  244.1 5.5 reduce_sum.174
  253.7 40.0 %all-gather.8.cloned.1.call-done = bf16[1,576,1536]{2,1,0:T(8,128)(2,1)} async-done(((bf16[1,144,1536]{2,1,0:T(8,128)(2,1)}), bf16[1,576,1536]{2,1,0:T(8,128)(2,1)}) %all-gather.8.cloned.1.call-update) | async-done | bytes 1769488 | tf_op jit(solution)/shard_map/all_gather | solution.py:467
  299.1 28.1 %reduce-scatter.27.cloned.1.call-done = bf16[1,144,1024]{2,1,0:T(8,128)(2,1)} async-done(((bf16[1,576,1024]{2,1,0:T(8,128)(2,1)}), bf16[1,144,1024]{2,1,0:T(8,128)(2,1)}) %reduce-scatter.27.cloned.1.call-update) | async-done | bytes 294928 | tf_op jit(solution)/shard_map/reduce_scatter | solution.py:475
  331.7 29.0 %all-gather.12.cloned.1.call-done = bf16[1,576,1024]{2,1,0:T(8,128)(2,1)} async-done(((bf16[1,144,1024]{2,1,0:T(8,128)(2,1)}), bf16[1,576,1024]{2,1,0:T(8,128)(2,1)}) %all-gather.12.cloned.1.call-update) | async-done | bytes 1179664 | tf_op jit(solution)/shard_map/all_gather | solution.py:467
  376.5 28.4 %reduce-scatter.29.cloned.1.call-done = bf16[1,144,1024]{2,1,0:T(8,128)(2,1)} async-done(((bf16[1,576,1024]{2,1,0:T(8,128)(2,1)}), bf16[1,144,1024]{2,1,0:T(8,128)(2,1)}) %reduce-scatter.29.cloned.1.call-update) | async-done | bytes 294928 | tf_op jit(solution)/shard_map/reduce_scatter | solution.py:475
  408.6 28.5 %all-gather.14.cloned.1.call-done = bf16[1,576,1024]{2,1,0:T(8,128)(2,1)} async-done(((bf16[1,144,1024]{2,1,0:T(8,128)(2,1)}), bf16[1,576,1024]{2,1,0:T(8,128)(2,1)}) %all-gather.14.cloned.1.call-update) | async-done | bytes 1179664 | tf_op jit(solution)/shard_map/all_gather | solution.py:467
  437.1 4.0 fusion.40
  441.1 27.1 %all-gather.16.cloned.1.call-done = bf16[1,576,1024]{2,1,0:T(8,128)(2,1)} async-done(((bf16[1,144,1024]{2,1,0:T(8,128)(2,1)}), bf16[1,576,1024]{2,1,0:T(8,128)(2,1)}) %all-gather.16.cloned.1.call-update) | async-done | bytes 1179664 | tf_op jit(solution)/shard_map/all_gather | solution.py:467
  468.2 5.3 fusion.9
  477.2 5.0 fusion.16
  482.6 23.0 %reduce-scatter.33.cloned.1.call-done = bf16[1,144,1024]{2,1,0:T(8,128)(2,1)} async-done(((bf16[1,576,1024]{2,1,0:T(8,128)(2,1)}), bf16[1,144,1024]{2,1,0:T(8,128)(2,1)}) %reduce-scatter.33.cloned.1.call-update) | async-done | bytes 294928 | tf_op jit(solution)/shard_map/reduce_scatter | solution.py:475
  506.9 29.5 %reduce-scatter.31.cloned.1.call-done = bf16[1,144,1024]{2,1,0:T(8,128)(2,1)} async-done(((bf16[1,576,1024]{2,1,0:T(8,128)(2,1)}), bf16[1,144,1024]{2,1,0:T(8,128)(2,1)}) %reduce-scatter.31.cloned.1.call-update) | async-done | bytes 294928 | tf_op jit(solution)/shard_map/reduce_scatter | solution.py:475
  539.4 29.2 %all-gather.18.cloned.1.call-done = bf16[1,576,1024]{2,1,0:T(8,128)(2,1)} async-done(((bf16[1,144,1024]{2,1,0:T(8,128)(2,1)}), bf16[1,576,1024]{2,1,0:T(8,128)(2,1)}) %all-gather.18.cloned.1.call-update) | async-done | bytes 1179664 | tf_op jit(solution)/shard_map/all_gather | solution.py:467
  570.7 4.7 convolution_convert_fusion.14
  575.4 4.4 multiply_reduce_fusion
  589.7 28.4 %reduce-scatter.35.cloned.1.call-done = bf16[1,144,1024]{2,1,0:T(8,128)(2,1)} async-done(((bf16[1,576,1024]{2,1,0:T(8,128)(2,1)}), bf16[1,144,1024]{2,1,0:T(8,128)(2,1)}) %reduce-scatter.35.cloned.1.call-update) | async-done | bytes 294928 | tf_op jit(solution)/shard_map/reduce_scatter | solution.py:475
  623.0 29.3 %all-gather.20.cloned.1.call-done = bf16[1,576,1024]{2,1,0:T(8,128)(2,1)} async-done(((bf16[1,144,1024]{2,1,0:T(8,128)(2,1)}), bf16[1,576,1024]{2,1,0:T(8,128)(2,1)}) %all-gather.20.cloned.1.call-update) | async-done | bytes 1179664 | tf_op jit(solution)/shard_map/all_gather | solution.py:467
  657.0 37.4 %reduce-scatter.39.cloned.1.call-done = bf16[1,144,1536]{2,1,0:T(8,128)(2,1)} async-done(((bf16[1,576,1536]{2,1,0:T(8,128)(2,1)}), bf16[1,144,1536]{2,1,0:T(8,128)(2,1)}) %reduce-scatter.39.cloned.1.call-update) | async-done | bytes 442384 | tf_op jit(solution)/shard_map/reduce_scatter | solution.py:475
  698.6 5.6 broadcast_in_dim.23
  707.8 194.4 %shard_map.307 = (f32[6,96,1536]{2,1,0:T(8,128)}, bf16[4,6,96,1536]{3,2,1,0:T(8,128)(2,1)}, bf16[4,6,96,1536]{3,2,1,0:T(8,128)(2,1)}) custom-call(bf16[6,96,1536]{2,1,0:T(8,128)(2,1)} %bitcast.207, bf16[4,6,96,1536]{3,2,1,0:T(8,128)(2,1)} %get-tuple-element.27.slopes, bf16[1536,1536]{1,0:T(8,128)(2,1)} %wu.3, bf16[1536,1536]{1,0:T(8,128)(2,1)} %wd.3), custom_call_target="tpu_custom_call" | custom-call | flops 21743271936 | bytes 28311552 | tf_op jit(solution)/shard_map/pallas_call | solution.py:351
  911.3 4.2 collective-permute-done.2
  915.5 4.7 collective-permute-done.3
  920.5 36.5 %shard_map.308 = (f32[12,48,1536]{2,1,0:T(8,128)S(1)}, f32[49,1,1536]{2,1,0:T(1,128)S(1)}) custom-call(bf16[18,48,1536]{2,1,0:T(8,128)(2,1)S(1)} %maximum_bitcast_fusion.1.d_ref, bf16[18,48,1536]{2,1,0:T(8,128)(2,1)S(1)} %copy-done.5, f32[49,1,1536]{2,1,0:T(1,128)S(1)} %reshape.557.w_ref), custom_call_target="tpu_custom_call" | custom-call | tf_op jit(solution)/shard_map/pallas_call | solution.py:430
  960.4 4.0 convolution_convert_fusion.2
  967.2 5.0 convolution_convert_fusion.3
  974.0 3.9 fusion.15
  991.9 7.0 all-reduce.3.cloned.1.call-done
  998.9 16.5 %bitcast_convert_fusion = bf16[1536,1536]{0,1:T(8,128)(2,1)} fusion(bf16[4,6,96,1536]{3,2,1,0:T(8,128)(2,1)} %get-tuple-element.33, bf16[4,6,96,1536]{3,2,1,0:T(8,128)(2,1)} %get-tuple-element.34), kind=kOutput, calls=%fused_computation | convolution fusion | flops 10873995264 | bytes 18874368 | tf_op jit(solution)/shard_map/th,tc->hc/dot_general | solution.py:637
  1015.8 16.7 %bitcast_convert_fusion.1 = bf16[1536,1536]{1,0:T(8,128)(2,1)} fusion(bf16[4,6,96,1536]{3,2,1,0:T(8,128)(2,1)} %get-tuple-element.31, bf16[4,6,96,1536]{3,2,1,0:T(8,128)(2,1)} %get-tuple-element.32), kind=kOutput, calls=%fused_computation.1 | convolution fusion | flops 10873995264 | bytes 18874368 | tf_op jit(solution)/shard_map/tc,th->ch/dot_general | solution.py:638
  1032.5 11.0 reduce-scatter.57.cloned.1.call-done
  1045.6 42.4 %reduce-scatter.47.cloned.1.call-done = bf16[128,1024]{1,0:T(8,128)(2,1)} async-done(((bf16[1024,1024]{1,0:T(8,128)(2,1)}), bf16[128,1024]{1,0:T(8,128)(2,1)}) %reduce-scatter.47.cloned.1.call-update) | async-done | bytes 262160 | tf_op jit(solution)/shard_map/reduce_scatter | solution.py:657
  1089.7 35.6 %reduce-scatter.55.cloned.1.call-done = bf16[128,256]{1,0:T(8,128)(2,1)} async-done(((bf16[1024,256]{1,0:T(8,128)(2,1)}), bf16[128,256]{1,0:T(8,128)(2,1)}) %reduce-scatter.55.cloned.1.call-update) | async-done | bytes 65552
  1127.0 40.0 %reduce-scatter.53.cloned.1.call-done = bf16[128,768]{1,0:T(8,128)(2,1)} async-done(((bf16[1024,768]{1,0:T(8,128)(2,1)}), bf16[128,768]{1,0:T(8,128)(2,1)}) %reduce-scatter.53.cloned.1.call-update) | async-done | bytes 196624
  1169.1 35.0 %reduce-scatter.51.cloned.1.call-done = bf16[128,256]{1,0:T(8,128)(2,1)} async-done(((bf16[1024,256]{1,0:T(8,128)(2,1)}), bf16[128,256]{1,0:T(8,128)(2,1)}) %reduce-scatter.51.cloned.1.call-update) | async-done | bytes 65552
  1205.1 37.0 %reduce-scatter.49.cloned.1.call-done = bf16[128,256]{1,0:T(8,128)(2,1)} async-done(((bf16[1024,256]{1,0:T(8,128)(2,1)}), bf16[128,256]{1,0:T(8,128)(2,1)}) %reduce-scatter.49.cloned.1.call-update) | async-done | bytes 65552
  1244.5 36.3 %reduce-scatter.45.cloned.1.call-done = bf16[192,256]{1,0:T(8,128)(2,1)} async-done(((bf16[1536,256]{1,0:T(8,128)(2,1)}), bf16[192,256]{1,0:T(8,128)(2,1)}) %reduce-scatter.45.cloned.1.call-update) | async-done | bytes 98320 | tf_op jit(solution)/shard_map/reduce_scatter | solution.py:656
  1282.4 30.5 %reduce-scatter.37.cloned.1.call-done = bf16[1,144,1024]{2,1,0:T(8,128)(2,1)} async-done(((bf16[1,576,1024]{2,1,0:T(8,128)(2,1)}), bf16[1,144,1024]{2,1,0:T(8,128)(2,1)}) %reduce-scatter.37.cloned.1.call-update) | async-done | bytes 294928 | tf_op jit(solution)/shard_map/reduce_scatter | solution.py:475
  1314.8 6.5 fusion.1
  1321.3 47.3 %all-reduce.5.cloned.1.call-done = f32[78848]{0:T(1024)} async-done(((f32[78848]{0:T(1024)}), f32[78848]{0:T(1024)}) %all-reduce.5.cloned.1.call-update) | async-done | bytes 315408 | tf_op jit(solution)/shard_map/psum | solution.py:647
  1372.9 52.4 %reduce-scatter.43.cloned.1.call-done = bf16[1536,192]{0,1:T(8,128)(2,1)} async-done(((bf16[1536,1536]{0,1:T(8,128)(2,1)}), bf16[1536,192]{0,1:T(8,128)(2,1)}) %reduce-scatter.43.cloned.1.call-update) | async-done | bytes 589840 | tf_op jit(solution)/shard_map/reduce_scatter | solution.py:660
  1427.5 55.5 %reduce-scatter.41.cloned.1.call-done = bf16[192,1536]{1,0:T(8,128)(2,1)} async-done(((bf16[1536,1536]{1,0:T(8,128)(2,1)}), bf16[192,1536]{1,0:T(8,128)(2,1)}) %reduce-scatter.41.cloned.1.call-update) | async-done | bytes 589840 | tf_op jit(solution)/shard_map/reduce_scatter | solution.py:654
  (275 shorter events, 137.5 us)
Async XLA Ops:
  7.2 429.9 %copy-start = (bf16[1024,1024]{1,0:T(8,128)(2,1)S(1)}, bf16[1024,1024]{1,0:T(8,128)(2,1)}, u32[]{:S(2)}) copy-start(bf16[1024,1024]{1,0:T(8,128)(2,1)} %param.32) | copy-start | bytes 6291460
  7.2 244.5 %all-gather.10.cloned.1.call-start = ((), (), s32[]{:S(2)}) async-start(), calls=%async_computation.17 | async-start | bytes 1474560 | tf_op jit(solution)/shard_map/all_gather | solution.py:467
  8.1 10.8 copy-start.49
  8.1 10.9 copy-start.48
  8.1 11.2 copy-start.47
  11.9 14.6 collective-permute-start
  17.6 13.6 collective-permute-start.1
  18.9 274.7 %all-gather.8.cloned.1.call-start = ((), (), s32[]{:S(2)}) async-start(), calls=%async_computation.16 | async-start | bytes 2211840 | tf_op jit(solution)/shard_map/all_gather | solution.py:467
  33.2 17.6 %copy-start.4 = (bf16[18,48,1536]{2,1,0:T(8,128)(2,1)}, bf16[18,48,1536]{2,1,0:T(8,128)(2,1)S(1)}, u32[]{:S(2)}) copy-start(bf16[18,48,1536]{2,1,0:T(8,128)(2,1)S(1)} %maximum_bitcast_fusion.x_ref) | copy-start | bytes 7962628
  251.7 75.6 %reduce-scatter.27.cloned.1.call-start = ((), (), s32[]{:S(2)}) async-start(), calls=%async_computation.18 | async-start | bytes 1474560 | tf_op jit(solution)/shard_map/reduce_scatter | solution.py:475
  253.6 40.0 %copy-start.16 = (f32[576,256]{1,0:T(8,128)}, f32[576,256]{1,0:T(8,128)S(1)}, u32[]{:S(2)}) copy-start(f32[576,256]{1,0:T(8,128)S(1)} %fusion.25) | copy-start | bytes 1769476
  296.8 30.4 %copy-start.9 = (bf16[1,144,1024]{2,1,0:T(8,128)(2,1)S(1)}, bf16[1,144,1024]{2,1,0:T(8,128)(2,1)}, u32[]{:S(2)}) copy-start(bf16[1,144,1024]{2,1,0:T(8,128)(2,1)} %param.19) | copy-start | bytes 884740
  299.0 61.7 %all-gather.12.cloned.1.call-start = ((), (), s32[]{:S(2)}) async-start(), calls=%async_computation.19 | async-start | bytes 1474560 | tf_op jit(solution)/shard_map/all_gather | solution.py:467
  331.4 73.5 %reduce-scatter.29.cloned.1.call-start = ((), (), s32[]{:S(2)}) async-start(), calls=%async_computation.20 | async-start | bytes 1474560 | tf_op jit(solution)/shard_map/reduce_scatter | solution.py:475
  374.2 30.7 %copy-start.12 = (bf16[1,144,1024]{2,1,0:T(8,128)(2,1)S(1)}, bf16[1,144,1024]{2,1,0:T(8,128)(2,1)}, u32[]{:S(2)}) copy-start(bf16[1,144,1024]{2,1,0:T(8,128)(2,1)} %reduce-scatter.27.cloned.1.call-done) | copy-start | bytes 884740
  376.5 60.6 %all-gather.14.cloned.1.call-start = ((), (), s32[]{:S(2)}) async-start(), calls=%async_computation.21 | async-start | bytes 1474560 | tf_op jit(solution)/shard_map/all_gather | solution.py:467
  407.8 60.5 %all-gather.16.cloned.1.call-start = ((), (), s32[]{:S(2)}) async-start(), calls=%async_computation.23 | async-start | bytes 1474560 | tf_op jit(solution)/shard_map/all_gather | solution.py:467
  408.5 97.0 %reduce-scatter.33.cloned.1.call-start = ((), (), s32[]{:S(2)}) async-start(), calls=%async_computation.24 | async-start | bytes 1474560 | tf_op jit(solution)/shard_map/reduce_scatter | solution.py:475
  477.1 28.5 %copy-start.11 = (f32[1,144,1024]{2,1,0:T(8,128)S(1)}, f32[1,144,1024]{2,1,0:T(8,128)}, u32[]{:S(2)}) copy-start(f32[1,144,1024]{2,1,0:T(8,128)} %copy-done.10) | copy-start | bytes 1769476
  477.1 59.3 %reduce-scatter.31.cloned.1.call-start = ((), (), s32[]{:S(2)}) async-start(), calls=%async_computation.22 | async-start | bytes 1474560 | tf_op jit(solution)/shard_map/reduce_scatter | solution.py:475
  482.1 56.4 %copy-start.26 = (bf16[1,144,1024]{2,1,0:T(8,128)(2,1)S(1)}, bf16[1,144,1024]{2,1,0:T(8,128)(2,1)}, u32[]{:S(2)}) copy-start(bf16[1,144,1024]{2,1,0:T(8,128)(2,1)} %param.34) | copy-start | bytes 884740
  482.2 86.5 %copy-start.39 = (bf16[256,1024]{1,0:T(8,128)(2,1)S(1)}, bf16[256,1024]{1,0:T(8,128)(2,1)}, u32[]{:S(2)}) copy-start(bf16[256,1024]{1,0:T(8,128)(2,1)} %param.30) | copy-start | bytes 1572868
  482.2 86.5 %all-gather.18.cloned.1.call-start = ((), (), s32[]{:S(2)}) async-start(), calls=%async_computation.25 | async-start | bytes 1474560 | tf_op jit(solution)/shard_map/all_gather | solution.py:467
  539.4 78.7 %reduce-scatter.35.cloned.1.call-start = ((), (), s32[]{:S(2)}) async-start(), calls=%async_computation.26 | async-start | bytes 1474560 | tf_op jit(solution)/shard_map/reduce_scatter | solution.py:475
  589.6 31.1 %copy-start.27 = (bf16[1,144,1024]{2,1,0:T(8,128)(2,1)S(1)}, bf16[1,144,1024]{2,1,0:T(8,128)(2,1)}, u32[]{:S(2)}) copy-start(bf16[1,144,1024]{2,1,0:T(8,128)(2,1)} %param.34) | copy-start | bytes 884740
  589.6 62.7 %copy-start.17 = (f32[576,256]{1,0:T(8,128)S(1)}, f32[576,256]{1,0:T(8,128)}, u32[]{:S(2)}) copy-start(f32[576,256]{1,0:T(8,128)} %copy-done.16) | copy-start | bytes 1769476
  589.6 62.7 %copy-start.18 = (f32[576,256]{1,0:T(8,128)S(1)}, f32[576,256]{1,0:T(8,128)}, u32[]{:S(2)}) copy-start(f32[576,256]{1,0:T(8,128)} %get-tuple-element.113) | copy-start | bytes 1769476
  589.6 62.6 %all-gather.20.cloned.1.call-start = ((), (), s32[]{:S(2)}) async-start(), calls=%async_computation.27 | async-start | bytes 1474560 | tf_op jit(solution)/shard_map/all_gather | solution.py:467
  622.9 32.0 %copy-start.19 = (bf16[1536,256]{1,0:T(8,128)(2,1)S(1)}, bf16[1536,256]{1,0:T(8,128)(2,1)}, u32[]{:S(2)}) copy-start(bf16[1536,256]{1,0:T(8,128)(2,1)} %param.26) | copy-start | bytes 2359300
  622.9 71.5 %reduce-scatter.39.cloned.1.call-start = ((), (), s32[]{:S(2)}) async-start(), calls=%async_computation.29 | async-start | bytes 2211840 | tf_op jit(solution)/shard_map/reduce_scatter | solution.py:475
  654.9 40.7 %copy-start.36 = (bf16[576,256]{1,0:T(8,128)(2,1)}, bf16[576,256]{1,0:T(8,128)(2,1)S(1)}, u32[]{:S(2)}) copy-start(bf16[576,256]{1,0:T(8,128)(2,1)S(1)} %get-tuple-element.102) | copy-start | bytes 884740
  656.8 342.1 %all-reduce.3.cloned.1.call-start = ((), (), s32[]{:S(2)}) async-start(), calls=%async_computation.30 | async-start | bytes 630784 | tf_op jit(solution)/shard_map/psum | solution.py:647
  707.8 194.4 %copy-start.3 = (f32[12,48,1536]{2,1,0:T(8,128)S(1)}, f32[12,48,1536]{2,1,0:T(8,128)}, u32[]{:S(2)}) copy-start(f32[12,48,1536]{2,1,0:T(8,128)} %copy-done.2) | copy-start | bytes 10616836
  908.4 7.1 collective-permute-start.2
  909.7 10.5 collective-permute-start.3
  960.3 83.2 %reduce-scatter.57.cloned.1.call-start = ((), (), s32[]{:S(2)}) async-start(), calls=%async_computation.40 | async-start | bytes 2359296
  967.0 121.0 %reduce-scatter.47.cloned.1.call-start = ((), (), s32[]{:S(2)}) async-start(), calls=%async_computation.35 | async-start | bytes 2359296 | tf_op jit(solution)/shard_map/reduce_scatter | solution.py:657
  972.2 153.1 %reduce-scatter.55.cloned.1.call-start = ((), (), s32[]{:S(2)}) async-start(), calls=%async_computation.39 | async-start | bytes 589824
  973.9 193.0 %reduce-scatter.53.cloned.1.call-start = ((), (), s32[]{:S(2)}) async-start(), calls=%async_computation.38 | async-start | bytes 1769472
  982.5 221.7 %reduce-scatter.51.cloned.1.call-start = ((), (), s32[]{:S(2)}) async-start(), calls=%async_computation.37 | async-start | bytes 589824
  985.5 256.6 %reduce-scatter.49.cloned.1.call-start = ((), (), s32[]{:S(2)}) async-start(), calls=%async_computation.36 | async-start | bytes 589824
  988.5 292.4 %reduce-scatter.45.cloned.1.call-start = ((), (), s32[]{:S(2)}) async-start(), calls=%async_computation.34 | async-start | bytes 884736 | tf_op jit(solution)/shard_map/reduce_scatter | solution.py:656
  990.3 322.7 %reduce-scatter.37.cloned.1.call-start = ((), (), s32[]{:S(2)}) async-start(), calls=%async_computation.28 | async-start | bytes 1474560 | tf_op jit(solution)/shard_map/reduce_scatter | solution.py:475
  991.9 376.7 %all-reduce.5.cloned.1.call-start = ((), (), s32[]{:S(2)}) async-start(), calls=%async_computation.31 | async-start | bytes 630784 | tf_op jit(solution)/shard_map/psum | solution.py:647
  998.9 426.4 %reduce-scatter.43.cloned.1.call-start = ((), (), s32[]{:S(2)}) async-start(), calls=%async_computation.33 | async-start | bytes 5308416 | tf_op jit(solution)/shard_map/reduce_scatter | solution.py:660
  1015.5 467.5 %reduce-scatter.41.cloned.1.call-start = ((), (), s32[]{:S(2)}) async-start(), calls=%async_computation.32 | async-start | bytes 5308416 | tf_op jit(solution)/shard_map/reduce_scatter | solution.py:654
  1043.6 269.4 %copy-start.28 = (f32[1,144,1024]{2,1,0:T(8,128)S(1)}, f32[1,144,1024]{2,1,0:T(8,128)}, u32[]{:S(2)}) copy-start(f32[1,144,1024]{2,1,0:T(8,128)} %get-tuple-element.93) | copy-start | bytes 1769476
  1314.8 170.5 %copy-start.1 = (bf16[1024,1024]{1,0:T(8,128)(2,1)S(1)}, bf16[1024,1024]{1,0:T(8,128)(2,1)}, u32[]{:S(2)}) copy-start(bf16[1024,1024]{1,0:T(8,128)(2,1)} %param.32) | copy-start | bytes 6291460
  (36 other events, 112.5 us)
Sparse Core Ops, SparseCore 0:
  19.0 32.7 all-gather.9
  251.8 41.7 all-gather.7
  299.1 28.0 reduce-scatter.26
  331.5 29.1 all-gather.11
  376.6 28.2 reduce-scatter.28
  407.9 29.1 all-gather.13
  438.6 29.5 all-gather.15
  477.2 28.2 reduce-scatter.32
  508.5 27.8 reduce-scatter.30
  539.5 29.1 all-gather.17
  589.7 28.2 reduce-scatter.34
  623.1 29.1 all-gather.19
  656.9 37.4 reduce-scatter.38
  960.4 38.3 all-reduce.2
  1002.4 41.1 reduce-scatter.56
  1046.7 41.1 reduce-scatter.46
  1091.2 34.1 reduce-scatter.54
  1128.5 38.4 reduce-scatter.52
  1170.0 34.0 reduce-scatter.50
  1207.9 34.1 reduce-scatter.48
  1245.8 34.9 reduce-scatter.44
  1283.7 29.1 reduce-scatter.36
  1316.0 52.4 all-reduce.4
  1371.9 53.3 reduce-scatter.42
  1429.1 53.8 reduce-scatter.40

commit v2 on v1

--- a/solution.py
+++ b/solution.py
@@ -30,8 +30,73 @@
     return 0.5 * x * (1.0 + t)
 
 
+def dp_bit(position):
+    return lax.rem(lax.axis_index("dp") // 2**position, 2)
+
+
+def dp_mate(position):
+    return lax.axis_index("dp") + 2**position * (1 - 2 * dp_bit(position))
+
+
+class Halving:
+    def __init__(self, bits, lasts, shape, block):
+        self.lasts, self.shape, self.block = lasts, shape, block
+        left = list(bits)
+        self.bits = [left.pop(0 if last else -1) for last in lasts]
+
+    def split(self, count, p):
+        if count == 1:
+            return (1, 1)
+        return (count // 2, 2) if self.lasts[p] else (2, count // 2)
+
+    def buffers(self):
+        count, rows, cols = self.shape
+        got, held = [], []
+        for p in range(len(self.bits)):
+            count //= 2
+            got.append(jax.ShapeDtypeStruct((count, rows, cols), BF))
+            held.append(jax.ShapeDtypeStruct(self.split(count, p + 1) + (rows, cols), BF))
+        return got + held
+
+    def semaphores(self):
+        return [pltpu.SemaphoreType.DMA((len(self.bits),))] * 2
+
+    def bind(self, first, buffers, send, recv):
+        steps = len(self.bits)
+        self.now = [first] + list(buffers[steps:])
+        self.got, self.send, self.recv = buffers[:steps], send, recv
+
+    def part(self, p, mine):
+        bit = dp_bit(self.bits[p])
+        index = bit if mine else 1 - bit
+        return self.now[p].at[:, index] if self.lasts[p] else self.now[p].at[index]
+
+    def copy(self, p):
+        return pltpu.make_async_remote_copy(
+            src_ref=self.part(p, False), dst_ref=self.got[p], send_sem=self.send.at[p], recv_sem=self.recv.at[p],
+            device_id={"dp": dp_mate(self.bits[p])}, device_id_type=MESH,
+        )
+
+    def start(self, p):
+        self.copy(p).start()
+
+    def finish(self, p):
+        self.copy(p).wait()
+        count, rows, cols = self.got[p].shape
+        ways = self.split(count, p + 1)
+
+        def add(a, b, out):
+            out[...] = (a[...].astype(F32) + b[...].astype(F32)).astype(BF).reshape(out.shape)
+
+        flat = pl.BlockSpec((1, rows, self.block), lambda k, c: (k, 0, c))
+        paired = pl.BlockSpec((1, 1, rows, self.block), lambda k, c: (k // ways[1], lax.rem(k, ways[1]), 0, c))
+        pltpu.emit_pipeline(add, grid=(count, cols // self.block), in_specs=[flat, flat], out_specs=[paired])(
+            self.part(p, True), self.got[p], self.now[p + 1]
+        )
+
+
 def chain_exchange(n, chunks, lag, own_hbm, gathered, partial, travel, compute, result_hbm,
-                   sems, prepare, arrived):
+                   sems, prepare, arrived, mates=(), begin=None, turn=None):
     ag_send, ag_recv, rs_send, rs_recv, local_sem = sems
     d = lax.axis_index("mp")
     has_left, has_right = d > 0, d < n - 1
@@ -46,10 +111,15 @@
     def _():
         pl.semaphore_signal(barrier, inc=1, device_id={"mp": d + 1}, device_id_type=MESH)
 
+    for mate in mates:
+        pl.semaphore_signal(barrier, inc=1, device_id={"dp": mate}, device_id_type=MESH)
+
     load = pltpu.make_async_copy(own_hbm, gathered.at[d], local_sem)
     load.start()
 
-    pl.semaphore_wait(barrier, has_left.astype(jnp.int32) + has_right.astype(jnp.int32))
+    pl.semaphore_wait(barrier, has_left.astype(jnp.int32) + has_right.astype(jnp.int32) + len(mates))
+    if begin is not None:
+        begin()
     load.wait()
 
     def ag(way, s, j):
@@ -82,6 +152,8 @@
 
     def step(g, _):
         k, j = g // chunks, lax.rem(g, chunks)
+        if turn is not None:
+            turn(g)
 
         @pl.when(g < n * chunks)
         def _():
@@ -296,15 +368,41 @@
     )
 
 
-def big_backward(d, slope_all, w_up, w_down, n):
+def big_backward(d, slope_all, w_up, w_down, grads, n, devices):
     t, c = d.shape
     h = w_up.shape[1]
     rows = t // CHUNKS
-
-    def kernel(
-        d_ref, slopes, wu, wd, out, d_all, h_all,
-        gathered, partial, travel, slope, grad, copied, stored, *sems
-    ):
+    pairs, g_rows, g_cols = grads.shape
+    bits = range(1, devices.bit_length() - 1)
+    split = g_cols // 2
+    steps = len(bits)
+    plans = [Halving(bits, [last] * steps, (pairs, g_rows, split), min(split, 1024)) for last in (True, False)]
+
+    def kernel(d_ref, slopes, wu, wd, g_first, g_second, out, d_all, h_all, *rest):
+        extra, rest = rest[: 4 * steps], rest[4 * steps :]
+        gathered, partial, travel, slope, grad, copied, stored, send0, recv0, send1, recv1 = rest[:11]
+        sems = rest[11:]
+        plans[0].bind(g_first.at[:, :, :, pl.ds(0, split)], extra[: 2 * steps], send0, recv0)
+        plans[1].bind(g_second.at[:, :, :, pl.ds(split, split)], extra[2 * steps :], send1, recv1)
+
+        def begin():
+            for plan in plans:
+                plan.start(0)
+
+        def pass_on(p):
+            for plan in plans:
+                plan.finish(p)
+            if p + 1 < steps:
+                for plan in plans:
+                    plan.start(p + 1)
+
+        total = n * CHUNKS + n - 1
+        due = [total * (2 ** steps - 2 ** (steps - 1 - p)) * 8 // (10 * (2 ** steps - 1)) for p in range(steps)]
+
+        def turn(g):
+            for p in range(steps - 1):
+                pl.when(g == due[p])(lambda p=p: pass_on(p))
+
         def d_copy(s, j):
             return pltpu.make_async_copy(gathered.at[s, j], d_all.at[s, j], copied.at[s, j])
 
@@ -342,24 +440,29 @@
             keep.wait()
 
         chain_exchange(
-            n, CHUNKS, 1, d_ref, gathered, partial, travel, compute, out, sems, prepare, arrived
+            n, CHUNKS, 1, d_ref, gathered, partial, travel, compute, out, sems, prepare, arrived,
+            [dp_mate(b) for b in bits], begin, turn
         )
+        pass_on(steps - 1)
         drain_copies(n, d_copy)
 
     whole = pl.BlockSpec(memory_space=pl.ANY)
     local = pl.BlockSpec(memory_space=pltpu.VMEM)
-    out, d_all, h_all = pl.pallas_call(
+    out, d_all, h_all, *extra = pl.pallas_call(
         kernel,
         out_shape=(
             jax.ShapeDtypeStruct((CHUNKS, rows, c), F32),
             jax.ShapeDtypeStruct((n, CHUNKS, rows, c), BF),
             jax.ShapeDtypeStruct((n, CHUNKS, rows, h), BF),
+            *plans[0].buffers(),
+            *plans[1].buffers(),
         ),
-        in_specs=[whole, whole, local, local],
-        out_specs=(whole,) * 3,
+        in_specs=[whole, whole, local, local, whole, whole],
+        out_specs=(whole,) * (3 + 4 * steps),
         scratch_shapes=chunk_buffers(n, rows, c, F32)
         + [pltpu.VMEM((rows, h), BF)] * 2
         + [pltpu.SemaphoreType.DMA((n, CHUNKS)), pltpu.SemaphoreType.DMA((2,))]
+        + plans[0].semaphores() + plans[1].semaphores()
         + chain_sems(n, CHUNKS),
         compiler_params=pltpu.CompilerParams(
             collective_id=1, has_side_effects=True, vmem_limit_bytes=60 * MIB
@@ -367,8 +470,12 @@
         cost_estimate=pl.CostEstimate(
             flops=4 * n * t * c * h, bytes_accessed=8 * n * t * c, transcendentals=0
         ),
-    )(d.reshape(CHUNKS, rows, c), slope_all.reshape(n, CHUNKS, rows, h), w_up, w_down)
-    return out.reshape(t, c), d_all.reshape(n * t, c), h_all.reshape(n * t, h)
+    )(
+        d.reshape(CHUNKS, rows, c), slope_all.reshape(n, CHUNKS, rows, h), w_up, w_down,
+        grads.reshape(pairs // 2, 2, g_rows, g_cols), grads.reshape(2, pairs // 2, g_rows, g_cols),
+    )
+    sums = [extra[2 * steps - 1].reshape(g_rows, split), extra[4 * steps - 1].reshape(g_rows, split)]
+    return out.reshape(t, c), d_all.reshape(n * t, c), h_all.reshape(n * t, h), sums
 
 
 def frame(dst, src):
@@ -408,37 +515,467 @@
     )(x, w)
 
 
-def conv_backward(d, x, w, size, group=2, bgroup=2):
+def conv_backward(d, x, w, size, grads, devices, group=4, bgroup=4):
     high, cols, c = x.shape
     rows = high - size + 1
     reach = size // 2
-    def kernel(d_ref, x_ref, w_ref, out, g, dframed, xframed):
+    steps = devices.bit_length() - 1
+    shape = grads[0].shape
+    plans = [Halving(range(steps), [True] + [last] * (steps - 1), shape, shape[2]) for last in (True, False)]
+    blocks = c // LANES
+    due = [blocks * (p + 1) // (steps + 1) for p in range(steps)]
+
+    def kernel(d_ref, x_ref, w_ref, g0, g1, out, g, *rest):
+        extra, rest = rest[: 4 * steps], rest[4 * steps :]
+        dframed, xframed, *sems = rest
+        plans[0].bind(g0, extra[: 2 * steps], sems[0], sems[1])
+        plans[1].bind(g1, extra[2 * steps :], sems[2], sems[3])
+        i = pl.program_id(0)
+
+        @pl.when(i == 0)
+        def _():
+            barrier = pltpu.get_barrier_semaphore()
+            for b in range(steps):
+                pl.semaphore_signal(barrier, inc=1, device_id={"dp": dp_mate(b)}, device_id_type=MESH)
+            pl.semaphore_wait(barrier, steps)
+            for plan in plans:
+                plan.start(0)
+
+        for p in range(steps - 1):
+            @pl.when(i == due[p])
+            def _():
+                for plan in plans:
+                    plan.finish(p)
+                for plan in plans:
+                    plan.start(p + 1)
+
         frame(dframed, d_ref)
         frame(xframed, x_ref)
         correlate(out, dframed, w_ref, size, True, group)
         for a in range(size):
             def some(r, accs):
-                dv = dframed[pl.ds(reach + r * bgroup, bgroup), EDGE:EDGE + cols]
+                dv = dframed[pl.ds(reach + r * bgroup, bgroup), EDGE : EDGE + cols]
                 new = []
                 for b in range(size):
                     prod = dv * xframed[pl.ds(r * bgroup + a, bgroup), pl.ds(EDGE - reach + b, cols), :]
                     new.append(accs[b] + jnp.sum(prod.reshape(-1, 8, LANES), axis=0))
                 return tuple(new)
-            accs = lax.fori_loop(0, rows // bgroup, some, tuple(jnp.zeros((8, LANES), F32) for _ in range(size)))
+
+            accs = lax.fori_loop(
+                0, rows // bgroup, some, tuple(jnp.zeros((8, LANES), F32) for _ in range(size))
+            )
             for b in range(size):
                 g[a * size + b] = jnp.sum(accs[b], axis=0, keepdims=True)
+
+        @pl.when(i == blocks - 1)
+        def _():
+            for plan in plans:
+                plan.finish(steps - 1)
+
+    whole = pl.BlockSpec(memory_space=pl.ANY)
+    d_in, g, *extra = pl.pallas_call(
+        kernel,
+        grid=(blocks,),
+        out_shape=(
+            jax.ShapeDtypeStruct((rows, cols, c), F32),
+            jax.ShapeDtypeStruct((size * size, 1, c), F32),
+            *plans[0].buffers(),
+            *plans[1].buffers(),
+        ),
+        in_specs=[pl.BlockSpec((high, cols, LANES), lambda i: (0, 0, i))] * 2
+        + [pl.BlockSpec((size * size, 1, LANES), lambda i: (0, 0, i)), whole, whole],
+        out_specs=(
+            pl.BlockSpec((rows, cols, LANES), lambda i: (0, 0, i)),
+            pl.BlockSpec((size * size, 1, LANES), lambda i: (0, 0, i)),
+        )
+        + (whole,) * (4 * steps),
+        scratch_shapes=[pltpu.VMEM((high, cols + 2 * EDGE, LANES), F32)] * 2
+        + plans[0].semaphores() + plans[1].semaphores(),
+        compiler_params=pltpu.CompilerParams(
+            collective_id=3, has_side_effects=True, vmem_limit_bytes=40 * MIB
+        ),
+    )(
+        d, x, w, grads[0].reshape((shape[0] // 2, 2) + shape[1:]), grads[1].reshape((shape[0] // 2, 2) + shape[1:])
+    )
+    return d_in, g, [extra[2 * steps - 1].reshape(shape[1:]), extra[4 * steps - 1].reshape(shape[1:])]
+
+
+GATE, OUT, HIGH_A, HIGH_B, QUERY, KEY, VALUE, PROJ = range(8)
+L_LOW, L_DF, L_POOL_A, L_POOL_B, L_FIRST, L_DA, L_SECOND, L_COT = range(8)
+R_DGATE, R_MERGE, R_DHIGH, R_DQ, R_DK, R_DV, R_ATT, R_DUP, R_ACT = range(9)
+
+
+def nn(a, b):
+    return jnp.dot(a, b, preferred_element_type=F32)
+
+
+def nt(a, b):
+    return lax.dot_general(a, b, (((1,), (1,)), ((), ())), preferred_element_type=F32)
+
+
+def tn(a, b):
+    return lax.dot_general(a, b, (((0,), (0,)), ((), ())), preferred_element_type=F32)
+
+
+def normalise(x, gain):
+    centred = x - jnp.mean(x, -1, keepdims=True)
+    rate = lax.rsqrt(jnp.mean(centred * centred, -1, keepdims=True) + 1e-06)
+    return centred * rate * gain
+
+
+def normalise_back(x, gain, d):
+    centred = x - jnp.mean(x, -1, keepdims=True)
+    rate = lax.rsqrt(jnp.mean(centred * centred, -1, keepdims=True) + 1e-06)
+    hat = centred * rate
+    dg = d * gain
+    back = rate * (dg - jnp.mean(dg, -1, keepdims=True) - hat * jnp.mean(dg * hat, -1, keepdims=True))
+    return back, jnp.sum(d * hat, axis=0, keepdims=True)
+
+
+def low_stage(low, pool_a, pool_b, cot, gain1, gain2, w1, w2, n, devices, cid):
+    t, dim = low.shape
+    every = n * t
+    width = dim // n
+    heads = width // HEAD
+    pairs = devices // 2
+    rows = dim // devices
+    half = dim // 2
+    ff = 4 * dim
+    scale = HEAD ** (-0.5)
+
+    def kernel(
+        low_ref, pool_a_ref, pool_b_ref, cot_ref, gain1_ref, gain2_ref, w1_hbm, w2_hbm,
+        low_out, d_low, d_pool_a, d_pool_b, g_ln1, g_ln2, grads,
+        wv, lhs, lhs2, rhs, gate, high, merged, resid, d_res, slope, mixed, heads_in, att_all, d_att, d_mixed,
+        d_heads, probs, d_scores, stage, w_sem, q_send, q_got, a_send, a_got, b_send, b_got, c_send, c_got, own_sem,
+        l_send, l_got, r_send, r_got, stage_sem,
+    ):
+        d = lax.axis_index("mp")
+        dp = lax.axis_index("dp")
+        core = lax.rem(dp, 2)
+        mate = dp + 1 - 2 * core
+        barrier = pltpu.get_barrier_semaphore()
+        for k in range(1, n):
+            pl.semaphore_signal(barrier, inc=1, device_id={"mp": lax.rem(d + k, n)}, device_id_type=MESH)
+        pl.semaphore_signal(barrier, inc=1, device_id={"dp": mate}, device_id_type=MESH)
+
+        def w_copy(p, c):
+            src = (w1_hbm if p < 4 else w2_hbm).at[:, c, :, pl.ds((p % 4) * 2 * dim, 2 * dim)]
+            return pltpu.make_async_copy(src, wv.at[c, :, :, pl.ds(p * 2 * dim, 2 * dim)], w_sem.at[p, c])
+
+        for p in range(8):
+            for c in range(2):
+                w_copy(p, c).start()
+
+        def w_wait(p):
+            for c in range(2):
+                w_copy(p, c).wait()
+
+        def w_cols(at, size):
+            return wv[:, :, :, pl.ds(at, size)].reshape(dim, size)
+
+        def forward(x, first, count, put):
+            def one(i, _):
+                put(pl.multiple_of(i * TILE, TILE), nn(x, w_cols(pl.multiple_of(first * dim + i * TILE, TILE), TILE)))
+                return 0
+            lax.fori_loop(0, count * dim // TILE, one, 0)
+
+        def backward(get, first, count, dst, fresh):
+            def one(i, _):
+                for c in range(2):
+                    part = wv[c, :, :, pl.ds(pl.multiple_of((first + i) * dim, dim), dim)].reshape(half, dim)
+                    y = nt(get(pl.multiple_of(i * dim, dim)), part)
+                    cols = slice(c * half, (c + 1) * half)
+                    if fresh and count == 1:
+                        dst[:, cols] = y
+                    else:
+                        dst[:, cols] += y
+                return 0
+            if fresh and count > 1:
+                dst[...] = jnp.zeros(dst.shape, F32)
+            if count == 1:
+                one(0, 0)
+            else:
+                lax.fori_loop(0, count, one, 0)
+
+        def r_cols(block, count=1):
+            return pl.ds(block * dim, count * dim)
+
+        def r_at(block):
+            return block * dim if block <= R_DUP else block * dim + 3 * dim
+
+        def r_copy(block):
+            cols = pl.ds(r_at(block), dim if block < R_DUP else ff)
+            return pltpu.make_async_remote_copy(
+                src_ref=rhs.at[0, :, cols], dst_ref=rhs.at[1, :, cols], send_sem=r_send.at[block],
+                recv_sem=r_got.at[block], device_id={"dp": mate}, device_id_type=MESH)
+
+        def l_copy(i):
+            return pltpu.make_async_remote_copy(
+                src_ref=lhs.at[i, :, pl.ds(pl.multiple_of((1 - core) * half, half), half)], dst_ref=lhs2.at[i],
+                send_sem=l_send.at[i], recv_sem=l_got.at[i], device_id={"dp": mate}, device_id_type=MESH)
+
+        stage_count = [0]
+
+        def grad(i, block, at, count, shared=False):
+            if not shared:
+                r_copy(block).wait_recv()
+            own_l = pl.ds(pl.multiple_of(core * half, half), half)
+
+            def out_copy(slot, k):
+                return pltpu.make_async_copy(
+                    stage.at[slot], grads.at[:, :, pl.ds(at * dim + k * TILE, TILE)], stage_sem.at[slot])
+
+            for k in range(count * dim // TILE):
+                slot = stage_count[0] % 2
+                if stage_count[0] >= 2:
+                    out_copy(slot, k).wait()
+                stage_count[0] += 1
+                cols = pl.ds(r_at(block) + k * TILE, TILE)
+                y = tn(lhs[i, :, own_l], rhs[0, :, cols]) + tn(lhs2[i], rhs[1, :, cols])
+                stage[slot] = y.astype(BF).reshape(pairs, rows, TILE)
+                out_copy(slot, k).start()
+
+        def to_heads(k, src, dst, send, got):
+            out = []
+            for step in range(1, n):
+                peer = lax.rem(d + step, n)
+                out.append(pltpu.make_async_remote_copy(
+                    src_ref=src.at[:, pl.ds(pl.multiple_of(peer * width, width), width)],
+                    dst_ref=dst.at[pl.ds(pl.multiple_of(d * t, t), t)],
+                    send_sem=send.at[k, step], recv_sem=got.at[k, step], device_id={"mp": peer}, device_id_type=MESH))
+            out.append(pltpu.make_async_copy(
+                src.at[:, pl.ds(pl.multiple_of(d * width, width), width)], dst.at[pl.ds(pl.multiple_of(d * t, t), t)], own_sem.at[k]))
+            return out
+
+        def to_tokens(k, src, dst, send, got):
+            out = []
+            for step in range(1, n):
+                peer = lax.rem(d + step, n)
+                out.append(pltpu.make_async_remote_copy(
+                    src_ref=src.at[pl.ds(pl.multiple_of(peer * t, t), t)],
+                    dst_ref=dst.at[:, pl.ds(pl.multiple_of(d * width, width), width)],
+                    send_sem=send.at[k, step], recv_sem=got.at[k, step], device_id={"mp": peer}, device_id_type=MESH))
+            out.append(pltpu.make_async_copy(
+                src.at[pl.ds(pl.multiple_of(d * t, t), t)], dst.at[:, pl.ds(pl.multiple_of(d * width, width), width)], own_sem.at[k]))
+            return out
+
+        def start(copies):
+            for c in copies:
+                c.start()
+
+        def wait(copies):
+            for c in copies:
+                c.wait()
+
+        lhs[L_LOW] = low_ref[...]
+        lhs[L_POOL_A] = pool_a_ref[...]
+        lhs[L_POOL_B] = pool_b_ref[...]
+        lhs[L_COT] = cot_ref[...]
+        acc = d_low
+        w_wait(0)
+
+        def put_gate(at, y):
+            gate[:, pl.ds(at, TILE)] = 1.0 / (1.0 + jnp.exp(-y))
+        forward(lhs[L_LOW], GATE, 1, put_gate)
+        w_wait(1)
+
+        def put_high(at, y):
+            high[:, pl.ds(at, TILE)] = y
+        forward(lhs[L_POOL_A], HIGH_A, 1, put_high)
+
+        def put_merging(at, y):
+            cols = pl.ds(at, TILE)
+            total = high[:, cols] + y
+            high[:, cols] = total
+            rhs[0, :, pl.ds(R_MERGE * dim + at, TILE)] = (total * gate[:, cols]).astype(BF)
+        forward(lhs[L_POOL_B], HIGH_B, 1, put_merging)
+        backward(lambda at: rhs[0, :, r_cols(R_MERGE)], OUT, 1, merged, True)
+        merged[...] += lhs[L_LOW].astype(F32)
+        lhs[L_FIRST] = normalise(merged[...], gain1_ref[...]).astype(BF)
+
+        w_wait(2)
+        w_wait(3)
+        pl.semaphore_wait(barrier, n)
+        for i in (L_LOW, L_POOL_A, L_POOL_B, L_COT, L_FIRST):
+            l_copy(i).start()
+        r_copy(R_MERGE).start()
+        out_q = []
+        for k in range(3):
+            def put_mixed(at, y):
+                mixed[k, :, pl.ds(at, TILE)] = y.astype(BF)
+            forward(lhs[L_FIRST], QUERY + k, 1, put_mixed)
+            copies = to_heads(k, mixed.at[k], heads_in.at[k], q_send, q_got)
+            start(copies)
+            out_q += copies
+        wait(out_q)
+
+        for h in range(heads):
+            lanes = slice(h * HEAD, (h + 1) * HEAD)
+
+            def rows_of(b, _):
+                some = pl.ds(pl.multiple_of(b * t, t), t)
+                s = nt(heads_in[0, some, lanes], heads_in[1, :, lanes]) * scale
+                e = jnp.exp(s - jnp.max(s, -1, keepdims=True))
+                p = (e * (1.0 / jnp.sum(e, -1, keepdims=True))).astype(BF)
+                probs[h, some] = p
+                att_all[some, lanes] = nn(p, heads_in[2, :, lanes]).astype(BF)
+                return 0
+            lax.fori_loop(0, n, rows_of, 0)
+        out_a = to_tokens(0, att_all, rhs.at[0, :, r_cols(R_ATT)], a_send, a_got)
+        start(out_a)
+        wait(out_a)
+        r_copy(R_ATT).start()
+        backward(lambda at: rhs[0, :, r_cols(R_ATT)], PROJ, 1, resid, True)
+        resid[...] += merged[...]
+        lhs[L_SECOND] = normalise(resid[...], gain2_ref[...]).astype(BF)
+        l_copy(L_SECOND).start()
+
+        w_wait(4)
+        w_wait(5)
+
+        def put_up(at, y):
+            value, rate = gelu_parts(y)
+            rhs[0, :, pl.ds(r_at(R_ACT) + at, TILE)] = value.astype(BF)
+            slope[:, pl.ds(at, TILE)] = rate.astype(BF)
+        forward(lhs[L_SECOND], 8, 4, put_up)
+        r_copy(R_ACT).start()
+        w_wait(6)
+        w_wait(7)
+        backward(lambda at: rhs[0, :, pl.ds(r_at(R_ACT) + at, dim)], 12, 4, acc, True)
+        low_out[...] = resid[...] + acc[...]
+
+        def put_d_up(at, y):
+            rhs[0, :, pl.ds(r_at(R_DUP) + at, TILE)] = (y * slope[:, pl.ds(at, TILE)].astype(F32)).astype(BF)
+        forward(lhs[L_COT], 12, 4, put_d_up)
+        r_copy(R_DUP).start()
+        backward(lambda at: rhs[0, :, pl.ds(r_at(R_DUP) + at, dim)], 8, 4, acc, True)
+        back, g = normalise_back(resid[...], gain2_ref[...], acc[...])
+        g_ln2[...] = g
+        d_res[...] = lhs[L_COT].astype(F32) + back
+        lhs[L_DA] = d_res[...].astype(BF)
+        l_copy(L_DA).start()
+
+        def put_d_att(at, y):
+            mixed[0, :, pl.ds(at, TILE)] = y.astype(BF)
+        forward(lhs[L_DA], PROJ, 1, put_d_att)
+        out_b = to_heads(0, mixed.at[0], d_att, b_send, b_got)
+        start(out_b)
+        l_copy(L_COT).wait_recv()
+        grad(L_COT, R_ACT, 12, 4)
+        wait(out_b)
+        for h in range(heads):
+            lanes = slice(h * HEAD, (h + 1) * HEAD)
+
+            def rows_of(b, _):
+                some = pl.ds(pl.multiple_of(b * t, t), t)
+                p = probs[h, some].astype(F32)
+                dp_ = nt(d_att[some, lanes], heads_in[2, :, lanes])
+                ds = (p * (dp_ - jnp.sum(dp_ * p, -1, keepdims=True)) * scale).astype(BF)
+                d_scores[some] = ds
+                d_heads[0, some, lanes] = nn(ds, heads_in[1, :, lanes]).astype(BF)
+                return 0
+            lax.fori_loop(0, n, rows_of, 0)
+            d_heads[1, :, lanes] = tn(d_scores[...], heads_in[0, :, lanes]).astype(BF)
+            d_heads[2, :, lanes] = tn(probs[h], d_att[:, lanes]).astype(BF)
+        out_c = []
+        for k in range(3):
+            copies = to_tokens(k, d_heads.at[k], rhs.at[0, :, r_cols(R_DQ + k)], c_send, c_got)
+            start(copies)
+            out_c += copies
+        l_copy(L_SECOND).wait_recv()
+        grad(L_SECOND, R_DUP, 8, 4)
+        l_copy(L_DA).wait_recv()
+        grad(L_DA, R_ATT, PROJ, 1)
+        wait(out_c)
+        for k in range(3):
+            r_copy(R_DQ + k).start()
+        backward(lambda at: rhs[0, :, pl.ds(R_DQ * dim + at, dim)], QUERY, 3, acc, True)
+        back, g = normalise_back(merged[...], gain1_ref[...], acc[...])
+        g_ln1[...] = g
+        d_res[...] += back
+        lhs[L_DF] = d_res[...].astype(BF)
+        l_copy(L_DF).start()
+
+        def put_d_gate(at, y):
+            cols = pl.ds(at, TILE)
+            gv = gate[:, cols]
+            part = y * gv
+            rhs[0, :, pl.ds(R_DHIGH * dim + at, TILE)] = part.astype(BF)
+            rhs[0, :, pl.ds(R_DGATE * dim + at, TILE)] = (part * high[:, cols] * (1.0 - gv)).astype(BF)
+        forward(lhs[L_DF], OUT, 1, put_d_gate)
+        r_copy(R_DHIGH).start()
+        r_copy(R_DGATE).start()
+        backward(lambda at: rhs[0, :, r_cols(R_DHIGH)], HIGH_A, 1, d_pool_a, True)
+        backward(lambda at: rhs[0, :, r_cols(R_DHIGH)], HIGH_B, 1, d_pool_b, True)
+        backward(lambda at: rhs[0, :, r_cols(R_DGATE)], GATE, 1, acc, True)
+        d_low[...] = d_res[...] + acc[...]
+        l_copy(L_FIRST).wait_recv()
+        for k in range(3):
+            grad(L_FIRST, R_DQ + k, QUERY + k, 1)
+        l_copy(L_DF).wait_recv()
+        grad(L_DF, R_MERGE, OUT, 1)
+        l_copy(L_POOL_A).wait_recv()
+        grad(L_POOL_A, R_DHIGH, HIGH_A, 1)
+        l_copy(L_POOL_B).wait_recv()
+        grad(L_POOL_B, R_DHIGH, HIGH_B, 1, shared=True)
+        l_copy(L_LOW).wait_recv()
+        grad(L_LOW, R_DGATE, GATE, 1)
+        for slot in range(2):
+            pltpu.make_async_copy(stage.at[slot], grads.at[:, :, pl.ds(0, TILE)], stage_sem.at[slot]).wait()
+        for i in range(8):
+            l_copy(i).wait_send()
+        for b in range(9):
+            r_copy(b).wait_send()
+
+    whole = pl.BlockSpec(memory_space=pl.ANY)
+    local = pl.BlockSpec(memory_space=pltpu.VMEM)
+    vm, dma = pltpu.VMEM, pltpu.SemaphoreType.DMA
+    tok = jax.ShapeDtypeStruct((t, dim), F32)
+    one = jax.ShapeDtypeStruct((1, dim), F32)
     return pl.pallas_call(
-        kernel, grid=(c // LANES,),
-        out_shape=(jax.ShapeDtypeStruct((rows, cols, c), F32), jax.ShapeDtypeStruct((size * size, 1, c), F32)),
-        in_specs=[pl.BlockSpec((high, cols, LANES), lambda i: (0, 0, i))] * 2 + [pl.BlockSpec((size * size, 1, LANES), lambda i: (0, 0, i))],
-        out_specs=(pl.BlockSpec((rows, cols, LANES), lambda i: (0, 0, i)), pl.BlockSpec((size * size, 1, LANES), lambda i: (0, 0, i))),
-        scratch_shapes=[pltpu.VMEM((high, cols + 2 * EDGE, LANES), F32)] * 2,
-        compiler_params=pltpu.CompilerParams(vmem_limit_bytes=32 << 20),
-    )(d, x, w)
-
-
-def for_sending(value):
-    return jax.tree.map(lambda a: a.astype(jnp.bfloat16) if a.dtype == jnp.float32 else a, value)
+        kernel,
+        out_shape=(tok, tok, tok, tok, one, one, jax.ShapeDtypeStruct((pairs, rows, 16 * dim), BF)),
+        in_specs=[local] * 6 + [whole] * 2,
+        out_specs=(local,) * 6 + (whole,),
+        scratch_shapes=[
+            vm((2, pairs, rows, 16 * dim), BF), vm((8, t, dim), BF), vm((8, t, half), BF), vm((2, t, 15 * dim), BF),
+            vm((t, dim), F32), vm((t, dim), F32), vm((t, dim), F32), vm((t, dim), F32), vm((t, dim), F32),
+            vm((t, ff), BF), vm((3, t, dim), BF), vm((3, every, width), BF), vm((every, width), BF), vm((every, width), BF),
+            vm((1, 8, 128), BF), vm((3, every, width), BF), vm((heads, every, every), BF), vm((every, every), BF),
+            vm((2, pairs, rows, TILE), BF),
+            dma((8, 2)), dma((3, n)), dma((3, n)), dma((1, n)), dma((1, n)), dma((1, n)), dma((1, n)), dma((3, n)), dma((3, n)),
+            dma((3,)), dma((8,)), dma((8,)), dma((9,)), dma((9,)), dma((2,)),
+        ],
+        compiler_params=pltpu.CompilerParams(collective_id=cid, has_side_effects=True, vmem_limit_bytes=61 * MIB),
+        cost_estimate=pl.CostEstimate(flops=14 * 10**9, bytes_accessed=70 * 10**6, transcendentals=10**7),
+    )(low, pool_a, pool_b, cot, gain1, gain2, w1.reshape(pairs, 2, rows, 8 * dim), w2.reshape(pairs, 2, rows, 8 * dim))
+def own_part(w, axis):
+    length = w.shape[axis] // lax.axis_size("dp")
+    return lax.dynamic_slice_in_dim(w, lax.axis_index("dp") * length, length, axis)
+
+
+def fold(w, rows):
+    return w[:rows], jnp.pad(w[rows:], ((0, 2 * rows - w.shape[0]), (0, 0)))
+
+
+def gather_packed(pieces, every):
+    n = every.shape[0]
+    parts, at = [], 0
+    for w in pieces:
+        parts.append(every[:, :, at : at + w].transpose(1, 0, 2).reshape(-1, n * w))
+        at += w
+    return lax.all_gather(jnp.concatenate(parts, axis=1), "dp", axis=0, tiled=True)
+
+
+def core_first(x, devices):
+    shape = x.shape
+    return x.reshape(shape[:-1] + (devices // 2, 2, -1)).swapaxes(-3, -2).reshape(shape)
+
+
+def core_last(x, devices):
+    shape = x.shape
+    return x.reshape(shape[:-1] + (2, devices // 2, -1)).swapaxes(-3, -2).reshape(shape)
 
 
 def extended(value, sides, width):
@@ -459,21 +996,6 @@
     centred = values - centre
     variance = jnp.mean(centred * centred, -1, keepdims=True)
     return centred * lax.rsqrt(variance + 1e-06) * gain
-
-
-def spread(values):
-    return jax.tree.map(
-        lambda part, own: part.astype(own.dtype),
-        lax.all_gather(for_sending(values), "mp", axis=1, tiled=True),
-        values,
-    )
-
-
-def collect(values):
-    return jax.tree.map(
-        lambda part: part.astype(jnp.float32),
-        lax.psum_scatter(for_sending(values), "mp", scatter_dimension=1, tiled=True),
-    )
 
 
 def per_device(
@@ -497,6 +1019,17 @@
     cot_hr,
 ):
     item_count, row_count, col_count, chan_count = hr_in.shape
+    devices, shards = lax.axis_size("dp"), lax.axis_size("mp")
+    dims = low_in.shape[2]
+    share = dims // devices
+    qkv = own_part(w_qkv, 1)
+    first_pieces = [
+        own_part(ad_gate, 0), own_part(ad_out, 1).T, *fold(own_part(ad_high, 0), share),
+        qkv[0], qkv[1], qkv[2], own_part(w_proj, 1).T,
+    ]
+    second_pieces = [own_part(w_up, 0), own_part(w_down, 1).T]
+    first_every = lax.all_gather(jnp.concatenate(first_pieces, axis=1), "mp", axis=0)
+    second_every = lax.all_gather(jnp.concatenate(second_pieces, axis=1), "mp", axis=0)
     plane_mask = valid.astype(jnp.float32)
     cell_mask = plane_mask[..., None]
     masked = hr_in * valid.astype(jnp.bfloat16)[..., None]
@@ -504,10 +1037,14 @@
     size = conv_w.shape[0]
     taps = conv_w.astype(F32).reshape(size * size, 1, chan_count)
     conv_out = conv_forward(bordered[0], taps, size)[None]
+    conv_out, first_every, second_every = lax.optimization_barrier((conv_out, first_every, second_every))
+    first_widths = [p.shape[1] for p in first_pieces]
+    second_widths = [p.shape[1] for p in second_pieces]
+    packed_first = gather_packed(first_widths, first_every)
+    packed_second = gather_packed(second_widths, second_every)
     conv_out = conv_out * cell_mask
     hr_gainf = hr_gain.astype(jnp.float32)
     normed = layer_norm(conv_out, hr_gainf).astype(jnp.bfloat16)
-    shards = lax.axis_size("mp")
     branch, normed_all, hidden_act, hidden_slope = big_forward(
         normed.reshape(row_count * col_count, chan_count), cn_up, cn_down, shards
     )
@@ -522,124 +1059,61 @@
         .astype(jnp.bfloat16)
         .reshape(item_count, half_rows * half_cols, chan_count)
     )
-    low_all, pooled_all = spread((low_in, pooled))
-    gate_pre = jnp.einsum("itd,dh->ith", low_all, ad_gate, preferred_element_type=jnp.float32)
-    high_pre = jnp.einsum("itc,ch->ith", pooled_all, ad_high, preferred_element_type=jnp.float32)
-    gate_vals = jax.nn.sigmoid(gate_pre)
-    merging = (high_pre * gate_vals).astype(jnp.bfloat16)
-    merged_rows = low_in.astype(jnp.float32) + collect(
-        jnp.einsum("ith,hd->itd", merging, ad_out, preferred_element_type=jnp.float32)
+    tokens = half_rows * half_cols
+    by_share = pooled[0].reshape(tokens, devices, -1)
+    pool_a = by_share[:, :, :share].reshape(tokens, dims)
+    pool_b = jnp.pad(by_share[:, :, share:], ((0, 0), (0, 0), (0, 2 * share - by_share.shape[2]))).reshape(tokens, dims)
+    low_out, d_low_in, d_pool_a, d_pool_b, g_ln1, g_ln2, low_grads = low_stage(
+        *(core_first(v, devices) for v in (low_in[0], pool_a, pool_b, cot_low[0])),
+        *(core_first(v.astype(F32), devices)[None] for v in (ln1_gain, ln2_gain)),
+        packed_first, packed_second, shards, devices, 2,
     )
-    ln1f = ln1_gain.astype(jnp.float32)
-    first_norm = layer_norm(merged_rows, ln1f).astype(jnp.bfloat16)
-    first_all = spread(first_norm)
-    token_count = first_all.shape[1]
-    heads_local = w_qkv.shape[2] // HEAD
-    stacked = jnp.einsum(
-        "itd,kdh->kith", first_all, w_qkv, preferred_element_type=jnp.float32
-    ).astype(jnp.bfloat16)
-    stacked = stacked.reshape(3, item_count, token_count, heads_local, HEAD)
-    query_heads, key_heads, value_heads = (stacked[0], stacked[1], stacked[2])
-    score_scale = HEAD ** (-0.5)
-    scores = (
-        jnp.einsum("iqne,ikne->inqk", query_heads, key_heads, preferred_element_type=jnp.float32)
-        * score_scale
+    low_out = core_last(low_out, devices)[None]
+    d_low_in = core_last(d_low_in, devices)[None]
+    g_ln1, g_ln2 = core_last(g_ln1[0], devices), core_last(g_ln2[0], devices)
+    d_pooled = jnp.concatenate(
+        [
+            core_last(d_pool_a, devices).reshape(tokens, devices, share),
+            core_last(d_pool_b, devices).reshape(tokens, devices, share)[:, :, : by_share.shape[2] - share],
+        ],
+        axis=2,
     )
-    row_max = jnp.max(scores, -1, keepdims=True)
-    log_total = jnp.log(jnp.sum(jnp.exp(scores - row_max), -1, keepdims=True)) + row_max
-    attn_probs = jnp.exp(scores - log_total).astype(jnp.bfloat16)
-    attended = jnp.einsum(
-        "inqk,ikne->iqne", attn_probs, value_heads, preferred_element_type=jnp.float32
-    )
-    attended = attended.astype(jnp.bfloat16).reshape(item_count, token_count, heads_local * HEAD)
-    residual = merged_rows + collect(
-        jnp.einsum("itm,md->itd", attended, w_proj, preferred_element_type=jnp.float32)
-    )
-    ln2f = ln2_gain.astype(jnp.float32)
-    second_norm = layer_norm(residual, ln2f).astype(jnp.bfloat16)
-    second_all = spread(second_norm)
-    up_pre = jnp.einsum("itd,df->itf", second_all, w_up, preferred_element_type=jnp.float32)
-    up_act = jax.nn.gelu(up_pre).astype(jnp.bfloat16)
-    low_out = residual + collect(
-        jnp.einsum("itf,fd->itd", up_act, w_down, preferred_element_type=jnp.float32)
-    )
-    d_out_all = spread(cot_low)
-    g_down = jnp.einsum("itf,itd->fd", up_act, d_out_all, preferred_element_type=jnp.float32)
-    d_upact = jnp.einsum("itd,fd->itf", d_out_all, w_down, preferred_element_type=jnp.float32)
-    d_uppre = jax.vjp(jax.nn.gelu, up_pre)[1](d_upact)[0].astype(jnp.bfloat16)
-    g_up = jnp.einsum("itd,itf->df", second_all, d_uppre, preferred_element_type=jnp.float32)
-    d_second = collect(jnp.einsum("itf,df->itd", d_uppre, w_up, preferred_element_type=jnp.float32))
-    d_res_norm, g_ln2 = jax.vjp(layer_norm, residual, ln2f)[1](d_second)
-    d_res = cot_low.astype(jnp.float32) + d_res_norm
-    d_attn_all = spread(d_res.astype(jnp.bfloat16))
-    g_proj = jnp.einsum("itm,itd->md", attended, d_attn_all, preferred_element_type=jnp.float32)
-    d_att = jnp.einsum(
-        "itd,md->itm", d_attn_all, w_proj, preferred_element_type=jnp.float32
-    ).astype(jnp.bfloat16)
-    d_att = d_att.reshape(item_count, token_count, heads_local, HEAD)
-    scores_again = (
-        jnp.einsum("iqne,ikne->inqk", query_heads, key_heads, preferred_element_type=jnp.float32)
-        * score_scale
-    )
-    probs_full = jnp.exp(scores_again - log_total)
-    d_value = jnp.einsum(
-        "inqk,iqne->ikne",
-        probs_full.astype(jnp.bfloat16),
-        d_att,
-        preferred_element_type=jnp.float32,
-    ).astype(jnp.bfloat16)
-    d_probs = jnp.einsum("iqne,ikne->inqk", d_att, value_heads, preferred_element_type=jnp.float32)
-    d_scores = (probs_full * (d_probs - jnp.sum(d_probs * probs_full, -1, keepdims=True))).astype(
-        jnp.bfloat16
-    )
-    d_query = (
-        jnp.einsum("inqk,ikne->iqne", d_scores, key_heads, preferred_element_type=jnp.float32)
-        * score_scale
-    ).astype(jnp.bfloat16)
-    d_key = (
-        jnp.einsum("inqk,iqne->ikne", d_scores, query_heads, preferred_element_type=jnp.float32)
-        * score_scale
-    ).astype(jnp.bfloat16)
-    d_stacked = jnp.stack([d_query, d_key, d_value]).reshape(
-        3, item_count, token_count, heads_local * HEAD
-    )
-    g_qkv = jnp.einsum("itd,kith->kdh", first_all, d_stacked, preferred_element_type=jnp.float32)
-    d_first = collect(
-        jnp.einsum("kith,kdh->itd", d_stacked, w_qkv, preferred_element_type=jnp.float32)
-    )
-    d_merged_norm, g_ln1 = jax.vjp(layer_norm, merged_rows, ln1f)[1](d_first)
-    d_merged = d_res + d_merged_norm
-    d_merging_all = spread(d_merged.astype(jnp.bfloat16))
-    g_ad_out = jnp.einsum("ith,itd->hd", merging, d_merging_all, preferred_element_type=jnp.float32)
-    d_merging = jnp.einsum("itd,hd->ith", d_merging_all, ad_out, preferred_element_type=jnp.float32)
-    d_high = (d_merging * gate_vals).astype(jnp.bfloat16)
-    d_gate = (d_merging * high_pre * gate_vals * (1.0 - gate_vals)).astype(jnp.bfloat16)
-    g_ad_high = jnp.einsum("itc,ith->ch", pooled_all, d_high, preferred_element_type=jnp.float32)
-    g_ad_gate = jnp.einsum("itd,ith->dh", low_all, d_gate, preferred_element_type=jnp.float32)
-    d_pooled, d_low = collect(
-        (
-            jnp.einsum("ith,ch->itc", d_high, ad_high, preferred_element_type=jnp.float32),
-            jnp.einsum("ith,dh->itd", d_gate, ad_gate, preferred_element_type=jnp.float32),
-        )
-    )
-    d_low_in = d_merged + d_low
     d_block = d_pooled.reshape(item_count, half_rows, half_cols, chan_count) / divisor
     d_block = d_block.reshape(item_count, half_rows, 1, half_cols, 1, chan_count)
     d_map = cot_hr.astype(jnp.float32) + jnp.broadcast_to(
         d_block, (item_count, half_rows, 2, half_cols, 2, chan_count)
     ).reshape(hr_in.shape)
     d_branch = d_map * cell_mask
-    d_normed, d_branch_all, d_hidden = big_backward(
+    d_normed, d_branch_all, d_hidden, low_sums = big_backward(
         d_branch.astype(BF).reshape(row_count * col_count, chan_count),
-        hidden_slope, cn_up, cn_down, shards,
+        hidden_slope, cn_up, cn_down, low_grads, shards, devices,
     )
     d_normed = d_normed.reshape(hr_in.shape)
-    g_cn_down = jnp.einsum("th,tc->hc", hidden_act, d_branch_all, preferred_element_type=F32).astype(BF)
+    by_slice, at = [], 0
+    for whole, widths in zip(low_sums, (first_widths, second_widths)):
+        at = 0
+        for w in widths:
+            by_slice.append(whole[:, at : at + shards * w].reshape(share, shards, w).transpose(1, 0, 2))
+            at += shards * w
+    own = lax.psum_scatter(jnp.concatenate(by_slice, axis=2), "mp", scatter_dimension=0).astype(F32)
+    split, at = [], 0
+    for w in first_widths + second_widths:
+        split.append(own[:, at : at + w])
+        at += w
+    g_ad_gate, g_ad_out, g_high_a, g_high_b, g_query, g_key, g_value, g_proj, g_up, g_down = split
+    g_ad_high = jnp.concatenate([g_high_a, g_high_b[: ad_high.shape[0] // devices - share]], axis=0)
+    g_qkv = jnp.stack([g_query, g_key, g_value])
+    g_ad_out, g_proj, g_down = g_ad_out.T, g_proj.T, g_down.T
+    g_cn_down = jnp.einsum("tc,th->ch", d_branch_all, hidden_act, preferred_element_type=F32).astype(BF)
     g_cn_up = jnp.einsum("tc,th->ch", normed_all, d_hidden, preferred_element_type=F32).astype(BF)
+    cn_grads = [g.reshape(devices, chan_count // devices, -1) for g in (g_cn_up, g_cn_down)]
     d_conv, g_hr_gain = jax.vjp(layer_norm, conv_out, hr_gainf)[1](d_normed)
     d_conv = d_conv * cell_mask
     d_bordered = extended(d_conv.astype(BF), (("mp", 1),), 3)
-    d_conv_in, g_conv = conv_backward(d_bordered[0], bordered[0], taps, size)
+    d_conv_in, g_conv, (g_cn_up, g_cn_down) = conv_backward(
+        d_bordered[0], bordered[0], taps, size, cn_grads, devices
+    )
+    g_cn_up, g_cn_down = g_cn_up.astype(F32), g_cn_down.astype(F32).T
     g_conv = g_conv.reshape(conv_w.shape)
     d_hr_in = (d_branch + d_conv_in) * cell_mask
     small = (g_conv, g_hr_gain, g_ln1, g_ln2)
@@ -650,19 +1124,6 @@
         parts.append(packed[at : at + g.size].reshape(g.shape))
         at += g.size
     g_conv, g_hr_gain, g_ln1, g_ln2 = parts
-    g_cn_up, g_ad_gate, g_ad_high, g_up = (
-        lax.psum_scatter(g_cn_up.astype(BF), "dp", scatter_dimension=0, tiled=True).astype(F32),
-        lax.psum_scatter(g_ad_gate.astype(BF), "dp", scatter_dimension=0, tiled=True).astype(F32),
-        lax.psum_scatter(g_ad_high.astype(BF), "dp", scatter_dimension=0, tiled=True).astype(F32),
-        lax.psum_scatter(g_up.astype(BF), "dp", scatter_dimension=0, tiled=True).astype(F32),
-    )
-    g_cn_down, g_ad_out, g_qkv, g_proj, g_down = (
-        lax.psum_scatter(g_cn_down.astype(BF), "dp", scatter_dimension=1, tiled=True).astype(F32),
-        lax.psum_scatter(g_ad_out.astype(BF), "dp", scatter_dimension=1, tiled=True).astype(F32),
-        lax.psum_scatter(g_qkv.astype(BF), "dp", scatter_dimension=1, tiled=True).astype(F32),
-        lax.psum_scatter(g_proj.astype(BF), "dp", scatter_dimension=1, tiled=True).astype(F32),
-        lax.psum_scatter(g_down.astype(BF), "dp", scatter_dimension=1, tiled=True).astype(F32),
-    )
     return (
         low_out,
         hr_out,

time: 1500 us -> 1100 us (0.73)
  waiting for transfers between devices: 809 us -> 213 us
  Pallas kernels: 428 us -> 609 us
  local copies, waits for them, and re-layouts: 51.9 us -> 158 us
  matrix products: 107 us -> 33.5 us
  other arithmetic: 68.5 us -> 42.9 us
    reduce_scatter x11 -> x1, waiting for transfers between devices: 392 us -> 74.2 us  [per_device(): lax.psum_scatter(jnp.concatenate(by_slice, axis=2), 'mp', scatter_dimensi...]
    unnamed x30 -> x7, waiting for transfers between devices: 160 us -> 0.11 us
    pallas_call x1 -> x2, Pallas kernels: 36.5 us -> 186 us  [the longest x1 107 us: low_stage(): pl.pallas_call(kernel, out_shape=(tok, tok, tok, tok, one, one, jax.Shape...]
    all_gather x7 -> x4, waiting for transfers between devices: 183 us -> 41.1 us  [the longest x1 41.1 us: per_device(): lax.all_gather(jnp.concatenate(first_pieces, axis=1), 'mp', axis=0)]
    dot_general x28 -> x1, matrix products: 90.1 us -> 16.6 us  [per_device(): jnp.einsum('tc,th->ch', d_branch_all, hidden_act, preferred_element_type=...]
    pallas_call x1, Pallas kernels: 194 us -> 229 us  [big_backward(): pl.pallas_call(kernel, out_shape=(jax.ShapeDtypeStruct((CHUNKS, rows, c),...]
    transpose x0 -> x19, local copies, waits for them, and re-layouts: none -> 33.4 us  [the longest x12 29 us: gather_packed(): parts.append(every[:, :, at:at + w].transpose(1, 0, 2).reshape(-1, n * w))]
    unnamed x126 -> x127, local copies, waits for them, and re-layouts: 25.6 us -> 48.8 us
  transfers between devices with their start and end apart: 29 -> 11, of which waited for: 28 -> 6; matrix products, arithmetic and copies ran while one was open for 8% -> 13% of each run, Pallas kernels for 13% -> 18%
where the time goes in v2:
time: 1100 us; the launch traced here: 1080 us
  Pallas kernels  609 us (55%)
  waiting for transfers between devices  213 us (19%)
  local copies, waits for them, and re-layouts  158 us (14%)
  other arithmetic  42.9 us (4%)
  matrix products  33.5 us (3%)
  between operations  15.4 us (1%)
    pallas_call x1, Pallas kernels, big_backward(): pl.pallas_call(kernel, out_shape=(jax.ShapeDtypeStruct((CHUNKS, rows, c),...  229 us
    pallas_call x1, Pallas kernels, big_forward(): pl.pallas_call(kernel, out_shape=(jax.ShapeDtypeStruct((CHUNKS, rows, c),...  177 us
    pallas_call x1, Pallas kernels, low_stage(): pl.pallas_call(kernel, out_shape=(tok, tok, tok, tok, one, one, jax.Shape...  107 us
    pallas_call x1, Pallas kernels, conv_backward(): pl.pallas_call(kernel, grid=(blocks,), out_shape=(jax.ShapeDtypeStruct((r...  78.4 us
    reduce_scatter x1, waiting for transfers between devices, per_device(): lax.psum_scatter(jnp.concatenate(by_slice, axis=2), 'mp', scatter_dimensi...  74.2 us
    psum x2, waiting for transfers between devices, per_device(): packed = lax.psum(lax.psum(packed, 'mp'), 'dp')  73.2 us
    unnamed x127, local copies, waits for them, and re-layouts  48.8 us
    all_gather x1, waiting for transfers between devices, per_device(): lax.all_gather(jnp.concatenate(first_pieces, axis=1), 'mp', axis=0)  41.1 us
  transfers between devices with their start and end apart: 11, of which 6 were waited for; matrix products, arithmetic and copies ran while one was open for 13% of the time, Pallas kernels for 18%

profile of v2, /device:TPU:0, one launch (start us, length us, event | category | flops | bytes accessed | tf_op | source)
XLA Modules:
  0.0 1082.2 jit_solution(6191450479036372128)
XLA Ops:
  18.1 5.0 collective-permute-start
  24.4 2.1 reshape.341.w_ref
  26.5 16.1 %collective-permute-done = bf16[1,3,48,1536]{3,2,1,0:T(8,128)(2,1)S(1)} collective-permute-done((bf16[1,3,48,1536]{3,2,1,0:T(8,128)(2,1)S(1)}, bf16[1,3,48,1536]{3,2,1,0:T(8,128)(2,1)S(1)}, u32[]{:S(2)}, u32[]{:S(2)}) %collective-permute-start) | collective-permute-done | bytes 442400 | tf_op jit(solution)/shard_map/ppermute | solution.py:988
  42.6 8.6 collective-permute-done.1
  51.5 17.6 %shard_map.305 = f32[12,48,1536]{2,1,0:T(8,128)S(1)} custom-call(bf16[18,48,1536]{2,1,0:T(8,128)(2,1)S(1)} %maximum_bitcast_fusion.x_ref, f32[49,1,1536]{2,1,0:T(1,128)S(1)} %copy-done.5), custom_call_target="tpu_custom_call" | custom-call | tf_op jit(solution)/shard_map/pallas_call | solution.py:508
  70.7 4.3 reshape.350
  75.0 41.1 %all-gather.11.cloned.1.call-done = bf16[512,2048]{0,1:T(8,128)(2,1)} async-done(((bf16[128,2048]{0,1:T(8,128)(2,1)}), bf16[512,2048]{0,1:T(8,128)(2,1)}) %all-gather.11.cloned.1.call-update) | async-done | bytes 2097168 | tf_op jit(solution)/shard_map/all_gather | solution.py:1031
  116.1 4.0 reshape.349
  120.0 3.3 slice_bitcast_fusion.3
  123.3 1.9 copy.126
  126.9 1.9 copy.125
  130.5 1.9 copy.124
  134.2 1.9 copy.123
  137.7 1.9 copy.122
  141.3 1.9 copy.121
  144.9 1.9 copy.120
  148.5 1.9 copy.119
  162.2 3.6 slice_bitcast_fusion.1
  165.7 3.5 copy.127
  169.2 2.7 copy.182
  171.9 3.5 copy.128
  177.0 2.7 pad_maximum_fusion
  186.2 1.9 reshape_squeeze.12
  189.8 1.9 reshape.297.low_ref
  191.7 1.9 reshape_squeeze.13
  195.3 1.9 reshape.304.cot_ref
  198.8 1.8 multiply_convert_fusion.1
  200.6 176.9 %shard_map.306 = (f32[6,96,1536]{2,1,0:T(8,128)}, bf16[4,6,96,1536]{3,2,1,0:T(8,128)(2,1)}, bf16[4,6,96,1536]{3,2,1,0:T(8,128)(2,1)}, bf16[4,6,96,1536]{3,2,1,0:T(8,128)(2,1)}) custom-call(bf16[6,96,1536]{2,1,0:T(8,128)(2,1)} %bitcast.213, bf16[1536,1536]{1,0:T(8,128)(2,1)} %wu.3, bf16[1536,1536]{1,0:T(8,128)(2,1)} %wd.3), custom_call_target="tpu_custom_call" | custom-call | flops 21743271936 | bytes 28311552 | tf_op jit(solution)/shard_map/pallas_call | solution.py:342
  377.5 3.1 add_multiply_fusion.1
  380.6 3.9 reshape.300
  384.5 5.5 reduce_sum.69
  394.8 107.2 %shard_map.307 = (f32[144,1024]{1,0:T(8,128)}, f32[144,1024]{1,0:T(8,128)}, f32[144,1024]{1,0:T(8,128)}, f32[144,1024]{1,0:T(8,128)}, f32[1,1024]{1,0:T(1,128)},...) custom-call(bf16[144,1024]{1,0:T(8,128)(2,1)} %reshape.297.low_ref, bf16[144,1024]{1,0:T(8,128)(2,1)} %reshape.302.pool_a_ref, ...), custom_call_target="tpu_custom_call" | custom-call | flops 14000000000 | bytes 70000000 | tf_op jit(solution)/shard_map/pallas_call | solution.py:936
  508.8 3.0 broadcast_in_dim.13
  511.8 4.2 broadcast_in_dim.14
  516.1 4.4 fusion.1
  520.5 229.2 %shard_map.308 = (f32[6,96,1536]{2,1,0:T(8,128)}, bf16[4,6,96,1536]{3,2,1,0:T(8,128)(2,1)}, bf16[4,6,96,1536]{3,2,1,0:T(8,128)(2,1)}, bf16[2,128,8192]{2,1,0:T(8...) custom-call(bf16[6,96,1536]{2,1,0:T(8,128)(2,1)} %bitcast.212, ...), custom_call_target="tpu_custom_call" | custom-call | flops 21743271936 | bytes 28311552 | tf_op jit(solution)/shard_map/pallas_call | solution.py:451
  749.8 2.9 multiply_reduce_fusion.1
  758.0 2.1 collective-permute-start.2
  774.9 16.6 %bitcast_convert_fusion = bf16[1536,1536]{1,0:T(8,128)(2,1)} fusion(bf16[4,6,96,1536]{3,2,1,0:T(8,128)(2,1)} %get-tuple-element.53, bf16[4,6,96,1536]{3,2,1,0:T(8,128)(2,1)} %get-tuple-element.54), kind=kOutput, calls=%fused_computation | convolution fusion | flops 10873995264 | bytes 18874368 | tf_op jit(solution)/shard_map/tc,th->ch/dot_general | solution.py:1107
  791.6 16.9 %bitcast_convert_fusion.1 = bf16[1536,1536]{1,0:T(8,128)(2,1)} fusion(bf16[4,6,96,1536]{3,2,1,0:T(8,128)(2,1)} %get-tuple-element.51, bf16[4,6,96,1536]{3,2,1,0:T(8,128)(2,1)} %get-tuple-element.52), kind=kOutput, calls=%fused_computation.1 | convolution fusion | flops 10873995264 | bytes 18874368 | tf_op jit(solution)/shard_map/tc,th->ch/dot_general | solution.py:1108
  811.5 2.9 maximum_bitcast_fusion.1.d_ref
  814.5 78.4 %shard_map.309 = (f32[12,48,1536]{2,1,0:T(8,128)}, f32[49,1,1536]{2,1,0:T(1,128)S(1)}, bf16[4,192,1536]{2,1,0:T(8,128)(2,1)}, bf16[2,192,1536]{2,1,0:T(8,128)(2,...) custom-call(bf16[18,48,1536]{2,1,0:T(8,128)(2,1)} %maximum_bitcast_f, ...), custom_call_target="tpu_custom_call" | custom-call | tf_op jit(solution)/shard_map/pallas_call | solution.py:576
  897.8 35.4 %all-reduce.5.cloned.1.call-done = f32[78848]{0:T(1024)} async-done(((f32[78848]{0:T(1024)}), f32[78848]{0:T(1024)}) %all-reduce.5.cloned.1.call-update) | async-done | bytes 315408 | tf_op jit(solution)/shard_map/psum | solution.py:1121
  934.4 1.8 copy.161
  941.9 2.4 broadcast_in_dim_reshape.21
  947.2 4.8 fusion
  952.0 37.8 %all-reduce.7.cloned.1.call-done = f32[78848]{0:T(1024)} async-done(((f32[78848]{0:T(1024)}), f32[78848]{0:T(1024)}) %all-reduce.7.cloned.1.call-update) | async-done | bytes 315408 | tf_op jit(solution)/shard_map/psum | solution.py:1121
  994.2 74.2 %reduce-scatter.2.cloned.1.call-done = bf16[1,128,4096]{1,2,0:T(8,128)(2,1)} async-done(((bf16[4,128,4096]{1,2,0:T(8,128)(2,1)}), bf16[1,128,4096]{1,2,0:T(8,128)(2,1)}) %reduce-scatter.2.cloned.1.call-update) | async-done | bytes 1048592 | tf_op jit(solution)/shard_map/reduce_scatter | solution.py:1098
  (232 shorter events, 110.8 us)
Async XLA Ops:
  7.2 1.6 copy-start
  7.2 10.6 copy-start.36
  7.2 63.5 %all-gather.13.cloned.1.call-start = ((), (), s32[]{:S(2)}) async-start(), calls=%async_computation.7 | async-start | bytes 2621440 | tf_op jit(solution)/shard_map/all_gather | solution.py:1032
  8.8 9.0 copy-start.13
  10.9 105.2 %all-gather.11.cloned.1.call-start = ((), (), s32[]{:S(2)}) async-start(), calls=%async_computation.6 | async-start | bytes 2621440 | tf_op jit(solution)/shard_map/all_gather | solution.py:1031
  17.7 377.0 %all-gather.7.cloned.1.call-start = ((), (), s32[]{:S(2)}) async-start(), calls=%async_computation.1 | async-start | bytes 18874368 | tf_op jit(solution)/shard_map/all_gather | solution.py:968
  17.8 5.2 copy-start.34
  18.1 24.5 %collective-permute-start = (bf16[1,3,48,1536]{3,2,1,0:T(8,128)(2,1)S(1)}, bf16[1,3,48,1536]{3,2,1,0:T(8,128)(2,1)S(1)}, u32[]{:S(2)}, u32[]{:S(2)}) collective-permute-start(bf16[1,3,48,1536]{3,2,1,0:T(8,128)(2,1)S(1)} %get-tuple-element.147), channel_id=1, source_target_pairs={{0,1},{1,2},{2,3},{4,5},{5,6},{6,7},{8,9},{9,10},{10,11},{12,13},{... | collective-permute-start | bytes 1327112 | tf_op jit(solution)/shard_map/ppermute | solution.py:988
  23.1 28.1 %collective-permute-start.1 = (bf16[1,3,48,1536]{3,2,1,0:T(8,128)(2,1)S(1)}, bf16[1,3,48,1536]{3,2,1,0:T(8,128)(2,1)S(1)}, u32[]{:S(2)}, u32[]{:S(2)}) collective-permute-start(bf16[1,3,48,1536]{3,2,1,0:T(8,128)(2,1)S(1)} %get-tuple-element.148), channel_id=1, source_target_pairs={{1,0},{2,1},{3,2},{5,4},{6,5},{7,6},{9,8},{10,9},{11,10},{13,12},{... | collective-permute-start | bytes 1327112 | tf_op jit(solution)/shard_map/ppermute | solution.py:989
  26.5 25.0 %copy-start.5 = (f32[49,1,1536]{2,1,0:T(1,128)S(1)}, f32[49,1,1536]{2,1,0:T(1,128)}, u32[]{:S(2)}) copy-start(f32[49,1,1536]{2,1,0:T(1,128)} %reshape.341.w_ref) | copy-start | bytes 903172
  69.1 1.6 copy-start.4
  70.7 128.1 %copy-start.2 = (f32[12,48,1536]{2,1,0:T(8,128)}, f32[12,48,1536]{2,1,0:T(8,128)S(1)}, u32[]{:S(2)}) copy-start(f32[12,48,1536]{2,1,0:T(8,128)S(1)} %shard_map.305) | copy-start | bytes 10616836
  150.4 10.2 copy-start.20
  150.4 11.0 %copy-start.19 = (bf16[16,8,4,256]{3,1,2,0:T(8,128)(2,1)S(1)}, bf16[16,8,4,256]{3,1,2,0:T(8,128)(2,1)}, u32[]{:S(2)}) copy-start(bf16[16,8,4,256]{3,1,2,0:T(8,128)(2,1)} %copy.181) | copy-start | bytes 786436
  162.1 232.7 %all-gather.9.cloned.1.call-start = ((), (), s32[]{:S(2)}) async-start(), calls=%async_computation.2 | async-start | bytes 18874368 | tf_op jit(solution)/shard_map/all_gather | solution.py:968
  177.0 5.4 copy-start.39
  179.8 753.4 %all-reduce.5.cloned.1.call-start = ((), (), s32[]{:S(2)}) async-start(), calls=%async_computation.3 | async-start | bytes 630784 | tf_op jit(solution)/shard_map/psum | solution.py:1121
  185.5 11.7 %copy-start.32 = (f32[6,24]{1,0:T(8,128)}, f32[6,24]{1,0:T(8,128)S(1)}, u32[]{:S(2)}) copy-start(f32[6,24]{1,0:T(8,128)S(1)} %broadcast_maximum_fusion) | copy-start | bytes 1732
  197.2 1.6 copy-start.26
  198.8 1.8 copy-start.28
  200.6 176.9 %copy-start.35 = (bf16[1,12,48]{2,1,0:T(8,128)(2,1)S(1)}, bf16[1,12,48]{2,1,0:T(8,128)(2,1)}, u32[]{:S(2)}) copy-start(bf16[1,12,48]{2,1,0:T(8,128)(2,1)} %copy-done.34) | copy-start | bytes 3460
  380.6 3.9 copy-start.10
  516.1 4.4 copy-start.8
  520.5 229.2 %copy-start.3 = (f32[12,48,1536]{2,1,0:T(8,128)S(1)}, f32[12,48,1536]{2,1,0:T(8,128)}, u32[]{:S(2)}) copy-start(f32[12,48,1536]{2,1,0:T(8,128)} %copy-done.2) | copy-start | bytes 10616836
  520.5 229.2 %copy-start.27 = (f32[1536]{0:T(1024)S(1)}, f32[1536]{0:T(1024)}, u32[]{:S(2)}) copy-start(f32[1536]{0:T(1024)} %convert_element_type.62) | copy-start | bytes 18436
  749.7 2.9 copy-start.31
  749.7 3.1 copy-start.7
  749.8 3.1 copy-start.29
  754.5 6.9 copy-start.16
  755.8 1.2 copy-start.11
  758.0 53.6 %collective-permute-start.2 = (bf16[1,3,48,1536]{3,2,1,0:T(8,128)(2,1)}, bf16[1,3,48,1536]{3,2,1,0:T(8,128)(2,1)}, u32[]{:S(2)}, u32[]{:S(2)}) collective-permute-start(bf16[1,3,48,1536]{3,2,1,0:T(8,128)(2,1)} %get-tuple-element.145), channel_id=1, source_target_pairs={{0,1},{1,2},{2,3},{4,5},{5,6},{6,7},{8,9},{9,10},{10,11},{12,13},{... | collective-permute-start | bytes 1327112 | tf_op jit(solution)/shard_map/ppermute | solution.py:988
  760.0 51.5 %collective-permute-start.3 = (bf16[1,3,48,1536]{3,2,1,0:T(8,128)(2,1)}, bf16[1,3,48,1536]{3,2,1,0:T(8,128)(2,1)}, u32[]{:S(2)}, u32[]{:S(2)}) collective-permute-start(bf16[1,3,48,1536]{3,2,1,0:T(8,128)(2,1)} %get-tuple-element.146), channel_id=1, source_target_pairs={{1,0},{2,1},{3,2},{5,4},{6,5},{7,6},{9,8},{10,9},{11,10},{13,12},{... | collective-permute-start | bytes 1327112 | tf_op jit(solution)/shard_map/ppermute | solution.py:989
  761.3 9.9 copy-start.15
  791.6 16.9 %copy-start.23 = (bf16[128,1024]{0,1:T(8,128)(2,1)S(1)}, bf16[128,1024]{0,1:T(8,128)(2,1)}, u32[]{:S(2)}) copy-start(bf16[128,1024]{0,1:T(8,128)(2,1)} %copy.153) | copy-start | bytes 786436
  791.6 17.7 %copy-start.22 = (bf16[128,1024]{0,1:T(8,128)(2,1)S(1)}, bf16[128,1024]{0,1:T(8,128)(2,1)}, u32[]{:S(2)}) copy-start(bf16[128,1024]{0,1:T(8,128)(2,1)} %copy.154) | copy-start | bytes 786436
  791.6 19.2 %copy-start.21 = (bf16[128,1024]{0,1:T(8,128)(2,1)S(1)}, bf16[128,1024]{0,1:T(8,128)(2,1)}, u32[]{:S(2)}) copy-start(bf16[128,1024]{0,1:T(8,128)(2,1)} %copy.156) | copy-start | bytes 786436
  791.6 20.0 %copy-start.12 = (bf16[1,12,48,1536]{3,2,1,0:T(8,128)(2,1)S(1)}, bf16[1,12,48,1536]{3,2,1,0:T(8,128)(2,1)}, u32[]{:S(2)}) copy-start(bf16[1,12,48,1536]{3,2,1,0:T(8,128)(2,1)} %copy-done.11) | copy-start | bytes 5308420
  809.3 5.2 copy-start.6
  814.5 79.2 %copy-start.37 = (f32[2,4,128]{2,0,1:T(2,128)S(1)}, f32[2,4,128]{2,0,1:T(2,128)}, u32[]{:S(2)}) copy-start(f32[2,4,128]{2,0,1:T(2,128)} %copy.134) | copy-start | bytes 12292
  814.5 79.2 %copy-start.38 = (f32[2,4,128]{2,0,1:T(2,128)S(1)}, f32[2,4,128]{2,0,1:T(2,128)}, u32[]{:S(2)}) copy-start(f32[2,4,128]{2,0,1:T(2,128)} %copy.135) | copy-start | bytes 12292
  814.5 81.7 %copy-start.18 = (bf16[128,1024]{0,1:T(8,128)(2,1)S(1)}, bf16[128,1024]{0,1:T(8,128)(2,1)}, u32[]{:S(2)}) copy-start(bf16[128,1024]{0,1:T(8,128)(2,1)} %copy.158) | copy-start | bytes 786436
  814.5 82.5 %copy-start.17 = (bf16[128,1024]{0,1:T(8,128)(2,1)S(1)}, bf16[128,1024]{0,1:T(8,128)(2,1)}, u32[]{:S(2)}) copy-start(bf16[128,1024]{0,1:T(8,128)(2,1)} %copy.159) | copy-start | bytes 786436
  894.5 95.3 %all-reduce.7.cloned.1.call-start = ((), (), s32[]{:S(2)}) async-start(), calls=%async_computation.4 | async-start | bytes 630784 | tf_op jit(solution)/shard_map/psum | solution.py:1121
  933.2 135.2 %reduce-scatter.2.cloned.1.call-start = ((), (), s32[]{:S(2)}) async-start(), calls=%async_computation.5 | async-start | bytes 5242880 | tf_op jit(solution)/shard_map/reduce_scatter | solution.py:1098
  936.2 1.2 copy-start.25
  939.4 6.6 copy-start.14
  944.3 2.9 copy-start.9
  1069.7 5.2 copy-start.1
  (3 other events, 2.6 us)
Sparse Core Ops, SparseCore 0:
  11.0 58.4 all-gather.12
  71.6 44.4 all-gather.10
  162.2 88.1 all-gather.6
  252.1 90.0 all-gather.8
  894.6 38.4 all-reduce.4
  936.1 53.6 all-reduce.6
  992.1 76.1 reduce-scatter.1

commit v3 on v2

--- a/solution.py
+++ b/solution.py
@@ -374,16 +374,18 @@
     rows = t // CHUNKS
     pairs, g_rows, g_cols = grads.shape
     bits = range(1, devices.bit_length() - 1)
-    split = g_cols // 2
+    split = g_rows // 2
     steps = len(bits)
-    plans = [Halving(bits, [last] * steps, (pairs, g_rows, split), min(split, 1024)) for last in (True, False)]
+    plans = [Halving(bits, [last] * steps, (pairs, split, g_cols), min(g_cols, 512)) for last in (True, False)]
+    extras = [b for plan in plans for b in plan.buffers()[:-1]]
+    each = 2 * steps - 1
 
     def kernel(d_ref, slopes, wu, wd, g_first, g_second, out, d_all, h_all, *rest):
-        extra, rest = rest[: 4 * steps], rest[4 * steps :]
+        sums, extra, rest = rest[0], rest[1 : 1 + 2 * each], rest[1 + 2 * each :]
         gathered, partial, travel, slope, grad, copied, stored, send0, recv0, send1, recv1 = rest[:11]
         sems = rest[11:]
-        plans[0].bind(g_first.at[:, :, :, pl.ds(0, split)], extra[: 2 * steps], send0, recv0)
-        plans[1].bind(g_second.at[:, :, :, pl.ds(split, split)], extra[2 * steps :], send1, recv1)
+        plans[0].bind(g_first.at[:, :, pl.ds(0, split)], extra[:each] + (sums.at[0],), send0, recv0)
+        plans[1].bind(g_second.at[:, :, pl.ds(split, split)], extra[each:] + (sums.at[1],), send1, recv1)
 
         def begin():
             for plan in plans:
@@ -448,17 +450,17 @@
 
     whole = pl.BlockSpec(memory_space=pl.ANY)
     local = pl.BlockSpec(memory_space=pltpu.VMEM)
-    out, d_all, h_all, *extra = pl.pallas_call(
+    out, d_all, h_all, sums, *_ = pl.pallas_call(
         kernel,
         out_shape=(
             jax.ShapeDtypeStruct((CHUNKS, rows, c), F32),
             jax.ShapeDtypeStruct((n, CHUNKS, rows, c), BF),
             jax.ShapeDtypeStruct((n, CHUNKS, rows, h), BF),
-            *plans[0].buffers(),
-            *plans[1].buffers(),
+            jax.ShapeDtypeStruct((2, 1, 1, split, g_cols), BF),
+            *extras,
         ),
         in_specs=[whole, whole, local, local, whole, whole],
-        out_specs=(whole,) * (3 + 4 * steps),
+        out_specs=(whole,) * (4 + 2 * each),
         scratch_shapes=chunk_buffers(n, rows, c, F32)
         + [pltpu.VMEM((rows, h), BF)] * 2
         + [pltpu.SemaphoreType.DMA((n, CHUNKS)), pltpu.SemaphoreType.DMA((2,))]
@@ -474,8 +476,7 @@
         d.reshape(CHUNKS, rows, c), slope_all.reshape(n, CHUNKS, rows, h), w_up, w_down,
         grads.reshape(pairs // 2, 2, g_rows, g_cols), grads.reshape(2, pairs // 2, g_rows, g_cols),
     )
-    sums = [extra[2 * steps - 1].reshape(g_rows, split), extra[4 * steps - 1].reshape(g_rows, split)]
-    return out.reshape(t, c), d_all.reshape(n * t, c), h_all.reshape(n * t, h), sums
+    return out.reshape(t, c), d_all.reshape(n * t, c), h_all.reshape(n * t, h), sums.reshape(g_rows, g_cols)
 
 
 def frame(dst, src):
@@ -499,19 +500,92 @@
     lax.fori_loop(0, rows // group, some, 0)
 
 
-def conv_forward(x, w, size, group=2):
-    high, cols, c = x.shape
-    rows = high - size + 1
-    def kernel(x_ref, w_ref, out, framed):
-        frame(framed, x_ref)
-        correlate(out, framed, w_ref, size, False, group)
+def conv_forward(x, w, size, n):
+    rows, cols, c = x.shape
+    reach = size // 2
+
+    def kernel(x_ref, w_ref, out, bordered, framed, sent, got, own):
+        d = lax.axis_index("mp")
+        has_up, has_down = d > 0, d < n - 1
+        barrier = pltpu.get_barrier_semaphore()
+
+        @pl.when(has_up)
+        def _():
+            pl.semaphore_signal(barrier, inc=1, device_id={"mp": d - 1}, device_id_type=MESH)
+
+        @pl.when(has_down)
+        def _():
+            pl.semaphore_signal(barrier, inc=1, device_id={"mp": d + 1}, device_id_type=MESH)
+
+        keep = pltpu.make_async_copy(x_ref, bordered.at[pl.ds(reach, rows)], own)
+        keep.start()
+        pl.semaphore_wait(barrier, has_up.astype(jnp.int32) + has_down.astype(jnp.int32))
+        up = pltpu.make_async_remote_copy(
+            src_ref=x_ref.at[pl.ds(0, reach)], dst_ref=bordered.at[pl.ds(reach + rows, reach)],
+            send_sem=sent.at[0], recv_sem=got.at[0], device_id={"mp": d - 1}, device_id_type=MESH,
+        )
+        down = pltpu.make_async_remote_copy(
+            src_ref=x_ref.at[pl.ds(rows - reach, reach)], dst_ref=bordered.at[pl.ds(0, reach)],
+            send_sem=sent.at[1], recv_sem=got.at[1], device_id={"mp": d + 1}, device_id_type=MESH,
+        )
+        nothing = jnp.zeros((reach, cols, c), BF)
+
+        @pl.when(has_up)
+        def _():
+            up.start()
+
+        @pl.when(has_down)
+        def _():
+            down.start()
+
+        @pl.when(d == 0)
+        def _():
+            bordered[:reach] = nothing
+
+        @pl.when(d == n - 1)
+        def _():
+            bordered[reach + rows :] = nothing
+
+        keep.wait()
+
+        @pl.when(has_up)
+        def _():
+            down.wait_recv()
+
+        @pl.when(has_down)
+        def _():
+            up.wait_recv()
+
+        def block(i, _):
+            lanes = pl.ds(pl.multiple_of(i * LANES, LANES), LANES)
+            frame(framed, bordered.at[:, :, lanes])
+            correlate(out.at[:, :, lanes], framed, w_ref.at[:, :, lanes], size, False, 4)
+            return 0
+
+        lax.fori_loop(0, c // LANES, block, 0)
+
+        @pl.when(has_up)
+        def _():
+            up.wait_send()
+
+        @pl.when(has_down)
+        def _():
+            down.wait_send()
+
+    local = pl.BlockSpec(memory_space=pltpu.VMEM)
+    dma = pltpu.SemaphoreType.DMA
     return pl.pallas_call(
-        kernel, grid=(c // LANES,),
-        out_shape=jax.ShapeDtypeStruct((rows, cols, c), F32),
-        in_specs=[pl.BlockSpec((high, cols, LANES), lambda i: (0, 0, i)), pl.BlockSpec((size * size, 1, LANES), lambda i: (0, 0, i))],
-        out_specs=pl.BlockSpec((rows, cols, LANES), lambda i: (0, 0, i)),
-        scratch_shapes=[pltpu.VMEM((high, cols + 2 * EDGE, LANES), F32)],
-        compiler_params=pltpu.CompilerParams(vmem_limit_bytes=32 << 20),
+        kernel,
+        out_shape=(
+            jax.ShapeDtypeStruct((rows, cols, c), F32),
+            jax.ShapeDtypeStruct((rows + 2 * reach, cols, c), BF),
+        ),
+        in_specs=[local, local],
+        out_specs=(local, local),
+        scratch_shapes=[pltpu.VMEM((rows + 2 * reach, cols + 2 * EDGE, LANES), F32), dma((2,)), dma((2,)), dma],
+        compiler_params=pltpu.CompilerParams(
+            collective_id=5, has_side_effects=True, vmem_limit_bytes=40 * MIB
+        ),
     )(x, w)
 
 
@@ -632,7 +706,7 @@
     return back, jnp.sum(d * hat, axis=0, keepdims=True)
 
 
-def low_stage(low, pool_a, pool_b, cot, gain1, gain2, w1, w2, n, devices, cid):
+def low_stage(low, pool_a, pool_b, cot, gain1, gain2, packed, n, devices, cid):
     t, dim = low.shape
     every = n * t
     width = dim // n
@@ -644,7 +718,7 @@
     scale = HEAD ** (-0.5)
 
     def kernel(
-        low_ref, pool_a_ref, pool_b_ref, cot_ref, gain1_ref, gain2_ref, w1_hbm, w2_hbm,
+        low_ref, pool_a_ref, pool_b_ref, cot_ref, gain1_ref, gain2_ref, w_hbm,
         low_out, d_low, d_pool_a, d_pool_b, g_ln1, g_ln2, grads,
         wv, lhs, lhs2, rhs, gate, high, merged, resid, d_res, slope, mixed, heads_in, att_all, d_att, d_mixed,
         d_heads, probs, d_scores, stage, w_sem, q_send, q_got, a_send, a_got, b_send, b_got, c_send, c_got, own_sem,
@@ -659,17 +733,31 @@
             pl.semaphore_signal(barrier, inc=1, device_id={"mp": lax.rem(d + k, n)}, device_id_type=MESH)
         pl.semaphore_signal(barrier, inc=1, device_id={"dp": mate}, device_id_type=MESH)
 
-        def w_copy(p, c):
-            src = (w1_hbm if p < 4 else w2_hbm).at[:, c, :, pl.ds((p % 4) * 2 * dim, 2 * dim)]
-            return pltpu.make_async_copy(src, wv.at[c, :, :, pl.ds(p * 2 * dim, 2 * dim)], w_sem.at[p, c])
-
-        for p in range(8):
-            for c in range(2):
-                w_copy(p, c).start()
-
-        def w_wait(p):
-            for c in range(2):
-                w_copy(p, c).wait()
+        def w_copy(w, k):
+            c, z = k // n, lax.rem(k, n)
+            wide, base, at = w_place(w)
+            src = w_hbm.at[:, c, z, :, pl.ds(base, wide)]
+            dst = wv.at[c, :, :, pl.ds(pl.multiple_of(at + z * wide, wide), wide)]
+            return pltpu.make_async_copy(src, dst, w_sem.at[w, k])
+
+        def w_place(w):
+            if w < 8:
+                return width, w * width, w * dim
+            return ff // n, 8 * width + (w - 8) * ff // n, 8 * dim + (w - 8) * ff
+
+        def w_each(w, act):
+            def one(k, _):
+                act(w_copy(w, k))
+                return 0
+
+            lax.fori_loop(0, 2 * n, one, 0)
+
+        for w in range(10):
+            w_each(w, lambda copy: copy.start())
+
+        def w_wait(*which):
+            for w in which:
+                w_each(w, lambda copy: copy.wait())
 
         def w_cols(at, size):
             return wv[:, :, :, pl.ds(at, size)].reshape(dim, size)
@@ -715,26 +803,38 @@
                 src_ref=lhs.at[i, :, pl.ds(pl.multiple_of((1 - core) * half, half), half)], dst_ref=lhs2.at[i],
                 send_sem=l_send.at[i], recv_sem=l_got.at[i], device_id={"dp": mate}, device_id_type=MESH)
 
-        stage_count = [0]
+        stored = []
 
         def grad(i, block, at, count, shared=False):
             if not shared:
                 r_copy(block).wait_recv()
             own_l = pl.ds(pl.multiple_of(core * half, half), half)
 
-            def out_copy(slot, k):
-                return pltpu.make_async_copy(
-                    stage.at[slot], grads.at[:, :, pl.ds(at * dim + k * TILE, TILE)], stage_sem.at[slot])
+            wide, base, first = w_place(at if at < 8 else 8 + (at - 8) * dim // ff)
+            piece = min(TILE, wide)
+
+            def out_copies(slot, k):
+                out = []
+                for q in range(TILE // piece):
+                    z, col = divmod(at * dim - first + k * TILE + q * piece, wide)
+                    out.append(
+                        pltpu.make_async_copy(
+                            stage.at[slot, :, :, pl.ds(q * piece, piece)],
+                            grads.at[:, pl.ds(z * rows, rows), pl.ds(base + col, piece)],
+                            stage_sem.at[slot, q],
+                        )
+                    )
+                return out
 
             for k in range(count * dim // TILE):
-                slot = stage_count[0] % 2
-                if stage_count[0] >= 2:
-                    out_copy(slot, k).wait()
-                stage_count[0] += 1
+                slot = len(stored) % 2
+                if len(stored) >= 2:
+                    wait(stored[-2])
                 cols = pl.ds(r_at(block) + k * TILE, TILE)
                 y = tn(lhs[i, :, own_l], rhs[0, :, cols]) + tn(lhs2[i], rhs[1, :, cols])
                 stage[slot] = y.astype(BF).reshape(pairs, rows, TILE)
-                out_copy(slot, k).start()
+                stored.append(out_copies(slot, k))
+                start(stored[-1])
 
         def to_heads(k, src, dst, send, got):
             out = []
@@ -773,12 +873,12 @@
         lhs[L_POOL_B] = pool_b_ref[...]
         lhs[L_COT] = cot_ref[...]
         acc = d_low
-        w_wait(0)
+        w_wait(GATE)
 
         def put_gate(at, y):
             gate[:, pl.ds(at, TILE)] = 1.0 / (1.0 + jnp.exp(-y))
         forward(lhs[L_LOW], GATE, 1, put_gate)
-        w_wait(1)
+        w_wait(HIGH_A, HIGH_B, OUT)
 
         def put_high(at, y):
             high[:, pl.ds(at, TILE)] = y
@@ -794,8 +894,7 @@
         merged[...] += lhs[L_LOW].astype(F32)
         lhs[L_FIRST] = normalise(merged[...], gain1_ref[...]).astype(BF)
 
-        w_wait(2)
-        w_wait(3)
+        w_wait(QUERY, KEY, VALUE, PROJ)
         pl.semaphore_wait(barrier, n)
         for i in (L_LOW, L_POOL_A, L_POOL_B, L_COT, L_FIRST):
             l_copy(i).start()
@@ -831,8 +930,7 @@
         lhs[L_SECOND] = normalise(resid[...], gain2_ref[...]).astype(BF)
         l_copy(L_SECOND).start()
 
-        w_wait(4)
-        w_wait(5)
+        w_wait(8)
 
         def put_up(at, y):
             value, rate = gelu_parts(y)
@@ -840,8 +938,7 @@
             slope[:, pl.ds(at, TILE)] = rate.astype(BF)
         forward(lhs[L_SECOND], 8, 4, put_up)
         r_copy(R_ACT).start()
-        w_wait(6)
-        w_wait(7)
+        w_wait(9)
         backward(lambda at: rhs[0, :, pl.ds(r_at(R_ACT) + at, dim)], 12, 4, acc, True)
         low_out[...] = resid[...] + acc[...]
 
@@ -921,8 +1018,8 @@
         grad(L_POOL_B, R_DHIGH, HIGH_B, 1, shared=True)
         l_copy(L_LOW).wait_recv()
         grad(L_LOW, R_DGATE, GATE, 1)
-        for slot in range(2):
-            pltpu.make_async_copy(stage.at[slot], grads.at[:, :, pl.ds(0, TILE)], stage_sem.at[slot]).wait()
+        wait(stored[-2])
+        wait(stored[-1])
         for i in range(8):
             l_copy(i).wait_send()
         for b in range(9):
@@ -935,8 +1032,8 @@
     one = jax.ShapeDtypeStruct((1, dim), F32)
     return pl.pallas_call(
         kernel,
-        out_shape=(tok, tok, tok, tok, one, one, jax.ShapeDtypeStruct((pairs, rows, 16 * dim), BF)),
-        in_specs=[local] * 6 + [whole] * 2,
+        out_shape=(tok, tok, tok, tok, one, one, jax.ShapeDtypeStruct((pairs, n * rows, 16 * width), BF)),
+        in_specs=[local] * 6 + [whole],
         out_specs=(local,) * 6 + (whole,),
         scratch_shapes=[
             vm((2, pairs, rows, 16 * dim), BF), vm((8, t, dim), BF), vm((8, t, half), BF), vm((2, t, 15 * dim), BF),
@@ -944,12 +1041,79 @@
             vm((t, ff), BF), vm((3, t, dim), BF), vm((3, every, width), BF), vm((every, width), BF), vm((every, width), BF),
             vm((1, 8, 128), BF), vm((3, every, width), BF), vm((heads, every, every), BF), vm((every, every), BF),
             vm((2, pairs, rows, TILE), BF),
-            dma((8, 2)), dma((3, n)), dma((3, n)), dma((1, n)), dma((1, n)), dma((1, n)), dma((1, n)), dma((3, n)), dma((3, n)),
-            dma((3,)), dma((8,)), dma((8,)), dma((9,)), dma((9,)), dma((2,)),
+            dma((10, 2 * n)), dma((3, n)), dma((3, n)), dma((1, n)), dma((1, n)), dma((1, n)), dma((1, n)), dma((3, n)), dma((3, n)),
+            dma((3,)), dma((8,)), dma((8,)), dma((9,)), dma((9,)), dma((2, 2)),
         ],
         compiler_params=pltpu.CompilerParams(collective_id=cid, has_side_effects=True, vmem_limit_bytes=61 * MIB),
         cost_estimate=pl.CostEstimate(flops=14 * 10**9, bytes_accessed=70 * 10**6, transcendentals=10**7),
-    )(low, pool_a, pool_b, cot, gain1, gain2, w1.reshape(pairs, 2, rows, 8 * dim), w2.reshape(pairs, 2, rows, 8 * dim))
+    )(low, pool_a, pool_b, cot, gain1, gain2, packed.reshape(pairs, 2, n, rows, 16 * width))
+def sum_everywhere(x, devices, n, cid):
+    rows = x.shape[1]
+
+    def kernel(x_ref, out, here, level, send1, recv1, send2, recv2, send3, recv3):
+        me, d = lax.axis_index("dp"), lax.axis_index("mp")
+        barrier = pltpu.get_barrier_semaphore()
+
+        def greet(k, _):
+            pl.semaphore_signal(
+                barrier, inc=1, device_id={"dp": lax.rem(me + k, devices)}, device_id_type=MESH
+            )
+            return 0
+
+        lax.fori_loop(1, devices, greet, 0)
+        for k in range(1, n):
+            pl.semaphore_signal(barrier, inc=1, device_id={"mp": lax.rem(d + k, n)}, device_id_type=MESH)
+        here[me] = x_ref[me]
+        pl.semaphore_wait(barrier, devices + n - 2)
+
+        def spread(k):
+            peer = lax.rem(me + k, devices)
+            return pltpu.make_async_remote_copy(
+                src_ref=x_ref.at[peer], dst_ref=here.at[me], send_sem=send1.at[k], recv_sem=recv1.at[k],
+                device_id={"dp": peer}, device_id_type=MESH,
+            )
+
+        def across(k):
+            return pltpu.make_async_remote_copy(
+                src_ref=level.at[d], dst_ref=level.at[d], send_sem=send2.at[k], recv_sem=recv2.at[k],
+                device_id={"mp": lax.rem(d + k, n)}, device_id_type=MESH,
+            )
+
+        def give(k):
+            return pltpu.make_async_remote_copy(
+                src_ref=out.at[me], dst_ref=out.at[me], send_sem=send3.at[k], recv_sem=recv3.at[k],
+                device_id={"dp": lax.rem(me + k, devices)}, device_id_type=MESH,
+            )
+
+        def each(count, make, act):
+            def one(k, _):
+                act(make(k))
+                return 0
+
+            lax.fori_loop(1, count, one, 0)
+
+        each(devices, spread, lambda c: c.start())
+        each(devices, spread, lambda c: c.wait())
+        level[d] = jnp.sum(here[...], axis=0)
+        each(n, across, lambda c: c.start())
+        each(n, across, lambda c: c.wait())
+        out[me] = jnp.sum(level[...], axis=0)
+        each(devices, give, lambda c: c.start())
+        each(devices, give, lambda c: c.wait())
+
+    vm, dma = pltpu.VMEM, pltpu.SemaphoreType.DMA
+    return pl.pallas_call(
+        kernel,
+        out_shape=jax.ShapeDtypeStruct(x.shape, F32),
+        in_specs=[pl.BlockSpec(memory_space=pltpu.VMEM)],
+        out_specs=pl.BlockSpec(memory_space=pltpu.VMEM),
+        scratch_shapes=[vm(x.shape, F32), vm((n, rows, LANES), F32)] + [dma((devices,)), dma((devices,)), dma((n,)), dma((n,)), dma((devices,)), dma((devices,))],
+        compiler_params=pltpu.CompilerParams(
+            collective_id=cid, has_side_effects=True, vmem_limit_bytes=16 * MIB
+        ),
+    )(x)
+
+
 def own_part(w, axis):
     length = w.shape[axis] // lax.axis_size("dp")
     return lax.dynamic_slice_in_dim(w, lax.axis_index("dp") * length, length, axis)
@@ -957,15 +1121,6 @@
 
 def fold(w, rows):
     return w[:rows], jnp.pad(w[rows:], ((0, 2 * rows - w.shape[0]), (0, 0)))
-
-
-def gather_packed(pieces, every):
-    n = every.shape[0]
-    parts, at = [], 0
-    for w in pieces:
-        parts.append(every[:, :, at : at + w].transpose(1, 0, 2).reshape(-1, n * w))
-        at += w
-    return lax.all_gather(jnp.concatenate(parts, axis=1), "dp", axis=0, tiled=True)
 
 
 def core_first(x, devices):
@@ -1023,25 +1178,18 @@
     dims = low_in.shape[2]
     share = dims // devices
     qkv = own_part(w_qkv, 1)
-    first_pieces = [
+    pieces = [
         own_part(ad_gate, 0), own_part(ad_out, 1).T, *fold(own_part(ad_high, 0), share),
-        qkv[0], qkv[1], qkv[2], own_part(w_proj, 1).T,
+        qkv[0], qkv[1], qkv[2], own_part(w_proj, 1).T, own_part(w_up, 0), own_part(w_down, 1).T,
     ]
-    second_pieces = [own_part(w_up, 0), own_part(w_down, 1).T]
-    first_every = lax.all_gather(jnp.concatenate(first_pieces, axis=1), "mp", axis=0)
-    second_every = lax.all_gather(jnp.concatenate(second_pieces, axis=1), "mp", axis=0)
+    packed = lax.all_gather(jnp.concatenate(pieces, axis=1), ("dp", "mp"), axis=0)
     plane_mask = valid.astype(jnp.float32)
     cell_mask = plane_mask[..., None]
     masked = hr_in * valid.astype(jnp.bfloat16)[..., None]
-    bordered = extended(masked, (("mp", 1),), 3)
     size = conv_w.shape[0]
     taps = conv_w.astype(F32).reshape(size * size, 1, chan_count)
-    conv_out = conv_forward(bordered[0], taps, size)[None]
-    conv_out, first_every, second_every = lax.optimization_barrier((conv_out, first_every, second_every))
-    first_widths = [p.shape[1] for p in first_pieces]
-    second_widths = [p.shape[1] for p in second_pieces]
-    packed_first = gather_packed(first_widths, first_every)
-    packed_second = gather_packed(second_widths, second_every)
+    conv_out, bordered = conv_forward(masked[0], taps, size, shards)
+    conv_out = conv_out[None]
     conv_out = conv_out * cell_mask
     hr_gainf = hr_gain.astype(jnp.float32)
     normed = layer_norm(conv_out, hr_gainf).astype(jnp.bfloat16)
@@ -1066,7 +1214,7 @@
     low_out, d_low_in, d_pool_a, d_pool_b, g_ln1, g_ln2, low_grads = low_stage(
         *(core_first(v, devices) for v in (low_in[0], pool_a, pool_b, cot_low[0])),
         *(core_first(v.astype(F32), devices)[None] for v in (ln1_gain, ln2_gain)),
-        packed_first, packed_second, shards, devices, 2,
+        packed, shards, devices, 2,
     )
     low_out = core_last(low_out, devices)[None]
     d_low_in = core_last(d_low_in, devices)[None]
@@ -1089,39 +1237,37 @@
         hidden_slope, cn_up, cn_down, low_grads, shards, devices,
     )
     d_normed = d_normed.reshape(hr_in.shape)
-    by_slice, at = [], 0
-    for whole, widths in zip(low_sums, (first_widths, second_widths)):
-        at = 0
-        for w in widths:
-            by_slice.append(whole[:, at : at + shards * w].reshape(share, shards, w).transpose(1, 0, 2))
-            at += shards * w
-    own = lax.psum_scatter(jnp.concatenate(by_slice, axis=2), "mp", scatter_dimension=0).astype(F32)
-    split, at = [], 0
-    for w in first_widths + second_widths:
-        split.append(own[:, at : at + w])
-        at += w
-    g_ad_gate, g_ad_out, g_high_a, g_high_b, g_query, g_key, g_value, g_proj, g_up, g_down = split
-    g_ad_high = jnp.concatenate([g_high_a, g_high_b[: ad_high.shape[0] // devices - share]], axis=0)
-    g_qkv = jnp.stack([g_query, g_key, g_value])
-    g_ad_out, g_proj, g_down = g_ad_out.T, g_proj.T, g_down.T
+    low_sums = lax.psum_scatter(low_sums.reshape(shards, share, -1), "mp", scatter_dimension=0)
     g_cn_down = jnp.einsum("tc,th->ch", d_branch_all, hidden_act, preferred_element_type=F32).astype(BF)
     g_cn_up = jnp.einsum("tc,th->ch", normed_all, d_hidden, preferred_element_type=F32).astype(BF)
     cn_grads = [g.reshape(devices, chan_count // devices, -1) for g in (g_cn_up, g_cn_down)]
     d_conv, g_hr_gain = jax.vjp(layer_norm, conv_out, hr_gainf)[1](d_normed)
     d_conv = d_conv * cell_mask
     d_bordered = extended(d_conv.astype(BF), (("mp", 1),), 3)
+    d_bordered, low_sums = lax.optimization_barrier((d_bordered, low_sums))
     d_conv_in, g_conv, (g_cn_up, g_cn_down) = conv_backward(
-        d_bordered[0], bordered[0], taps, size, cn_grads, devices
+        d_bordered[0], bordered, taps, size, cn_grads, devices
     )
+    own = low_sums.astype(F32)
+    split, at = [], 0
+    for p in pieces:
+        split.append(own[:, at : at + p.shape[1]])
+        at += p.shape[1]
+    g_ad_gate, g_ad_out, g_high_a, g_high_b, g_query, g_key, g_value, g_proj, g_up, g_down = split
+    g_ad_high = jnp.concatenate([g_high_a, g_high_b[: ad_high.shape[0] // devices - share]], axis=0)
+    g_qkv = jnp.stack([g_query, g_key, g_value])
+    g_ad_out, g_proj, g_down = g_ad_out.T, g_proj.T, g_down.T
     g_cn_up, g_cn_down = g_cn_up.astype(F32), g_cn_down.astype(F32).T
     g_conv = g_conv.reshape(conv_w.shape)
     d_hr_in = (d_branch + d_conv_in) * cell_mask
     small = (g_conv, g_hr_gain, g_ln1, g_ln2)
-    packed = jnp.concatenate([g.reshape(-1) for g in small])
-    packed = lax.psum(lax.psum(packed, "mp"), "dp")
+    flat = jnp.concatenate([g.reshape(-1) for g in small])
+    room = -(-flat.size // (devices * 8 * LANES)) * (devices * 8 * LANES)
+    flat = jnp.pad(flat, (0, room - flat.size)).reshape(devices, -1, LANES)
+    flat = sum_everywhere(flat, devices, shards, 4).reshape(-1)
     parts, at = [], 0
     for g in small:
-        parts.append(packed[at : at + g.size].reshape(g.shape))
+        parts.append(flat[at : at + g.size].reshape(g.shape))
         at += g.size
     g_conv, g_hr_gain, g_ln1, g_ln2 = parts
     return (

time: 1100 us -> 1010 us (0.918)
  waiting for transfers between devices: 213 us -> 69.3 us
  Pallas kernels: 609 us -> 738 us
  local copies, waits for them, and re-layouts: 158 us -> 108 us
    pallas_call x1, Pallas kernels: 177 us -> 259 us  [big_forward(): pl.pallas_call(kernel, out_shape=(jax.ShapeDtypeStruct((CHUNKS, rows, c),...]
    psum x2 -> x0, waiting for transfers between devices: 73.2 us -> none  [per_device(): packed = lax.psum(lax.psum(packed, 'mp'), 'dp')]
    reduce_scatter x1, waiting for transfers between devices: 74.2 us -> 37.4 us  [per_device(): lax.psum_scatter(low_sums.reshape(shards, share, -1), 'mp', scatter_dimen...]
    pallas_call x1 -> x2, Pallas kernels: 17.6 us -> 53 us  [the longest x1 34.5 us: conv_forward(): pl.pallas_call(kernel, out_shape=(jax.ShapeDtypeStruct((rows, cols, c), F...]
    all_gather x2 -> x1, local copies, waits for them, and re-layouts: 8.26 us -> 41.3 us  [per_device(): lax.all_gather(jnp.concatenate(pieces, axis=1), ('dp', 'mp'), axis=0)]
    transpose x13 -> x0, local copies, waits for them, and re-layouts: 30.1 us -> none  [the longest x12 29 us: gather_packed(): parts.append(every[:, :, at:at + w].transpose(1, 0, 2).reshape(-1, n * w))]
    unnamed x127 -> x109, local copies, waits for them, and re-layouts: 48.8 us -> 19.6 us
    ppermute x2 -> x1, waiting for transfers between devices: 16.1 us -> 0.01 us  [extended(): before = lax.ppermute(last, axis, up)]
  transfers between devices with their start and end apart: 11 -> 4, of which waited for: 6 -> 2; matrix products, arithmetic and copies ran while one was open for 13% -> 7% of each run, Pallas kernels for 18% -> 29%
where the time goes in v3:
time: 1010 us; the launch traced here: 999 us
  Pallas kernels  738 us (73%)
  local copies, waits for them, and re-layouts  108 us (11%)
  waiting for transfers between devices  69.3 us (7%)
  other arithmetic  38.3 us (4%)
  matrix products  26.8 us (3%)
  between operations  15.1 us (1%)
    pallas_call x1, Pallas kernels, big_forward(): pl.pallas_call(kernel, out_shape=(jax.ShapeDtypeStruct((CHUNKS, rows, c),...  259 us
    pallas_call x1, Pallas kernels, big_backward(): pl.pallas_call(kernel, out_shape=(jax.ShapeDtypeStruct((CHUNKS, rows, c),...  228 us
    pallas_call x1, Pallas kernels, low_stage(): pl.pallas_call(kernel, out_shape=(tok, tok, tok, tok, one, one, jax.Shape...  123 us
    pallas_call x1, Pallas kernels, conv_backward(): pl.pallas_call(kernel, grid=(blocks,), out_shape=(jax.ShapeDtypeStruct((r...  75.6 us
    all_gather x1, local copies, waits for them, and re-layouts, per_device(): lax.all_gather(jnp.concatenate(pieces, axis=1), ('dp', 'mp'), axis=0)  41.3 us
    reduce_scatter x1, waiting for transfers between devices, per_device(): lax.psum_scatter(low_sums.reshape(shards, share, -1), 'mp', scatter_dimen...  37.4 us
    pallas_call x1, Pallas kernels, conv_forward(): pl.pallas_call(kernel, out_shape=(jax.ShapeDtypeStruct((rows, cols, c), F...  34.5 us
    all_gather x1, waiting for transfers between devices, per_device(): lax.all_gather(jnp.concatenate(pieces, axis=1), ('dp', 'mp'), axis=0)  31.8 us
  transfers between devices with their start and end apart: 4, of which 2 were waited for; matrix products, arithmetic and copies ran while one was open for 7% of the time, Pallas kernels for 29%

profile of v3, /device:TPU:0, one launch (start us, length us, event | category | flops | bytes accessed | tf_op | source)
XLA Modules:
  0.0 999.4 jit_solution(3352064392428832182)
XLA Ops:
  7.3 1.0 constant_dynamic-slice_fusion.2
  10.8 0.9 constant_dynamic-slice_fusion.4
  14.2 0.9 constant_dynamic-update-slice_fusion.2
  19.5 1.0 bitcast_dynamic-update-slice_fusion
  20.5 1.0 copy-done.14
  23.1 1.4 reshape.254.w_ref
  24.7 34.5 %shard_map.305 = (f32[12,48,1536]{2,1,0:T(8,128)S(1)}, bf16[18,48,1536]{2,1,0:T(8,128)(2,1)S(1)}) custom-call(bf16[12,48,1536]{2,1,0:T(8,128)(2,1)S(1)} %multiply_bitcast_fusion.x_ref, f32[49,1,1536]{2,1,0:T(1,128)S(1)} %reshape.254.w_ref), custom_call_target="tpu_custom_call" | custom-call | tf_op jit(solution)/shard_map/pallas_call | solution.py:577
  60.7 1.1 copy-done.2
  61.8 1.8 multiply_convert_fusion.1
  63.7 259.0 %shard_map.306 = (f32[6,96,1536]{2,1,0:T(8,128)}, bf16[4,6,96,1536]{3,2,1,0:T(8,128)(2,1)}, bf16[4,6,96,1536]{3,2,1,0:T(8,128)(2,1)}, bf16[4,6,96,1536]{3,2,1,0:T(8,128)(2,1)}) custom-call(bf16[6,96,1536]{2,1,0:T(8,128)(2,1)} %bitcast.134, bf16[1536,1536]{1,0:T(8,128)(2,1)} %wu.3, bf16[1536,1536]{1,0:T(8,128)(2,1)} %wd.3), custom_call_target="tpu_custom_call" | custom-call | flops 21743271936 | bytes 28311552 | tf_op jit(solution)/shard_map/pallas_call | solution.py:342
  322.7 3.2 add_multiply_fusion.1
  325.9 3.9 reshape.234
  329.8 5.7 reduce_sum.69
  335.5 1.7 reduce_sum.70
  340.9 0.9 reshape.238.cot_ref
  344.1 31.8 %all-gather.3.cloned.1.call-done = bf16[4096,4096]{0,1:T(8,128)(2,1)} async-done(((bf16[128,4096]{0,1:T(8,128)(2,1)}), bf16[4096,4096]{0,1:T(8,128)(2,1)}) %all-gather.3.cloned.1.call-update) | async-done | bytes 33554448 | tf_op jit(solution)/shard_map/all_gather | solution.py:1185
  375.9 41.3 %copy.83 = bf16[4096,4096]{1,0:T(8,128)(2,1)} copy(bf16[4096,4096]{0,1:T(8,128)(2,1)} %all-gather.3.cloned.1.call-done) | data formatting | bytes 67108864 | tf_op jit(solution)/shard_map/all_gather | solution.py:1185
  417.2 122.8 %shard_map.307 = (f32[144,1024]{1,0:T(8,128)}, f32[144,1024]{1,0:T(8,128)}, f32[144,1024]{1,0:T(8,128)}, f32[144,1024]{1,0:T(8,128)}, f32[1,1024]{1,0:T(1,128)},...) custom-call(bf16[144,1024]{1,0:T(8,128)(2,1)} %reshape.231.low_ref, bf16[144,1024]{1,0:T(8,128)(2,1)} %reshape.236.pool_a_ref, ...), custom_call_target="tpu_custom_call" | custom-call | flops 14000000000 | bytes 70000000 | tf_op jit(solution)/shard_map/pallas_call | solution.py:1033
  540.0 1.3 reshape.244
  541.5 1.3 reshape.245
  544.3 3.0 broadcast_in_dim.10
  547.3 4.2 broadcast_in_dim.11
  551.5 4.4 fusion.1
  555.9 227.6 %shard_map.308 = (f32[6,96,1536]{2,1,0:T(8,128)}, bf16[4,6,96,1536]{3,2,1,0:T(8,128)(2,1)}, bf16[4,6,96,1536]{3,2,1,0:T(8,128)(2,1)}, bf16[2,1,1,256,4096]{4,3,2...) custom-call(bf16[6,96,1536]{2,1,0:T(8,128)(2,1)} %bitcast.133, ...), custom_call_target="tpu_custom_call" | custom-call | flops 21743271936 | bytes 28311552 | tf_op jit(solution)/shard_map/pallas_call | solution.py:453
  783.5 6.4 copy.89
  789.9 2.0 copy-done.3
  791.9 2.9 multiply_reduce_fusion.1
  795.0 2.2 multiply_reduce_fusion
  797.2 1.3 fusion.2
  798.5 1.2 copy-done.11
  799.7 1.0 fusion.5
  800.7 2.3 collective-permute-start
  803.0 1.3 collective-permute-start.1
  804.4 13.3 %bitcast_convert_fusion = bf16[1536,1536]{1,0:T(8,128)(2,1)} fusion(bf16[4,6,96,1536]{3,2,1,0:T(8,128)(2,1)S(1)} %bitcast.163, bf16[4,6,96,1536]{3,2,1,0:T(8,128)(2,1)S(1)} %bitcast.167), kind=kOutput, calls=%fused_computation | convolution fusion | flops 10873995264 | bytes 18874368 | tf_op jit(solution)/shard_map/tc,th->ch/dot_general | solution.py:1241
  817.8 13.4 %bitcast_convert_fusion.1 = bf16[1536,1536]{1,0:T(8,128)(2,1)} fusion(bf16[4,6,96,1536]{3,2,1,0:T(8,128)(2,1)S(1)} %bitcast.165, bf16[4,6,96,1536]{3,2,1,0:T(8,128)(2,1)S(1)} %bitcast.161), kind=kOutput, calls=%fused_computation.1 | convolution fusion | flops 10873995264 | bytes 18874368 | tf_op jit(solution)/shard_map/tc,th->ch/dot_general | solution.py:1242
  831.8 1.3 broadcast_in_dim_reshape.20
  834.3 1.3 broadcast_in_dim_reshape.21
  835.6 2.9 pad_maximum_fusion
  838.6 37.4 %reduce-scatter.2.cloned.1.call-done = bf16[1,128,4096]{1,2,0:T(8,128)(2,1)} async-done(((bf16[4,128,4096]{1,2,0:T(8,128)(2,1)}), bf16[1,128,4096]{1,2,0:T(8,128)(2,1)}) %reduce-scatter.2.cloned.1.call-update) | async-done | bytes 1048592 | tf_op jit(solution)/shard_map/reduce_scatter | solution.py:1240
  876.9 0.9 fusion.6
  877.8 1.0 slice.115
  878.8 1.4 convert_element_type.77
  881.7 75.6 %shard_map.309 = (f32[12,48,1536]{2,1,0:T(8,128)}, f32[49,1,1536]{2,1,0:T(1,128)S(1)}, bf16[4,192,1536]{2,1,0:T(8,128)(2,1)}, bf16[2,192,1536]{2,1,0:T(8,128)(2,...) custom-call(bf16[18,48,1536]{2,1,0:T(8,128)(2,1)} %bitcast.120, ...), custom_call_target="tpu_custom_call" | custom-call | tf_op jit(solution)/shard_map/pallas_call | solution.py:650
  959.0 18.6 %shard_map.310 = f32[8,80,128]{2,1,0:T(8,128)S(1)} custom-call(f32[8,80,128]{2,1,0:T(8,128)S(1)} %bitcast.112), custom_call_target="tpu_custom_call" | custom-call | tf_op jit(solution)/shard_map/pallas_call | solution.py:1105
  980.4 1.0 copy.95
  981.4 0.9 copy.94
  982.3 6.5 fusion
  989.6 2.8 convert_bitcast_fusion
  (171 shorter events, 29.8 us)
Async XLA Ops:
  7.2 6.8 copy-start
  7.2 14.3 %copy-start.31 = (bf16[1536]{0:T(1024)(128)(2,1)S(1)}, bf16[1536]{0:T(1024)(128)(2,1)}, u32[]{:S(2)}) copy-start(bf16[1536]{0:T(1024)(128)(2,1)} %param.22) | copy-start | bytes 9220
  7.2 14.3 %copy-start.30 = (s32[1,12,48]{2,0,1:T(1,128)S(1)}, s32[1,12,48]{2,0,1:T(1,128)}, u32[]{:S(2)}) copy-start(s32[1,12,48]{2,0,1:T(1,128)} %param.20) | copy-start | bytes 6916
  7.2 368.7 %all-gather.3.cloned.1.call-start = ((), (), s32[]{:S(2)}) async-start(), calls=%async_computation.2 | async-start | bytes 34603008 | tf_op jit(solution)/shard_map/all_gather | solution.py:1185
  14.0 10.5 %copy-start.13 = (bf16[1,12,48,1536]{3,2,1,0:T(8,128)(2,1)S(1)}, bf16[1,12,48,1536]{3,2,1,0:T(8,128)(2,1)}, u32[]{:S(2)}) copy-start(bf16[1,12,48,1536]{3,2,1,0:T(8,128)(2,1)} %param.18) | copy-start | bytes 5308420
  20.5 1.0 copy-start.14
  21.5 854.5 %reduce-scatter.2.cloned.1.call-start = ((), (), s32[]{:S(2)}) async-start(), calls=%async_computation.1 | async-start | bytes 5242880 | tf_op jit(solution)/shard_map/reduce_scatter | solution.py:1240
  21.6 39.1 %copy-start.19 = (f32[1536]{0:T(1024)}, f32[1536]{0:T(1024)S(1)}, u32[]{:S(2)}) copy-start(f32[1536]{0:T(1024)S(1)} %convert_element_type.65) | copy-start | bytes 18436
  21.6 38.0 %copy-start.27 = (bf16[1,12,48]{2,1,0:T(8,128)(2,1)}, bf16[1,12,48]{2,1,0:T(8,128)(2,1)S(1)}, u32[]{:S(2)}) copy-start(bf16[1,12,48]{2,1,0:T(8,128)(2,1)S(1)} %copy.117) | copy-start | bytes 3460
  21.9 0.6 copy-start.25
  24.5 35.1 %copy-start.4 = (f32[49,1,1536]{2,1,0:T(1,128)}, f32[49,1,1536]{2,1,0:T(1,128)S(1)}, u32[]{:S(2)}) copy-start(f32[49,1,1536]{2,1,0:T(1,128)S(1)} %reshape.254.w_ref) | copy-start | bytes 903172
  59.2 1.5 copy-start.6
  59.2 2.6 copy-start.2
  60.7 262.0 %copy-start.23 = (f32[12,48]{1,0:T(8,128)}, f32[12,48]{1,0:T(8,128)S(1)}, u32[]{:S(2)}) copy-start(f32[12,48]{1,0:T(8,128)S(1)} %multiply_reduce_fusion.2) | copy-start | bytes 6916
  61.8 260.9 %copy-start.21 = (f32[12,48]{1,0:T(8,128)}, f32[12,48]{1,0:T(8,128)S(1)}, u32[]{:S(2)}) copy-start(f32[12,48]{1,0:T(8,128)S(1)} %fusion.4) | copy-start | bytes 6916
  63.7 259.0 %copy-start.28 = (bf16[1,12,48]{2,1,0:T(8,128)(2,1)S(1)}, bf16[1,12,48]{2,1,0:T(8,128)(2,1)}, u32[]{:S(2)}) copy-start(bf16[1,12,48]{2,1,0:T(8,128)(2,1)} %copy-done.27) | copy-start | bytes 3460
  325.9 3.9 copy-start.10
  335.5 2.7 copy-start.33
  335.5 3.3 copy-start.34
  335.5 3.9 copy-start.17
  335.5 5.1 copy-start.18
  542.9 1.2 copy-start.26
  551.5 232.0 %copy-start.9 = (f32[1,12,48,1536]{3,2,1,0:T(8,128)}, f32[1,12,48,1536]{3,2,1,0:T(8,128)S(1)}, u32[]{:S(2)}) copy-start(f32[1,12,48,1536]{3,2,1,0:T(8,128)S(1)} %broadcast_in_dim.11) | copy-start | bytes 10616836
  789.9 2.0 copy-start.3
  791.9 2.9 copy-start.24
  791.9 3.1 copy-start.8
  791.9 3.1 copy-start.20
  791.9 3.1 copy-start.22
  791.9 12.4 %slice-start.6 = ((s8[7077888]{0:T(1024)(128)(4,1)}), s8[4194304]{0:T(1024)(128)(4,1)S(1)}, s32[]{:S(2)}) async-start(s8[7077888]{0:T(1024)(128)(4,1)} %bitcast.166), calls=%async_computation.9 | async-start | bytes 8388608
  795.0 9.3 slice-start.2
  795.0 9.3 slice-start.7
  797.2 7.1 slice-start.3
  797.2 20.5 %slice-start.4 = ((s8[7077888]{0:T(1024)(128)(4,1)}), s8[4194304]{0:T(1024)(128)(4,1)S(1)}, s32[]{:S(2)}) async-start(s8[7077888]{0:T(1024)(128)(4,1)} %bitcast.164), calls=%async_computation.7 | async-start | bytes 8388608
  798.5 1.2 copy-start.11
  799.7 18.0 %slice-start = ((s8[7077888]{0:T(1024)(128)(4,1)}), s8[4194304]{0:T(1024)(128)(4,1)S(1)}, s32[]{:S(2)}) async-start(s8[7077888]{0:T(1024)(128)(4,1)} %bitcast.160), calls=%async_computation.3 | async-start | bytes 8388608
  800.7 34.9 %collective-permute-start = (bf16[1,3,48,1536]{3,2,1,0:T(8,128)(2,1)}, bf16[1,3,48,1536]{3,2,1,0:T(8,128)(2,1)}, u32[]{:S(2)}, u32[]{:S(2)}) collective-permute-start(bf16[1,3,48,1536]{3,2,1,0:T(8,128)(2,1)} %get-tuple-element.121), channel_id=1, source_target_pairs={{0,1},{1,2},{2,3},{4,5},{5,6},{6,7},{8,9},{9,10},{10,11},{12,13},{... | collective-permute-start | bytes 1327112 | tf_op jit(solution)/shard_map/ppermute | solution.py:1143
  803.0 32.6 %collective-permute-start.1 = (bf16[1,3,48,1536]{3,2,1,0:T(8,128)(2,1)}, bf16[1,3,48,1536]{3,2,1,0:T(8,128)(2,1)}, u32[]{:S(2)}, u32[]{:S(2)}) collective-permute-start(bf16[1,3,48,1536]{3,2,1,0:T(8,128)(2,1)} %get-tuple-element.122), channel_id=1, source_target_pairs={{1,0},{2,1},{3,2},{5,4},{6,5},{7,6},{9,8},{10,9},{11,10},{13,12},{... | collective-permute-start | bytes 1327112 | tf_op jit(solution)/shard_map/ppermute | solution.py:1144
  804.3 13.4 %slice-start.1 = ((s8[7077888]{0:T(1024)(128)(4,1)}), s8[2883584]{0:T(1024)(128)(4,1)S(1)}, s32[]{:S(2)}) async-start(s8[7077888]{0:T(1024)(128)(4,1)} %bitcast.160), calls=%async_computation.4 | async-start | bytes 5767168
  804.4 13.4 %slice-start.5 = ((s8[7077888]{0:T(1024)(128)(4,1)}), s8[2883584]{0:T(1024)(128)(4,1)S(1)}, s32[]{:S(2)}) async-start(s8[7077888]{0:T(1024)(128)(4,1)} %bitcast.164), calls=%async_computation.8 | async-start | bytes 5767168
  817.7 13.4 %copy-start.16 = (f32[144,1024]{1,0:T(8,128)S(1)}, f32[144,1024]{1,0:T(8,128)}, u32[]{:S(2)}) copy-start(f32[144,1024]{1,0:T(8,128)} %get-tuple-element.42) | copy-start | bytes 1769476
  831.2 1.9 copy-start.32
  831.2 2.6 copy-start.15
  831.2 4.5 copy-start.12
  876.8 4.9 copy-start.5
  881.7 77.3 %copy-start.29 = (f32[1536]{0:T(1024)S(1)}, f32[1536]{0:T(1024)}, u32[]{:S(2)}) copy-start(f32[1536]{0:T(1024)} %get-tuple-element.114) | copy-start | bytes 18436
  957.4 0.8 copy-start.7
  982.3 10.0 %copy-start.1 = (bf16[1024,1024]{1,0:T(8,128)(2,1)S(1)}, bf16[1024,1024]{1,0:T(8,128)(2,1)}, u32[]{:S(2)}) copy-start(bf16[1024,1024]{1,0:T(8,128)(2,1)} %param.32) | copy-start | bytes 6291460
Sparse Core Ops, SparseCore 0:
  21.6 354.2 all-gather.2
  790.0 85.9 reduce-scatter.1

commit v4 on v3

--- a/solution.py
+++ b/solution.py
@@ -1,6 +1,7 @@
 import jax
 import jax.numpy as jnp
 from jax import lax
+from jax.experimental.layout import Layout, with_layout_constraint
 from jax.experimental import pallas as pl
 from jax.experimental.pallas import tpu as pltpu
 from jax.sharding import PartitionSpec as P
@@ -376,7 +377,7 @@
     bits = range(1, devices.bit_length() - 1)
     split = g_rows // 2
     steps = len(bits)
-    plans = [Halving(bits, [last] * steps, (pairs, split, g_cols), min(g_cols, 512)) for last in (True, False)]
+    plans = [Halving(bits, [last] * steps, (pairs, split, g_cols), min(g_cols, 2048)) for last in (True, False)]
     extras = [b for plan in plans for b in plan.buffers()[:-1]]
     each = 2 * steps - 1
 
@@ -486,10 +487,11 @@
     dst[:, EDGE:EDGE + cols] = src[...].astype(F32)
 
 
-def correlate(out, framed, taps, size, flip, group):
+def correlate(out, framed, taps, size, flip, group, first=0, last=None, every=1):
     rows, cols, _ = out.shape
     reach = size // 2
-    def some(r, _):
+    def some(k, _):
+        r = first + k * every
         acc = jnp.zeros((group, cols, LANES), F32)
         for a in range(size):
             for b in range(size):
@@ -497,7 +499,7 @@
                 acc = acc + framed[pl.ds(r * group + a, group), pl.ds(EDGE - reach + b, cols), :] * taps[tap]
         out[pl.ds(r * group, group)] = acc
         return 0
-    lax.fori_loop(0, rows // group, some, 0)
+    lax.fori_loop(0, (rows // group if last is None else last) - first if every == 1 else 2, some, 0)
 
 
 def conv_forward(x, w, size, n):
@@ -546,6 +548,15 @@
         def _():
             bordered[reach + rows :] = nothing
 
+        groups = rows // reach
+
+        def inner(i, _):
+            lanes = pl.ds(pl.multiple_of(i * LANES, LANES), LANES)
+            frame(framed.at[pl.ds(reach, rows)], x_ref.at[:, :, lanes])
+            correlate(out.at[:, :, lanes], framed, w_ref.at[:, :, lanes], size, False, reach, 1, groups - 1)
+            return 0
+
+        lax.fori_loop(0, c // LANES, inner, 0)
         keep.wait()
 
         @pl.when(has_up)
@@ -559,7 +570,7 @@
         def block(i, _):
             lanes = pl.ds(pl.multiple_of(i * LANES, LANES), LANES)
             frame(framed, bordered.at[:, :, lanes])
-            correlate(out.at[:, :, lanes], framed, w_ref.at[:, :, lanes], size, False, 4)
+            correlate(out.at[:, :, lanes], framed, w_ref.at[:, :, lanes], size, False, reach, 0, None, groups - 1)
             return 0
 
         lax.fori_loop(0, c // LANES, block, 0)
@@ -597,7 +608,7 @@
     shape = grads[0].shape
     plans = [Halving(range(steps), [True] + [last] * (steps - 1), shape, shape[2]) for last in (True, False)]
     blocks = c // LANES
-    due = [blocks * (p + 1) // (steps + 1) for p in range(steps)]
+    due = [3 + (blocks - 4) * p // max(steps - 2, 1) for p in range(steps)]
 
     def kernel(d_ref, x_ref, w_ref, g0, g1, out, g, *rest):
         extra, rest = rest[: 4 * steps], rest[4 * steps :]
@@ -668,6 +679,7 @@
         compiler_params=pltpu.CompilerParams(
             collective_id=3, has_side_effects=True, vmem_limit_bytes=40 * MIB
         ),
+        cost_estimate=pl.CostEstimate(flops=6 * 10**10, bytes_accessed=10**8, transcendentals=0),
     )(
         d, x, w, grads[0].reshape((shape[0] // 2, 2) + shape[1:]), grads[1].reshape((shape[0] // 2, 2) + shape[1:])
     )
@@ -1114,6 +1126,10 @@
     )(x)
 
 
+def rows_first(x):
+    return with_layout_constraint(x, Layout(major_to_minor=tuple(range(x.ndim))))
+
+
 def own_part(w, axis):
     length = w.shape[axis] // lax.axis_size("dp")
     return lax.dynamic_slice_in_dim(w, lax.axis_index("dp") * length, length, axis)
@@ -1182,7 +1198,8 @@
         own_part(ad_gate, 0), own_part(ad_out, 1).T, *fold(own_part(ad_high, 0), share),
         qkv[0], qkv[1], qkv[2], own_part(w_proj, 1).T, own_part(w_up, 0), own_part(w_down, 1).T,
     ]
-    packed = lax.all_gather(jnp.concatenate(pieces, axis=1), ("dp", "mp"), axis=0)
+    packed = rows_first(jnp.concatenate(pieces, axis=1))
+    packed = rows_first(lax.all_gather(packed, "mp", axis=0, tiled=True))
     plane_mask = valid.astype(jnp.float32)
     cell_mask = plane_mask[..., None]
     masked = hr_in * valid.astype(jnp.bfloat16)[..., None]
@@ -1193,6 +1210,8 @@
     conv_out = conv_out * cell_mask
     hr_gainf = hr_gain.astype(jnp.float32)
     normed = layer_norm(conv_out, hr_gainf).astype(jnp.bfloat16)
+    normed, packed = lax.optimization_barrier((normed, packed))
+    packed = rows_first(lax.all_gather(packed, "dp", axis=0, tiled=True))
     branch, normed_all, hidden_act, hidden_slope = big_forward(
         normed.reshape(row_count * col_count, chan_count), cn_up, cn_down, shards
     )
@@ -1237,17 +1256,31 @@
         hidden_slope, cn_up, cn_down, low_grads, shards, devices,
     )
     d_normed = d_normed.reshape(hr_in.shape)
-    low_sums = lax.psum_scatter(low_sums.reshape(shards, share, -1), "mp", scatter_dimension=0)
+    low_sums = rows_first(low_sums.reshape(shards, share, -1))
+    low_sums = rows_first(lax.psum_scatter(low_sums, "mp", scatter_dimension=0))
     g_cn_down = jnp.einsum("tc,th->ch", d_branch_all, hidden_act, preferred_element_type=F32).astype(BF)
     g_cn_up = jnp.einsum("tc,th->ch", normed_all, d_hidden, preferred_element_type=F32).astype(BF)
     cn_grads = [g.reshape(devices, chan_count // devices, -1) for g in (g_cn_up, g_cn_down)]
     d_conv, g_hr_gain = jax.vjp(layer_norm, conv_out, hr_gainf)[1](d_normed)
     d_conv = d_conv * cell_mask
     d_bordered = extended(d_conv.astype(BF), (("mp", 1),), 3)
-    d_bordered, low_sums = lax.optimization_barrier((d_bordered, low_sums))
     d_conv_in, g_conv, (g_cn_up, g_cn_down) = conv_backward(
         d_bordered[0], bordered, taps, size, cn_grads, devices
     )
+    g_cn_up, g_cn_down = g_cn_up.astype(F32), g_cn_down.astype(F32).T
+    g_conv = g_conv.reshape(conv_w.shape)
+    d_hr_in = (d_branch + d_conv_in) * cell_mask
+    small = (g_conv, g_hr_gain, g_ln1, g_ln2)
+    flat = jnp.concatenate([g.reshape(-1) for g in small])
+    room = -(-flat.size // (devices * 8 * LANES)) * (devices * 8 * LANES)
+    flat = jnp.pad(flat, (0, room - flat.size)).reshape(devices, -1, LANES)
+    flat, low_sums = lax.optimization_barrier((flat, low_sums))
+    flat = sum_everywhere(flat, devices, shards, 4).reshape(-1)
+    parts, at = [], 0
+    for g in small:
+        parts.append(flat[at : at + g.size].reshape(g.shape))
+        at += g.size
+    g_conv, g_hr_gain, g_ln1, g_ln2 = parts
     own = low_sums.astype(F32)
     split, at = [], 0
     for p in pieces:
@@ -1257,19 +1290,6 @@
     g_ad_high = jnp.concatenate([g_high_a, g_high_b[: ad_high.shape[0] // devices - share]], axis=0)
     g_qkv = jnp.stack([g_query, g_key, g_value])
     g_ad_out, g_proj, g_down = g_ad_out.T, g_proj.T, g_down.T
-    g_cn_up, g_cn_down = g_cn_up.astype(F32), g_cn_down.astype(F32).T
-    g_conv = g_conv.reshape(conv_w.shape)
-    d_hr_in = (d_branch + d_conv_in) * cell_mask
-    small = (g_conv, g_hr_gain, g_ln1, g_ln2)
-    flat = jnp.concatenate([g.reshape(-1) for g in small])
-    room = -(-flat.size // (devices * 8 * LANES)) * (devices * 8 * LANES)
-    flat = jnp.pad(flat, (0, room - flat.size)).reshape(devices, -1, LANES)
-    flat = sum_everywhere(flat, devices, shards, 4).reshape(-1)
-    parts, at = [], 0
-    for g in small:
-        parts.append(flat[at : at + g.size].reshape(g.shape))
-        at += g.size
-    g_conv, g_hr_gain, g_ln1, g_ln2 = parts
     return (
         low_out,
         hr_out,

time: 1010 us -> 812 us (0.80)
  Pallas kernels: 738 us -> 617 us
  local copies, waits for them, and re-layouts: 108 us -> 52.4 us
  waiting for transfers between devices: 69.3 us -> 54.9 us
    pallas_call x1, Pallas kernels: 259 us -> 177 us  [big_forward(): pl.pallas_call(kernel, out_shape=(jax.ShapeDtypeStruct((CHUNKS, rows, c),...]
    all_gather x1 -> x0, local copies, waits for them, and re-layouts: 41.3 us -> none  [per_device(): lax.all_gather(jnp.concatenate(pieces, axis=1), ('dp', 'mp'), axis=0)]
    reduce_scatter x1, waiting for transfers between devices: 37.4 us -> 0.02 us  [per_device(): low_sums = rows_first(lax.psum_scatter(low_sums, 'mp', scatter_dimension=0))]
    pallas_call x1, Pallas kernels: 228 us -> 207 us  [big_backward(): pl.pallas_call(kernel, out_shape=(jax.ShapeDtypeStruct((CHUNKS, rows, c),...]
    all_gather x1 -> x2, waiting for transfers between devices: 31.8 us -> 50.6 us  [the longest x1 50.6 us: per_device(): packed = rows_first(lax.all_gather(packed, 'mp', axis=0, tiled=True))]
    pallas_call x1, Pallas kernels: 123 us -> 109 us  [low_stage(): pl.pallas_call(kernel, out_shape=(tok, tok, tok, tok, one, one, jax.Shape...]
  transfers between devices with their start and end apart: 4 -> 5, of which waited for: 2 -> 2; matrix products, arithmetic and copies ran while one was open for 7% -> 9% of each run, Pallas kernels for 29% -> 34%
where the time goes in v4:
time: 812 us; the launch traced here: 805 us
  Pallas kernels  617 us (76%)
  waiting for transfers between devices  54.9 us (7%)
  local copies, waits for them, and re-layouts  52.4 us (6%)
  other arithmetic  36.9 us (5%)
  matrix products  26 us (3%)
  between operations  14.9 us (2%)
    pallas_call x1, Pallas kernels, big_backward(): pl.pallas_call(kernel, out_shape=(jax.ShapeDtypeStruct((CHUNKS, rows, c),...  207 us
    pallas_call x1, Pallas kernels, big_forward(): pl.pallas_call(kernel, out_shape=(jax.ShapeDtypeStruct((CHUNKS, rows, c),...  177 us
    pallas_call x1, Pallas kernels, low_stage(): pl.pallas_call(kernel, out_shape=(tok, tok, tok, tok, one, one, jax.Shape...  109 us
    pallas_call x1, Pallas kernels, conv_backward(): pl.pallas_call(kernel, grid=(blocks,), out_shape=(jax.ShapeDtypeStruct((r...  70.6 us
    all_gather x1, waiting for transfers between devices, per_device(): packed = rows_first(lax.all_gather(packed, 'mp', axis=0, tiled=True))  50.6 us
    pallas_call x1, Pallas kernels, conv_forward(): pl.pallas_call(kernel, out_shape=(jax.ShapeDtypeStruct((rows, cols, c), F...  28.7 us
    pallas_call x1, Pallas kernels, sum_everywhere(): pl.pallas_call(kernel, out_shape=jax.ShapeDtypeStruct(x.shape, F32), in_s...  24.3 us
  transfers between devices with their start and end apart: 5, of which 2 were waited for; matrix products, arithmetic and copies ran while one was open for 9% of the time, Pallas kernels for 34%

profile of v4, /device:TPU:0, one launch (start us, length us, event | category | flops | bytes accessed | tf_op | source)
XLA Modules:
  0.0 805.1 jit_solution(18236318649852663829)
XLA Ops:
  7.3 1.0 constant_dynamic-slice_fusion.1
  9.1 0.9 dynamic-slice_dynamic-update-slice_fusion.2
  14.2 1.0 dynamic-slice_dynamic-update-slice_fusion
  15.2 1.0 copy-done.14
  16.4 1.4 reshape.253.w_ref
  17.9 28.7 %shard_map.305 = (f32[12,48,1536]{2,1,0:T(8,128)S(1)}, bf16[18,48,1536]{2,1,0:T(8,128)(2,1)S(1)}) custom-call(bf16[12,48,1536]{2,1,0:T(8,128)(2,1)S(1)} %multiply_bitcast_fusion.x_ref, f32[49,1,1536]{2,1,0:T(1,128)S(1)} %reshape.253.w_ref), custom_call_target="tpu_custom_call" | custom-call | tf_op jit(solution)/shard_map/pallas_call | solution.py:588
  48.2 1.1 copy-done.2
  49.3 1.8 fusion.2
  51.1 50.6 %all-gather.3.cloned.1.call-done = bf16[512,4096]{1,0:T(8,128)(2,1)} async-done(((bf16[128,4096]{1,0:T(8,128)(2,1)}), bf16[512,4096]{1,0:T(8,128)(2,1)}) %all-gather.3.cloned.1.call-update) | async-done | bytes 4194320 | tf_op jit(solution)/shard_map/all_gather | solution.py:1202
  104.2 0.9 reshape.230.low_ref
  105.4 0.9 reshape.237.cot_ref
  106.4 177.0 %shard_map.306 = (f32[6,96,1536]{2,1,0:T(8,128)}, bf16[4,6,96,1536]{3,2,1,0:T(8,128)(2,1)}, bf16[4,6,96,1536]{3,2,1,0:T(8,128)(2,1)}, bf16[4,6,96,1536]{3,2,1,0:T(8,128)(2,1)}) custom-call(bf16[6,96,1536]{2,1,0:T(8,128)(2,1)} %bitcast.139, bf16[1536,1536]{1,0:T(8,128)(2,1)} %wu.3, bf16[1536,1536]{1,0:T(8,128)(2,1)} %wd.3), custom_call_target="tpu_custom_call" | custom-call | flops 21743271936 | bytes 28311552 | tf_op jit(solution)/shard_map/pallas_call | solution.py:343
  283.4 3.1 add_multiply_fusion.1
  286.5 3.9 reshape.233
  290.4 5.5 reduce_sum.69
  295.9 1.5 reduce_sum.70
  297.4 0.9 divide_convert_fusion
  298.6 0.9 reshape.235.pool_a_ref
  299.8 0.9 reshape.236.pool_b_ref
  300.7 108.9 %shard_map.307 = (f32[144,1024]{1,0:T(8,128)}, f32[144,1024]{1,0:T(8,128)}, f32[144,1024]{1,0:T(8,128)}, f32[144,1024]{1,0:T(8,128)}, f32[1,1024]{1,0:T(1,128)},...) custom-call(bf16[144,1024]{1,0:T(8,128)(2,1)} %reshape.230.low_ref, bf16[144,1024]{1,0:T(8,128)(2,1)} %reshape.235.pool_a_ref, ...), custom_call_target="tpu_custom_call" | custom-call | flops 14000000000 | bytes 70000000 | tf_op jit(solution)/shard_map/pallas_call | solution.py:1045
  409.6 1.4 reshape.241
  411.3 1.3 broadcast_in_dim_reshape.20
  414.4 1.3 broadcast_in_dim_reshape.21
  417.9 3.0 broadcast_in_dim.10
  420.9 4.2 broadcast_in_dim.11
  425.1 4.4 fusion.1
  429.6 207.3 %shard_map.308 = (f32[6,96,1536]{2,1,0:T(8,128)}, bf16[4,6,96,1536]{3,2,1,0:T(8,128)(2,1)}, bf16[4,6,96,1536]{3,2,1,0:T(8,128)(2,1)}, bf16[2,1,1,256,4096]{4,3,2...) custom-call(bf16[6,96,1536]{2,1,0:T(8,128)(2,1)} %bitcast.138, ...), custom_call_target="tpu_custom_call" | custom-call | flops 21743271936 | bytes 28311552 | tf_op jit(solution)/shard_map/pallas_call | solution.py:454
  637.0 2.0 copy-done.3
  638.9 2.9 multiply_reduce_fusion.1
  642.0 2.2 multiply_reduce_fusion
  644.3 1.3 fusion.3
  645.7 1.6 collective-permute-start
  647.2 1.6 collective-permute-start.1
  648.9 13.1 %bitcast_convert_fusion = bf16[1536,1536]{1,0:T(8,128)(2,1)} fusion(bf16[4,6,96,1536]{3,2,1,0:T(8,128)(2,1)S(1)} %bitcast.171, bf16[4,6,96,1536]{3,2,1,0:T(8,128)(2,1)S(1)} %bitcast.175), kind=kOutput, calls=%fused_computation | convolution fusion | flops 10873995264 | bytes 18874368 | tf_op jit(solution)/shard_map/tc,th->ch/dot_general | solution.py:1261
  662.1 12.9 %bitcast_convert_fusion.1 = bf16[1536,1536]{1,0:T(8,128)(2,1)} fusion(bf16[4,6,96,1536]{3,2,1,0:T(8,128)(2,1)S(1)} %bitcast.173, bf16[4,6,96,1536]{3,2,1,0:T(8,128)(2,1)S(1)} %bitcast.169), kind=kOutput, calls=%fused_computation.1 | convolution fusion | flops 10873995264 | bytes 18874368 | tf_op jit(solution)/shard_map/tc,th->ch/dot_general | solution.py:1262
  675.0 4.2 collective-permute-done.1
  679.2 1.9 maximum_bitcast_fusion.d_ref
  681.1 70.6 %shard_map.309 = (f32[12,48,1536]{2,1,0:T(8,128)}, f32[49,1,1536]{2,1,0:T(1,128)S(1)}, bf16[4,192,1536]{2,1,0:T(8,128)(2,1)}, bf16[2,192,1536]{2,1,0:T(8,128)(2,...) custom-call(bf16[18,48,1536]{2,1,0:T(8,128)(2,1)} %maximum_bitcast_f, ...), custom_call_target="tpu_custom_call" | custom-call | flops 60000002048 | bytes 100000000 | tf_op jit(solution)/shard_map/pallas_call | solution.py:661
  751.7 1.5 reduce.13
  753.2 1.0 reshape_reshape.46
  754.2 1.1 bitcast_convert_fusion.2
  755.4 1.1 convert_bitcast_fusion
  757.1 4.9 fusion
  762.0 24.3 %shard_map.310 = f32[8,80,128]{2,1,0:T(8,128)S(1)} custom-call(f32[8,80,128]{2,1,0:T(8,128)S(1)} %bitcast.121), custom_call_target="tpu_custom_call" | custom-call | tf_op jit(solution)/shard_map/pallas_call | solution.py:1117
  788.3 1.5 fusion.10
  789.8 1.8 slice.115
  794.2 1.0 copy.83
  796.6 1.7 pad_maximum_fusion.1
  (174 shorter events, 21.1 us)
Async XLA Ops:
  7.2 1.7 copy-start
  7.2 9.1 %copy-start.34 = (bf16[1536]{0:T(1024)(128)(2,1)S(1)}, bf16[1536]{0:T(1024)(128)(2,1)}, u32[]{:S(2)}) copy-start(bf16[1536]{0:T(1024)(128)(2,1)} %param.22) | copy-start | bytes 9220
  7.2 9.1 %copy-start.31 = (s32[1,12,48]{2,0,1:T(1,128)S(1)}, s32[1,12,48]{2,0,1:T(1,128)}, u32[]{:S(2)}) copy-start(s32[1,12,48]{2,0,1:T(1,128)} %param.20) | copy-start | bytes 6916
  7.2 94.5 %all-gather.3.cloned.1.call-start = ((), (), s32[]{:S(2)}) async-start(), calls=%async_computation.1 | async-start | bytes 5242880 | tf_op jit(solution)/shard_map/all_gather | solution.py:1202
  8.9 8.8 %copy-start.11 = (bf16[1,12,48,1536]{3,2,1,0:T(8,128)(2,1)S(1)}, bf16[1,12,48,1536]{3,2,1,0:T(8,128)(2,1)}, u32[]{:S(2)}) copy-start(bf16[1,12,48,1536]{3,2,1,0:T(8,128)(2,1)} %param.18) | copy-start | bytes 5308420
  16.2 284.4 %all-gather.5.cloned.1.call-start = ((), (), s32[]{:S(2)}) async-start(), calls=%async_computation.2 | async-start | bytes 37748736 | tf_op jit(solution)/shard_map/all_gather | solution.py:1214
  16.3 31.9 %copy-start.20 = (f32[1536]{0:T(1024)}, f32[1536]{0:T(1024)S(1)}, u32[]{:S(2)}) copy-start(f32[1536]{0:T(1024)S(1)} %convert_element_type.67) | copy-start | bytes 18436
  16.4 30.7 %copy-start.28 = (bf16[1,12,48]{2,1,0:T(8,128)(2,1)}, bf16[1,12,48]{2,1,0:T(8,128)(2,1)S(1)}, u32[]{:S(2)}) copy-start(bf16[1,12,48]{2,1,0:T(8,128)(2,1)S(1)} %copy.99) | copy-start | bytes 3460
  17.7 29.4 %copy-start.4 = (f32[49,1,1536]{2,1,0:T(1,128)}, f32[49,1,1536]{2,1,0:T(1,128)S(1)}, u32[]{:S(2)}) copy-start(f32[49,1,1536]{2,1,0:T(1,128)S(1)} %reshape.253.w_ref) | copy-start | bytes 903172
  46.7 2.6 copy-start.2
  48.2 53.6 %copy-start.24 = (f32[12,48]{1,0:T(8,128)}, f32[12,48]{1,0:T(8,128)S(1)}, u32[]{:S(2)}) copy-start(f32[12,48]{1,0:T(8,128)S(1)} %multiply_reduce_fusion.2) | copy-start | bytes 6916
  49.3 52.4 %copy-start.22 = (f32[12,48]{1,0:T(8,128)}, f32[12,48]{1,0:T(8,128)S(1)}, u32[]{:S(2)}) copy-start(f32[12,48]{1,0:T(8,128)S(1)} %fusion.8) | copy-start | bytes 6916
  49.3 52.5 %copy-start.37 = (bf16[1024]{0:T(1024)(128)(2,1)S(1)}, bf16[1024]{0:T(1024)(128)(2,1)}, u32[]{:S(2)}) copy-start(bf16[1024]{0:T(1024)(128)(2,1)} %param.28) | copy-start | bytes 6148
  49.3 53.1 %copy-start.38 = (bf16[1024]{0:T(1024)(128)(2,1)S(1)}, bf16[1024]{0:T(1024)(128)(2,1)}, u32[]{:S(2)}) copy-start(bf16[1024]{0:T(1024)(128)(2,1)} %param.31) | copy-start | bytes 6148
  51.1 52.8 %copy-start.18 = (bf16[1,144,1024]{2,1,0:T(8,128)(2,1)S(1)}, bf16[1,144,1024]{2,1,0:T(8,128)(2,1)}, u32[]{:S(2)}) copy-start(bf16[1,144,1024]{2,1,0:T(8,128)(2,1)} %param.19) | copy-start | bytes 884740
  51.1 54.0 %copy-start.19 = (bf16[1,144,1024]{2,1,0:T(8,128)(2,1)S(1)}, bf16[1,144,1024]{2,1,0:T(8,128)(2,1)}, u32[]{:S(2)}) copy-start(bf16[1,144,1024]{2,1,0:T(8,128)(2,1)} %param.34) | copy-start | bytes 884740
  101.8 660.3 %reduce-scatter.2.cloned.1.call-start = ((), (), s32[]{:S(2)}) async-start(), calls=%async_computation.3 | async-start | bytes 5242880 | tf_op jit(solution)/shard_map/reduce_scatter | solution.py:1260
  106.4 177.0 %copy-start.29 = (bf16[1,12,48]{2,1,0:T(8,128)(2,1)S(1)}, bf16[1,12,48]{2,1,0:T(8,128)(2,1)}, u32[]{:S(2)}) copy-start(bf16[1,12,48]{2,1,0:T(8,128)(2,1)} %copy-done.28) | copy-start | bytes 3460
  286.5 3.9 copy-start.10
  409.6 3.1 copy-start.36
  409.6 3.7 copy-start.35
  409.6 4.3 copy-start.17
  409.6 6.1 copy-start.16
  411.3 4.8 copy-start.15
  425.1 4.5 copy-start.8
  636.9 2.0 copy-start.3
  638.9 2.9 copy-start.25
  638.9 3.1 copy-start.7
  638.9 3.1 copy-start.21
  638.9 3.1 copy-start.23
  638.9 9.9 %slice-start.6 = ((s8[7077888]{0:T(1024)(128)(4,1)}), s8[4194304]{0:T(1024)(128)(4,1)S(1)}, s32[]{:S(2)}) async-start(s8[7077888]{0:T(1024)(128)(4,1)} %bitcast.174), calls=%async_computation.10 | async-start | bytes 8388608
  642.0 6.8 slice-start.2
  642.0 6.8 slice-start.7
  644.3 4.6 slice-start.3
  644.3 17.7 %slice-start.4 = ((s8[7077888]{0:T(1024)(128)(4,1)}), s8[4194304]{0:T(1024)(128)(4,1)S(1)}, s32[]{:S(2)}) async-start(s8[7077888]{0:T(1024)(128)(4,1)} %bitcast.172), calls=%async_computation.8 | async-start | bytes 8388608
  645.6 16.4 %slice-start = ((s8[7077888]{0:T(1024)(128)(4,1)}), s8[4194304]{0:T(1024)(128)(4,1)S(1)}, s32[]{:S(2)}) async-start(s8[7077888]{0:T(1024)(128)(4,1)} %bitcast.168), calls=%async_computation.4 | async-start | bytes 8388608
  645.7 29.3 %collective-permute-start = (bf16[1,3,48,1536]{3,2,1,0:T(8,128)(2,1)S(1)}, bf16[1,3,48,1536]{3,2,1,0:T(8,128)(2,1)S(1)}, u32[]{:S(2)}, u32[]{:S(2)}) collective-permute-start(bf16[1,3,48,1536]{3,2,1,0:T(8,128)(2,1)S(1)} %get-tuple-element.125), channel_id=1, source_target_pairs={{0,1},{1,2},{2,3},{4,5},{5,6},{6,7},{8,9},{9,10},{10,11},{12,13},{... | collective-permute-start | bytes 1327112 | tf_op jit(solution)/shard_map/ppermute | solution.py:1159
  647.2 31.9 %collective-permute-start.1 = (bf16[1,3,48,1536]{3,2,1,0:T(8,128)(2,1)S(1)}, bf16[1,3,48,1536]{3,2,1,0:T(8,128)(2,1)S(1)}, u32[]{:S(2)}, u32[]{:S(2)}) collective-permute-start(bf16[1,3,48,1536]{3,2,1,0:T(8,128)(2,1)S(1)} %get-tuple-element.126), channel_id=1, source_target_pairs={{1,0},{2,1},{3,2},{5,4},{6,5},{7,6},{9,8},{10,9},{11,10},{13,12},{... | collective-permute-start | bytes 1327112 | tf_op jit(solution)/shard_map/ppermute | solution.py:1160
  648.9 13.2 %slice-start.1 = ((s8[7077888]{0:T(1024)(128)(4,1)}), s8[2883584]{0:T(1024)(128)(4,1)S(1)}, s32[]{:S(2)}) async-start(s8[7077888]{0:T(1024)(128)(4,1)} %bitcast.168), calls=%async_computation.5 | async-start | bytes 5767168
  648.9 13.2 %slice-start.5 = ((s8[7077888]{0:T(1024)(128)(4,1)}), s8[2883584]{0:T(1024)(128)(4,1)S(1)}, s32[]{:S(2)}) async-start(s8[7077888]{0:T(1024)(128)(4,1)} %bitcast.172), calls=%async_computation.9 | async-start | bytes 5767168
  675.0 6.2 copy-start.5
  681.1 75.4 %copy-start.12 = (bf16[1,12,48,1536]{3,2,1,0:T(8,128)(2,1)S(1)}, bf16[1,12,48,1536]{3,2,1,0:T(8,128)(2,1)}, u32[]{:S(2)}) copy-start(bf16[1,12,48,1536]{3,2,1,0:T(8,128)(2,1)} %param.35) | copy-start | bytes 5308420
  754.2 2.9 copy-start.9
  757.1 4.9 copy-start.30
  757.1 4.9 copy-start.32
  757.1 4.9 copy-start.33
  762.0 29.6 %copy-start.13 = (bf16[1,128,4096]{2,1,0:T(8,128)(2,1)S(1)}, bf16[1,128,4096]{2,1,0:T(8,128)(2,1)}, u32[]{:S(2)}) copy-start(bf16[1,128,4096]{2,1,0:T(8,128)(2,1)} %reduce-scatter.2.cloned.1.call-done) | copy-start | bytes 3145732
  791.6 6.7 copy-start.1
  (4 other events, 4.3 us)
Sparse Core Ops, SparseCore 0:
  16.3 85.3 all-gather.2
  103.6 159.7 all-gather.4
  637.1 88.2 reduce-scatter.1

commit v5 on v4

--- a/solution.py
+++ b/solution.py
@@ -96,9 +96,10 @@
         )
 
 
-def chain_exchange(n, chunks, lag, own_hbm, gathered, partial, travel, compute, result_hbm,
-                   sems, prepare, arrived, mates=(), begin=None, turn=None):
-    ag_send, ag_recv, rs_send, rs_recv, local_sem = sems
+def chain_exchange(
+    n, chunks, lag, gathered, partial, travel, sems, own_chunk, prepare, arrived, compute, mates=(), begin=None, turn=None
+):
+    ag_send, ag_recv, rs_send, rs_recv = sems
     d = lax.axis_index("mp")
     has_left, has_right = d > 0, d < n - 1
 
@@ -115,19 +116,17 @@
     for mate in mates:
         pl.semaphore_signal(barrier, inc=1, device_id={"dp": mate}, device_id_type=MESH)
 
-    load = pltpu.make_async_copy(own_hbm, gathered.at[d], local_sem)
-    load.start()
-
+    own_chunk(0)
     pl.semaphore_wait(barrier, has_left.astype(jnp.int32) + has_right.astype(jnp.int32) + len(mates))
     if begin is not None:
         begin()
-    load.wait()
 
     def ag(way, s, j):
         return pltpu.make_async_remote_copy(
             src_ref=gathered.at[s, j], dst_ref=gathered.at[s, j],
             send_sem=ag_send.at[way, s, j], recv_sem=ag_recv.at[s, j],
-            device_id={"mp": d + 1 - 2 * way}, device_id_type=MESH)
+            device_id={"mp": d + 1 - 2 * way}, device_id_type=MESH,
+        )
 
     def rs(way, s, j):
         there = d + 1 - 2 * way
@@ -135,12 +134,17 @@
         return pltpu.make_async_remote_copy(
             src_ref=travel.at[s, j], dst_ref=travel.at[slot, j],
             send_sem=rs_send.at[s, j], recv_sem=rs_recv.at[slot, j],
-            device_id={"mp": there}, device_id_type=MESH)
+            device_id={"mp": there}, device_id_type=MESH,
+        )
 
     def rs_wait(slot, j):
         pltpu.make_async_copy(travel.at[slot, j], travel.at[slot, j], rs_recv.at[slot, j]).wait()
 
     def first(j, _):
+        @pl.when(j > 0)
+        def _():
+            own_chunk(j)
+
         @pl.when(has_right)
         def _():
             ag(0, d, j).start()
@@ -148,8 +152,36 @@
         @pl.when(has_left)
         def _():
             ag(1, d, j).start()
+
         return 0
+
     lax.fori_loop(0, chunks, first, 0)
+
+    def flow(way, q):
+        ql = jnp.clip(q, 0, n * chunks - 1)
+        s, jj = ql // chunks, lax.rem(ql, chunks)
+        if way == 1:
+            s = n - 1 - s
+        ahead = (s > d) if way == 0 else (s < d)
+        source = has_left if way == 0 else has_right
+
+        @pl.when((q >= 0) & (q < n * chunks) & (ahead | ((s == d) & source)))
+        def _():
+            @pl.when(source)
+            def _():
+                rs_wait(jnp.where(s == d, n, s) if way == 0 else s, jj)
+
+            @pl.when(ahead & source)
+            def _():
+                travel[s, jj] = (partial[s, jj].astype(F32) + travel[s, jj].astype(F32)).astype(BF)
+
+            @pl.when(ahead & jnp.logical_not(source))
+            def _():
+                travel[s, jj] = partial[s, jj].astype(BF)
+
+            @pl.when(ahead)
+            def _():
+                rs(way, s, jj).start()
 
     def step(g, _):
         k, j = g // chunks, lax.rem(g, chunks)
@@ -164,11 +196,13 @@
 
                 @pl.when(ok)
                 def _():
-                    prepare(s, j)
+                    prepare(way, s, j)
 
                     @pl.when(k > 0)
                     def _():
-                        pltpu.make_async_copy(gathered.at[s, j], gathered.at[s, j], ag_recv.at[s, j]).wait()
+                        pltpu.make_async_copy(
+                            gathered.at[s, j], gathered.at[s, j], ag_recv.at[s, j]
+                        ).wait()
 
                         @pl.when((way == 0) & has_right)
                         def _():
@@ -177,69 +211,19 @@
                         @pl.when((way == 1) & has_left)
                         def _():
                             ag(1, s, j).start()
+
                     arrived(s, j)
-                    compute(s, j)
+                    compute(way, s, j)
+
                 return 0
+
             lax.fori_loop(0, 2, side, 0)
 
-        q = g - (n - 1 - d) * lag
-        ql = jnp.clip(q, 0, n * chunks - 1)
-        s, jj = n - 1 - ql // chunks, lax.rem(ql, chunks)
-
-        @pl.when((q >= 0) & (q < n * chunks) & (s <= d) & (has_right | (s < d)))
-        def _():
-            @pl.when(has_right)
-            def _():
-                rs_wait(s, jj)
-
-                @pl.when(s < d)
-                def _():
-                    travel[s, jj] = (partial[s, jj].astype(F32) + travel[s, jj].astype(F32)).astype(BF)
-
-                @pl.when(s == d)
-                def _():
-                    partial[s, jj] = (partial[s, jj].astype(F32) + travel[s, jj].astype(F32)).astype(partial.dtype)
-
-            @pl.when(d == n - 1)
-            def _():
-                travel[s, jj] = partial[s, jj].astype(BF)
-
-            @pl.when(s < d)
-            def _():
-                rs(1, s, jj).start()
-
-        q2 = g - d * lag
-        qr = jnp.clip(q2, 0, n * chunks - 1)
-        s2, j2 = qr // chunks, lax.rem(qr, chunks)
-
-        @pl.when((q2 >= 0) & (q2 < n * chunks) & (s2 >= d) & (has_left | (s2 > d)))
-        def _():
-            @pl.when(has_left)
-            def _():
-                slot = jnp.where(s2 == d, n, s2)
-                rs_wait(slot, j2)
-
-                @pl.when(s2 > d)
-                def _():
-                    travel[s2, j2] = (partial[s2, j2].astype(F32) + travel[s2, j2].astype(F32)).astype(BF)
-
-                @pl.when(s2 == d)
-                def _():
-                    partial[s2, j2] = (partial[s2, j2].astype(F32) + travel[n, j2].astype(F32)).astype(partial.dtype)
-
-            @pl.when(d == 0)
-            def _():
-                travel[s2, j2] = partial[s2, j2].astype(BF)
-
-            @pl.when(s2 > d)
-            def _():
-                rs(0, s2, j2).start()
+        flow(1, g - (n - 1 - d) * lag)
+        flow(0, g - d * lag)
         return 0
 
     lax.fori_loop(0, n * chunks + (n - 1) * lag, step, 0)
-
-    store = pltpu.make_async_copy(partial.at[d], result_hbm, local_sem)
-    store.start()
 
     def drain(i, _):
         s, j = i // chunks, lax.rem(i, chunks)
@@ -259,14 +243,27 @@
         @pl.when(s > d)
         def _():
             rs(0, s, j).wait_send()
+
         return 0
+
     lax.fori_loop(0, n * chunks, drain, 0)
-    store.wait()
+
+
+def own_sum(n, d, j, partial, travel, total):
+    total[...] = partial[d, j].astype(F32)
+
+    @pl.when(d > 0)
+    def _():
+        total[...] += travel[n, j].astype(F32)
+
+    @pl.when(d < n - 1)
+    def _():
+        total[...] += travel[d, j].astype(F32)
 
 
 def chain_sems(n, chunks):
     dma = pltpu.SemaphoreType.DMA
-    return [dma((2, n, chunks)), dma((n, chunks)), dma((n, chunks)), dma((n + 1, chunks)), dma]
+    return [dma((2, n, chunks)), dma((n, chunks)), dma((n, chunks)), dma((n + 1, chunks))]
 
 
 def chunk_buffers(n, rows, c, kept):
@@ -289,25 +286,36 @@
     lax.fori_loop(0, n * CHUNKS, one, 0)
 
 
-def big_forward(x, w_up, w_down, n):
+def big_forward(x, w_up, w_down, residual, mask, share, n):
     t, c = x.shape
     h = w_up.shape[1]
     rows = t // CHUNKS
+    cols = residual.shape[1]
+    half = cols // 2
+    pairs = rows // cols // 2
 
     def kernel(
-        x_ref, wu, wd, out, x_all, act_all, slope_all,
-        gathered, partial, travel, act, slope, copied, stored, *sems
+        x_ref, wu, wd, res, mask_ref, share_ref, out, pooled, x_all, act_all, slope_all,
+        gathered, partial, travel, act, slope, total, folded, copied, stored, load_sem, *sems
     ):
+        d = lax.axis_index("mp")
+        load = pltpu.make_async_copy(x_ref, gathered.at[d], load_sem)
+
+        def own_chunk(j):
+            if isinstance(j, int):
+                load.start()
+                load.wait()
+
         def x_copy(s, j):
             return pltpu.make_async_copy(gathered.at[s, j], x_all.at[s, j], copied.at[s, j])
 
-        def prepare(s, j):
+        def prepare(way, s, j):
             pass
 
         def arrived(s, j):
             x_copy(s, j).start()
 
-        def compute(s, j):
+        def compute(way, s, j):
             block = gathered.at[s, j]
 
             def up(i, _):
@@ -333,26 +341,43 @@
             keep_act.wait()
             keep_slope.wait()
 
-        chain_exchange(
-            n, CHUNKS, 1, x_ref, gathered, partial, travel, compute, out, sems, prepare, arrived
-        )
+        chain_exchange(n, CHUNKS, 1, gathered, partial, travel, sems, own_chunk, prepare, arrived, compute)
+
+        def finish(j, _):
+            own_sum(n, d, j, partial, travel, total)
+            values = (res[pl.ds(j * 2 * pairs, 2 * pairs)].reshape(rows, c).astype(F32) + total[...]) * mask_ref[j]
+            partial[d, j] = values
+            pltpu.make_async_copy(partial.at[d, j], out.at[j], stored.at[0]).start()
+            both = values.reshape(pairs, 2, cols, c)
+            summed = (both[:, 0] + both[:, 1]).reshape(pairs * cols, c)
+            for b in range(c // LANES):
+                lanes = slice(b * LANES, (b + 1) * LANES)
+                folded[b] = summed[:, lanes]
+                every = folded[b, pl.ds(0, pairs * half, 2), :] + folded[b, pl.ds(1, pairs * half, 2), :]
+                pooled[j, :, lanes] = (every * share_ref[j]).astype(BF)
+            pltpu.make_async_copy(partial.at[d, j], out.at[j], stored.at[0]).wait()
+            return 0
+
+        lax.fori_loop(0, CHUNKS, finish, 0)
         drain_copies(n, x_copy)
 
     whole = pl.BlockSpec(memory_space=pl.ANY)
     local = pl.BlockSpec(memory_space=pltpu.VMEM)
-    out, x_all, act_all, slope_all = pl.pallas_call(
+    out, pooled, x_all, act_all, slope_all = pl.pallas_call(
         kernel,
         out_shape=(
             jax.ShapeDtypeStruct((CHUNKS, rows, c), F32),
+            jax.ShapeDtypeStruct((CHUNKS, pairs * half, c), BF),
             jax.ShapeDtypeStruct((n, CHUNKS, rows, c), BF),
             jax.ShapeDtypeStruct((n, CHUNKS, rows, h), BF),
             jax.ShapeDtypeStruct((n, CHUNKS, rows, h), BF),
         ),
-        in_specs=[whole, local, local],
-        out_specs=(whole,) * 4,
+        in_specs=[whole, local, local, local, local, local],
+        out_specs=(whole, local, whole, whole, whole),
         scratch_shapes=chunk_buffers(n, rows, c, F32)
         + [pltpu.VMEM((rows, h), BF)] * 2
-        + [pltpu.SemaphoreType.DMA((n, CHUNKS)), pltpu.SemaphoreType.DMA((2,))]
+        + [pltpu.VMEM((rows, c), F32), pltpu.VMEM((c // LANES, pairs * cols, LANES), F32)]
+        + [pltpu.SemaphoreType.DMA((n, CHUNKS)), pltpu.SemaphoreType.DMA((2,)), pltpu.SemaphoreType.DMA]
         + chain_sems(n, CHUNKS),
         compiler_params=pltpu.CompilerParams(
             collective_id=0, has_side_effects=True, vmem_limit_bytes=60 * MIB
@@ -360,31 +385,44 @@
         cost_estimate=pl.CostEstimate(
             flops=4 * n * t * c * h, bytes_accessed=8 * n * t * c, transcendentals=n * t * h
         ),
-    )(x.reshape(CHUNKS, rows, c), w_up, w_down)
+    )(
+        x.reshape(CHUNKS, rows, c), w_up, w_down, residual,
+        mask.reshape(CHUNKS, rows, 1), share.reshape(CHUNKS, pairs * half, 1),
+    )
     return (
         out.reshape(t, c),
-        x_all.reshape(n * t, c),
-        act_all.reshape(n * t, h),
-        slope_all.reshape(n * t, h),
+        pooled.reshape(t // 4, c),
+        x_all,
+        act_all,
+        slope_all,
     )
 
 
-def big_backward(d, slope_all, w_up, w_down, grads, n, devices):
-    t, c = d.shape
+def big_backward(cot, d_pooled, share, mask, x_all, act_all, slope_all, w_up, w_down, grads, n, devices):
+    _, cols, c = cot.shape
+    t = cot.shape[0] * cols
     h = w_up.shape[1]
     rows = t // CHUNKS
+    half = cols // 2
+    pairs_here = rows // cols // 2
+    pieces = c // rows
     pairs, g_rows, g_cols = grads.shape
     bits = range(1, devices.bit_length() - 1)
     split = g_rows // 2
     steps = len(bits)
-    plans = [Halving(bits, [last] * steps, (pairs, split, g_cols), min(g_cols, 2048)) for last in (True, False)]
+    plans = [Halving(bits, [last] * steps, (pairs, split, g_cols), min(g_cols, 1024)) for last in (True, False)]
     extras = [b for plan in plans for b in plan.buffers()[:-1]]
     each = 2 * steps - 1
 
-    def kernel(d_ref, slopes, wu, wd, g_first, g_second, out, d_all, h_all, *rest):
+    def kernel(
+        cot_ref, pool_ref, share_ref, mask_ref, x_hbm, act_hbm, slopes, wu, wd, g_first, g_second,
+        out, d_own, g_up_out, g_down_out, *rest
+    ):
         sums, extra, rest = rest[0], rest[1 : 1 + 2 * each], rest[1 + 2 * each :]
-        gathered, partial, travel, slope, grad, copied, stored, send0, recv0, send1, recv1 = rest[:11]
-        sems = rest[11:]
+        gathered, partial, travel, slope, grad, left, right, g_up, g_down, total, spread_rows = rest[:11]
+        copied, stored, send0, recv0, send1, recv1 = rest[11:17]
+        sems = rest[17:]
+        d = lax.axis_index("mp")
         plans[0].bind(g_first.at[:, :, pl.ds(0, split)], extra[:each] + (sums.at[0],), send0, recv0)
         plans[1].bind(g_second.at[:, :, pl.ds(split, split)], extra[each:] + (sums.at[1],), send1, recv1)
 
@@ -399,85 +437,184 @@
                 for plan in plans:
                     plan.start(p + 1)
 
-        total = n * CHUNKS + n - 1
-        due = [total * (2 ** steps - 2 ** (steps - 1 - p)) * 8 // (10 * (2 ** steps - 1)) for p in range(steps)]
+        all_steps = n * CHUNKS + n - 1
+        due = [all_steps * (2**steps - 2 ** (steps - 1 - p)) // (2**steps - 1) for p in range(steps)]
 
         def turn(g):
             for p in range(steps - 1):
                 pl.when(g == due[p])(lambda p=p: pass_on(p))
 
-        def d_copy(s, j):
-            return pltpu.make_async_copy(gathered.at[s, j], d_all.at[s, j], copied.at[s, j])
+        def own_chunk(j):
+            part = pool_ref[j] * share_ref[j]
+            here = cot_ref.at[pl.ds(j * 2 * pairs_here, 2 * pairs_here)]
+            for b in range(c // LANES):
+                lanes = slice(b * LANES, (b + 1) * LANES)
+                spread_rows[b, pl.ds(0, pairs_here * half, 2), :] = part[:, lanes]
+                spread_rows[b, pl.ds(1, pairs_here * half, 2), :] = part[:, lanes]
+                block = jnp.broadcast_to(
+                    spread_rows[b].reshape(pairs_here, 1, cols, LANES), (pairs_here, 2, cols, LANES)
+                ).reshape(rows, LANES)
+                cell = here[:, :, lanes].reshape(rows, LANES).astype(F32)
+                gathered[d, j, :, lanes] = ((cell + block) * mask_ref[j]).astype(BF)
 
         def slope_copy(s, j):
             return pltpu.make_async_copy(slopes.at[s, j], slope, stored.at[0])
 
-        def prepare(s, j):
+        def pair_copies(s, j):
+            two = pl.ds(j - 1, 2)
+            return (
+                pltpu.make_async_copy(x_hbm.at[s, two], left, stored.at[1]),
+                pltpu.make_async_copy(act_hbm.at[s, two], right, stored.at[2]),
+            )
+
+        def prepare(way, s, j):
             slope_copy(s, j).start()
 
+            @pl.when(lax.rem(j, 2) == 1)
+            def _():
+                for copy in pair_copies(s, j):
+                    copy.start()
+
         def arrived(s, j):
-            d_copy(s, j).start()
-
-        def compute(s, j):
+            pass
+
+        def compute(way, s, j):
             block = gathered.at[s, j]
+            mine = grad.at[way, lax.rem(j, 2)]
             slope_copy(s, j).wait()
 
             def up(i, _):
-                back = lax.dot_general(
-                    block[...], wd[columns(i), :], (((1,), (1,)), ((), ())), preferred_element_type=F32
-                )
-                grad[:, columns(i)] = (back * slope[:, columns(i)].astype(F32)).astype(BF)
+                back = nt(block[...], wd[columns(i), :])
+                mine[:, columns(i)] = (back * slope[:, columns(i)].astype(F32)).astype(BF)
                 return 0
 
             lax.fori_loop(0, h // TILE, up, 0)
-            keep = pltpu.make_async_copy(grad, h_all.at[s, j], stored.at[1])
-            keep.start()
 
             def down(i, _):
-                partial[s, j, :, columns(i)] = lax.dot_general(
-                    grad[...], wu[columns(i), :], (((1,), (1,)), ((), ())), preferred_element_type=F32
-                )
+                partial[s, j, :, columns(i)] = nt(mine[...], wu[columns(i), :]).astype(BF)
                 return 0
 
             lax.fori_loop(0, c // TILE, down, 0)
-            keep.wait()
+
+            @pl.when(lax.rem(j, 2) == 1)
+            def _():
+                for copy in pair_copies(s, j):
+                    copy.wait()
+
+                def tile(i, _):
+                    a, b = columns(i // (h // TILE)), columns(lax.rem(i, h // TILE))
+                    two = pl.ds(j - 1, 2)
+                    g_up[a, b] += tn(
+                        left[:, :, a].reshape(2 * rows, TILE), grad[way, :, :, b].reshape(2 * rows, TILE)
+                    )
+                    g_down[a, b] += tn(
+                        gathered[s, two, :, a].reshape(2 * rows, TILE), right[:, :, b].reshape(2 * rows, TILE)
+                    )
+                    return 0
+
+                lax.fori_loop(0, (c // TILE) * (h // TILE), tile, 0)
+
+        def clear(i, _):
+            some = pl.ds(pl.multiple_of(i * rows, rows), rows)
+            g_up[some] = jnp.zeros((rows, h), F32)
+            g_down[some] = jnp.zeros((rows, h), F32)
+            return 0
+
+        def begin_all():
+            begin()
+            lax.fori_loop(0, pieces, clear, 0)
 
         chain_exchange(
-            n, CHUNKS, 1, d_ref, gathered, partial, travel, compute, out, sems, prepare, arrived,
-            [dp_mate(b) for b in bits], begin, turn
+            n, CHUNKS, 1, gathered, partial, travel, sems, own_chunk, prepare, arrived, compute,
+            [dp_mate(b) for b in bits], begin_all, turn,
         )
+        keep = pltpu.make_async_copy(gathered.at[d], d_own, stored.at[0])
+        keep.start()
+
+        def result(j):
+            return pltpu.make_async_copy(total, out.at[j], stored.at[1])
+
+        def finish(j, _):
+            @pl.when(j > 0)
+            def _():
+                result(j - 1).wait()
+
+            own_sum(n, d, j, partial, travel, total)
+            result(j).start()
+            return 0
+
+        lax.fori_loop(0, CHUNKS, finish, 0)
+        result(CHUNKS - 1).wait()
+        keep.wait()
+
+        def place(i):
+            return i // CHUNKS, lax.rem(i, CHUNKS)
+
+        def up_copy(i):
+            s, j = place(i)
+            return pltpu.make_async_copy(travel.at[s, j], g_up_out.at[i], copied.at[0, i])
+
+        def down_copy(i):
+            s, j = place(i)
+            return pltpu.make_async_copy(gathered.at[s, j], g_down_out.at[i], copied.at[1, i])
+
+        def give(i, _):
+            s, j = place(i)
+            some = pl.ds(pl.multiple_of(i * rows, rows), rows)
+            travel[s, j] = g_up[some].astype(BF)
+            up_copy(i).start()
+            gathered[s, j] = g_down[some].astype(BF)
+            down_copy(i).start()
+            return 0
+
+        lax.fori_loop(0, pieces, give, 0)
         pass_on(steps - 1)
-        drain_copies(n, d_copy)
+
+        def given(i, _):
+            up_copy(i).wait()
+            down_copy(i).wait()
+            return 0
+
+        lax.fori_loop(0, pieces, given, 0)
 
     whole = pl.BlockSpec(memory_space=pl.ANY)
     local = pl.BlockSpec(memory_space=pltpu.VMEM)
-    out, d_all, h_all, sums, *_ = pl.pallas_call(
+    dma = pltpu.SemaphoreType.DMA
+    out, d_own, g_up, g_down, sums, *_ = pl.pallas_call(
         kernel,
         out_shape=(
             jax.ShapeDtypeStruct((CHUNKS, rows, c), F32),
-            jax.ShapeDtypeStruct((n, CHUNKS, rows, c), BF),
-            jax.ShapeDtypeStruct((n, CHUNKS, rows, h), BF),
+            jax.ShapeDtypeStruct((CHUNKS, rows, c), BF),
+            jax.ShapeDtypeStruct((pieces, rows, h), BF),
+            jax.ShapeDtypeStruct((pieces, rows, h), BF),
             jax.ShapeDtypeStruct((2, 1, 1, split, g_cols), BF),
             *extras,
         ),
-        in_specs=[whole, whole, local, local, whole, whole],
-        out_specs=(whole,) * (4 + 2 * each),
-        scratch_shapes=chunk_buffers(n, rows, c, F32)
-        + [pltpu.VMEM((rows, h), BF)] * 2
-        + [pltpu.SemaphoreType.DMA((n, CHUNKS)), pltpu.SemaphoreType.DMA((2,))]
+        in_specs=[local] * 4 + [whole] * 3 + [local] * 2 + [whole] * 2,
+        out_specs=(whole,) * (5 + 2 * each),
+        scratch_shapes=chunk_buffers(n, rows, c, BF)
+        + [
+            pltpu.VMEM((rows, h), BF), pltpu.VMEM((2, 2, rows, h), BF),
+            pltpu.VMEM((2, rows, c), BF), pltpu.VMEM((2, rows, h), BF),
+            pltpu.VMEM((c, h), F32), pltpu.VMEM((c, h), F32),
+            pltpu.VMEM((rows, c), F32), pltpu.VMEM((c // LANES, pairs_here * cols, LANES), F32),
+            dma((2, pieces)), dma((3,)),
+        ]
         + plans[0].semaphores() + plans[1].semaphores()
         + chain_sems(n, CHUNKS),
         compiler_params=pltpu.CompilerParams(
-            collective_id=1, has_side_effects=True, vmem_limit_bytes=60 * MIB
+            collective_id=1, has_side_effects=True, vmem_limit_bytes=62 * MIB
         ),
         cost_estimate=pl.CostEstimate(
-            flops=4 * n * t * c * h, bytes_accessed=8 * n * t * c, transcendentals=0
+            flops=8 * n * t * c * h, bytes_accessed=8 * n * t * c, transcendentals=0
         ),
     )(
-        d.reshape(CHUNKS, rows, c), slope_all.reshape(n, CHUNKS, rows, h), w_up, w_down,
+        cot, d_pooled.reshape(CHUNKS, pairs_here * half, c), share.reshape(CHUNKS, pairs_here * half, 1),
+        mask.reshape(CHUNKS, rows, 1), x_all, act_all, slope_all, w_up, w_down,
         grads.reshape(pairs // 2, 2, g_rows, g_cols), grads.reshape(2, pairs // 2, g_rows, g_cols),
     )
-    return out.reshape(t, c), d_all.reshape(n * t, c), h_all.reshape(n * t, h), sums.reshape(g_rows, g_cols)
+    shaped = [g.reshape(devices, c // devices, h) for g in (g_up, g_down)]
+    return out.reshape(cot.shape), d_own.reshape(cot.shape), shaped, sums.reshape(g_rows, g_cols)
 
 
 def frame(dst, src):
@@ -600,90 +737,165 @@
     )(x, w)
 
 
-def conv_backward(d, x, w, size, grads, devices, group=4, bgroup=4):
-    high, cols, c = x.shape
-    rows = high - size + 1
+def conv_backward(d_normed, conv_out, gain, mask, bordered, d_map, w, size, grads, devices, n):
+    rows, cols, c = conv_out.shape
     reach = size // 2
+    high = rows + 2 * reach
+    group = 4 if rows % 4 == 0 else 1
     steps = devices.bit_length() - 1
     shape = grads[0].shape
     plans = [Halving(range(steps), [True] + [last] * (steps - 1), shape, shape[2]) for last in (True, False)]
     blocks = c // LANES
-    due = [3 + (blocks - 4) * p // max(steps - 2, 1) for p in range(steps)]
-
-    def kernel(d_ref, x_ref, w_ref, g0, g1, out, g, *rest):
+    stops = [blocks * 3 * p // (4 * max(steps - 2, 1)) for p in range(1, steps - 1)] + [blocks]
+
+    def kernel(dn, co, gain_ref, mask_ref, w_ref, b_hbm, dm_hbm, g0, g1, out, g, g_gain, *rest):
         extra, rest = rest[: 4 * steps], rest[4 * steps :]
-        dframed, xframed, *sems = rest
+        around, x_around, d_here, dframed, xframed, sent, got, own, *sems = rest
         plans[0].bind(g0, extra[: 2 * steps], sems[0], sems[1])
         plans[1].bind(g1, extra[2 * steps :], sems[2], sems[3])
-        i = pl.program_id(0)
-
-        @pl.when(i == 0)
-        def _():
-            barrier = pltpu.get_barrier_semaphore()
-            for b in range(steps):
-                pl.semaphore_signal(barrier, inc=1, device_id={"dp": dp_mate(b)}, device_id_type=MESH)
-            pl.semaphore_wait(barrier, steps)
+        d = lax.axis_index("mp")
+        has_up, has_down = d > 0, d < n - 1
+        barrier = pltpu.get_barrier_semaphore()
+        for b in range(steps):
+            pl.semaphore_signal(barrier, inc=1, device_id={"dp": dp_mate(b)}, device_id_type=MESH)
+
+        @pl.when(has_up)
+        def _():
+            pl.semaphore_signal(barrier, inc=1, device_id={"mp": d - 1}, device_id_type=MESH)
+
+        @pl.when(has_down)
+        def _():
+            pl.semaphore_signal(barrier, inc=1, device_id={"mp": d + 1}, device_id_type=MESH)
+
+        load_x = pltpu.make_async_copy(b_hbm, x_around, own.at[0])
+        load_d = pltpu.make_async_copy(dm_hbm, d_here, own.at[1])
+        load_x.start()
+        load_d.start()
+        pl.semaphore_wait(barrier, has_up.astype(jnp.int32) + has_down.astype(jnp.int32) + steps)
+        for plan in plans:
+            plan.start(0)
+
+        g_gain[...] = jnp.zeros(g_gain.shape, F32)
+
+        def norm(r, _):
+            cells = mask_ref[r]
+            back, part = normalise_back(co[r] * cells, gain_ref[...], dn[r])
+            around[reach + r] = (back * cells).astype(BF)
+            g_gain[...] += part
+            return 0
+
+        lax.fori_loop(0, rows, norm, 0)
+        up = pltpu.make_async_remote_copy(
+            src_ref=around.at[pl.ds(reach, reach)], dst_ref=around.at[pl.ds(reach + rows, reach)],
+            send_sem=sent.at[0], recv_sem=got.at[0], device_id={"mp": d - 1}, device_id_type=MESH,
+        )
+        down = pltpu.make_async_remote_copy(
+            src_ref=around.at[pl.ds(rows, reach)], dst_ref=around.at[pl.ds(0, reach)],
+            send_sem=sent.at[1], recv_sem=got.at[1], device_id={"mp": d + 1}, device_id_type=MESH,
+        )
+        nothing = jnp.zeros((reach, cols, c), BF)
+
+        @pl.when(has_up)
+        def _():
+            up.start()
+
+        @pl.when(has_down)
+        def _():
+            down.start()
+
+        @pl.when(d == 0)
+        def _():
+            around[:reach] = nothing
+
+        @pl.when(d == n - 1)
+        def _():
+            around[reach + rows :] = nothing
+
+        def pass_on(p):
             for plan in plans:
-                plan.start(0)
-
-        for p in range(steps - 1):
-            @pl.when(i == due[p])
-            def _():
-                for plan in plans:
-                    plan.finish(p)
+                plan.finish(p)
+            if p + 1 < steps:
                 for plan in plans:
                     plan.start(p + 1)
 
-        frame(dframed, d_ref)
-        frame(xframed, x_ref)
-        correlate(out, dframed, w_ref, size, True, group)
-        for a in range(size):
-            def some(r, accs):
-                dv = dframed[pl.ds(reach + r * bgroup, bgroup), EDGE : EDGE + cols]
-                new = []
+        pass_on(0)
+        load_x.wait()
+        load_d.wait()
+
+        @pl.when(has_up)
+        def _():
+            down.wait_recv()
+
+        @pl.when(has_down)
+        def _():
+            up.wait_recv()
+
+        def block(i, _):
+            lanes = pl.ds(pl.multiple_of(i * LANES, LANES), LANES)
+            frame(dframed, around.at[:, :, lanes])
+            frame(xframed, x_around.at[:, :, lanes])
+            correlate(out.at[:, :, lanes], dframed, w_ref.at[:, :, lanes], size, True, group)
+            for r in range(rows):
+                out[r, :, lanes] = (out[r, :, lanes] + d_here[r, :, lanes].astype(F32)) * mask_ref[r]
+            for a in range(size):
+                def some(r, accs):
+                    dv = dframed[pl.ds(reach + r * group, group), EDGE : EDGE + cols]
+                    new = []
+                    for b in range(size):
+                        prod = dv * xframed[pl.ds(r * group + a, group), pl.ds(EDGE - reach + b, cols), :]
+                        new.append(accs[b] + jnp.sum(prod.reshape(-1, 8, LANES), axis=0))
+                    return tuple(new)
+
+                accs = lax.fori_loop(
+                    0, rows // group, some, tuple(jnp.zeros((8, LANES), F32) for _ in range(size))
+                )
                 for b in range(size):
-                    prod = dv * xframed[pl.ds(r * bgroup + a, bgroup), pl.ds(EDGE - reach + b, cols), :]
-                    new.append(accs[b] + jnp.sum(prod.reshape(-1, 8, LANES), axis=0))
-                return tuple(new)
-
-            accs = lax.fori_loop(
-                0, rows // bgroup, some, tuple(jnp.zeros((8, LANES), F32) for _ in range(size))
-            )
-            for b in range(size):
-                g[a * size + b] = jnp.sum(accs[b], axis=0, keepdims=True)
-
-        @pl.when(i == blocks - 1)
-        def _():
-            for plan in plans:
-                plan.finish(steps - 1)
+                    g[a * size + b, :, lanes] = jnp.sum(accs[b], axis=0, keepdims=True)
+            return 0
+
+        at = 0
+        for p, stop in enumerate(stops):
+            lax.fori_loop(at, stop, block, 0)
+            at = stop
+            pass_on(p + 1)
+
+        @pl.when(has_up)
+        def _():
+            up.wait_send()
+
+        @pl.when(has_down)
+        def _():
+            down.wait_send()
 
     whole = pl.BlockSpec(memory_space=pl.ANY)
-    d_in, g, *extra = pl.pallas_call(
+    local = pl.BlockSpec(memory_space=pltpu.VMEM)
+    vm, dma = pltpu.VMEM, pltpu.SemaphoreType.DMA
+    d_in, g, g_gain, *extra = pl.pallas_call(
         kernel,
-        grid=(blocks,),
         out_shape=(
             jax.ShapeDtypeStruct((rows, cols, c), F32),
             jax.ShapeDtypeStruct((size * size, 1, c), F32),
+            jax.ShapeDtypeStruct((1, c), F32),
             *plans[0].buffers(),
             *plans[1].buffers(),
         ),
-        in_specs=[pl.BlockSpec((high, cols, LANES), lambda i: (0, 0, i))] * 2
-        + [pl.BlockSpec((size * size, 1, LANES), lambda i: (0, 0, i)), whole, whole],
-        out_specs=(
-            pl.BlockSpec((rows, cols, LANES), lambda i: (0, 0, i)),
-            pl.BlockSpec((size * size, 1, LANES), lambda i: (0, 0, i)),
-        )
-        + (whole,) * (4 * steps),
-        scratch_shapes=[pltpu.VMEM((high, cols + 2 * EDGE, LANES), F32)] * 2
+        in_specs=[local] * 5 + [whole] * 4,
+        out_specs=(local,) * 3 + (whole,) * (4 * steps),
+        scratch_shapes=[
+            vm((high, cols, c), BF), vm((high, cols, c), BF), vm((rows, cols, c), BF),
+            vm((high, cols + 2 * EDGE, LANES), F32), vm((high, cols + 2 * EDGE, LANES), F32),
+            dma((2,)), dma((2,)), dma((2,)),
+        ]
         + plans[0].semaphores() + plans[1].semaphores(),
         compiler_params=pltpu.CompilerParams(
-            collective_id=3, has_side_effects=True, vmem_limit_bytes=40 * MIB
+            collective_id=3, has_side_effects=True, vmem_limit_bytes=50 * MIB
         ),
         cost_estimate=pl.CostEstimate(flops=6 * 10**10, bytes_accessed=10**8, transcendentals=0),
     )(
-        d, x, w, grads[0].reshape((shape[0] // 2, 2) + shape[1:]), grads[1].reshape((shape[0] // 2, 2) + shape[1:])
+        d_normed, conv_out, gain, mask, w, bordered, d_map,
+        *(v.reshape((shape[0] // 2, 2) + shape[1:]) for v in grads),
     )
-    return d_in, g, [extra[2 * steps - 1].reshape(shape[1:]), extra[4 * steps - 1].reshape(shape[1:])]
+    return d_in, g, g_gain[0], [extra[2 * steps - 1].reshape(shape[1:]), extra[4 * steps - 1].reshape(shape[1:])]
 
 
 GATE, OUT, HIGH_A, HIGH_B, QUERY, KEY, VALUE, PROJ = range(8)
@@ -1149,19 +1361,6 @@
     return x.reshape(shape[:-1] + (2, devices // 2, -1)).swapaxes(-3, -2).reshape(shape)
 
 
-def extended(value, sides, width):
-    for axis, dim in sides:
-        devices, length = (lax.axis_size(axis), value.shape[dim])
-        up = [(i, (i + 1) % devices) for i in range(devices - 1)]
-        down = [(j, i) for i, j in up]
-        last = lax.slice_in_dim(value, length - width, length, axis=dim)
-        first = lax.slice_in_dim(value, 0, width, axis=dim)
-        before = lax.ppermute(last, axis, up)
-        after = lax.ppermute(first, axis, down)
-        value = jnp.concatenate([before, value, after], axis=dim)
-    return value
-
-
 def layer_norm(values, gain):
     centre = jnp.mean(values, -1, keepdims=True)
     centred = values - centre
@@ -1189,7 +1388,7 @@
     cot_low,
     cot_hr,
 ):
-    item_count, row_count, col_count, chan_count = hr_in.shape
+    _, row_count, col_count, chan_count = hr_in.shape
     devices, shards = lax.axis_size("dp"), lax.axis_size("mp")
     dims = low_in.shape[2]
     share = dims // devices
@@ -1200,34 +1399,25 @@
     ]
     packed = rows_first(jnp.concatenate(pieces, axis=1))
     packed = rows_first(lax.all_gather(packed, "mp", axis=0, tiled=True))
-    plane_mask = valid.astype(jnp.float32)
+    plane_mask = valid[0].astype(F32)
     cell_mask = plane_mask[..., None]
-    masked = hr_in * valid.astype(jnp.bfloat16)[..., None]
+    masked = hr_in[0] * valid[0].astype(BF)[..., None]
+    half_rows, half_cols = (row_count // 2, col_count // 2)
+    counts = plane_mask.reshape(half_rows, 2, half_cols, 2).sum(axis=(1, 3))
+    shares = 1.0 / jnp.maximum(counts, 1.0)
     size = conv_w.shape[0]
     taps = conv_w.astype(F32).reshape(size * size, 1, chan_count)
-    conv_out, bordered = conv_forward(masked[0], taps, size, shards)
-    conv_out = conv_out[None]
-    conv_out = conv_out * cell_mask
-    hr_gainf = hr_gain.astype(jnp.float32)
-    normed = layer_norm(conv_out, hr_gainf).astype(jnp.bfloat16)
+    conv_out, bordered = conv_forward(masked, taps, size, shards)
+    hr_gainf = hr_gain.astype(F32)
+    normed = layer_norm(conv_out * cell_mask, hr_gainf).astype(BF)
     normed, packed = lax.optimization_barrier((normed, packed))
     packed = rows_first(lax.all_gather(packed, "dp", axis=0, tiled=True))
-    branch, normed_all, hidden_act, hidden_slope = big_forward(
-        normed.reshape(row_count * col_count, chan_count), cn_up, cn_down, shards
+    hr_out, pooled, normed_all, hidden_act, hidden_slope = big_forward(
+        normed.reshape(row_count * col_count, chan_count), cn_up, cn_down, masked, plane_mask, shares, shards
     )
-    branch = branch.reshape(hr_in.shape)
-    hr_out = (masked.astype(jnp.float32) + branch) * cell_mask
-    half_rows, half_cols = (row_count // 2, col_count // 2)
-    block_sum = hr_out.reshape(item_count, half_rows, 2, half_cols, 2, chan_count).sum(axis=(2, 4))
-    counts = plane_mask.reshape(item_count, half_rows, 2, half_cols, 2).sum(axis=(2, 4))
-    divisor = jnp.maximum(counts, 1.0)[..., None]
-    pooled = (
-        (block_sum / divisor)
-        .astype(jnp.bfloat16)
-        .reshape(item_count, half_rows * half_cols, chan_count)
-    )
+    hr_out = hr_out.reshape(hr_in.shape)
     tokens = half_rows * half_cols
-    by_share = pooled[0].reshape(tokens, devices, -1)
+    by_share = pooled.reshape(tokens, devices, -1)
     pool_a = by_share[:, :, :share].reshape(tokens, dims)
     pool_b = jnp.pad(by_share[:, :, share:], ((0, 0), (0, 0), (0, 2 * share - by_share.shape[2]))).reshape(tokens, dims)
     low_out, d_low_in, d_pool_a, d_pool_b, g_ln1, g_ln2, low_grads = low_stage(
@@ -1245,31 +1435,18 @@
         ],
         axis=2,
     )
-    d_block = d_pooled.reshape(item_count, half_rows, half_cols, chan_count) / divisor
-    d_block = d_block.reshape(item_count, half_rows, 1, half_cols, 1, chan_count)
-    d_map = cot_hr.astype(jnp.float32) + jnp.broadcast_to(
-        d_block, (item_count, half_rows, 2, half_cols, 2, chan_count)
-    ).reshape(hr_in.shape)
-    d_branch = d_map * cell_mask
-    d_normed, d_branch_all, d_hidden, low_sums = big_backward(
-        d_branch.astype(BF).reshape(row_count * col_count, chan_count),
-        hidden_slope, cn_up, cn_down, low_grads, shards, devices,
+    d_normed, d_map, cn_grads, low_sums = big_backward(
+        cot_hr[0], d_pooled.reshape(tokens, chan_count), shares, plane_mask, normed_all, hidden_act, hidden_slope,
+        cn_up, cn_down, low_grads, shards, devices,
     )
-    d_normed = d_normed.reshape(hr_in.shape)
     low_sums = rows_first(low_sums.reshape(shards, share, -1))
     low_sums = rows_first(lax.psum_scatter(low_sums, "mp", scatter_dimension=0))
-    g_cn_down = jnp.einsum("tc,th->ch", d_branch_all, hidden_act, preferred_element_type=F32).astype(BF)
-    g_cn_up = jnp.einsum("tc,th->ch", normed_all, d_hidden, preferred_element_type=F32).astype(BF)
-    cn_grads = [g.reshape(devices, chan_count // devices, -1) for g in (g_cn_up, g_cn_down)]
-    d_conv, g_hr_gain = jax.vjp(layer_norm, conv_out, hr_gainf)[1](d_normed)
-    d_conv = d_conv * cell_mask
-    d_bordered = extended(d_conv.astype(BF), (("mp", 1),), 3)
-    d_conv_in, g_conv, (g_cn_up, g_cn_down) = conv_backward(
-        d_bordered[0], bordered, taps, size, cn_grads, devices
+    d_hr_in, g_conv, g_hr_gain, (g_cn_up, g_cn_down) = conv_backward(
+        d_normed, conv_out, hr_gainf[None], cell_mask, bordered, d_map, taps, size, cn_grads, devices, shards
     )
+    d_hr_in = d_hr_in[None]
     g_cn_up, g_cn_down = g_cn_up.astype(F32), g_cn_down.astype(F32).T
     g_conv = g_conv.reshape(conv_w.shape)
-    d_hr_in = (d_branch + d_conv_in) * cell_mask
     small = (g_conv, g_hr_gain, g_ln1, g_ln2)
     flat = jnp.concatenate([g.reshape(-1) for g in small])
     room = -(-flat.size // (devices * 8 * LANES)) * (devices * 8 * LANES)

time: 812 us -> 841 us (1.036)
  Pallas kernels: 617 us -> 709 us
  matrix products: 26 us -> 0 us
  other arithmetic: 36.9 us -> 12.6 us
    pallas_call x1, Pallas kernels: 207 us -> 271 us  [big_backward(): pl.pallas_call(kernel, out_shape=(jax.ShapeDtypeStruct((CHUNKS, rows, c),...]
    dot_general x2 -> x0, matrix products: 26 us -> none  [the longest x1 13.1 us: per_device(): jnp.einsum('tc,th->ch', d_branch_all, hidden_act, preferred_element_type=...]
    pallas_call x1, Pallas kernels: 70.6 us -> 92.8 us  [conv_backward(): pl.pallas_call(kernel, out_shape=(jax.ShapeDtypeStruct((rows, cols, c), F...]
    reduce_sum x4 -> x1, other arithmetic: 10.7 us -> 0.09 us  [per_device(): counts = plane_mask.reshape(half_rows, 2, half_cols, 2).sum(axis=(1, 3))]
    unnamed x112 -> x57, local copies, waits for them, and re-layouts: 14 us -> 19.6 us
  transfers between devices with their start and end apart: 5 -> 3, of which waited for: 2 -> 1; matrix products, arithmetic and copies ran while one was open for 9% -> 3% of each run, Pallas kernels for 34% -> 37%
where the time goes in v5:
time: 841 us; the launch traced here: 835 us
  Pallas kernels  709 us (84%)
  local copies, waits for them, and re-layouts  49.5 us (6%)
  waiting for transfers between devices  49 us (6%)
  between operations  14.5 us (2%)
  other arithmetic  12.6 us (1%)
    pallas_call x1, Pallas kernels, big_backward(): pl.pallas_call(kernel, out_shape=(jax.ShapeDtypeStruct((CHUNKS, rows, c),...  271 us
    pallas_call x1, Pallas kernels, big_forward(): pl.pallas_call(kernel, out_shape=(jax.ShapeDtypeStruct((CHUNKS, rows, c),...  184 us
    pallas_call x1, Pallas kernels, low_stage(): pl.pallas_call(kernel, out_shape=(tok, tok, tok, tok, one, one, jax.Shape...  112 us
    pallas_call x1, Pallas kernels, conv_backward(): pl.pallas_call(kernel, out_shape=(jax.ShapeDtypeStruct((rows, cols, c), F...  92.8 us
    all_gather x1, waiting for transfers between devices, per_device(): packed = rows_first(lax.all_gather(packed, 'mp', axis=0, tiled=True))  48.9 us
    pallas_call x1, Pallas kernels, conv_forward(): pl.pallas_call(kernel, out_shape=(jax.ShapeDtypeStruct((rows, cols, c), F...  30.3 us
    unnamed x57, local copies, waits for them, and re-layouts  19.6 us
    pallas_call x1, Pallas kernels, sum_everywhere(): pl.pallas_call(kernel, out_shape=jax.ShapeDtypeStruct(x.shape, F32), in_s...  19.2 us
  transfers between devices with their start and end apart: 3, of which 1 were waited for; matrix products, arithmetic and copies ran while one was open for 3% of the time, Pallas kernels for 37%

profile of v5, /device:TPU:0, one launch (start us, length us, event | category | flops | bytes accessed | tf_op | source)
XLA Modules:
  0.0 834.6 jit_solution(12721490761705521594)
XLA Ops:
  7.3 0.9 dynamic-slice_dynamic-update-slice_fusion.2
  8.2 0.9 constant_dynamic-slice_fusion.1
  9.2 0.8 dynamic-slice_dynamic-update-slice_fusion.1
  10.9 1.0 constant_dynamic-slice_fusion
  12.0 0.9 fusion.2
  12.9 0.8 fusion.1
  13.7 0.8 fusion
  14.6 1.0 dynamic-slice_dynamic-update-slice_fusion
  15.6 1.0 copy-done.6
  17.2 1.7 bitcast_multiply_fusion.x_ref.res
  18.9 30.3 %shard_map.305 = (f32[12,48,1536]{2,1,0:T(8,128)S(1)}, bf16[18,48,1536]{2,1,0:T(8,128)(2,1)S(1)}) custom-call(bf16[12,48,1536]{2,1,0:T(8,128)(2,1)S(1)} %bitcast_multiply_fusion.x_ref.res, f32[49,1,1536]{2,1,0:T(1,128)S(1)} %reshape.191.w_ref), custom_call_target="tpu_custom_call" | custom-call | tf_op jit(solution)/shard_map/pallas_call | solution.py:725
  50.7 1.2 copy-done
  51.8 1.8 multiply_convert_fusion
  53.7 48.9 %all-gather.3.cloned.1.call-done = bf16[512,4096]{1,0:T(8,128)(2,1)} async-done(((bf16[128,4096]{1,0:T(8,128)(2,1)}), bf16[512,4096]{1,0:T(8,128)(2,1)}) %all-gather.3.cloned.1.call-update) | async-done | bytes 4194320 | tf_op jit(solution)/shard_map/all_gather | solution.py:1401
  102.7 0.9 convert_element_type.87.mask_ref
  104.0 0.9 reshape.169.low_ref
  106.1 0.9 reshape.174.cot_ref
  108.2 183.8 %shard_map.306 = (f32[6,96,1536]{2,1,0:T(8,128)}, bf16[6,24,1536]{2,1,0:T(8,128)(2,1)}, bf16[4,6,96,1536]{3,2,1,0:T(8,128)(2,1)}, bf16[4,6,96,1536]{3,2,1,0:T(8,128)(2,1)}, bf16[4,6,96,1536]{3,2,1,0:T(8,128)(2,1)}) custom-call(bf16[6,96,1536]{2,1,0:T(8,128)(2,1)} %bitcast.118, bf16[1536,1536]{1,0:T(8,128)(2,1)} %wu.3, bf16[1536,1536]{1,0:T(8,128)(2,1)} %wd.3, ...), custom_call_target="tpu_custom_call" | custom-call | flops 21743271936 | bytes 28311552 | tf_op jit(solution)/shard_map/pallas_call | solution.py:366
  292.0 1.5 reshape_reshape.37
  293.8 0.9 reshape.172.pool_a_ref
  295.0 0.9 reshape.173.pool_b_ref
  295.9 112.2 %shard_map.307 = (f32[144,1024]{1,0:T(8,128)}, f32[144,1024]{1,0:T(8,128)}, f32[144,1024]{1,0:T(8,128)}, f32[144,1024]{1,0:T(8,128)}, f32[1,1024]{1,0:T(1,128)},...) custom-call(bf16[144,1024]{1,0:T(8,128)(2,1)} %reshape.169.low_ref, bf16[144,1024]{1,0:T(8,128)(2,1)} %reshape.172.pool_a_ref, ...), custom_call_target="tpu_custom_call" | custom-call | flops 14000000000 | bytes 70000000 | tf_op jit(solution)/shard_map/pallas_call | solution.py:1257
  408.1 1.3 reshape.181
  409.8 1.3 reshape.180
  411.5 1.3 reshape_reshape.43.pool_ref
  412.8 270.5 %shard_map.308 = (f32[6,96,1536]{2,1,0:T(8,128)}, bf16[6,96,1536]{2,1,0:T(8,128)(2,1)}, bf16[16,96,1536]{2,1,0:T(8,128)(2,1)}, bf16[16,96,1536]{2,1,0:T(8,128)(2...) custom-call(bf16[12,48,1536]{2,1,0:T(8,128)(2,1)} %bitcast.136, ...), custom_call_target="tpu_custom_call" | custom-call | flops 43486543872 | bytes 28311552 | tf_op jit(solution)/shard_map/pallas_call | solution.py:583
  683.5 0.8 copy-done.8
  685.0 1.3 broadcast_in_dim_reshape.20
  686.9 1.3 broadcast_in_dim_reshape.21
  688.1 92.8 %shard_map.309 = (f32[12,48,1536]{2,1,0:T(8,128)}, f32[49,1,1536]{2,1,0:T(1,128)S(1)}, f32[1,1536]{1,0:T(1,128)S(1)}, bf16[4,192,1536]{2,1,0:T(8,128)(2,1)}, bf1...) custom-call(f32[12,48,1536]{2,1,0:T(8,128)} %bitcast.141, ...), custom_call_target="tpu_custom_call" | custom-call | flops 60000002048 | bytes 100000000 | tf_op jit(solution)/shard_map/pallas_call | solution.py:873
  781.8 1.1 bitcast_convert_fusion
  783.0 1.1 convert_bitcast_fusion
  784.2 19.2 %shard_map.310 = f32[8,80,128]{2,1,0:T(8,128)S(1)} custom-call(f32[8,80,128]{2,1,0:T(8,128)S(1)} %bitcast.101), custom_call_target="tpu_custom_call" | custom-call | tf_op jit(solution)/shard_map/pallas_call | solution.py:1329
  804.8 1.6 fusion.3
  806.3 1.4 slice.97
  807.7 1.4 convert_element_type.85
  809.8 0.8 slice.105
  810.6 0.8 slice_bitcast_fusion.1
  811.5 0.8 slice_bitcast_fusion
  812.3 1.7 reshape.189
  814.0 1.7 copy.72
  815.7 1.7 copy.73
  817.3 2.0 copy.74
  819.4 1.6 pad_maximum_fusion.2
  821.0 1.8 pad_maximum_fusion.1
  822.8 1.8 copy.101
  824.6 1.5 copy-done.4
  826.1 1.8 copy.102
  (95 shorter events, 11.4 us)
Async XLA Ops:
  7.2 9.5 %copy-start.12 = (s32[1,12,48]{2,0,1:T(1,128)S(1)}, s32[1,12,48]{2,0,1:T(1,128)}, u32[]{:S(2)}) copy-start(s32[1,12,48]{2,0,1:T(1,128)} %param.20) | copy-start | bytes 6916
  7.2 9.5 %copy-start.11 = (bf16[7,7,1536]{2,1,0:T(8,128)(2,1)S(1)}, bf16[7,7,1536]{2,1,0:T(8,128)(2,1)}, u32[]{:S(2)}) copy-start(bf16[7,7,1536]{2,1,0:T(8,128)(2,1)} %param.21) | copy-start | bytes 451588
  7.2 9.9 %copy-start.13 = (bf16[1536]{0:T(1024)(128)(2,1)S(1)}, bf16[1536]{0:T(1024)(128)(2,1)}, u32[]{:S(2)}) copy-start(bf16[1536]{0:T(1024)(128)(2,1)} %param.22) | copy-start | bytes 9220
  7.2 95.4 %all-gather.3.cloned.1.call-start = ((), (), s32[]{:S(2)}) async-start(), calls=%async_computation.1 | async-start | bytes 5242880 | tf_op jit(solution)/shard_map/all_gather | solution.py:1401
  15.6 1.0 copy-start.6
  16.6 279.3 %all-gather.5.cloned.1.call-start = ((), (), s32[]{:S(2)}) async-start(), calls=%async_computation.2 | async-start | bytes 37748736 | tf_op jit(solution)/shard_map/all_gather | solution.py:1414
  18.8 31.3 %copy-start.1 = (bf16[12,48,1536]{2,1,0:T(8,128)(2,1)}, bf16[12,48,1536]{2,1,0:T(8,128)(2,1)S(1)}, u32[]{:S(2)}) copy-start(bf16[12,48,1536]{2,1,0:T(8,128)(2,1)S(1)} %bitcast_multiply_fusion.x_ref.res) | copy-start | bytes 5308420
  49.2 1.5 copy-start.2
  49.2 2.7 copy-start
  53.7 50.0 %copy-start.9 = (bf16[1,144,1024]{2,1,0:T(8,128)(2,1)S(1)}, bf16[1,144,1024]{2,1,0:T(8,128)(2,1)}, u32[]{:S(2)}) copy-start(bf16[1,144,1024]{2,1,0:T(8,128)(2,1)} %param.19) | copy-start | bytes 884740
  53.7 52.1 %copy-start.10 = (bf16[1,144,1024]{2,1,0:T(8,128)(2,1)S(1)}, bf16[1,144,1024]{2,1,0:T(8,128)(2,1)}, u32[]{:S(2)}) copy-start(bf16[1,144,1024]{2,1,0:T(8,128)(2,1)} %param.34) | copy-start | bytes 884740
  102.6 4.4 copy-start.16
  102.6 5.0 copy-start.17
  102.6 681.6 %reduce-scatter.2.cloned.1.call-start = ((), (), s32[]{:S(2)}) async-start(), calls=%async_computation.3 | async-start | bytes 5242880 | tf_op jit(solution)/shard_map/reduce_scatter | solution.py:1443
  683.3 1.1 copy-start.8
  683.3 2.9 copy-start.7
  688.1 92.9 %copy-start.15 = (f32[1,1024]{1,0:T(1,128)S(1)}, f32[1,1024]{1,0:T(1,128)}, u32[]{:S(2)}) copy-start(f32[1,1024]{1,0:T(1,128)} %get-tuple-element.67) | copy-start | bytes 12292
  688.1 92.9 %copy-start.14 = (f32[1,1024]{1,0:T(1,128)S(1)}, f32[1,1024]{1,0:T(1,128)}, u32[]{:S(2)}) copy-start(f32[1,1024]{1,0:T(1,128)} %get-tuple-element.66) | copy-start | bytes 12292
  784.2 25.6 %copy-start.5 = (bf16[1,128,4096]{2,1,0:T(8,128)(2,1)S(1)}, bf16[1,128,4096]{2,1,0:T(8,128)(2,1)}, u32[]{:S(2)}) copy-start(bf16[1,128,4096]{2,1,0:T(8,128)(2,1)} %reduce-scatter.2.cloned.1.call-done) | copy-start | bytes 3145732
  809.2 13.7 %copy-start.3 = (f32[6,96,1536]{2,1,0:T(8,128)S(1)}, f32[6,96,1536]{2,1,0:T(8,128)}, u32[]{:S(2)}) copy-start(f32[6,96,1536]{2,1,0:T(8,128)} %get-tuple-element.50) | copy-start | bytes 10616836
  822.8 3.3 copy-start.4
Sparse Core Ops, SparseCore 0:
  16.7 85.8 all-gather.2
  104.5 159.7 all-gather.4
  683.5 86.9 reduce-scatter.1

commit v6 on v5

--- a/solution.py
+++ b/solution.py
@@ -81,8 +81,9 @@
     def start(self, p):
         self.copy(p).start()
 
-    def finish(self, p):
-        self.copy(p).wait()
+    def finish(self, p, wait=True):
+        if wait:
+            self.copy(p).wait()
         count, rows, cols = self.got[p].shape
         ways = self.split(count, p + 1)
 
@@ -97,7 +98,7 @@
 
 
 def chain_exchange(
-    n, chunks, lag, gathered, partial, travel, sems, own_chunk, prepare, arrived, compute, mates=(), begin=None, turn=None
+    n, chunks, lag, gathered, partial, travel, sems, own_chunk, prepare, arrived, compute, mates=(), begin=None, turn=None, after=None
 ):
     ag_send, ag_recv, rs_send, rs_recv = sems
     d = lax.axis_index("mp")
@@ -221,6 +222,8 @@
 
         flow(1, g - (n - 1 - d) * lag)
         flow(0, g - d * lag)
+        if after is not None:
+            after(g)
         return 0
 
     lax.fori_loop(0, n * chunks + (n - 1) * lag, step, 0)
@@ -405,7 +408,8 @@
     rows = t // CHUNKS
     half = cols // 2
     pairs_here = rows // cols // 2
-    pieces = c // rows
+    piece = c // devices
+    items = n * CHUNKS // 2
     pairs, g_rows, g_cols = grads.shape
     bits = range(1, devices.bit_length() - 1)
     split = g_rows // 2
@@ -416,12 +420,12 @@
 
     def kernel(
         cot_ref, pool_ref, share_ref, mask_ref, x_hbm, act_hbm, slopes, wu, wd, g_first, g_second,
-        out, d_own, g_up_out, g_down_out, *rest
+        out, d_own, g_up_out, g_down_out, got_up, got_down, h_all, *rest
     ):
         sums, extra, rest = rest[0], rest[1 : 1 + 2 * each], rest[1 + 2 * each :]
-        gathered, partial, travel, slope, grad, left, right, g_up, g_down, total, spread_rows = rest[:11]
-        copied, stored, send0, recv0, send1, recv1 = rest[11:17]
-        sems = rest[17:]
+        gathered, partial, travel, slope, grad, left, right, middle, g_up, g_down, total, spread_rows = rest[:12]
+        core_send, core_recv, stored, send0, recv0, send1, recv1 = rest[12:19]
+        sems = rest[19:]
         d = lax.axis_index("mp")
         plans[0].bind(g_first.at[:, :, pl.ds(0, split)], extra[:each] + (sums.at[0],), send0, recv0)
         plans[1].bind(g_second.at[:, :, pl.ds(split, split)], extra[each:] + (sums.at[1],), send1, recv1)
@@ -443,6 +447,11 @@
         def turn(g):
             for p in range(steps - 1):
                 pl.when(g == due[p])(lambda p=p: pass_on(p))
+
+            @pl.when(item_due(g))
+            def _():
+                for copy in item_copies((g - 3) // 2):
+                    copy.start()
 
         def own_chunk(j):
             part = pool_ref[j] * share_ref[j]
@@ -460,76 +469,113 @@
         def slope_copy(s, j):
             return pltpu.make_async_copy(slopes.at[s, j], slope, stored.at[0])
 
-        def pair_copies(s, j):
-            two = pl.ds(j - 1, 2)
-            return (
-                pltpu.make_async_copy(x_hbm.at[s, two], left, stored.at[1]),
-                pltpu.make_async_copy(act_hbm.at[s, two], right, stored.at[2]),
-            )
-
         def prepare(way, s, j):
             slope_copy(s, j).start()
 
-            @pl.when(lax.rem(j, 2) == 1)
-            def _():
-                for copy in pair_copies(s, j):
-                    copy.start()
-
         def arrived(s, j):
             pass
 
         def compute(way, s, j):
             block = gathered.at[s, j]
-            mine = grad.at[way, lax.rem(j, 2)]
             slope_copy(s, j).wait()
 
             def up(i, _):
                 back = nt(block[...], wd[columns(i), :])
-                mine[:, columns(i)] = (back * slope[:, columns(i)].astype(F32)).astype(BF)
+                grad[:, columns(i)] = (back * slope[:, columns(i)].astype(F32)).astype(BF)
                 return 0
 
             lax.fori_loop(0, h // TILE, up, 0)
+            half_pair = pl.ds(pl.multiple_of(lax.rem(j, 2) * rows, rows), rows)
+            keep = pltpu.make_async_copy(grad, h_all.at[s, j // 2, half_pair], stored.at[1])
+            keep.start()
 
             def down(i, _):
-                partial[s, j, :, columns(i)] = nt(mine[...], wu[columns(i), :]).astype(BF)
+                partial[s, j, :, columns(i)] = nt(grad[...], wu[columns(i), :]).astype(BF)
                 return 0
 
             lax.fori_loop(0, c // TILE, down, 0)
-
-            @pl.when(lax.rem(j, 2) == 1)
+            keep.wait()
+
+        def item_place(q):
+            s, jj, base = d, q, CHUNKS // 2
+            for k in range(1, n):
+                to_left, to_right = d - k >= 0, d + k < n
+                two = to_left & to_right
+                r = q - base
+                here = (r >= 0) & (to_left | to_right)
+                s = jnp.where(here, jnp.where(to_left & (jnp.logical_not(two) | (lax.rem(r, 2) == 0)), d - k, d + k), s)
+                jj = jnp.where(here, jnp.where(two, r // 2, r), jj)
+                base = base + (CHUNKS // 2) * (to_left.astype(jnp.int32) + to_right.astype(jnp.int32))
+            return s, jj
+
+        def item_copies(q):
+            s, jj = item_place(q)
+            return (
+                pltpu.make_async_copy(x_hbm.at[s, jj], left, stored.at[2]),
+                pltpu.make_async_copy(act_hbm.at[s, jj], right, stored.at[3]),
+                pltpu.make_async_copy(h_all.at[s, jj], middle, stored.at[4]),
+            )
+
+        def item_due(g):
+            return (lax.rem(g, 2) == 1) & (g >= 3) & (g < 2 * items + 3)
+
+        def after(g):
+            @pl.when(item_due(g))
             def _():
-                for copy in pair_copies(s, j):
+                q = (g - 3) // 2
+                s, jj = item_place(q)
+                for copy in item_copies(q):
                     copy.wait()
 
                 def tile(i, _):
-                    a, b = columns(i // (h // TILE)), columns(lax.rem(i, h // TILE))
-                    two = pl.ds(j - 1, 2)
-                    g_up[a, b] += tn(
-                        left[:, :, a].reshape(2 * rows, TILE), grad[way, :, :, b].reshape(2 * rows, TILE)
-                    )
-                    g_down[a, b] += tn(
-                        gathered[s, two, :, a].reshape(2 * rows, TILE), right[:, :, b].reshape(2 * rows, TILE)
-                    )
+                    a = columns(i)
+                    g_up[a] += tn(left[:, a], middle[...])
+                    db = gathered[s, pl.ds(2 * jj, 2), :, a].reshape(2 * rows, TILE)
+                    g_down[a] += tn(db, right[...])
                     return 0
 
-                lax.fori_loop(0, (c // TILE) * (h // TILE), tile, 0)
+                lax.fori_loop(0, c // TILE, tile, 0)
 
         def clear(i, _):
-            some = pl.ds(pl.multiple_of(i * rows, rows), rows)
-            g_up[some] = jnp.zeros((rows, h), F32)
-            g_down[some] = jnp.zeros((rows, h), F32)
+            some = pl.ds(pl.multiple_of(i * TILE, TILE), TILE)
+            g_up[some] = jnp.zeros((TILE, h), F32)
+            g_down[some] = jnp.zeros((TILE, h), F32)
             return 0
 
         def begin_all():
             begin()
-            lax.fori_loop(0, pieces, clear, 0)
+            lax.fori_loop(0, c // TILE, clear, 0)
 
         chain_exchange(
             n, CHUNKS, 1, gathered, partial, travel, sems, own_chunk, prepare, arrived, compute,
-            [dp_mate(b) for b in bits], begin_all, turn,
+            [dp_mate(b) for b in range(steps + 1)], begin_all, turn, after,
         )
         keep = pltpu.make_async_copy(gathered.at[d], d_own, stored.at[0])
         keep.start()
+        core = dp_bit(0)
+
+        def give(i, _):
+            some = pl.ds(pl.multiple_of(i * piece, piece), piece)
+            left[pl.ds(0, piece)] = g_up[some].astype(BF)
+            up = pltpu.make_async_copy(left.at[pl.ds(0, piece)], g_up_out.at[i // 2, lax.rem(i, 2)], stored.at[2])
+            up.start()
+            right[pl.ds(0, piece)] = g_down[some].astype(BF)
+            down = pltpu.make_async_copy(right.at[pl.ds(0, piece)], g_down_out.at[i // 2, lax.rem(i, 2)], stored.at[3])
+            down.start()
+            up.wait()
+            down.wait()
+            return 0
+
+        lax.fori_loop(0, devices, give, 0)
+        swaps = [
+            pltpu.make_async_remote_copy(
+                src_ref=src.at[:, 1 - core], dst_ref=dst, send_sem=core_send.at[i], recv_sem=core_recv.at[i],
+                device_id={"dp": dp_mate(0)}, device_id_type=MESH,
+            )
+            for i, (src, dst) in enumerate(((g_up_out, got_up), (g_down_out, got_down)))
+        ]
+        for swap in swaps:
+            swap.start()
 
         def result(j):
             return pltpu.make_async_copy(total, out.at[j], stored.at[1])
@@ -546,59 +592,35 @@
         lax.fori_loop(0, CHUNKS, finish, 0)
         result(CHUNKS - 1).wait()
         keep.wait()
-
-        def place(i):
-            return i // CHUNKS, lax.rem(i, CHUNKS)
-
-        def up_copy(i):
-            s, j = place(i)
-            return pltpu.make_async_copy(travel.at[s, j], g_up_out.at[i], copied.at[0, i])
-
-        def down_copy(i):
-            s, j = place(i)
-            return pltpu.make_async_copy(gathered.at[s, j], g_down_out.at[i], copied.at[1, i])
-
-        def give(i, _):
-            s, j = place(i)
-            some = pl.ds(pl.multiple_of(i * rows, rows), rows)
-            travel[s, j] = g_up[some].astype(BF)
-            up_copy(i).start()
-            gathered[s, j] = g_down[some].astype(BF)
-            down_copy(i).start()
-            return 0
-
-        lax.fori_loop(0, pieces, give, 0)
         pass_on(steps - 1)
-
-        def given(i, _):
-            up_copy(i).wait()
-            down_copy(i).wait()
-            return 0
-
-        lax.fori_loop(0, pieces, given, 0)
+        for swap in swaps:
+            swap.wait()
 
     whole = pl.BlockSpec(memory_space=pl.ANY)
     local = pl.BlockSpec(memory_space=pltpu.VMEM)
     dma = pltpu.SemaphoreType.DMA
-    out, d_own, g_up, g_down, sums, *_ = pl.pallas_call(
+    out, d_own, g_up, g_down, got_up, got_down, _, sums, *_ = pl.pallas_call(
         kernel,
         out_shape=(
             jax.ShapeDtypeStruct((CHUNKS, rows, c), F32),
             jax.ShapeDtypeStruct((CHUNKS, rows, c), BF),
-            jax.ShapeDtypeStruct((pieces, rows, h), BF),
-            jax.ShapeDtypeStruct((pieces, rows, h), BF),
+            jax.ShapeDtypeStruct((devices // 2, 2, piece, h), BF),
+            jax.ShapeDtypeStruct((devices // 2, 2, piece, h), BF),
+            jax.ShapeDtypeStruct((devices // 2, piece, h), BF),
+            jax.ShapeDtypeStruct((devices // 2, piece, h), BF),
+            jax.ShapeDtypeStruct((n, CHUNKS // 2, 2 * rows, h), BF),
             jax.ShapeDtypeStruct((2, 1, 1, split, g_cols), BF),
             *extras,
         ),
         in_specs=[local] * 4 + [whole] * 3 + [local] * 2 + [whole] * 2,
-        out_specs=(whole,) * (5 + 2 * each),
+        out_specs=(whole,) * (8 + 2 * each),
         scratch_shapes=chunk_buffers(n, rows, c, BF)
         + [
-            pltpu.VMEM((rows, h), BF), pltpu.VMEM((2, 2, rows, h), BF),
-            pltpu.VMEM((2, rows, c), BF), pltpu.VMEM((2, rows, h), BF),
+            pltpu.VMEM((rows, h), BF), pltpu.VMEM((rows, h), BF),
+            pltpu.VMEM((2 * rows, c), BF), pltpu.VMEM((2 * rows, h), BF), pltpu.VMEM((2 * rows, h), BF),
             pltpu.VMEM((c, h), F32), pltpu.VMEM((c, h), F32),
             pltpu.VMEM((rows, c), F32), pltpu.VMEM((c // LANES, pairs_here * cols, LANES), F32),
-            dma((2, pieces)), dma((3,)),
+            dma((2,)), dma((2,)), dma((5,)),
         ]
         + plans[0].semaphores() + plans[1].semaphores()
         + chain_sems(n, CHUNKS),
@@ -610,11 +632,14 @@
         ),
     )(
         cot, d_pooled.reshape(CHUNKS, pairs_here * half, c), share.reshape(CHUNKS, pairs_here * half, 1),
-        mask.reshape(CHUNKS, rows, 1), x_all, act_all, slope_all, w_up, w_down,
+        mask.reshape(CHUNKS, rows, 1), *(v.reshape(n, CHUNKS // 2, 2 * rows, -1) for v in (x_all, act_all)),
+        slope_all, w_up, w_down,
         grads.reshape(pairs // 2, 2, g_rows, g_cols), grads.reshape(2, pairs // 2, g_rows, g_cols),
     )
-    shaped = [g.reshape(devices, c // devices, h) for g in (g_up, g_down)]
-    return out.reshape(cot.shape), d_own.reshape(cot.shape), shaped, sums.reshape(g_rows, g_cols)
+    return (
+        out.reshape(cot.shape), d_own.reshape(cot.shape), [(g_up, got_up), (g_down, got_down)],
+        sums.reshape(g_rows, g_cols),
+    )
 
 
 def frame(dst, src):
@@ -737,54 +762,71 @@
     )(x, w)
 
 
-def conv_backward(d_normed, conv_out, gain, mask, bordered, d_map, w, size, grads, devices, n):
+def conv_backward(d_normed, conv_out, gain, mask, bordered, d_map, w, low_gains, size, grads, devices, n):
     rows, cols, c = conv_out.shape
     reach = size // 2
     high = rows + 2 * reach
     group = 4 if rows % 4 == 0 else 1
     steps = devices.bit_length() - 1
-    shape = grads[0].shape
+    shape = (devices,) + grads[0][0].shape[2:]
     plans = [Halving(range(steps), [True] + [last] * (steps - 1), shape, shape[2]) for last in (True, False)]
+    each = 2 * steps - 1
     blocks = c // LANES
-    stops = [blocks * 3 * p // (4 * max(steps - 2, 1)) for p in range(1, steps - 1)] + [blocks]
-
-    def kernel(dn, co, gain_ref, mask_ref, w_ref, b_hbm, dm_hbm, g0, g1, out, g, g_gain, *rest):
-        extra, rest = rest[: 4 * steps], rest[4 * steps :]
-        around, x_around, d_here, dframed, xframed, sent, got, own, *sems = rest
-        plans[0].bind(g0, extra[: 2 * steps], sems[0], sems[1])
-        plans[1].bind(g1, extra[2 * steps :], sems[2], sems[3])
-        d = lax.axis_index("mp")
+    taps = size * size
+    count = taps + 1 + low_gains.shape[0]
+    small = -(-count // devices)
+    halving = {2 * blocks * 2 * p // (3 * max(steps - 2, 1)): p for p in range(1, steps - 1)}
+    rounds = {blocks + blocks // 3: 1, blocks + 2 * blocks // 3: 2}
+
+    def kernel(
+        dn, co, gain_ref, mask_ref, w_ref, low_ref, b_hbm, dm_hbm, g0, got0, g1, got1, out, g_all, *rest
+    ):
+        extra, rest = rest[: 2 * each], rest[2 * each :]
+        around, x_around, d_here, dframed, xframed, g_own, here, level, sent, got, own = rest[:11]
+        ar, halving_sems = rest[11:17], rest[17:]
+        plans[0].bind(g0, (got0,) + extra[:each], halving_sems[0], halving_sems[1])
+        plans[1].bind(g1, (got1,) + extra[each:], halving_sems[2], halving_sems[3])
+        me, d = lax.axis_index("dp"), lax.axis_index("mp")
         has_up, has_down = d > 0, d < n - 1
         barrier = pltpu.get_barrier_semaphore()
-        for b in range(steps):
-            pl.semaphore_signal(barrier, inc=1, device_id={"dp": dp_mate(b)}, device_id_type=MESH)
-
-        @pl.when(has_up)
-        def _():
-            pl.semaphore_signal(barrier, inc=1, device_id={"mp": d - 1}, device_id_type=MESH)
-
-        @pl.when(has_down)
-        def _():
-            pl.semaphore_signal(barrier, inc=1, device_id={"mp": d + 1}, device_id_type=MESH)
-
+
+        def greet(k, _):
+            pl.semaphore_signal(
+                barrier, inc=1, device_id={"dp": lax.rem(me + k, devices)}, device_id_type=MESH
+            )
+            return 0
+
+        lax.fori_loop(1, devices, greet, 0)
+        for k in range(1, n):
+            pl.semaphore_signal(barrier, inc=1, device_id={"mp": lax.rem(d + k, n)}, device_id_type=MESH)
         load_x = pltpu.make_async_copy(b_hbm, x_around, own.at[0])
         load_d = pltpu.make_async_copy(dm_hbm, d_here, own.at[1])
         load_x.start()
         load_d.start()
-        pl.semaphore_wait(barrier, has_up.astype(jnp.int32) + has_down.astype(jnp.int32) + steps)
-        for plan in plans:
-            plan.start(0)
-
-        g_gain[...] = jnp.zeros(g_gain.shape, F32)
-
-        def norm(r, _):
+
+        def pass_on(p):
+            for plan in plans:
+                plan.finish(p, p > 0)
+                if p + 1 < steps:
+                    plan.start(p + 1)
+
+        def keep(row, lanes, value):
+            g_own[row // small, row % small : row % small + 1, lanes] = value
+
+        pl.semaphore_wait(barrier, devices + n - 2)
+        pass_on(0)
+
+        g_own[...] = jnp.zeros(g_own.shape, F32)
+
+        def norm(r, total):
             cells = mask_ref[r]
             back, part = normalise_back(co[r] * cells, gain_ref[...], dn[r])
             around[reach + r] = (back * cells).astype(BF)
-            g_gain[...] += part
-            return 0
-
-        lax.fori_loop(0, rows, norm, 0)
+            return total + part
+
+        keep(taps, slice(None), lax.fori_loop(0, rows, norm, jnp.zeros((1, c), F32)))
+        for i in range(low_gains.shape[0]):
+            keep(taps + 1 + i, slice(None), low_ref[i : i + 1])
         up = pltpu.make_async_remote_copy(
             src_ref=around.at[pl.ds(reach, reach)], dst_ref=around.at[pl.ds(reach + rows, reach)],
             send_sem=sent.at[0], recv_sem=got.at[0], device_id={"mp": d - 1}, device_id_type=MESH,
@@ -811,32 +853,15 @@
         def _():
             around[reach + rows :] = nothing
 
-        def pass_on(p):
-            for plan in plans:
-                plan.finish(p)
-            if p + 1 < steps:
-                for plan in plans:
-                    plan.start(p + 1)
-
-        pass_on(0)
         load_x.wait()
-        load_d.wait()
-
-        @pl.when(has_up)
-        def _():
-            down.wait_recv()
-
-        @pl.when(has_down)
-        def _():
-            up.wait_recv()
-
-        def block(i, _):
-            lanes = pl.ds(pl.multiple_of(i * LANES, LANES), LANES)
-            frame(dframed, around.at[:, :, lanes])
+
+        def lanes_of(i):
+            return pl.ds(pl.multiple_of(i * LANES, LANES), LANES)
+
+        def kernel_block(i, _):
+            lanes = lanes_of(i)
+            frame(dframed.at[pl.ds(reach, rows)], around.at[pl.ds(reach, rows), :, lanes])
             frame(xframed, x_around.at[:, :, lanes])
-            correlate(out.at[:, :, lanes], dframed, w_ref.at[:, :, lanes], size, True, group)
-            for r in range(rows):
-                out[r, :, lanes] = (out[r, :, lanes] + d_here[r, :, lanes].astype(F32)) * mask_ref[r]
             for a in range(size):
                 def some(r, accs):
                     dv = dframed[pl.ds(reach + r * group, group), EDGE : EDGE + cols]
@@ -850,14 +875,83 @@
                     0, rows // group, some, tuple(jnp.zeros((8, LANES), F32) for _ in range(size))
                 )
                 for b in range(size):
-                    g[a * size + b, :, lanes] = jnp.sum(accs[b], axis=0, keepdims=True)
+                    keep(a * size + b, lanes, jnp.sum(accs[b], axis=0, keepdims=True))
             return 0
 
+        def input_block(i, _):
+            lanes = lanes_of(i)
+            frame(dframed, around.at[:, :, lanes])
+            correlate(out.at[:, :, lanes], dframed, w_ref.at[:, :, lanes], size, True, group)
+            for r in range(rows):
+                out[r, :, lanes] = (out[r, :, lanes] + d_here[r, :, lanes].astype(F32)) * mask_ref[r]
+            return 0
+
+        def spread(k):
+            peer = lax.rem(me + k, devices)
+            return pltpu.make_async_remote_copy(
+                src_ref=g_own.at[peer], dst_ref=here.at[me], send_sem=ar[0].at[k], recv_sem=ar[1].at[k],
+                device_id={"dp": peer}, device_id_type=MESH,
+            )
+
+        def across(k):
+            return pltpu.make_async_remote_copy(
+                src_ref=level.at[d], dst_ref=level.at[d], send_sem=ar[2].at[k], recv_sem=ar[3].at[k],
+                device_id={"mp": lax.rem(d + k, n)}, device_id_type=MESH,
+            )
+
+        def tell(k):
+            return pltpu.make_async_remote_copy(
+                src_ref=g_all.at[me], dst_ref=g_all.at[me], send_sem=ar[4].at[k], recv_sem=ar[5].at[k],
+                device_id={"dp": lax.rem(me + k, devices)}, device_id_type=MESH,
+            )
+
+        def all_of(length, make, act):
+            def one(k, _):
+                act(make(k))
+                return 0
+
+            lax.fori_loop(1, length, one, 0)
+
+        def sum_round(p):
+            if p == 0:
+                here[me] = g_own[me]
+                all_of(devices, spread, lambda x: x.start())
+            elif p == 1:
+                all_of(devices, spread, lambda x: x.wait())
+                level[d] = jnp.sum(here[...], axis=0)
+                all_of(n, across, lambda x: x.start())
+            elif p == 2:
+                all_of(n, across, lambda x: x.wait())
+                g_all[me] = jnp.sum(level[...], axis=0)
+                all_of(devices, tell, lambda x: x.start())
+            else:
+                all_of(devices, tell, lambda x: x.wait())
+
+        marks = sorted(set(halving) | set(rounds) | {blocks, 2 * blocks})
         at = 0
-        for p, stop in enumerate(stops):
-            lax.fori_loop(at, stop, block, 0)
-            at = stop
-            pass_on(p + 1)
+        for mark in marks:
+            if at < blocks:
+                lax.fori_loop(at, min(mark, blocks), kernel_block, 0)
+            else:
+                lax.fori_loop(at - blocks, mark - blocks, input_block, 0)
+            at = mark
+            if mark in halving:
+                pass_on(halving[mark])
+            if mark == blocks:
+                sum_round(0)
+                load_d.wait()
+
+                @pl.when(has_up)
+                def _():
+                    down.wait_recv()
+
+                @pl.when(has_down)
+                def _():
+                    up.wait_recv()
+            if mark in rounds:
+                sum_round(rounds[mark])
+        pass_on(steps - 1)
+        sum_round(3)
 
         @pl.when(has_up)
         def _():
@@ -870,32 +964,31 @@
     whole = pl.BlockSpec(memory_space=pl.ANY)
     local = pl.BlockSpec(memory_space=pltpu.VMEM)
     vm, dma = pltpu.VMEM, pltpu.SemaphoreType.DMA
-    d_in, g, g_gain, *extra = pl.pallas_call(
+    d_in, g_all, *extra = pl.pallas_call(
         kernel,
         out_shape=(
             jax.ShapeDtypeStruct((rows, cols, c), F32),
-            jax.ShapeDtypeStruct((size * size, 1, c), F32),
-            jax.ShapeDtypeStruct((1, c), F32),
-            *plans[0].buffers(),
-            *plans[1].buffers(),
+            jax.ShapeDtypeStruct((devices, small, c), F32),
+            *plans[0].buffers()[1:],
+            *plans[1].buffers()[1:],
         ),
-        in_specs=[local] * 5 + [whole] * 4,
-        out_specs=(local,) * 3 + (whole,) * (4 * steps),
+        in_specs=[local] * 6 + [whole] * 6,
+        out_specs=(local,) * 2 + (whole,) * (2 * each),
         scratch_shapes=[
             vm((high, cols, c), BF), vm((high, cols, c), BF), vm((rows, cols, c), BF),
             vm((high, cols + 2 * EDGE, LANES), F32), vm((high, cols + 2 * EDGE, LANES), F32),
+            vm((devices, small, c), F32), vm((devices, small, c), F32), vm((n, small, c), F32),
             dma((2,)), dma((2,)), dma((2,)),
+            dma((devices,)), dma((devices,)), dma((n,)), dma((n,)), dma((devices,)), dma((devices,)),
         ]
         + plans[0].semaphores() + plans[1].semaphores(),
         compiler_params=pltpu.CompilerParams(
             collective_id=3, has_side_effects=True, vmem_limit_bytes=50 * MIB
         ),
         cost_estimate=pl.CostEstimate(flops=6 * 10**10, bytes_accessed=10**8, transcendentals=0),
-    )(
-        d_normed, conv_out, gain, mask, w, bordered, d_map,
-        *(v.reshape((shape[0] // 2, 2) + shape[1:]) for v in grads),
-    )
-    return d_in, g, g_gain[0], [extra[2 * steps - 1].reshape(shape[1:]), extra[4 * steps - 1].reshape(shape[1:])]
+    )(d_normed, conv_out, gain, mask, w, low_gains, bordered, d_map, *grads[0], *grads[1])
+    sums = g_all.reshape(devices * small, c)[:count]
+    return d_in, sums, [extra[each - 1].reshape(shape[1:]), extra[2 * each - 1].reshape(shape[1:])]
 
 
 GATE, OUT, HIGH_A, HIGH_B, QUERY, KEY, VALUE, PROJ = range(8)
@@ -1271,73 +1364,6 @@
         compiler_params=pltpu.CompilerParams(collective_id=cid, has_side_effects=True, vmem_limit_bytes=61 * MIB),
         cost_estimate=pl.CostEstimate(flops=14 * 10**9, bytes_accessed=70 * 10**6, transcendentals=10**7),
     )(low, pool_a, pool_b, cot, gain1, gain2, packed.reshape(pairs, 2, n, rows, 16 * width))
-def sum_everywhere(x, devices, n, cid):
-    rows = x.shape[1]
-
-    def kernel(x_ref, out, here, level, send1, recv1, send2, recv2, send3, recv3):
-        me, d = lax.axis_index("dp"), lax.axis_index("mp")
-        barrier = pltpu.get_barrier_semaphore()
-
-        def greet(k, _):
-            pl.semaphore_signal(
-                barrier, inc=1, device_id={"dp": lax.rem(me + k, devices)}, device_id_type=MESH
-            )
-            return 0
-
-        lax.fori_loop(1, devices, greet, 0)
-        for k in range(1, n):
-            pl.semaphore_signal(barrier, inc=1, device_id={"mp": lax.rem(d + k, n)}, device_id_type=MESH)
-        here[me] = x_ref[me]
-        pl.semaphore_wait(barrier, devices + n - 2)
-
-        def spread(k):
-            peer = lax.rem(me + k, devices)
-            return pltpu.make_async_remote_copy(
-                src_ref=x_ref.at[peer], dst_ref=here.at[me], send_sem=send1.at[k], recv_sem=recv1.at[k],
-                device_id={"dp": peer}, device_id_type=MESH,
-            )
-
-        def across(k):
-            return pltpu.make_async_remote_copy(
-                src_ref=level.at[d], dst_ref=level.at[d], send_sem=send2.at[k], recv_sem=recv2.at[k],
-                device_id={"mp": lax.rem(d + k, n)}, device_id_type=MESH,
-            )
-
-        def give(k):
-            return pltpu.make_async_remote_copy(
-                src_ref=out.at[me], dst_ref=out.at[me], send_sem=send3.at[k], recv_sem=recv3.at[k],
-                device_id={"dp": lax.rem(me + k, devices)}, device_id_type=MESH,
-            )
-
-        def each(count, make, act):
-            def one(k, _):
-                act(make(k))
-                return 0
-
-            lax.fori_loop(1, count, one, 0)
-
-        each(devices, spread, lambda c: c.start())
-        each(devices, spread, lambda c: c.wait())
-        level[d] = jnp.sum(here[...], axis=0)
-        each(n, across, lambda c: c.start())
-        each(n, across, lambda c: c.wait())
-        out[me] = jnp.sum(level[...], axis=0)
-        each(devices, give, lambda c: c.start())
-        each(devices, give, lambda c: c.wait())
-
-    vm, dma = pltpu.VMEM, pltpu.SemaphoreType.DMA
-    return pl.pallas_call(
-        kernel,
-        out_shape=jax.ShapeDtypeStruct(x.shape, F32),
-        in_specs=[pl.BlockSpec(memory_space=pltpu.VMEM)],
-        out_specs=pl.BlockSpec(memory_space=pltpu.VMEM),
-        scratch_shapes=[vm(x.shape, F32), vm((n, rows, LANES), F32)] + [dma((devices,)), dma((devices,)), dma((n,)), dma((n,)), dma((devices,)), dma((devices,))],
-        compiler_params=pltpu.CompilerParams(
-            collective_id=cid, has_side_effects=True, vmem_limit_bytes=16 * MIB
-        ),
-    )(x)
-
-
 def rows_first(x):
     return with_layout_constraint(x, Layout(major_to_minor=tuple(range(x.ndim))))
 
@@ -1441,23 +1467,14 @@
     )
     low_sums = rows_first(low_sums.reshape(shards, share, -1))
     low_sums = rows_first(lax.psum_scatter(low_sums, "mp", scatter_dimension=0))
-    d_hr_in, g_conv, g_hr_gain, (g_cn_up, g_cn_down) = conv_backward(
-        d_normed, conv_out, hr_gainf[None], cell_mask, bordered, d_map, taps, size, cn_grads, devices, shards
+    low_gains = jnp.pad(jnp.stack([g_ln1, g_ln2]), ((0, 0), (0, chan_count - dims)))
+    d_hr_in, small_sums, (g_cn_up, g_cn_down) = conv_backward(
+        d_normed, conv_out, hr_gainf[None], cell_mask, bordered, d_map, taps, low_gains, size, cn_grads, devices, shards
     )
     d_hr_in = d_hr_in[None]
     g_cn_up, g_cn_down = g_cn_up.astype(F32), g_cn_down.astype(F32).T
-    g_conv = g_conv.reshape(conv_w.shape)
-    small = (g_conv, g_hr_gain, g_ln1, g_ln2)
-    flat = jnp.concatenate([g.reshape(-1) for g in small])
-    room = -(-flat.size // (devices * 8 * LANES)) * (devices * 8 * LANES)
-    flat = jnp.pad(flat, (0, room - flat.size)).reshape(devices, -1, LANES)
-    flat, low_sums = lax.optimization_barrier((flat, low_sums))
-    flat = sum_everywhere(flat, devices, shards, 4).reshape(-1)
-    parts, at = [], 0
-    for g in small:
-        parts.append(flat[at : at + g.size].reshape(g.shape))
-        at += g.size
-    g_conv, g_hr_gain, g_ln1, g_ln2 = parts
+    g_conv = small_sums[: size * size].reshape(conv_w.shape)
+    g_hr_gain, g_ln1, g_ln2 = small_sums[size * size], small_sums[-2, :dims], small_sums[-1, :dims]
     own = low_sums.astype(F32)
     split, at = [], 0
     for p in pieces:

time: 841 us -> 795 us (0.945)
  Pallas kernels: 709 us -> 664 us
    pallas_call x1, Pallas kernels: 271 us -> 251 us  [big_backward(): pl.pallas_call(kernel, out_shape=(jax.ShapeDtypeStruct((CHUNKS, rows, c),...]
    pallas_call x1 -> x0, Pallas kernels: 19.2 us -> none  [sum_everywhere(): pl.pallas_call(kernel, out_shape=jax.ShapeDtypeStruct(x.shape, F32), in_s...]
    unnamed x57 -> x55, local copies, waits for them, and re-layouts: 19.6 us -> 19.2 us
  transfers between devices with their start and end apart: 3 -> 3, of which waited for: 1 -> 1; matrix products, arithmetic and copies ran while one was open for 3% -> 3% of each run, Pallas kernels for 37% -> 38%
where the time goes in v6:
time: 795 us; the launch traced here: 787 us
  Pallas kernels  664 us (84%)
  waiting for transfers between devices  48.9 us (6%)
  local copies, waits for them, and re-layouts  46.9 us (6%)
  between operations  14.5 us (2%)
  other arithmetic  11.9 us (1%)
    pallas_call x1, Pallas kernels, big_backward(): pl.pallas_call(kernel, out_shape=(jax.ShapeDtypeStruct((CHUNKS, rows, c),...  251 us
    pallas_call x1, Pallas kernels, big_forward(): pl.pallas_call(kernel, out_shape=(jax.ShapeDtypeStruct((CHUNKS, rows, c),...  184 us
    pallas_call x1, Pallas kernels, low_stage(): pl.pallas_call(kernel, out_shape=(tok, tok, tok, tok, one, one, jax.Shape...  112 us
    pallas_call x1, Pallas kernels, conv_backward(): pl.pallas_call(kernel, out_shape=(jax.ShapeDtypeStruct((rows, cols, c), F...  87.3 us
    all_gather x1, waiting for transfers between devices, per_device(): packed = rows_first(lax.all_gather(packed, 'mp', axis=0, tiled=True))  48.9 us
    pallas_call x1, Pallas kernels, conv_forward(): pl.pallas_call(kernel, out_shape=(jax.ShapeDtypeStruct((rows, cols, c), F...  30.3 us
    unnamed x55, local copies, waits for them, and re-layouts  19.2 us
  transfers between devices with their start and end apart: 3, of which 1 were waited for; matrix products, arithmetic and copies ran while one was open for 3% of the time, Pallas kernels for 38%

profile of v6, /device:TPU:0, one launch (start us, length us, event | category | flops | bytes accessed | tf_op | source)
XLA Modules:
  0.0 786.6 jit_solution(3141452829493930322)
XLA Ops:
  7.3 0.9 dynamic-slice_dynamic-update-slice_fusion.2
  8.2 0.9 constant_dynamic-slice_fusion.1
  9.2 0.8 dynamic-slice_dynamic-update-slice_fusion.1
  10.0 0.8 constant_dynamic-slice_fusion.2
  10.9 1.0 constant_dynamic-slice_fusion
  12.0 0.9 fusion.2
  12.9 0.8 fusion.1
  13.7 0.8 fusion
  14.6 1.0 dynamic-slice_dynamic-update-slice_fusion
  15.6 1.0 copy-done.5
  17.2 1.7 bitcast_multiply_fusion.x_ref.res
  18.9 30.3 %shard_map.305 = (f32[12,48,1536]{2,1,0:T(8,128)S(1)}, bf16[18,48,1536]{2,1,0:T(8,128)(2,1)S(1)}) custom-call(bf16[12,48,1536]{2,1,0:T(8,128)(2,1)S(1)} %bitcast_multiply_fusion.x_ref.res, f32[49,1,1536]{2,1,0:T(1,128)S(1)} %reshape.186.w_ref), custom_call_target="tpu_custom_call" | custom-call | tf_op jit(solution)/shard_map/pallas_call | solution.py:750
  50.7 1.2 copy-done
  51.8 1.9 multiply_convert_fusion
  53.7 48.9 %all-gather.3.cloned.1.call-done = bf16[512,4096]{1,0:T(8,128)(2,1)} async-done(((bf16[128,4096]{1,0:T(8,128)(2,1)}), bf16[512,4096]{1,0:T(8,128)(2,1)}) %all-gather.3.cloned.1.call-update) | async-done | bytes 4194320 | tf_op jit(solution)/shard_map/all_gather | solution.py:1427
  102.7 0.9 convert_element_type.87.mask_ref
  104.0 0.9 reshape.166.low_ref
  105.0 0.8 copy.57.share_ref
  106.1 0.9 reshape.171.cot_ref
  108.2 183.9 %shard_map.306 = (f32[6,96,1536]{2,1,0:T(8,128)}, bf16[6,24,1536]{2,1,0:T(8,128)(2,1)}, bf16[4,6,96,1536]{3,2,1,0:T(8,128)(2,1)}, bf16[4,6,96,1536]{3,2,1,0:T(8,128)(2,1)}, bf16[4,6,96,1536]{3,2,1,0:T(8,128)(2,1)}) custom-call(bf16[6,96,1536]{2,1,0:T(8,128)(2,1)} %bitcast.111, bf16[1536,1536]{1,0:T(8,128)(2,1)} %wu.3, bf16[1536,1536]{1,0:T(8,128)(2,1)} %wd.3, ...), custom_call_target="tpu_custom_call" | custom-call | flops 21743271936 | bytes 28311552 | tf_op jit(solution)/shard_map/pallas_call | solution.py:369
  292.1 1.5 reshape_reshape.28
  293.8 0.9 reshape.169.pool_a_ref
  295.0 0.9 reshape.170.pool_b_ref
  295.9 111.9 %shard_map.307 = (f32[144,1024]{1,0:T(8,128)}, f32[144,1024]{1,0:T(8,128)}, f32[144,1024]{1,0:T(8,128)}, f32[144,1024]{1,0:T(8,128)}, f32[1,1024]{1,0:T(1,128)},...) custom-call(bf16[144,1024]{1,0:T(8,128)(2,1)} %reshape.166.low_ref, bf16[144,1024]{1,0:T(8,128)(2,1)} %reshape.169.pool_a_ref, ...), custom_call_target="tpu_custom_call" | custom-call | flops 14000000000 | bytes 70000000 | tf_op jit(solution)/shard_map/pallas_call | solution.py:1350
  407.9 1.3 reshape.178
  409.5 1.3 reshape.177
  411.3 1.3 reshape_reshape.34.pool_ref
  412.6 250.9 %shard_map.308 = (f32[6,96,1536]{2,1,0:T(8,128)}, bf16[6,96,1536]{2,1,0:T(8,128)(2,1)}, bf16[4,2,192,1536]{3,2,1,0:T(8,128)(2,1)}, bf16[4,2,192,1536]{3,2,1,0:T(...) custom-call(bf16[12,48,1536]{2,1,0:T(8,128)(2,1)} %bitcast.131, ...), custom_call_target="tpu_custom_call" | custom-call | flops 43486543872 | bytes 28311552 | tf_op jit(solution)/shard_map/pallas_call | solution.py:602
  664.2 87.3 %shard_map.309 = (f32[12,48,1536]{2,1,0:T(8,128)}, f32[8,7,1536]{2,1,0:T(8,128)S(1)}, bf16[2,192,1536]{2,1,0:T(8,128)(2,1)}, bf16[1,192,1536]{2,1,0:T(8,128)(2,1...) custom-call(f32[12,48,1536]{2,1,0:T(8,128)} %bitcast.136, ...), custom_call_target="tpu_custom_call" | custom-call | flops 60000002048 | bytes 100000000 | tf_op jit(solution)/shard_map/pallas_call | solution.py:967
  751.6 0.8 slice.82
  752.3 0.8 reshape.184
  753.7 1.3 broadcast_in_dim_reshape.20
  755.6 1.3 broadcast_in_dim_reshape.21
  756.9 1.4 slice_reduce_fusion
  758.3 1.4 fusion.3
  759.7 1.1 bitcast_convert_fusion.1
  760.9 1.1 convert_bitcast_fusion
  762.0 1.4 bitcast_convert_fusion
  763.4 0.9 slice_bitcast_fusion.1
  765.0 1.0 slice_bitcast_fusion
  766.0 1.7 copy.74
  767.7 1.7 copy.75
  769.4 2.0 copy.76
  771.4 1.6 pad_maximum_fusion.2
  773.0 1.8 pad_maximum_fusion.1
  774.8 1.8 copy.103
  776.6 1.5 copy-done.4
  778.1 1.8 copy.104
  (87 shorter events, 8.2 us)
Async XLA Ops:
  7.2 9.5 %copy-start.11 = (s32[1,12,48]{2,0,1:T(1,128)S(1)}, s32[1,12,48]{2,0,1:T(1,128)}, u32[]{:S(2)}) copy-start(s32[1,12,48]{2,0,1:T(1,128)} %param.20) | copy-start | bytes 6916
  7.2 9.5 %copy-start.10 = (bf16[7,7,1536]{2,1,0:T(8,128)(2,1)S(1)}, bf16[7,7,1536]{2,1,0:T(8,128)(2,1)}, u32[]{:S(2)}) copy-start(bf16[7,7,1536]{2,1,0:T(8,128)(2,1)} %param.21) | copy-start | bytes 451588
  7.2 9.9 %copy-start.12 = (bf16[1536]{0:T(1024)(128)(2,1)S(1)}, bf16[1536]{0:T(1024)(128)(2,1)}, u32[]{:S(2)}) copy-start(bf16[1536]{0:T(1024)(128)(2,1)} %param.22) | copy-start | bytes 9220
  7.2 95.4 %all-gather.3.cloned.1.call-start = ((), (), s32[]{:S(2)}) async-start(), calls=%async_computation.1 | async-start | bytes 5242880 | tf_op jit(solution)/shard_map/all_gather | solution.py:1427
  15.6 1.0 copy-start.5
  16.6 279.3 %all-gather.5.cloned.1.call-start = ((), (), s32[]{:S(2)}) async-start(), calls=%async_computation.2 | async-start | bytes 37748736 | tf_op jit(solution)/shard_map/all_gather | solution.py:1440
  18.8 31.3 %copy-start.1 = (bf16[12,48,1536]{2,1,0:T(8,128)(2,1)}, bf16[12,48,1536]{2,1,0:T(8,128)(2,1)S(1)}, u32[]{:S(2)}) copy-start(bf16[12,48,1536]{2,1,0:T(8,128)(2,1)S(1)} %bitcast_multiply_fusion.x_ref.res) | copy-start | bytes 5308420
  49.2 1.5 copy-start.2
  49.2 2.7 copy-start
  53.7 50.0 %copy-start.8 = (bf16[1,144,1024]{2,1,0:T(8,128)(2,1)S(1)}, bf16[1,144,1024]{2,1,0:T(8,128)(2,1)}, u32[]{:S(2)}) copy-start(bf16[1,144,1024]{2,1,0:T(8,128)(2,1)} %param.19) | copy-start | bytes 884740
  53.7 52.1 %copy-start.9 = (bf16[1,144,1024]{2,1,0:T(8,128)(2,1)S(1)}, bf16[1,144,1024]{2,1,0:T(8,128)(2,1)}, u32[]{:S(2)}) copy-start(bf16[1,144,1024]{2,1,0:T(8,128)(2,1)} %param.34) | copy-start | bytes 884740
  102.6 4.4 copy-start.15
  102.6 5.0 copy-start.16
  102.6 659.4 %reduce-scatter.2.cloned.1.call-start = ((), (), s32[]{:S(2)}) async-start(), calls=%async_computation.3 | async-start | bytes 5242880 | tf_op jit(solution)/shard_map/reduce_scatter | solution.py:1469
  663.5 0.7 copy-start.14
  663.5 0.7 copy-start.13
  664.2 88.9 %copy-start.7 = (f32[144,1024]{1,0:T(8,128)S(1)}, f32[144,1024]{1,0:T(8,128)}, u32[]{:S(2)}) copy-start(f32[144,1024]{1,0:T(8,128)} %get-tuple-element.48) | copy-start | bytes 1769476
  751.5 3.4 copy-start.6
  763.4 11.4 %copy-start.3 = (f32[6,96,1536]{2,1,0:T(8,128)S(1)}, f32[6,96,1536]{2,1,0:T(8,128)}, u32[]{:S(2)}) copy-start(f32[6,96,1536]{2,1,0:T(8,128)} %get-tuple-element.49) | copy-start | bytes 10616836
  774.8 3.3 copy-start.4
Sparse Core Ops, SparseCore 0:
  16.7 85.8 all-gather.2
  104.5 159.7 all-gather.4
  663.7 92.5 reduce-scatter.1

commit v7 on v6

--- a/solution.py
+++ b/solution.py
@@ -98,7 +98,7 @@
 
 
 def chain_exchange(
-    n, chunks, lag, gathered, partial, travel, sems, own_chunk, prepare, arrived, compute, mates=(), begin=None, turn=None, after=None
+    n, chunks, lag, gathered, partial, travel, sems, own_chunk, prepare, arrived, compute, mates=(), begin=None, turn=None, after=None, early=False
 ):
     ag_send, ag_recv, rs_send, rs_recv = sems
     d = lax.axis_index("mp")
@@ -184,49 +184,68 @@
             def _():
                 rs(way, s, jj).start()
 
+    def block_of(k, way):
+        s = d - k + 2 * k * way
+        return s, (s >= 0) & (s < n) & ((k > 0) | (way == 0))
+
+    def receive(k, way, s, j):
+        @pl.when(k > 0)
+        def _():
+            pltpu.make_async_copy(gathered.at[s, j], gathered.at[s, j], ag_recv.at[s, j]).wait()
+
+            @pl.when((way == 0) & has_right)
+            def _():
+                ag(0, s, j).start()
+
+            @pl.when((way == 1) & has_left)
+            def _():
+                ag(1, s, j).start()
+
+        arrived(s, j)
+
+    wait_one = 1 if early else 0
+
     def step(g, _):
         k, j = g // chunks, lax.rem(g, chunks)
+
+        def sides(act):
+            @pl.when(g < n * chunks)
+            def _():
+                def side(way, _):
+                    s, ok = block_of(k, way)
+                    pl.when(ok)(lambda: act(way, s))
+                    return 0
+
+                lax.fori_loop(0, 2, side, 0)
+
+        def flows():
+            flow(1, g - wait_one - (n - 1 - d) * lag)
+            flow(0, g - wait_one - d * lag)
+
         if turn is not None:
             turn(g)
-
-        @pl.when(g < n * chunks)
-        def _():
-            def side(way, _):
-                s = d - k + 2 * k * way
-                ok = (s >= 0) & (s < n) & ((k > 0) | (way == 0))
-
-                @pl.when(ok)
-                def _():
-                    prepare(way, s, j)
-
-                    @pl.when(k > 0)
-                    def _():
-                        pltpu.make_async_copy(
-                            gathered.at[s, j], gathered.at[s, j], ag_recv.at[s, j]
-                        ).wait()
-
-                        @pl.when((way == 0) & has_right)
-                        def _():
-                            ag(0, s, j).start()
-
-                        @pl.when((way == 1) & has_left)
-                        def _():
-                            ag(1, s, j).start()
-
-                    arrived(s, j)
-                    compute(way, s, j)
-
-                return 0
-
-            lax.fori_loop(0, 2, side, 0)
-
-        flow(1, g - (n - 1 - d) * lag)
-        flow(0, g - d * lag)
+        if early:
+            sides(lambda way, s: receive(k, way, s, j))
+            flows()
+
+            def later(way, s):
+                prepare(way, s, j)
+                compute(way, s, j)
+
+            sides(later)
+        else:
+            def work(way, s):
+                prepare(way, s, j)
+                receive(k, way, s, j)
+                compute(way, s, j)
+
+            sides(work)
+            flows()
         if after is not None:
             after(g)
         return 0
 
-    lax.fori_loop(0, n * chunks + (n - 1) * lag, step, 0)
+    lax.fori_loop(0, n * chunks + (n - 1) * lag + wait_one, step, 0)
 
     def drain(i, _):
         s, j = i // chunks, lax.rem(i, chunks)
@@ -298,8 +317,8 @@
     pairs = rows // cols // 2
 
     def kernel(
-        x_ref, wu, wd, res, mask_ref, share_ref, out, pooled, x_all, act_all, slope_all,
-        gathered, partial, travel, act, slope, total, folded, copied, stored, load_sem, *sems
+        x_ref, wu, wd, res, mask_ref, share_ref, out, pooled, x_all, act_all, slope_all, wu_t, wd_t,
+        gathered, partial, travel, act, slope, total, folded, turned, copied, stored, load_sem, *sems
     ):
         d = lax.axis_index("mp")
         load = pltpu.make_async_copy(x_ref, gathered.at[d], load_sem)
@@ -344,7 +363,19 @@
             keep_act.wait()
             keep_slope.wait()
 
-        chain_exchange(n, CHUNKS, 1, gathered, partial, travel, sems, own_chunk, prepare, arrived, compute)
+        def after(g):
+            for i, (w, target, size) in enumerate(((wu, wu_t, h), (wd, wd_t, c))):
+                @pl.when(g < size // LANES)
+                def _():
+                    some = pl.ds(pl.multiple_of(g * LANES, LANES), LANES)
+                    turned[i, :, pl.ds(0, w.shape[0])] = w[:, some].T
+                    copy = pltpu.make_async_copy(turned.at[i, :, pl.ds(0, w.shape[0])], target.at[some], stored.at[i])
+                    copy.start()
+                    copy.wait()
+
+        chain_exchange(
+            n, CHUNKS, 1, gathered, partial, travel, sems, own_chunk, prepare, arrived, compute, after=after
+        )
 
         def finish(j, _):
             own_sum(n, d, j, partial, travel, total)
@@ -366,7 +397,7 @@
 
     whole = pl.BlockSpec(memory_space=pl.ANY)
     local = pl.BlockSpec(memory_space=pltpu.VMEM)
-    out, pooled, x_all, act_all, slope_all = pl.pallas_call(
+    out, pooled, x_all, act_all, slope_all, wu_t, wd_t = pl.pallas_call(
         kernel,
         out_shape=(
             jax.ShapeDtypeStruct((CHUNKS, rows, c), F32),
@@ -374,12 +405,14 @@
             jax.ShapeDtypeStruct((n, CHUNKS, rows, c), BF),
             jax.ShapeDtypeStruct((n, CHUNKS, rows, h), BF),
             jax.ShapeDtypeStruct((n, CHUNKS, rows, h), BF),
+            jax.ShapeDtypeStruct((h, c), BF),
+            jax.ShapeDtypeStruct((c, h), BF),
         ),
         in_specs=[whole, local, local, local, local, local],
-        out_specs=(whole, local, whole, whole, whole),
+        out_specs=(whole, local, whole, whole, whole, whole, whole),
         scratch_shapes=chunk_buffers(n, rows, c, F32)
         + [pltpu.VMEM((rows, h), BF)] * 2
-        + [pltpu.VMEM((rows, c), F32), pltpu.VMEM((c // LANES, pairs * cols, LANES), F32)]
+        + [pltpu.VMEM((rows, c), F32), pltpu.VMEM((c // LANES, pairs * cols, LANES), F32), pltpu.VMEM((2, LANES, max(c, h)), BF)]
         + [pltpu.SemaphoreType.DMA((n, CHUNKS)), pltpu.SemaphoreType.DMA((2,)), pltpu.SemaphoreType.DMA]
         + chain_sems(n, CHUNKS),
         compiler_params=pltpu.CompilerParams(
@@ -398,13 +431,15 @@
         x_all,
         act_all,
         slope_all,
+        wu_t,
+        wd_t,
     )
 
 
-def big_backward(cot, d_pooled, share, mask, x_all, act_all, slope_all, w_up, w_down, grads, n, devices):
+def big_backward(cot, d_pooled, share, mask, x_all, act_all, slope_all, up_t, down_t, grads, n, devices):
     _, cols, c = cot.shape
     t = cot.shape[0] * cols
-    h = w_up.shape[1]
+    h = up_t.shape[0]
     rows = t // CHUNKS
     half = cols // 2
     pairs_here = rows // cols // 2
@@ -434,23 +469,24 @@
             for plan in plans:
                 plan.start(0)
 
-        def pass_on(p):
-            for plan in plans:
-                plan.finish(p)
+        def pass_on(p, plan):
+            plan.finish(p)
             if p + 1 < steps:
-                for plan in plans:
-                    plan.start(p + 1)
-
-        all_steps = n * CHUNKS + n - 1
-        due = [all_steps * (2**steps - 2 ** (steps - 1 - p)) // (2**steps - 1) for p in range(steps)]
+                plan.start(p + 1)
+
+        all_steps = n * CHUNKS + n
+        due = [all_steps * 9 * (2**steps - 2 ** (steps - 1 - p)) // (10 * (2**steps - 1)) // 2 * 2 for p in range(steps)]
 
         def turn(g):
             for p in range(steps - 1):
-                pl.when(g == due[p])(lambda p=p: pass_on(p))
-
-            @pl.when(item_due(g))
+                for i, plan in enumerate(plans):
+                    pl.when(g == due[p] + 2 * i)(lambda p=p, plan=plan: pass_on(p, plan))
+
+            q, due_now = item_of(g)
+
+            @pl.when(due_now)
             def _():
-                for copy in item_copies((g - 3) // 2):
+                for copy in item_copies(q):
                     copy.start()
 
         def own_chunk(j):
@@ -480,7 +516,7 @@
             slope_copy(s, j).wait()
 
             def up(i, _):
-                back = nt(block[...], wd[columns(i), :])
+                back = nn(block[...], wd[:, columns(i)])
                 grad[:, columns(i)] = (back * slope[:, columns(i)].astype(F32)).astype(BF)
                 return 0
 
@@ -490,7 +526,7 @@
             keep.start()
 
             def down(i, _):
-                partial[s, j, :, columns(i)] = nt(grad[...], wu[columns(i), :]).astype(BF)
+                partial[s, j, :, columns(i)] = nn(grad[...], wu[:, columns(i)]).astype(BF)
                 return 0
 
             lax.fori_loop(0, c // TILE, down, 0)
@@ -516,13 +552,17 @@
                 pltpu.make_async_copy(h_all.at[s, jj], middle, stored.at[4]),
             )
 
-        def item_due(g):
-            return (lax.rem(g, 2) == 1) & (g >= 3) & (g < 2 * items + 3)
+        between = (d > 0) & (d < n - 1)
+
+        def item_of(g):
+            q = jnp.where(between, g - items, (g - 3) // 2)
+            return q, (q >= 0) & (q < items) & (g >= 3) & (between | (lax.rem(g, 2) == 1))
 
         def after(g):
-            @pl.when(item_due(g))
+            q, due_now = item_of(g)
+
+            @pl.when(due_now)
             def _():
-                q = (g - 3) // 2
                 s, jj = item_place(q)
                 for copy in item_copies(q):
                     copy.wait()
@@ -536,37 +576,28 @@
 
                 lax.fori_loop(0, c // TILE, tile, 0)
 
-        def clear(i, _):
-            some = pl.ds(pl.multiple_of(i * TILE, TILE), TILE)
-            g_up[some] = jnp.zeros((TILE, h), F32)
-            g_down[some] = jnp.zeros((TILE, h), F32)
-            return 0
-
-        def begin_all():
-            begin()
-            lax.fori_loop(0, c // TILE, clear, 0)
-
-        chain_exchange(
-            n, CHUNKS, 1, gathered, partial, travel, sems, own_chunk, prepare, arrived, compute,
-            [dp_mate(b) for b in range(steps + 1)], begin_all, turn, after,
-        )
-        keep = pltpu.make_async_copy(gathered.at[d], d_own, stored.at[0])
-        keep.start()
+            @pl.when(g == 2 * items + 2)
+            def _():
+                give(g_up, left, g_up_out, stored.at[2])
+                swaps[0].start()
+
+            @pl.when(g == 2 * items + 3)
+            def _():
+                give(g_down, right, g_down_out, stored.at[3])
+                swaps[1].start()
+
         core = dp_bit(0)
 
-        def give(i, _):
-            some = pl.ds(pl.multiple_of(i * piece, piece), piece)
-            left[pl.ds(0, piece)] = g_up[some].astype(BF)
-            up = pltpu.make_async_copy(left.at[pl.ds(0, piece)], g_up_out.at[i // 2, lax.rem(i, 2)], stored.at[2])
-            up.start()
-            right[pl.ds(0, piece)] = g_down[some].astype(BF)
-            down = pltpu.make_async_copy(right.at[pl.ds(0, piece)], g_down_out.at[i // 2, lax.rem(i, 2)], stored.at[3])
-            down.start()
-            up.wait()
-            down.wait()
-            return 0
-
-        lax.fori_loop(0, devices, give, 0)
+        def give(source, stage, target, sem):
+            def one(i, _):
+                stage[pl.ds(0, piece)] = source[pl.ds(pl.multiple_of(i * piece, piece), piece)].astype(BF)
+                copy = pltpu.make_async_copy(stage.at[pl.ds(0, piece)], target.at[i // 2, lax.rem(i, 2)], sem)
+                copy.start()
+                copy.wait()
+                return 0
+
+            lax.fori_loop(0, devices, one, 0)
+
         swaps = [
             pltpu.make_async_remote_copy(
                 src_ref=src.at[:, 1 - core], dst_ref=dst, send_sem=core_send.at[i], recv_sem=core_recv.at[i],
@@ -574,9 +605,22 @@
             )
             for i, (src, dst) in enumerate(((g_up_out, got_up), (g_down_out, got_down)))
         ]
-        for swap in swaps:
-            swap.start()
-
+        def clear(i, _):
+            some = pl.ds(pl.multiple_of(i * TILE, TILE), TILE)
+            g_up[some] = jnp.zeros((TILE, h), F32)
+            g_down[some] = jnp.zeros((TILE, h), F32)
+            return 0
+
+        def begin_all():
+            begin()
+            lax.fori_loop(0, c // TILE, clear, 0)
+
+        chain_exchange(
+            n, CHUNKS, 1, gathered, partial, travel, sems, own_chunk, prepare, arrived, compute,
+            [dp_mate(b) for b in range(steps + 1)], begin_all, turn, after, True,
+        )
+        keep = pltpu.make_async_copy(gathered.at[d], d_own, stored.at[0])
+        keep.start()
         def result(j):
             return pltpu.make_async_copy(total, out.at[j], stored.at[1])
 
@@ -592,7 +636,8 @@
         lax.fori_loop(0, CHUNKS, finish, 0)
         result(CHUNKS - 1).wait()
         keep.wait()
-        pass_on(steps - 1)
+        for plan in plans:
+            pass_on(steps - 1, plan)
         for swap in swaps:
             swap.wait()
 
@@ -633,7 +678,7 @@
     )(
         cot, d_pooled.reshape(CHUNKS, pairs_here * half, c), share.reshape(CHUNKS, pairs_here * half, 1),
         mask.reshape(CHUNKS, rows, 1), *(v.reshape(n, CHUNKS // 2, 2 * rows, -1) for v in (x_all, act_all)),
-        slope_all, w_up, w_down,
+        slope_all, up_t, down_t,
         grads.reshape(pairs // 2, 2, g_rows, g_cols), grads.reshape(2, pairs // 2, g_rows, g_cols),
     )
     return (
@@ -1438,7 +1483,7 @@
     normed = layer_norm(conv_out * cell_mask, hr_gainf).astype(BF)
     normed, packed = lax.optimization_barrier((normed, packed))
     packed = rows_first(lax.all_gather(packed, "dp", axis=0, tiled=True))
-    hr_out, pooled, normed_all, hidden_act, hidden_slope = big_forward(
+    hr_out, pooled, normed_all, hidden_act, hidden_slope, up_t, down_t = big_forward(
         normed.reshape(row_count * col_count, chan_count), cn_up, cn_down, masked, plane_mask, shares, shards
     )
     hr_out = hr_out.reshape(hr_in.shape)
@@ -1463,7 +1508,7 @@
     )
     d_normed, d_map, cn_grads, low_sums = big_backward(
         cot_hr[0], d_pooled.reshape(tokens, chan_count), shares, plane_mask, normed_all, hidden_act, hidden_slope,
-        cn_up, cn_down, low_grads, shards, devices,
+        up_t, down_t, low_grads, shards, devices,
     )
     low_sums = rows_first(low_sums.reshape(shards, share, -1))
     low_sums = rows_first(lax.psum_scatter(low_sums, "mp", scatter_dimension=0))

time: 795 us -> 770 us (0.969)
  Pallas kernels: 664 us -> 641 us
    pallas_call x1, Pallas kernels: 251 us -> 231 us  [big_backward(): pl.pallas_call(kernel, out_shape=(jax.ShapeDtypeStruct((CHUNKS, rows, c),...]
  transfers between devices with their start and end apart: 3 -> 3, of which waited for: 1 -> 1; matrix products, arithmetic and copies ran while one was open for 3% -> 3% of each run, Pallas kernels for 38% -> 39%
where the time goes in v7:
time: 770 us; the launch traced here: 763 us
  Pallas kernels  641 us (83%)
  waiting for transfers between devices  48.9 us (6%)
  local copies, waits for them, and re-layouts  46.9 us (6%)
  between operations  14.5 us (2%)
  other arithmetic  11.9 us (2%)
    pallas_call x1, Pallas kernels, big_backward(): pl.pallas_call(kernel, out_shape=(jax.ShapeDtypeStruct((CHUNKS, rows, c),...  231 us
    pallas_call x1, Pallas kernels, big_forward(): pl.pallas_call(kernel, out_shape=(jax.ShapeDtypeStruct((CHUNKS, rows, c),...  184 us
    pallas_call x1, Pallas kernels, low_stage(): pl.pallas_call(kernel, out_shape=(tok, tok, tok, tok, one, one, jax.Shape...  112 us
    pallas_call x1, Pallas kernels, conv_backward(): pl.pallas_call(kernel, out_shape=(jax.ShapeDtypeStruct((rows, cols, c), F...  83.4 us
    all_gather x1, waiting for transfers between devices, per_device(): packed = rows_first(lax.all_gather(packed, 'mp', axis=0, tiled=True))  48.9 us
    pallas_call x1, Pallas kernels, conv_forward(): pl.pallas_call(kernel, out_shape=(jax.ShapeDtypeStruct((rows, cols, c), F...  30.3 us
    unnamed x55, local copies, waits for them, and re-layouts  19.2 us
  transfers between devices with their start and end apart: 3, of which 1 were waited for; matrix products, arithmetic and copies ran while one was open for 3% of the time, Pallas kernels for 39%

profile of v7, /device:TPU:0, one launch (start us, length us, event | category | flops | bytes accessed | tf_op | source)
XLA Modules:
  0.0 763.3 jit_solution(13221652419558146509)
XLA Ops:
  7.3 0.9 dynamic-slice_dynamic-update-slice_fusion.2
  8.2 0.9 constant_dynamic-slice_fusion.1
  9.2 0.8 dynamic-slice_dynamic-update-slice_fusion.1
  10.0 0.8 constant_dynamic-slice_fusion.2
  10.9 1.0 constant_dynamic-slice_fusion
  12.0 0.9 fusion.2
  12.9 0.8 fusion.1
  13.7 0.8 fusion
  14.6 1.0 dynamic-slice_dynamic-update-slice_fusion
  15.6 1.0 copy-done.5
  17.2 1.7 bitcast_multiply_fusion.x_ref.res
  18.9 30.3 %shard_map.305 = (f32[12,48,1536]{2,1,0:T(8,128)S(1)}, bf16[18,48,1536]{2,1,0:T(8,128)(2,1)S(1)}) custom-call(bf16[12,48,1536]{2,1,0:T(8,128)(2,1)S(1)} %bitcast_multiply_fusion.x_ref.res, f32[49,1,1536]{2,1,0:T(1,128)S(1)} %reshape.186.w_ref), custom_call_target="tpu_custom_call" | custom-call | tf_op jit(solution)/shard_map/pallas_call | solution.py:795
  50.7 1.2 copy-done
  51.8 1.8 multiply_convert_fusion
  53.7 48.9 %all-gather.3.cloned.1.call-done = bf16[512,4096]{1,0:T(8,128)(2,1)} async-done(((bf16[128,4096]{1,0:T(8,128)(2,1)}), bf16[512,4096]{1,0:T(8,128)(2,1)}) %all-gather.3.cloned.1.call-update) | async-done | bytes 4194320 | tf_op jit(solution)/shard_map/all_gather | solution.py:1472
  102.7 0.9 convert_element_type.87.mask_ref
  104.0 0.9 reshape.166.low_ref
  105.0 0.8 copy.57.share_ref
  106.1 0.9 reshape.171.cot_ref
  108.2 183.8 %shard_map.306 = (f32[6,96,1536]{2,1,0:T(8,128)}, bf16[6,24,1536]{2,1,0:T(8,128)(2,1)}, bf16[4,6,96,1536]{3,2,1,0:T(8,128)(2,1)}, bf16[4,6,96,1536]{3,2,1,0:T(8,...) custom-call(bf16[6,96,1536]{2,1,0:T(8,128)(2,1)} %bitcast.111, ...), custom_call_target="tpu_custom_call" | custom-call | flops 21743271936 | bytes 28311552 | tf_op jit(solution)/shard_map/pallas_call | solution.py:400
  292.0 1.5 reshape_reshape.28
  293.7 0.9 reshape.169.pool_a_ref
  294.9 0.9 reshape.170.pool_b_ref
  295.8 112.2 %shard_map.307 = (f32[144,1024]{1,0:T(8,128)}, f32[144,1024]{1,0:T(8,128)}, f32[144,1024]{1,0:T(8,128)}, f32[144,1024]{1,0:T(8,128)}, f32[1,1024]{1,0:T(1,128)},...) custom-call(bf16[144,1024]{1,0:T(8,128)(2,1)} %reshape.166.low_ref, bf16[144,1024]{1,0:T(8,128)(2,1)} %reshape.169.pool_a_ref, ...), custom_call_target="tpu_custom_call" | custom-call | flops 14000000000 | bytes 70000000 | tf_op jit(solution)/shard_map/pallas_call | solution.py:1395
  408.0 1.3 reshape.178
  409.7 1.3 reshape.177
  411.4 1.3 reshape_reshape.34.pool_ref
  412.7 231.3 %shard_map.308 = (f32[6,96,1536]{2,1,0:T(8,128)}, bf16[6,96,1536]{2,1,0:T(8,128)(2,1)}, bf16[4,2,192,1536]{3,2,1,0:T(8,128)(2,1)}, bf16[4,2,192,1536]{3,2,1,0:T(...) custom-call(bf16[12,48,1536]{2,1,0:T(8,128)(2,1)} %bitcast.131, ...), custom_call_target="tpu_custom_call" | custom-call | flops 43486543872 | bytes 28311552 | tf_op jit(solution)/shard_map/pallas_call | solution.py:647
  644.7 83.4 %shard_map.309 = (f32[12,48,1536]{2,1,0:T(8,128)}, f32[8,7,1536]{2,1,0:T(8,128)S(1)}, bf16[2,192,1536]{2,1,0:T(8,128)(2,1)}, bf16[1,192,1536]{2,1,0:T(8,128)(2,1...) custom-call(f32[12,48,1536]{2,1,0:T(8,128)} %bitcast.136, ...), custom_call_target="tpu_custom_call" | custom-call | flops 60000002048 | bytes 100000000 | tf_op jit(solution)/shard_map/pallas_call | solution.py:1012
  728.2 0.8 slice.82
  728.9 0.8 reshape.184
  730.3 1.3 broadcast_in_dim_reshape.20
  732.2 1.3 broadcast_in_dim_reshape.21
  733.5 1.4 slice_reduce_fusion
  734.9 1.4 fusion.3
  736.3 1.1 bitcast_convert_fusion.1
  737.5 1.1 convert_bitcast_fusion
  738.6 1.4 bitcast_convert_fusion
  740.1 0.9 slice_bitcast_fusion.1
  741.6 1.0 slice_bitcast_fusion
  742.7 1.7 copy.74
  744.3 1.7 copy.75
  746.0 2.0 copy.76
  748.0 1.6 pad_maximum_fusion.2
  749.7 1.8 pad_maximum_fusion.1
  751.5 1.8 copy.103
  753.3 1.5 copy-done.4
  754.7 1.8 copy.104
  (87 shorter events, 8.2 us)
Async XLA Ops:
  7.2 9.5 %copy-start.11 = (s32[1,12,48]{2,0,1:T(1,128)S(1)}, s32[1,12,48]{2,0,1:T(1,128)}, u32[]{:S(2)}) copy-start(s32[1,12,48]{2,0,1:T(1,128)} %param.20) | copy-start | bytes 6916
  7.2 9.5 %copy-start.10 = (bf16[7,7,1536]{2,1,0:T(8,128)(2,1)S(1)}, bf16[7,7,1536]{2,1,0:T(8,128)(2,1)}, u32[]{:S(2)}) copy-start(bf16[7,7,1536]{2,1,0:T(8,128)(2,1)} %param.21) | copy-start | bytes 451588
  7.2 9.9 %copy-start.12 = (bf16[1536]{0:T(1024)(128)(2,1)S(1)}, bf16[1536]{0:T(1024)(128)(2,1)}, u32[]{:S(2)}) copy-start(bf16[1536]{0:T(1024)(128)(2,1)} %param.22) | copy-start | bytes 9220
  7.2 95.4 %all-gather.3.cloned.1.call-start = ((), (), s32[]{:S(2)}) async-start(), calls=%async_computation.1 | async-start | bytes 5242880 | tf_op jit(solution)/shard_map/all_gather | solution.py:1472
  15.6 1.0 copy-start.5
  16.6 279.2 %all-gather.5.cloned.1.call-start = ((), (), s32[]{:S(2)}) async-start(), calls=%async_computation.2 | async-start | bytes 37748736 | tf_op jit(solution)/shard_map/all_gather | solution.py:1485
  18.8 31.3 %copy-start.1 = (bf16[12,48,1536]{2,1,0:T(8,128)(2,1)}, bf16[12,48,1536]{2,1,0:T(8,128)(2,1)S(1)}, u32[]{:S(2)}) copy-start(bf16[12,48,1536]{2,1,0:T(8,128)(2,1)S(1)} %bitcast_multiply_fusion.x_ref.res) | copy-start | bytes 5308420
  49.2 1.5 copy-start.2
  49.2 2.7 copy-start
  53.7 50.0 %copy-start.8 = (bf16[1,144,1024]{2,1,0:T(8,128)(2,1)S(1)}, bf16[1,144,1024]{2,1,0:T(8,128)(2,1)}, u32[]{:S(2)}) copy-start(bf16[1,144,1024]{2,1,0:T(8,128)(2,1)} %param.19) | copy-start | bytes 884740
  53.7 52.1 %copy-start.9 = (bf16[1,144,1024]{2,1,0:T(8,128)(2,1)S(1)}, bf16[1,144,1024]{2,1,0:T(8,128)(2,1)}, u32[]{:S(2)}) copy-start(bf16[1,144,1024]{2,1,0:T(8,128)(2,1)} %param.34) | copy-start | bytes 884740
  102.6 4.4 copy-start.15
  102.6 5.0 copy-start.16
  102.6 636.0 %reduce-scatter.2.cloned.1.call-start = ((), (), s32[]{:S(2)}) async-start(), calls=%async_computation.3 | async-start | bytes 5242880 | tf_op jit(solution)/shard_map/reduce_scatter | solution.py:1514
  644.0 0.7 copy-start.14
  644.0 0.7 copy-start.13
  644.7 85.0 %copy-start.7 = (f32[144,1024]{1,0:T(8,128)S(1)}, f32[144,1024]{1,0:T(8,128)}, u32[]{:S(2)}) copy-start(f32[144,1024]{1,0:T(8,128)} %get-tuple-element.50) | copy-start | bytes 1769476
  728.2 3.4 copy-start.6
  740.1 11.4 %copy-start.3 = (f32[6,96,1536]{2,1,0:T(8,128)S(1)}, f32[6,96,1536]{2,1,0:T(8,128)}, u32[]{:S(2)}) copy-start(f32[6,96,1536]{2,1,0:T(8,128)} %get-tuple-element.51) | copy-start | bytes 10616836
  751.5 3.3 copy-start.4
Sparse Core Ops, SparseCore 0:
  16.7 85.8 all-gather.2
  104.5 159.9 all-gather.4
  644.2 89.6 reduce-scatter.1

commit v8 on v7

--- a/solution.py
+++ b/solution.py
@@ -455,7 +455,7 @@
 
     def kernel(
         cot_ref, pool_ref, share_ref, mask_ref, x_hbm, act_hbm, slopes, wu, wd, g_first, g_second,
-        out, d_own, g_up_out, g_down_out, got_up, got_down, h_all, *rest
+        out, d_own, g_up_out, g_down_out, out_up, out_down, got_up, got_down, h_all, *rest
     ):
         sums, extra, rest = rest[0], rest[1 : 1 + 2 * each], rest[1 + 2 * each :]
         gathered, partial, travel, slope, grad, left, right, middle, g_up, g_down, total, spread_rows = rest[:12]
@@ -578,32 +578,60 @@
 
             @pl.when(g == 2 * items + 2)
             def _():
-                give(g_up, left, g_up_out, stored.at[2])
+                give(g_up, left, out_up, stored.at[2])
                 swaps[0].start()
 
             @pl.when(g == 2 * items + 3)
             def _():
-                give(g_down, right, g_down_out, stored.at[3])
+                give(g_down, right, out_down, stored.at[3])
                 swaps[1].start()
 
         core = dp_bit(0)
+
+        def rows_at(i):
+            return pl.ds(pl.multiple_of(i * piece, piece), piece)
 
         def give(source, stage, target, sem):
             def one(i, _):
-                stage[pl.ds(0, piece)] = source[pl.ds(pl.multiple_of(i * piece, piece), piece)].astype(BF)
-                copy = pltpu.make_async_copy(stage.at[pl.ds(0, piece)], target.at[i // 2, lax.rem(i, 2)], sem)
+                stage[pl.ds(0, piece)] = source[rows_at(2 * i + 1 - core)].astype(BF)
+                copy = pltpu.make_async_copy(stage.at[pl.ds(0, piece)], target.at[i], sem)
                 copy.start()
                 copy.wait()
                 return 0
 
-            lax.fori_loop(0, devices, one, 0)
+            lax.fori_loop(0, devices // 2, one, 0)
+
+        def keep_sums():
+            sets = ((g_up, left, got_up, g_up_out, 2), (g_down, right, got_down, g_down_out, 3))
+
+            def loads(i):
+                return [
+                    pltpu.make_async_copy(got.at[i], stage.at[pl.ds(0, piece)], stored.at[sem])
+                    for _, stage, got, _, sem in sets
+                ]
+
+            def one(i, _):
+                for load in loads(i):
+                    load.start()
+                saves = []
+                for load, (source, stage, _, target, sem) in zip(loads(i), sets):
+                    load.wait()
+                    here = stage.at[pl.ds(0, piece)]
+                    here[...] = (source[rows_at(2 * i + core)] + here[...].astype(F32)).astype(BF)
+                    saves.append(pltpu.make_async_copy(here, target.at[i], stored.at[sem]))
+                    saves[-1].start()
+                for save in saves:
+                    save.wait()
+                return 0
+
+            lax.fori_loop(0, devices // 2, one, 0)
 
         swaps = [
             pltpu.make_async_remote_copy(
-                src_ref=src.at[:, 1 - core], dst_ref=dst, send_sem=core_send.at[i], recv_sem=core_recv.at[i],
+                src_ref=src, dst_ref=dst, send_sem=core_send.at[i], recv_sem=core_recv.at[i],
                 device_id={"dp": dp_mate(0)}, device_id_type=MESH,
             )
-            for i, (src, dst) in enumerate(((g_up_out, got_up), (g_down_out, got_down)))
+            for i, (src, dst) in enumerate(((out_up, got_up), (out_down, got_down)))
         ]
         def clear(i, _):
             some = pl.ds(pl.multiple_of(i * TILE, TILE), TILE)
@@ -640,25 +668,23 @@
             pass_on(steps - 1, plan)
         for swap in swaps:
             swap.wait()
+        keep_sums()
 
     whole = pl.BlockSpec(memory_space=pl.ANY)
     local = pl.BlockSpec(memory_space=pltpu.VMEM)
     dma = pltpu.SemaphoreType.DMA
-    out, d_own, g_up, g_down, got_up, got_down, _, sums, *_ = pl.pallas_call(
+    out, d_own, g_up, g_down, _, _, _, _, _, sums, *_ = pl.pallas_call(
         kernel,
         out_shape=(
             jax.ShapeDtypeStruct((CHUNKS, rows, c), F32),
             jax.ShapeDtypeStruct((CHUNKS, rows, c), BF),
-            jax.ShapeDtypeStruct((devices // 2, 2, piece, h), BF),
-            jax.ShapeDtypeStruct((devices // 2, 2, piece, h), BF),
-            jax.ShapeDtypeStruct((devices // 2, piece, h), BF),
-            jax.ShapeDtypeStruct((devices // 2, piece, h), BF),
+            *[jax.ShapeDtypeStruct((devices // 2, piece, h), BF)] * 6,
             jax.ShapeDtypeStruct((n, CHUNKS // 2, 2 * rows, h), BF),
             jax.ShapeDtypeStruct((2, 1, 1, split, g_cols), BF),
             *extras,
         ),
         in_specs=[local] * 4 + [whole] * 3 + [local] * 2 + [whole] * 2,
-        out_specs=(whole,) * (8 + 2 * each),
+        out_specs=(whole,) * (10 + 2 * each),
         scratch_shapes=chunk_buffers(n, rows, c, BF)
         + [
             pltpu.VMEM((rows, h), BF), pltpu.VMEM((rows, h), BF),
@@ -682,7 +708,7 @@
         grads.reshape(pairs // 2, 2, g_rows, g_cols), grads.reshape(2, pairs // 2, g_rows, g_cols),
     )
     return (
-        out.reshape(cot.shape), d_own.reshape(cot.shape), [(g_up, got_up), (g_down, got_down)],
+        out.reshape(cot.shape), d_own.reshape(cot.shape), [g_up, g_down],
         sums.reshape(g_rows, g_cols),
     )
 
@@ -812,25 +838,27 @@
     reach = size // 2
     high = rows + 2 * reach
     group = 4 if rows % 4 == 0 else 1
-    steps = devices.bit_length() - 1
-    shape = (devices,) + grads[0][0].shape[2:]
-    plans = [Halving(range(steps), [True] + [last] * (steps - 1), shape, shape[2]) for last in (True, False)]
-    each = 2 * steps - 1
+    bits = range(1, devices.bit_length() - 1)
+    steps = len(bits)
+    shape = grads[0].shape
+    plans = [Halving(bits, [last] * steps, shape, shape[2]) for last in (True, False)]
+    each = 2 * steps
     blocks = c // LANES
     taps = size * size
     count = taps + 1 + low_gains.shape[0]
     small = -(-count // devices)
-    halving = {2 * blocks * 2 * p // (3 * max(steps - 2, 1)): p for p in range(1, steps - 1)}
-    rounds = {blocks + blocks // 3: 1, blocks + 2 * blocks // 3: 2}
+    first_due = blocks + blocks // 3
+    halving = {first_due + 2 * blocks // 3 * p // (steps - 1): p for p in range(steps - 1)}
+    rounds = {blocks + 7 * blocks // 12: 1, blocks + 10 * blocks // 12: 2}
 
     def kernel(
-        dn, co, gain_ref, mask_ref, w_ref, low_ref, b_hbm, dm_hbm, g0, got0, g1, got1, out, g_all, *rest
+        dn, co, gain_ref, mask_ref, w_ref, low_ref, b_hbm, dm_hbm, g0, g1, out, g_all, *rest
     ):
         extra, rest = rest[: 2 * each], rest[2 * each :]
         around, x_around, d_here, dframed, xframed, g_own, here, level, sent, got, own = rest[:11]
         ar, halving_sems = rest[11:17], rest[17:]
-        plans[0].bind(g0, (got0,) + extra[:each], halving_sems[0], halving_sems[1])
-        plans[1].bind(g1, (got1,) + extra[each:], halving_sems[2], halving_sems[3])
+        plans[0].bind(g0, extra[:each], halving_sems[0], halving_sems[1])
+        plans[1].bind(g1, extra[each:], halving_sems[2], halving_sems[3])
         me, d = lax.axis_index("dp"), lax.axis_index("mp")
         has_up, has_down = d > 0, d < n - 1
         barrier = pltpu.get_barrier_semaphore()
@@ -851,16 +879,19 @@
 
         def pass_on(p):
             for plan in plans:
-                plan.finish(p, p > 0)
-                if p + 1 < steps:
+                plan.finish(p)
+            if p == 0:
+                sum_round(0)
+            if p + 1 < steps:
+                for plan in plans:
                     plan.start(p + 1)
 
         def keep(row, lanes, value):
             g_own[row // small, row % small : row % small + 1, lanes] = value
 
         pl.semaphore_wait(barrier, devices + n - 2)
-        pass_on(0)
-
+        for plan in plans:
+            plan.start(0)
         g_own[...] = jnp.zeros(g_own.shape, F32)
 
         def norm(r, total):
@@ -983,7 +1014,6 @@
             if mark in halving:
                 pass_on(halving[mark])
             if mark == blocks:
-                sum_round(0)
                 load_d.wait()
 
                 @pl.when(has_up)
@@ -1014,10 +1044,10 @@
         out_shape=(
             jax.ShapeDtypeStruct((rows, cols, c), F32),
             jax.ShapeDtypeStruct((devices, small, c), F32),
-            *plans[0].buffers()[1:],
-            *plans[1].buffers()[1:],
+            *plans[0].buffers(),
+            *plans[1].buffers(),
         ),
-        in_specs=[local] * 6 + [whole] * 6,
+        in_specs=[local] * 6 + [whole] * 4,
         out_specs=(local,) * 2 + (whole,) * (2 * each),
         scratch_shapes=[
             vm((high, cols, c), BF), vm((high, cols, c), BF), vm((rows, cols, c), BF),
@@ -1031,7 +1061,10 @@
             collective_id=3, has_side_effects=True, vmem_limit_bytes=50 * MIB
         ),
         cost_estimate=pl.CostEstimate(flops=6 * 10**10, bytes_accessed=10**8, transcendentals=0),
-    )(d_normed, conv_out, gain, mask, w, low_gains, bordered, d_map, *grads[0], *grads[1])
+    )(
+        d_normed, conv_out, gain, mask, w, low_gains, bordered, d_map,
+        grads[0].reshape((shape[0] // 2, 2) + shape[1:]), grads[1].reshape((2, shape[0] // 2) + shape[1:]),
+    )
     sums = g_all.reshape(devices * small, c)[:count]
     return d_in, sums, [extra[each - 1].reshape(shape[1:]), extra[2 * each - 1].reshape(shape[1:])]
 
@@ -1083,7 +1116,7 @@
         low_ref, pool_a_ref, pool_b_ref, cot_ref, gain1_ref, gain2_ref, w_hbm,
         low_out, d_low, d_pool_a, d_pool_b, g_ln1, g_ln2, grads,
         wv, lhs, lhs2, rhs, gate, high, merged, resid, d_res, slope, mixed, heads_in, att_all, d_att, d_mixed,
-        d_heads, probs, d_scores, stage, w_sem, q_send, q_got, a_send, a_got, b_send, b_got, c_send, c_got, own_sem,
+        d_heads, probs, d_scores, stage, left, w_sem, q_send, q_got, a_send, a_got, b_send, b_got, c_send, c_got, own_sem,
         l_send, l_got, r_send, r_got, stage_sem,
     ):
         d = lax.axis_index("mp")
@@ -1166,11 +1199,23 @@
                 send_sem=l_send.at[i], recv_sem=l_got.at[i], device_id={"dp": mate}, device_id_type=MESH)
 
         stored = []
+        turned = [None]
+
+        def put_natural(dst, value):
+            if rows % LANES:
+                dst[...] = value
+            else:
+                for k in range(devices):
+                    at = (k % 2) * half + k // 2 * rows
+                    dst[:, k * rows : (k + 1) * rows] = value[:, at : at + rows]
 
         def grad(i, block, at, count, shared=False):
             if not shared:
                 r_copy(block).wait_recv()
-            own_l = pl.ds(pl.multiple_of(core * half, half), half)
+            if turned[0] != i:
+                left[0] = lhs[i, :, pl.ds(pl.multiple_of(core * half, half), half)].T
+                left[1] = lhs2[i].T
+                turned[0] = i
 
             wide, base, first = w_place(at if at < 8 else 8 + (at - 8) * dim // ff)
             piece = min(TILE, wide)
@@ -1193,7 +1238,7 @@
                 if len(stored) >= 2:
                     wait(stored[-2])
                 cols = pl.ds(r_at(block) + k * TILE, TILE)
-                y = tn(lhs[i, :, own_l], rhs[0, :, cols]) + tn(lhs2[i], rhs[1, :, cols])
+                y = nn(left[0], rhs[0, :, cols]) + nn(left[1], rhs[1, :, cols])
                 stage[slot] = y.astype(BF).reshape(pairs, rows, TILE)
                 stored.append(out_copies(slot, k))
                 start(stored[-1])
@@ -1302,7 +1347,7 @@
         r_copy(R_ACT).start()
         w_wait(9)
         backward(lambda at: rhs[0, :, pl.ds(r_at(R_ACT) + at, dim)], 12, 4, acc, True)
-        low_out[...] = resid[...] + acc[...]
+        put_natural(low_out, resid[...] + acc[...])
 
         def put_d_up(at, y):
             rhs[0, :, pl.ds(r_at(R_DUP) + at, TILE)] = (y * slope[:, pl.ds(at, TILE)].astype(F32)).astype(BF)
@@ -1368,7 +1413,7 @@
         backward(lambda at: rhs[0, :, r_cols(R_DHIGH)], HIGH_A, 1, d_pool_a, True)
         backward(lambda at: rhs[0, :, r_cols(R_DHIGH)], HIGH_B, 1, d_pool_b, True)
         backward(lambda at: rhs[0, :, r_cols(R_DGATE)], GATE, 1, acc, True)
-        d_low[...] = d_res[...] + acc[...]
+        put_natural(d_low, d_res[...] + acc[...])
         l_copy(L_FIRST).wait_recv()
         for k in range(3):
             grad(L_FIRST, R_DQ + k, QUERY + k, 1)
@@ -1402,13 +1447,90 @@
             vm((t, dim), F32), vm((t, dim), F32), vm((t, dim), F32), vm((t, dim), F32), vm((t, dim), F32),
             vm((t, ff), BF), vm((3, t, dim), BF), vm((3, every, width), BF), vm((every, width), BF), vm((every, width), BF),
             vm((1, 8, 128), BF), vm((3, every, width), BF), vm((heads, every, every), BF), vm((every, every), BF),
-            vm((2, pairs, rows, TILE), BF),
+            vm((2, pairs, rows, TILE), BF), vm((2, half, t), BF),
             dma((10, 2 * n)), dma((3, n)), dma((3, n)), dma((1, n)), dma((1, n)), dma((1, n)), dma((1, n)), dma((3, n)), dma((3, n)),
             dma((3,)), dma((8,)), dma((8,)), dma((9,)), dma((9,)), dma((2, 2)),
         ],
-        compiler_params=pltpu.CompilerParams(collective_id=cid, has_side_effects=True, vmem_limit_bytes=61 * MIB),
+        compiler_params=pltpu.CompilerParams(collective_id=cid, has_side_effects=True, vmem_limit_bytes=62 * MIB),
         cost_estimate=pl.CostEstimate(flops=14 * 10**9, bytes_accessed=70 * 10**6, transcendentals=10**7),
     )(low, pool_a, pool_b, cot, gain1, gain2, packed.reshape(pairs, 2, n, rows, 16 * width))
+def weight_outputs(own, g_cn_up, g_cn_down, widths, high_rows):
+    share = own.shape[0]
+    width, wide = widths[0], widths[-1]
+    piece, h = g_cn_up.shape
+
+    def kernel(x, cn_up, cn_down, gate, high, out, qkv, proj, up, down, o_cn_up, o_cn_down):
+        def part(i, size=width):
+            at = sum(widths[:i])
+            return x[:, at : at + size].astype(F32)
+
+        gate[...] = part(0)
+        out[...] = part(1).T
+        high[:share] = part(2)
+        high[share:] = part(3)[: high_rows - share]
+        for k in range(3):
+            qkv[k] = part(4 + k)
+        proj[...] = part(7).T
+        up[...] = part(8, wide)
+        down[...] = part(9, wide).T
+        o_cn_up[...] = cn_up[...].astype(F32)
+        o_cn_down[...] = cn_down[...].astype(F32).T
+
+    local = pl.BlockSpec(memory_space=pltpu.VMEM)
+    shapes = [
+        (share, width), (high_rows, width), (width, share), (3, share, width), (width, share), (share, wide),
+        (wide, share), (piece, h), (h, piece),
+    ]
+    return pl.pallas_call(
+        kernel,
+        out_shape=[jax.ShapeDtypeStruct(s, F32) for s in shapes],
+        in_specs=[local] * 3,
+        out_specs=[local] * 9,
+        compiler_params=pltpu.CompilerParams(vmem_limit_bytes=32 * MIB),
+    )(own, g_cn_up, g_cn_down)
+
+
+def pack_weights(ad_gate, ad_out, ad_high, w_qkv, w_proj, w_up, w_down, devices):
+    dim, width = ad_gate.shape
+    share, high_rows, wide = dim // devices, ad_high.shape[0] // devices, w_up.shape[1]
+    rest = high_rows - share
+
+    def kernel(gate, out, high, qkv, proj, up, down, packed, side, side_wide, sems):
+        me = lax.axis_index("dp")
+        mine = pl.ds(pl.multiple_of(me * share, share), share)
+        lanes = mine
+
+        def at(i, size=width):
+            return packed.at[:, pl.ds(i * width, size)]
+
+        straight = [(gate.at[mine], at(0)), (up.at[mine], at(8, wide))]
+        straight += [(qkv.at[k, mine], at(4 + k)) for k in range(3)]
+        straight.append((high.at[pl.ds(pl.multiple_of(me * high_rows, rest), share)], at(2)))
+        straight.append((high.at[pl.ds(pl.multiple_of(me * high_rows + share, rest), rest)], at(3).at[pl.ds(0, rest)]))
+        straight += [(out.at[:, lanes], side.at[0]), (proj.at[:, lanes], side.at[1]), (down.at[:, lanes], side_wide)]
+        copies = [pltpu.make_async_copy(a, b, sems.at[i]) for i, (a, b) in enumerate(straight)]
+        for copy in copies:
+            copy.start()
+        packed[rest:, 3 * width : 4 * width] = jnp.zeros((share - rest, width), BF)
+        for copy in copies:
+            copy.wait()
+        packed[:, width : 2 * width] = side[0].T
+        packed[:, 7 * width : 8 * width] = side[1].T
+        packed[:, 8 * width + wide :] = side_wide[...].T
+
+    whole = pl.BlockSpec(memory_space=pl.ANY)
+    return pl.pallas_call(
+        kernel,
+        out_shape=jax.ShapeDtypeStruct((share, 8 * width + 2 * wide), BF),
+        in_specs=[whole] * 7,
+        out_specs=pl.BlockSpec(memory_space=pltpu.VMEM),
+        scratch_shapes=[
+            pltpu.VMEM((2, width, share), BF), pltpu.VMEM((wide, share), BF), pltpu.SemaphoreType.DMA((10,)),
+        ],
+        compiler_params=pltpu.CompilerParams(vmem_limit_bytes=16 * MIB),
+    )(ad_gate, ad_out, ad_high, w_qkv, w_proj, w_up, w_down)
+
+
 def rows_first(x):
     return with_layout_constraint(x, Layout(major_to_minor=tuple(range(x.ndim))))
 
@@ -1464,11 +1586,15 @@
     dims = low_in.shape[2]
     share = dims // devices
     qkv = own_part(w_qkv, 1)
+    low_weights = (ad_gate, ad_out, ad_high, w_qkv, w_proj, w_up, w_down)
     pieces = [
         own_part(ad_gate, 0), own_part(ad_out, 1).T, *fold(own_part(ad_high, 0), share),
         qkv[0], qkv[1], qkv[2], own_part(w_proj, 1).T, own_part(w_up, 0), own_part(w_down, 1).T,
     ]
-    packed = rows_first(jnp.concatenate(pieces, axis=1))
+    if share % LANES:
+        packed = rows_first(jnp.concatenate(pieces, axis=1))
+    else:
+        packed = pack_weights(*low_weights, devices)
     packed = rows_first(lax.all_gather(packed, "mp", axis=0, tiled=True))
     plane_mask = valid[0].astype(F32)
     cell_mask = plane_mask[..., None]
@@ -1496,8 +1622,9 @@
         *(core_first(v.astype(F32), devices)[None] for v in (ln1_gain, ln2_gain)),
         packed, shards, devices, 2,
     )
-    low_out = core_last(low_out, devices)[None]
-    d_low_in = core_last(d_low_in, devices)[None]
+    if share % LANES:
+        low_out, d_low_in = core_last(low_out, devices), core_last(d_low_in, devices)
+    low_out, d_low_in = low_out[None], d_low_in[None]
     g_ln1, g_ln2 = core_last(g_ln1[0], devices), core_last(g_ln2[0], devices)
     d_pooled = jnp.concatenate(
         [
@@ -1517,18 +1644,11 @@
         d_normed, conv_out, hr_gainf[None], cell_mask, bordered, d_map, taps, low_gains, size, cn_grads, devices, shards
     )
     d_hr_in = d_hr_in[None]
-    g_cn_up, g_cn_down = g_cn_up.astype(F32), g_cn_down.astype(F32).T
     g_conv = small_sums[: size * size].reshape(conv_w.shape)
     g_hr_gain, g_ln1, g_ln2 = small_sums[size * size], small_sums[-2, :dims], small_sums[-1, :dims]
-    own = low_sums.astype(F32)
-    split, at = [], 0
-    for p in pieces:
-        split.append(own[:, at : at + p.shape[1]])
-        at += p.shape[1]
-    g_ad_gate, g_ad_out, g_high_a, g_high_b, g_query, g_key, g_value, g_proj, g_up, g_down = split
-    g_ad_high = jnp.concatenate([g_high_a, g_high_b[: ad_high.shape[0] // devices - share]], axis=0)
-    g_qkv = jnp.stack([g_query, g_key, g_value])
-    g_ad_out, g_proj, g_down = g_ad_out.T, g_proj.T, g_down.T
+    g_ad_gate, g_ad_high, g_ad_out, g_qkv, g_proj, g_up, g_down, g_cn_up, g_cn_down = weight_outputs(
+        low_sums.reshape(share, -1), g_cn_up, g_cn_down, [p.shape[1] for p in pieces], ad_high.shape[0] // devices
+    )
     return (
         low_out,
         hr_out,

time: 770 us -> 762 us (0.990)
  waiting for transfers between devices: 48.9 us -> 57.6 us
  local copies, waits for them, and re-layouts: 46.9 us -> 38.7 us
    reduce_scatter x1, waiting for transfers between devices: 0.01 us -> 8.63 us  [per_device(): low_sums = rows_first(lax.psum_scatter(low_sums, 'mp', scatter_dimension=0))]
    unnamed x55 -> x53, local copies, waits for them, and re-layouts: 19.2 us -> 22.5 us
  transfers between devices with their start and end apart: 3 -> 3, of which waited for: 1 -> 2; matrix products, arithmetic and copies ran while one was open for 3% -> 2% of each run, Pallas kernels for 39% -> 39%
where the time goes in v8:
time: 762 us; the launch traced here: 756 us
  Pallas kernels  640 us (84%)
  waiting for transfers between devices  57.6 us (8%)
  local copies, waits for them, and re-layouts  38.7 us (5%)
  between operations  14.3 us (2%)
    pallas_call x1, Pallas kernels, big_backward(): pl.pallas_call(kernel, out_shape=(jax.ShapeDtypeStruct((CHUNKS, rows, c),...  233 us
    pallas_call x1, Pallas kernels, big_forward(): pl.pallas_call(kernel, out_shape=(jax.ShapeDtypeStruct((CHUNKS, rows, c),...  184 us
    pallas_call x1, Pallas kernels, low_stage(): pl.pallas_call(kernel, out_shape=(tok, tok, tok, tok, one, one, jax.Shape...  112 us
    pallas_call x1, Pallas kernels, conv_backward(): pl.pallas_call(kernel, out_shape=(jax.ShapeDtypeStruct((rows, cols, c), F...  78.1 us
    all_gather x1, waiting for transfers between devices, per_device(): packed = rows_first(lax.all_gather(packed, 'mp', axis=0, tiled=True))  48.9 us
    pallas_call x1, Pallas kernels, conv_forward(): pl.pallas_call(kernel, out_shape=(jax.ShapeDtypeStruct((rows, cols, c), F...  30.3 us
    unnamed x53, local copies, waits for them, and re-layouts  22.5 us
  transfers between devices with their start and end apart: 3, of which 2 were waited for; matrix products, arithmetic and copies ran while one was open for 2% of the time, Pallas kernels for 39%

profile of v8, /device:TPU:0, one launch (start us, length us, event | category | flops | bytes accessed | tf_op | source)
XLA Modules:
  0.0 755.7 jit_solution(3895706399263613245)
XLA Ops:
  7.2 1.6 copy-done.2
  8.8 1.6 copy-done.3
  10.4 1.4 copy-done.4
  11.8 1.1 copy-done.6
  13.0 1.0 copy-done.7
  14.0 1.0 copy-done.8
  15.1 1.0 copy-done.9
  16.1 1.4 shard_map.306
  17.6 0.4 reshape.188.w_ref
  18.1 1.7 bitcast_multiply_fusion.x_ref.res
  19.8 30.3 %shard_map.305 = (f32[12,48,1536]{2,1,0:T(8,128)S(1)}, bf16[18,48,1536]{2,1,0:T(8,128)(2,1)S(1)}) custom-call(bf16[12,48,1536]{2,1,0:T(8,128)(2,1)S(1)} %bitcast_multiply_fusion.x_ref.res, f32[49,1,1536]{2,1,0:T(1,128)S(1)} %reshape.188.w_ref), custom_call_target="tpu_custom_call" | custom-call | tf_op jit(solution)/shard_map/pallas_call | solution.py:821
  50.1 0.4 multiply_reduce_fusion.1
  50.5 0.6 multiply_reduce_fusion
  51.1 0.5 copy-done.10
  51.6 1.2 copy-done
  52.8 1.8 multiply_convert_fusion
  54.6 48.9 %all-gather.3.cloned.1.call-done = bf16[512,4096]{1,0:T(8,128)(2,1)} async-done(((bf16[128,4096]{1,0:T(8,128)(2,1)}), bf16[512,4096]{1,0:T(8,128)(2,1)}) %all-gather.3.cloned.1.call-update) | async-done | bytes 4194320 | tf_op jit(solution)/shard_map/all_gather | solution.py:1598
  103.6 0.9 convert_element_type.67.mask_ref
  104.6 0.2 reshape_squeeze.12
  104.9 0.9 reshape.166.low_ref
  105.9 0.8 copy.47.share_ref
  107.0 0.9 reshape.171.cot_ref
  107.9 0.6 copy.53
  108.5 0.6 copy.54
  109.1 183.8 %shard_map.307 = (f32[6,96,1536]{2,1,0:T(8,128)}, bf16[6,24,1536]{2,1,0:T(8,128)(2,1)}, bf16[4,6,96,1536]{3,2,1,0:T(8,128)(2,1)}, bf16[4,6,96,1536]{3,2,1,0:T(8,...) custom-call(bf16[6,96,1536]{2,1,0:T(8,128)(2,1)} %bitcast.77, ...), custom_call_target="tpu_custom_call" | custom-call | flops 21743271936 | bytes 28311552 | tf_op jit(solution)/shard_map/pallas_call | solution.py:400
  292.9 1.5 reshape_reshape.28
  294.7 0.9 reshape.169.pool_a_ref
  295.9 0.9 reshape.170.pool_b_ref
  296.8 111.6 %shard_map.308 = (f32[144,1024]{1,0:T(8,128)}, f32[144,1024]{1,0:T(8,128)}, f32[144,1024]{1,0:T(8,128)}, f32[144,1024]{1,0:T(8,128)}, f32[1,1024]{1,0:T(1,128)},...) custom-call(bf16[144,1024]{1,0:T(8,128)(2,1)} %reshape.166.low_ref, bf16[144,1024]{1,0:T(8,128)(2,1)} %reshape.169.pool_a_ref, ...), custom_call_target="tpu_custom_call" | custom-call | flops 14000000000 | bytes 70000000 | tf_op jit(solution)/shard_map/pallas_call | solution.py:1440
  408.4 1.3 reshape.176
  409.7 0.3 copy.56
  410.1 1.3 reshape.175
  411.4 0.3 copy.55
  411.8 1.3 reshape_reshape.34.pool_ref
  413.1 233.0 %shard_map.309 = (f32[6,96,1536]{2,1,0:T(8,128)}, bf16[6,96,1536]{2,1,0:T(8,128)(2,1)}, bf16[4,192,1536]{2,1,0:T(8,128)(2,1)}, bf16[4,192,1536]{2,1,0:T(8,128)(2...) custom-call(bf16[12,48,1536]{2,1,0:T(8,128)(2,1)} %bitcast.99, ...), custom_call_target="tpu_custom_call" | custom-call | flops 43486543872 | bytes 28311552 | tf_op jit(solution)/shard_map/pallas_call | solution.py:676
  646.3 0.4 copy-done.19
  646.8 78.1 %shard_map.310 = (f32[12,48,1536]{2,1,0:T(8,128)}, f32[8,7,1536]{2,1,0:T(8,128)S(1)}, bf16[2,192,1536]{2,1,0:T(8,128)(2,1)}, bf16[1,192,1536]{2,1,0:T(8,128)(2,1...) custom-call(f32[12,48,1536]{2,1,0:T(8,128)} %bitcast.104, ...), custom_call_target="tpu_custom_call" | custom-call | flops 60000002048 | bytes 100000000 | tf_op jit(solution)/shard_map/pallas_call | solution.py:1042
  724.9 0.8 slice.30
  725.7 0.6 slice_reduce_fusion
  726.3 0.6 fusion
  726.9 8.6 %reduce-scatter.2.cloned.1.call-done = bf16[1,128,4096]{2,1,0:T(8,128)(2,1)} async-done(((bf16[4,128,4096]{2,1,0:T(8,128)(2,1)}), bf16[1,128,4096]{2,1,0:T(8,128)(2,1)}) %reduce-scatter.2.cloned.1.call-update) | async-done | bytes 1048592 | tf_op jit(solution)/shard_map/reduce_scatter | solution.py:1641
  735.6 1.2 copy-done.5
  736.8 2.0 shard_map.311
  738.8 1.5 copy.62
  740.3 1.9 copy.79
  742.2 4.2 copy.80
  746.4 0.8 copy.81
  747.2 1.8 copy.82
  (69 shorter events, 1.7 us)
Async XLA Ops:
  7.2 96.3 %all-gather.3.cloned.1.call-start = ((), (), s32[]{:S(2)}) async-start(), calls=%async_computation.1 | async-start | bytes 5242880 | tf_op jit(solution)/shard_map/all_gather | solution.py:1598
  7.2 1.6 copy-start.2
  8.8 1.6 copy-start.3
  10.4 1.4 copy-start.4
  11.8 1.1 copy-start.6
  13.0 1.0 copy-start.7
  14.0 1.0 copy-start.8
  15.0 1.0 copy-start.9
  16.1 1.5 copy-start.16
  16.1 1.5 copy-start.15
  16.1 2.0 copy-start.17
  17.5 279.3 %all-gather.5.cloned.1.call-start = ((), (), s32[]{:S(2)}) async-start(), calls=%async_computation.2 | async-start | bytes 37748736 | tf_op jit(solution)/shard_map/all_gather | solution.py:1611
  19.8 31.3 %copy-start.1 = (bf16[12,48,1536]{2,1,0:T(8,128)(2,1)}, bf16[12,48,1536]{2,1,0:T(8,128)(2,1)S(1)}, u32[]{:S(2)}) copy-start(bf16[12,48,1536]{2,1,0:T(8,128)(2,1)S(1)} %bitcast_multiply_fusion.x_ref.res) | copy-start | bytes 5308420
  50.1 1.5 copy-start.10
  50.1 2.7 copy-start
  54.6 50.0 %copy-start.13 = (bf16[1,144,1024]{2,1,0:T(8,128)(2,1)S(1)}, bf16[1,144,1024]{2,1,0:T(8,128)(2,1)}, u32[]{:S(2)}) copy-start(bf16[1,144,1024]{2,1,0:T(8,128)(2,1)} %param.19) | copy-start | bytes 884740
  54.6 52.1 %copy-start.14 = (bf16[1,144,1024]{2,1,0:T(8,128)(2,1)S(1)}, bf16[1,144,1024]{2,1,0:T(8,128)(2,1)}, u32[]{:S(2)}) copy-start(bf16[1,144,1024]{2,1,0:T(8,128)(2,1)} %param.34) | copy-start | bytes 884740
  103.5 4.4 copy-start.20
  103.5 5.0 copy-start.21
  103.5 632.0 %reduce-scatter.2.cloned.1.call-start = ((), (), s32[]{:S(2)}) async-start(), calls=%async_computation.3 | async-start | bytes 5242880 | tf_op jit(solution)/shard_map/reduce_scatter | solution.py:1641
  646.1 0.7 copy-start.19
  646.1 0.7 copy-start.18
  735.6 1.2 copy-start.5
  742.2 4.2 copy-start.12
  742.2 5.0 copy-start.11
Sparse Core Ops, SparseCore 0:
  17.6 85.8 all-gather.2
  105.4 159.8 all-gather.4
  646.3 89.2 reduce-scatter.1

commit v9 on v8

--- a/solution.py
+++ b/solution.py
@@ -363,7 +363,26 @@
             keep_act.wait()
             keep_slope.wait()
 
+        def finish(j):
+            pl.when(j > 0)(lambda: put(j - 1).wait())
+            own_sum(n, d, j, partial, travel, total)
+            values = (res[pl.ds(j * 2 * pairs, 2 * pairs)].reshape(rows, c).astype(F32) + total[...]) * mask_ref[j]
+            partial[d, j] = values
+            put(j).start()
+            both = values.reshape(pairs, 2, cols, c)
+            summed = (both[:, 0] + both[:, 1]).reshape(pairs * cols, c)
+            for b in range(c // LANES):
+                lanes = slice(b * LANES, (b + 1) * LANES)
+                folded[b] = summed[:, lanes]
+                every = folded[b, pl.ds(0, pairs * half, 2), :] + folded[b, pl.ds(1, pairs * half, 2), :]
+                pooled[j, :, lanes] = (every * share_ref[j]).astype(BF)
+
+        def put(j):
+            return pltpu.make_async_copy(partial.at[d, j], out.at[j], load_sem)
+
         def after(g):
+            last = g - (n - 1) * (CHUNKS + 1)
+            pl.when(last >= 0)(lambda: finish(last))
             for i, (w, target, size) in enumerate(((wu, wu_t, h), (wd, wd_t, c))):
                 @pl.when(g < size // LANES)
                 def _():
@@ -377,22 +396,7 @@
             n, CHUNKS, 1, gathered, partial, travel, sems, own_chunk, prepare, arrived, compute, after=after
         )
 
-        def finish(j, _):
-            own_sum(n, d, j, partial, travel, total)
-            values = (res[pl.ds(j * 2 * pairs, 2 * pairs)].reshape(rows, c).astype(F32) + total[...]) * mask_ref[j]
-            partial[d, j] = values
-            pltpu.make_async_copy(partial.at[d, j], out.at[j], stored.at[0]).start()
-            both = values.reshape(pairs, 2, cols, c)
-            summed = (both[:, 0] + both[:, 1]).reshape(pairs * cols, c)
-            for b in range(c // LANES):
-                lanes = slice(b * LANES, (b + 1) * LANES)
-                folded[b] = summed[:, lanes]
-                every = folded[b, pl.ds(0, pairs * half, 2), :] + folded[b, pl.ds(1, pairs * half, 2), :]
-                pooled[j, :, lanes] = (every * share_ref[j]).astype(BF)
-            pltpu.make_async_copy(partial.at[d, j], out.at[j], stored.at[0]).wait()
-            return 0
-
-        lax.fori_loop(0, CHUNKS, finish, 0)
+        put(CHUNKS - 1).wait()
         drain_copies(n, x_copy)
 
     whole = pl.BlockSpec(memory_space=pl.ANY)
@@ -458,9 +462,9 @@
         out, d_own, g_up_out, g_down_out, out_up, out_down, got_up, got_down, h_all, *rest
     ):
         sums, extra, rest = rest[0], rest[1 : 1 + 2 * each], rest[1 + 2 * each :]
-        gathered, partial, travel, slope, grad, left, right, middle, g_up, g_down, total, spread_rows = rest[:12]
-        core_send, core_recv, stored, send0, recv0, send1, recv1 = rest[12:19]
-        sems = rest[19:]
+        gathered, partial, travel, slope, grad, left, right, middle, g_up, g_down, total, spread_rows, addend = rest[:13]
+        core_send, core_recv, stored, add_sem, send0, recv0, send1, recv1 = rest[13:21]
+        sems = rest[21:]
         d = lax.axis_index("mp")
         plans[0].bind(g_first.at[:, :, pl.ds(0, split)], extra[:each] + (sums.at[0],), send0, recv0)
         plans[1].bind(g_second.at[:, :, pl.ds(split, split)], extra[each:] + (sums.at[1],), send1, recv1)
@@ -474,13 +478,61 @@
             if p + 1 < steps:
                 plan.start(p + 1)
 
+        first_due = 2 * CHUNKS + 3
+        ticks = {}
+        if steps == 2:
+            for p, start in ((0, first_due), (1, n * CHUNKS + n - 2)):
+                tiles = [
+                    (plan, k, q)
+                    for plan in plans
+                    for k in range(plan.got[p].shape[0])
+                    for q in range(g_cols // plan.block)
+                ]
+                for m in range(0, len(tiles), 4):
+                    ticks[start + m // 4] = (p, m == 0, m + 4 >= len(tiles), tiles[m : m + 4])
+
+        def tile_copy(which, p, i, plan, k, q):
+            lanes = pl.ds(q * plan.block, plan.block)
+            if which == 0:
+                source, target = plan.part(p, True).at[k, :, lanes], addend.at[0, i]
+            elif which == 1:
+                source, target = plan.got[p].at[k, :, lanes], addend.at[1, i]
+            else:
+                ways = plan.split(plan.got[p].shape[0], p + 1)
+                source, target = addend.at[0, i], plan.now[p + 1].at[k // ways[1], k % ways[1], :, lanes]
+            return pltpu.make_async_copy(source, target, add_sem.at[which, i])
+
+        def tick_begin(p, fresh, final, tiles):
+            if fresh:
+                for plan in plans:
+                    plan.copy(p).wait()
+            for i, tile in enumerate(tiles):
+                for which in range(2):
+                    tile_copy(which, p, i, *tile).start()
+
+        def tick_add(p, fresh, final, tiles):
+            for i, tile in enumerate(tiles):
+                for which in range(2):
+                    tile_copy(which, p, i, *tile).wait()
+                addend[0, i] = (addend[0, i].astype(F32) + addend[1, i].astype(F32)).astype(BF)
+                tile_copy(2, p, i, *tile).start()
+            for i, tile in enumerate(tiles):
+                tile_copy(2, p, i, *tile).wait()
+            if final and p + 1 < steps:
+                for plan in plans:
+                    plan.start(p + 1)
+
         all_steps = n * CHUNKS + n
         due = [all_steps * 9 * (2**steps - 2 ** (steps - 1 - p)) // (10 * (2**steps - 1)) // 2 * 2 for p in range(steps)]
 
         def turn(g):
-            for p in range(steps - 1):
-                for i, plan in enumerate(plans):
-                    pl.when(g == due[p] + 2 * i)(lambda p=p, plan=plan: pass_on(p, plan))
+            if ticks:
+                for at, tick in ticks.items():
+                    pl.when(g == at)(lambda tick=tick: tick_begin(*tick))
+            else:
+                for p in range(steps - 1):
+                    for i, plan in enumerate(plans):
+                        pl.when(g == due[p] + 2 * i)(lambda p=p, plan=plan: pass_on(p, plan))
 
             q, due_now = item_of(g)
 
@@ -559,6 +611,10 @@
             return q, (q >= 0) & (q < items) & (g >= 3) & (between | (lax.rem(g, 2) == 1))
 
         def after(g):
+            for at, tick in ticks.items():
+                pl.when(g == at)(lambda tick=tick: tick_add(*tick))
+            last = g - 1 - (n - 1) * (CHUNKS + 1)
+            pl.when(last >= 0)(lambda: finish(last))
             q, due_now = item_of(g)
 
             @pl.when(due_now)
@@ -587,6 +643,14 @@
                 swaps[1].start()
 
         core = dp_bit(0)
+
+        def result(j):
+            return pltpu.make_async_copy(total, out.at[j], stored.at[5])
+
+        def finish(j):
+            pl.when(j > 0)(lambda: result(j - 1).wait())
+            own_sum(n, d, j, partial, travel, total)
+            result(j).start()
 
         def rows_at(i):
             return pl.ds(pl.multiple_of(i * piece, piece), piece)
@@ -649,23 +713,11 @@
         )
         keep = pltpu.make_async_copy(gathered.at[d], d_own, stored.at[0])
         keep.start()
-        def result(j):
-            return pltpu.make_async_copy(total, out.at[j], stored.at[1])
-
-        def finish(j, _):
-            @pl.when(j > 0)
-            def _():
-                result(j - 1).wait()
-
-            own_sum(n, d, j, partial, travel, total)
-            result(j).start()
-            return 0
-
-        lax.fori_loop(0, CHUNKS, finish, 0)
         result(CHUNKS - 1).wait()
         keep.wait()
-        for plan in plans:
-            pass_on(steps - 1, plan)
+        if not ticks:
+            for plan in plans:
+                pass_on(steps - 1, plan)
         for swap in swaps:
             swap.wait()
         keep_sums()
@@ -691,7 +743,8 @@
             pltpu.VMEM((2 * rows, c), BF), pltpu.VMEM((2 * rows, h), BF), pltpu.VMEM((2 * rows, h), BF),
             pltpu.VMEM((c, h), F32), pltpu.VMEM((c, h), F32),
             pltpu.VMEM((rows, c), F32), pltpu.VMEM((c // LANES, pairs_here * cols, LANES), F32),
-            dma((2,)), dma((2,)), dma((5,)),
+            pltpu.VMEM((2, 4, split, plans[0].block), BF),
+            dma((2,)), dma((2,)), dma((6,)), dma((3, 4)),
         ]
         + plans[0].semaphores() + plans[1].semaphores()
         + chain_sems(n, CHUNKS),
@@ -1454,12 +1507,20 @@
         compiler_params=pltpu.CompilerParams(collective_id=cid, has_side_effects=True, vmem_limit_bytes=62 * MIB),
         cost_estimate=pl.CostEstimate(flops=14 * 10**9, bytes_accessed=70 * 10**6, transcendentals=10**7),
     )(low, pool_a, pool_b, cot, gain1, gain2, packed.reshape(pairs, 2, n, rows, 16 * width))
-def weight_outputs(own, g_cn_up, g_cn_down, widths, high_rows):
+def weight_outputs(own, g_cn_up, g_cn_down, widths, high_rows, others):
     share = own.shape[0]
     width, wide = widths[0], widths[-1]
     piece, h = g_cn_up.shape
 
-    def kernel(x, cn_up, cn_down, gate, high, out, qkv, proj, up, down, o_cn_up, o_cn_down):
+    def kernel(x, cn_up, cn_down, *rest):
+        sources, rest = rest[: len(others)], rest[len(others) :]
+        gate, high, out, qkv, proj, up, down, o_cn_up, o_cn_down = rest[:9]
+        copies = [
+            pltpu.make_async_copy(a, b, rest[-1].at[i]) for i, (a, b) in enumerate(zip(sources, rest[9:-1]))
+        ]
+        for copy in copies:
+            copy.start()
+
         def part(i, size=width):
             at = sum(widths[:i])
             return x[:, at : at + size].astype(F32)
@@ -1474,20 +1535,24 @@
         up[...] = part(8, wide)
         down[...] = part(9, wide).T
         o_cn_up[...] = cn_up[...].astype(F32)
-        o_cn_down[...] = cn_down[...].astype(F32).T
-
+        o_cn_down[...] = cn_down[...].astype(F32)
+        for copy in copies:
+            copy.wait()
+
+    whole = pl.BlockSpec(memory_space=pl.ANY)
     local = pl.BlockSpec(memory_space=pltpu.VMEM)
     shapes = [
         (share, width), (high_rows, width), (width, share), (3, share, width), (width, share), (share, wide),
-        (wide, share), (piece, h), (h, piece),
+        (wide, share), (piece, h), (piece, h),
     ]
     return pl.pallas_call(
         kernel,
-        out_shape=[jax.ShapeDtypeStruct(s, F32) for s in shapes],
-        in_specs=[local] * 3,
-        out_specs=[local] * 9,
-        compiler_params=pltpu.CompilerParams(vmem_limit_bytes=32 * MIB),
-    )(own, g_cn_up, g_cn_down)
+        out_shape=[jax.ShapeDtypeStruct(s, F32) for s in shapes + [o.shape for o in others]],
+        in_specs=[local] * 3 + [whole] * len(others),
+        out_specs=[local] * 9 + [whole] * len(others),
+        scratch_shapes=[pltpu.SemaphoreType.DMA((len(others),))],
+        compiler_params=pltpu.CompilerParams(vmem_limit_bytes=60 * MIB),
+    )(own, g_cn_up, g_cn_down, *others)
 
 
 def pack_weights(ad_gate, ad_out, ad_high, w_qkv, w_proj, w_up, w_down, devices):
@@ -1527,7 +1592,7 @@
         scratch_shapes=[
             pltpu.VMEM((2, width, share), BF), pltpu.VMEM((wide, share), BF), pltpu.SemaphoreType.DMA((10,)),
         ],
-        compiler_params=pltpu.CompilerParams(vmem_limit_bytes=16 * MIB),
+        compiler_params=pltpu.CompilerParams(vmem_limit_bytes=60 * MIB),
     )(ad_gate, ad_out, ad_high, w_qkv, w_proj, w_up, w_down)
 
 
@@ -1646,9 +1711,14 @@
     d_hr_in = d_hr_in[None]
     g_conv = small_sums[: size * size].reshape(conv_w.shape)
     g_hr_gain, g_ln1, g_ln2 = small_sums[size * size], small_sums[-2, :dims], small_sums[-1, :dims]
-    g_ad_gate, g_ad_high, g_ad_out, g_qkv, g_proj, g_up, g_down, g_cn_up, g_cn_down = weight_outputs(
-        low_sums.reshape(share, -1), g_cn_up, g_cn_down, [p.shape[1] for p in pieces], ad_high.shape[0] // devices
+    (
+        g_ad_gate, g_ad_high, g_ad_out, g_qkv, g_proj, g_up, g_down, g_cn_up, g_cn_down,
+        low_out, hr_out, d_low_in, d_hr_in,
+    ) = weight_outputs(
+        low_sums.reshape(share, -1), g_cn_up, g_cn_down, [p.shape[1] for p in pieces], ad_high.shape[0] // devices,
+        (low_out, hr_out, d_low_in, d_hr_in),
     )
+    g_cn_down = g_cn_down.T
     return (
         low_out,
         hr_out,

time: 762 us -> 975 us (1.28)
  Pallas kernels: 640 us -> 874 us
  local copies, waits for them, and re-layouts: 38.7 us -> 19.4 us
    pallas_call x1, Pallas kernels: 2 us -> 255 us  [weight_outputs(): pl.pallas_call(kernel, out_shape=[jax.ShapeDtypeStruct(s, F32) for s in s...]
    unnamed x53 -> x32, local copies, waits for them, and re-layouts: 22.5 us -> 3.05 us
    pallas_call x1, Pallas kernels: 233 us -> 214 us  [big_backward(): pl.pallas_call(kernel, out_shape=(jax.ShapeDtypeStruct((CHUNKS, rows, c),...]
  transfers between devices with their start and end apart: 3 -> 3, of which waited for: 2 -> 2; matrix products, arithmetic and copies ran while one was open for 2% -> 2% of each run, Pallas kernels for 39% -> 30%
where the time goes in v9:
time: 975 us; the launch traced here: 969 us
  Pallas kernels  874 us (90%)
  waiting for transfers between devices  57.1 us (6%)
  local copies, waits for them, and re-layouts  19.4 us (2%)
  between operations  14.4 us (1%)
    pallas_call x1, Pallas kernels, weight_outputs(): pl.pallas_call(kernel, out_shape=[jax.ShapeDtypeStruct(s, F32) for s in s...  255 us
    pallas_call x1, Pallas kernels, big_backward(): pl.pallas_call(kernel, out_shape=(jax.ShapeDtypeStruct((CHUNKS, rows, c),...  214 us
    pallas_call x1, Pallas kernels, big_forward(): pl.pallas_call(kernel, out_shape=(jax.ShapeDtypeStruct((CHUNKS, rows, c),...  179 us
    pallas_call x1, Pallas kernels, low_stage(): pl.pallas_call(kernel, out_shape=(tok, tok, tok, tok, one, one, jax.Shape...  111 us
    pallas_call x1, Pallas kernels, conv_backward(): pl.pallas_call(kernel, out_shape=(jax.ShapeDtypeStruct((rows, cols, c), F...  82.7 us
    all_gather x1, waiting for transfers between devices, per_device(): packed = rows_first(lax.all_gather(packed, 'mp', axis=0, tiled=True))  49.5 us
    pallas_call x1, Pallas kernels, conv_forward(): pl.pallas_call(kernel, out_shape=(jax.ShapeDtypeStruct((rows, cols, c), F...  29.7 us
  transfers between devices with their start and end apart: 3, of which 2 were waited for; matrix products, arithmetic and copies ran while one was open for 2% of the time, Pallas kernels for 30%

profile of v9, /device:TPU:0, one launch (start us, length us, event | category | flops | bytes accessed | tf_op | source)
XLA Modules:
  0.0 969.2 jit_solution(1583401624227846048)
XLA Ops:
  7.2 0.0 all-gather.3.cloned.1.call-start
  7.3 2.5 shard_map.306
  9.8 0.0 all-gather.5.cloned.1.call-start
  9.9 0.4 reshape.188.w_ref
  10.4 1.7 bitcast_multiply_fusion.x_ref.res
  12.0 29.7 %shard_map.305 = (f32[12,48,1536]{2,1,0:T(8,128)S(1)}, bf16[18,48,1536]{2,1,0:T(8,128)(2,1)S(1)}) custom-call(bf16[12,48,1536]{2,1,0:T(8,128)(2,1)S(1)} %bitcast_multiply_fusion.x_ref.res, f32[49,1,1536]{2,1,0:T(1,128)S(1)} %reshape.188.w_ref), custom_call_target="tpu_custom_call" | custom-call | tf_op jit(solution)/shard_map/pallas_call | solution.py:874
  41.8 0.4 multiply_reduce_fusion.1
  42.2 0.6 multiply_reduce_fusion
  42.8 0.5 copy-done.4
  43.3 1.2 copy-done
  44.4 1.8 multiply_convert_fusion
  46.2 49.5 %all-gather.3.cloned.1.call-done = bf16[512,4096]{1,0:T(8,128)(2,1)} async-done(((bf16[128,4096]{1,0:T(8,128)(2,1)}), bf16[512,4096]{1,0:T(8,128)(2,1)}) %all-gather.3.cloned.1.call-update) | async-done | bytes 4194320 | tf_op jit(solution)/shard_map/all_gather | solution.py:1663
  95.9 0.9 convert_element_type.67.mask_ref
  96.8 0.1 convert_element_type.65
  96.9 0.2 reshape_squeeze.12
  97.1 0.1 copy.70
  97.2 0.9 reshape.166.low_ref
  98.1 0.1 reduce_sum.29
  98.2 0.8 copy.46.share_ref
  99.0 0.2 reshape_squeeze.13
  99.2 0.1 copy.69
  99.3 0.9 reshape.171.cot_ref
  100.2 0.6 copy.52
  100.8 0.6 copy.53
  101.4 178.5 %shard_map.307 = (f32[6,96,1536]{2,1,0:T(8,128)}, bf16[6,24,1536]{2,1,0:T(8,128)(2,1)}, bf16[4,6,96,1536]{3,2,1,0:T(8,128)(2,1)}, bf16[4,6,96,1536]{3,2,1,0:T(8,...) custom-call(bf16[6,96,1536]{2,1,0:T(8,128)(2,1)} %bitcast.77, ...), custom_call_target="tpu_custom_call" | custom-call | flops 21743271936 | bytes 28311552 | tf_op jit(solution)/shard_map/pallas_call | solution.py:404
  279.9 1.5 reshape_reshape.28
  281.5 0.2 copy.48
  281.7 0.9 reshape.169.pool_a_ref
  282.6 0.1 pad.8
  282.7 0.2 copy.50
  282.8 0.9 reshape.170.pool_b_ref
  283.8 111.5 %shard_map.308 = (f32[144,1024]{1,0:T(8,128)}, f32[144,1024]{1,0:T(8,128)}, f32[144,1024]{1,0:T(8,128)}, f32[144,1024]{1,0:T(8,128)}, f32[1,1024]{1,0:T(1,128)},...) custom-call(bf16[144,1024]{1,0:T(8,128)(2,1)} %reshape.166.low_ref, bf16[144,1024]{1,0:T(8,128)(2,1)} %reshape.169.pool_a_ref, ...), custom_call_target="tpu_custom_call" | custom-call | flops 14000000000 | bytes 70000000 | tf_op jit(solution)/shard_map/pallas_call | solution.py:1493
  395.2 1.3 reshape.176
  396.6 0.3 copy.55
  396.9 1.3 reshape.175
  398.2 0.3 copy.54
  398.5 0.1 pad_maximum_fusion
  398.6 1.3 reshape_reshape.33.pool_ref
  399.9 213.8 %shard_map.309 = (f32[6,96,1536]{2,1,0:T(8,128)}, bf16[6,96,1536]{2,1,0:T(8,128)(2,1)}, bf16[4,192,1536]{2,1,0:T(8,128)(2,1)}, bf16[4,192,1536]{2,1,0:T(8,128)(2...) custom-call(bf16[12,48,1536]{2,1,0:T(8,128)(2,1)} %bitcast.100, ...), custom_call_target="tpu_custom_call" | custom-call | flops 43486543872 | bytes 28311552 | tf_op jit(solution)/shard_map/pallas_call | solution.py:728
  613.8 0.2 copy.60.mask_ref
  613.9 0.4 copy-done.11
  614.4 82.7 %shard_map.310 = (f32[12,48,1536]{2,1,0:T(8,128)}, f32[8,7,1536]{2,1,0:T(8,128)S(1)}, bf16[2,192,1536]{2,1,0:T(8,128)(2,1)}, bf16[1,192,1536]{2,1,0:T(8,128)(2,1...) custom-call(f32[12,48,1536]{2,1,0:T(8,128)} %bitcast.106, ...), custom_call_target="tpu_custom_call" | custom-call | flops 60000002048 | bytes 100000000 | tf_op jit(solution)/shard_map/pallas_call | solution.py:1095
  697.1 0.8 copy-done.2
  697.9 0.8 slice.30
  698.8 0.6 slice_reduce_fusion
  699.4 0.6 fusion
  700.0 7.5 reduce-scatter.2.cloned.1.call-done
  707.5 254.9 %shard_map.311 = (f32[128,256]{1,0:T(8,128)}, f32[192,256]{1,0:T(8,128)}, f32[256,128]{1,0:T(8,128)}, f32[3,128,256]{2,1,0:T(8,128)}, f32[256,128]{1,0:T(8,128)}...) custom-call(bf16[128,4096]{1,0:T(8,128)(2,1)} %bitcast.82, ...), custom_call_target="tpu_custom_call" | custom-call | tf_op jit(solution)/shard_map/pallas_call | solution.py:1548
  (48 shorter events, 0.4 us)
Async XLA Ops:
  7.2 2.6 copy-start.8
  7.2 2.7 copy-start.7
  7.2 3.1 copy-start.9
  7.2 88.5 %all-gather.3.cloned.1.call-start = ((), (), s32[]{:S(2)}) async-start(), calls=%async_computation.1 | async-start | bytes 5242880 | tf_op jit(solution)/shard_map/all_gather | solution.py:1663
  9.8 274.0 %all-gather.5.cloned.1.call-start = ((), (), s32[]{:S(2)}) async-start(), calls=%async_computation.2 | async-start | bytes 37748736 | tf_op jit(solution)/shard_map/all_gather | solution.py:1676
  12.0 30.7 %copy-start.1 = (bf16[12,48,1536]{2,1,0:T(8,128)(2,1)}, bf16[12,48,1536]{2,1,0:T(8,128)(2,1)S(1)}, u32[]{:S(2)}) copy-start(bf16[12,48,1536]{2,1,0:T(8,128)(2,1)S(1)} %bitcast_multiply_fusion.x_ref.res) | copy-start | bytes 5308420
  41.7 1.5 copy-start.4
  41.8 2.7 copy-start
  46.2 50.6 %copy-start.5 = (bf16[1,144,1024]{2,1,0:T(8,128)(2,1)S(1)}, bf16[1,144,1024]{2,1,0:T(8,128)(2,1)}, u32[]{:S(2)}) copy-start(bf16[1,144,1024]{2,1,0:T(8,128)(2,1)} %param.19) | copy-start | bytes 884740
  46.2 52.7 %copy-start.6 = (bf16[1,144,1024]{2,1,0:T(8,128)(2,1)S(1)}, bf16[1,144,1024]{2,1,0:T(8,128)(2,1)}, u32[]{:S(2)}) copy-start(bf16[1,144,1024]{2,1,0:T(8,128)(2,1)} %param.34) | copy-start | bytes 884740
  95.8 4.4 copy-start.12
  95.8 5.0 copy-start.13
  95.8 611.7 %reduce-scatter.2.cloned.1.call-start = ((), (), s32[]{:S(2)}) async-start(), calls=%async_computation.3 | async-start | bytes 5242880 | tf_op jit(solution)/shard_map/reduce_scatter | solution.py:1706
  613.7 0.7 copy-start.11
  613.7 0.7 copy-start.10
  697.1 0.8 copy-start.2
  697.9 9.6 copy-start.3
Sparse Core Ops, SparseCore 0:
  10.2 85.5 all-gather.2
  97.6 159.8 all-gather.4
  613.9 93.6 reduce-scatter.1

commit v10 on v9

--- a/solution.py
+++ b/solution.py
@@ -1515,11 +1515,12 @@
     def kernel(x, cn_up, cn_down, *rest):
         sources, rest = rest[: len(others)], rest[len(others) :]
         gate, high, out, qkv, proj, up, down, o_cn_up, o_cn_down = rest[:9]
-        copies = [
-            pltpu.make_async_copy(a, b, rest[-1].at[i]) for i, (a, b) in enumerate(zip(sources, rest[9:-1]))
-        ]
-        for copy in copies:
-            copy.start()
+        count = len(others)
+        targets, held, sems = rest[9 : 9 + count], rest[9 + count : -1], rest[-1]
+        loads = [pltpu.make_async_copy(a, b, sems.at[0, i]) for i, (a, b) in enumerate(zip(sources, held))]
+        saves = [pltpu.make_async_copy(a, b, sems.at[1, i]) for i, (a, b) in enumerate(zip(held, targets))]
+        for load in loads:
+            load.start()
 
         def part(i, size=width):
             at = sum(widths[:i])
@@ -1535,9 +1536,12 @@
         up[...] = part(8, wide)
         down[...] = part(9, wide).T
         o_cn_up[...] = cn_up[...].astype(F32)
+        for load, save in zip(loads, saves):
+            load.wait()
+            save.start()
         o_cn_down[...] = cn_down[...].astype(F32)
-        for copy in copies:
-            copy.wait()
+        for save in saves:
+            save.wait()
 
     whole = pl.BlockSpec(memory_space=pl.ANY)
     local = pl.BlockSpec(memory_space=pltpu.VMEM)
@@ -1550,7 +1554,7 @@
         out_shape=[jax.ShapeDtypeStruct(s, F32) for s in shapes + [o.shape for o in others]],
         in_specs=[local] * 3 + [whole] * len(others),
         out_specs=[local] * 9 + [whole] * len(others),
-        scratch_shapes=[pltpu.SemaphoreType.DMA((len(others),))],
+        scratch_shapes=[pltpu.VMEM(o.shape, o.dtype) for o in others] + [pltpu.SemaphoreType.DMA((2, len(others)))],
         compiler_params=pltpu.CompilerParams(vmem_limit_bytes=60 * MIB),
     )(own, g_cn_up, g_cn_down, *others)
 

time: 975 us -> 730 us (0.75)
  Pallas kernels: 874 us -> 628 us
    pallas_call x1, Pallas kernels: 255 us -> 9.7 us  [weight_outputs(): pl.pallas_call(kernel, out_shape=[jax.ShapeDtypeStruct(s, F32) for s in s...]
  transfers between devices with their start and end apart: 3 -> 3, of which waited for: 2 -> 2; matrix products, arithmetic and copies ran while one was open for 2% -> 2% of each run, Pallas kernels for 30% -> 40%
where the time goes in v10:
time: 730 us; the launch traced here: 724 us
  Pallas kernels  628 us (86%)
  waiting for transfers between devices  57.1 us (8%)
  local copies, waits for them, and re-layouts  19.4 us (3%)
  between operations  14.4 us (2%)
    pallas_call x1, Pallas kernels, big_backward(): pl.pallas_call(kernel, out_shape=(jax.ShapeDtypeStruct((CHUNKS, rows, c),...  214 us
    pallas_call x1, Pallas kernels, big_forward(): pl.pallas_call(kernel, out_shape=(jax.ShapeDtypeStruct((CHUNKS, rows, c),...  179 us
    pallas_call x1, Pallas kernels, low_stage(): pl.pallas_call(kernel, out_shape=(tok, tok, tok, tok, one, one, jax.Shape...  111 us
    pallas_call x1, Pallas kernels, conv_backward(): pl.pallas_call(kernel, out_shape=(jax.ShapeDtypeStruct((rows, cols, c), F...  82.7 us
    all_gather x1, waiting for transfers between devices, per_device(): packed = rows_first(lax.all_gather(packed, 'mp', axis=0, tiled=True))  49.5 us
    pallas_call x1, Pallas kernels, conv_forward(): pl.pallas_call(kernel, out_shape=(jax.ShapeDtypeStruct((rows, cols, c), F...  29.7 us
  transfers between devices with their start and end apart: 3, of which 2 were waited for; matrix products, arithmetic and copies ran while one was open for 2% of the time, Pallas kernels for 40%

profile of v10, /device:TPU:0, one launch (start us, length us, event | category | flops | bytes accessed | tf_op | source)
XLA Modules:
  0.0 724.0 jit_solution(2104074578744931213)
XLA Ops:
  7.2 0.0 all-gather.3.cloned.1.call-start
  7.3 2.5 shard_map.306
  9.8 0.0 all-gather.5.cloned.1.call-start
  9.9 0.4 reshape.188.w_ref
  10.4 1.7 bitcast_multiply_fusion.x_ref.res
  12.0 29.7 %shard_map.305 = (f32[12,48,1536]{2,1,0:T(8,128)S(1)}, bf16[18,48,1536]{2,1,0:T(8,128)(2,1)S(1)}) custom-call(bf16[12,48,1536]{2,1,0:T(8,128)(2,1)S(1)} %bitcast_multiply_fusion.x_ref.res, f32[49,1,1536]{2,1,0:T(1,128)S(1)} %reshape.188.w_ref), custom_call_target="tpu_custom_call" | custom-call | tf_op jit(solution)/shard_map/pallas_call | solution.py:874
  41.8 0.4 multiply_reduce_fusion.1
  42.2 0.6 multiply_reduce_fusion
  42.8 0.5 copy-done.4
  43.3 1.2 copy-done
  44.4 1.8 multiply_convert_fusion
  46.2 49.5 %all-gather.3.cloned.1.call-done = bf16[512,4096]{1,0:T(8,128)(2,1)} async-done(((bf16[128,4096]{1,0:T(8,128)(2,1)}), bf16[512,4096]{1,0:T(8,128)(2,1)}) %all-gather.3.cloned.1.call-update) | async-done | bytes 4194320 | tf_op jit(solution)/shard_map/all_gather | solution.py:1667
  95.9 0.9 convert_element_type.67.mask_ref
  96.8 0.1 convert_element_type.65
  96.9 0.2 reshape_squeeze.12
  97.1 0.1 copy.70
  97.2 0.9 reshape.166.low_ref
  98.1 0.1 reduce_sum.29
  98.2 0.8 copy.46.share_ref
  99.0 0.2 reshape_squeeze.13
  99.2 0.1 copy.69
  99.3 0.9 reshape.171.cot_ref
  100.2 0.6 copy.52
  100.8 0.6 copy.53
  101.4 178.5 %shard_map.307 = (f32[6,96,1536]{2,1,0:T(8,128)}, bf16[6,24,1536]{2,1,0:T(8,128)(2,1)}, bf16[4,6,96,1536]{3,2,1,0:T(8,128)(2,1)}, bf16[4,6,96,1536]{3,2,1,0:T(8,...) custom-call(bf16[6,96,1536]{2,1,0:T(8,128)(2,1)} %bitcast.77, ...), custom_call_target="tpu_custom_call" | custom-call | flops 21743271936 | bytes 28311552 | tf_op jit(solution)/shard_map/pallas_call | solution.py:404
  279.9 1.5 reshape_reshape.28
  281.5 0.2 copy.48
  281.7 0.9 reshape.169.pool_a_ref
  282.6 0.1 pad.8
  282.7 0.2 copy.50
  282.8 0.9 reshape.170.pool_b_ref
  283.8 111.5 %shard_map.308 = (f32[144,1024]{1,0:T(8,128)}, f32[144,1024]{1,0:T(8,128)}, f32[144,1024]{1,0:T(8,128)}, f32[144,1024]{1,0:T(8,128)}, f32[1,1024]{1,0:T(1,128)},...) custom-call(bf16[144,1024]{1,0:T(8,128)(2,1)} %reshape.166.low_ref, bf16[144,1024]{1,0:T(8,128)(2,1)} %reshape.169.pool_a_ref, ...), custom_call_target="tpu_custom_call" | custom-call | flops 14000000000 | bytes 70000000 | tf_op jit(solution)/shard_map/pallas_call | solution.py:1493
  395.2 1.3 reshape.176
  396.6 0.3 copy.55
  396.9 1.3 reshape.175
  398.2 0.3 copy.54
  398.5 0.1 pad_maximum_fusion
  398.6 1.3 reshape_reshape.33.pool_ref
  399.9 213.8 %shard_map.309 = (f32[6,96,1536]{2,1,0:T(8,128)}, bf16[6,96,1536]{2,1,0:T(8,128)(2,1)}, bf16[4,192,1536]{2,1,0:T(8,128)(2,1)}, bf16[4,192,1536]{2,1,0:T(8,128)(2...) custom-call(bf16[12,48,1536]{2,1,0:T(8,128)(2,1)} %bitcast.100, ...), custom_call_target="tpu_custom_call" | custom-call | flops 43486543872 | bytes 28311552 | tf_op jit(solution)/shard_map/pallas_call | solution.py:728
  613.8 0.2 copy.60.mask_ref
  613.9 0.4 copy-done.11
  614.4 82.7 %shard_map.310 = (f32[12,48,1536]{2,1,0:T(8,128)}, f32[8,7,1536]{2,1,0:T(8,128)S(1)}, bf16[2,192,1536]{2,1,0:T(8,128)(2,1)}, bf16[1,192,1536]{2,1,0:T(8,128)(2,1...) custom-call(f32[12,48,1536]{2,1,0:T(8,128)} %bitcast.106, ...), custom_call_target="tpu_custom_call" | custom-call | flops 60000002048 | bytes 100000000 | tf_op jit(solution)/shard_map/pallas_call | solution.py:1095
  697.1 0.8 copy-done.2
  697.9 0.8 slice.30
  698.8 0.6 slice_reduce_fusion
  699.4 0.6 fusion
  700.0 7.5 %reduce-scatter.2.cloned.1.call-done = bf16[1,128,4096]{2,1,0:T(8,128)(2,1)} async-done(((bf16[4,128,4096]{2,1,0:T(8,128)(2,1)}), bf16[1,128,4096]{2,1,0:T(8,128)(2,1)}) %reduce-scatter.2.cloned.1.call-update) | async-done | bytes 1048592 | tf_op jit(solution)/shard_map/reduce_scatter | solution.py:1710
  707.5 9.7 %shard_map.311 = (f32[128,256]{1,0:T(8,128)}, f32[192,256]{1,0:T(8,128)}, f32[256,128]{1,0:T(8,128)}, f32[3,128,256]{2,1,0:T(8,128)}, f32[256,128]{1,0:T(8,128)}...) custom-call(bf16[128,4096]{1,0:T(8,128)(2,1)} %bitcast.82, ...), custom_call_target="tpu_custom_call" | custom-call | tf_op jit(solution)/shard_map/pallas_call | solution.py:1552
  (48 shorter events, 0.4 us)
Async XLA Ops:
  7.2 2.6 copy-start.8
  7.2 2.7 copy-start.7
  7.2 3.1 copy-start.9
  7.2 88.5 %all-gather.3.cloned.1.call-start = ((), (), s32[]{:S(2)}) async-start(), calls=%async_computation.1 | async-start | bytes 5242880 | tf_op jit(solution)/shard_map/all_gather | solution.py:1667
  9.8 274.0 %all-gather.5.cloned.1.call-start = ((), (), s32[]{:S(2)}) async-start(), calls=%async_computation.2 | async-start | bytes 37748736 | tf_op jit(solution)/shard_map/all_gather | solution.py:1680
  12.0 30.7 %copy-start.1 = (bf16[12,48,1536]{2,1,0:T(8,128)(2,1)}, bf16[12,48,1536]{2,1,0:T(8,128)(2,1)S(1)}, u32[]{:S(2)}) copy-start(bf16[12,48,1536]{2,1,0:T(8,128)(2,1)S(1)} %bitcast_multiply_fusion.x_ref.res) | copy-start | bytes 5308420
  41.7 1.5 copy-start.4
  41.8 2.7 copy-start
  46.2 50.6 %copy-start.5 = (bf16[1,144,1024]{2,1,0:T(8,128)(2,1)S(1)}, bf16[1,144,1024]{2,1,0:T(8,128)(2,1)}, u32[]{:S(2)}) copy-start(bf16[1,144,1024]{2,1,0:T(8,128)(2,1)} %param.19) | copy-start | bytes 884740
  46.2 52.7 %copy-start.6 = (bf16[1,144,1024]{2,1,0:T(8,128)(2,1)S(1)}, bf16[1,144,1024]{2,1,0:T(8,128)(2,1)}, u32[]{:S(2)}) copy-start(bf16[1,144,1024]{2,1,0:T(8,128)(2,1)} %param.34) | copy-start | bytes 884740
  95.8 4.4 copy-start.12
  95.8 5.0 copy-start.13
  95.8 611.7 %reduce-scatter.2.cloned.1.call-start = ((), (), s32[]{:S(2)}) async-start(), calls=%async_computation.3 | async-start | bytes 5242880 | tf_op jit(solution)/shard_map/reduce_scatter | solution.py:1710
  613.7 0.7 copy-start.11
  613.7 0.7 copy-start.10
  697.1 0.8 copy-start.2
  697.9 9.6 %copy-start.3 = (bf16[1,1,192,1536]{3,2,1,0:T(8,128)(2,1)}, bf16[1,1,192,1536]{3,2,1,0:T(8,128)(2,1)S(1)}, u32[]{:S(2)}) copy-start(bf16[1,1,192,1536]{3,2,1,0:T(8,128)(2,1)S(1)} %get-tuple-element.78) | copy-start | bytes 1769476
Sparse Core Ops, SparseCore 0:
  10.2 85.5 all-gather.2
  97.6 159.8 all-gather.4
  613.9 93.6 reduce-scatter.1

commit v11 on v10

--- a/solution.py
+++ b/solution.py
@@ -901,15 +901,16 @@
     count = taps + 1 + low_gains.shape[0]
     small = -(-count // devices)
     first_due = blocks + blocks // 3
-    halving = {first_due + 2 * blocks // 3 * p // (steps - 1): p for p in range(steps - 1)}
-    rounds = {blocks + 7 * blocks // 12: 1, blocks + 10 * blocks // 12: 2}
+    begins = {first_due + blocks // 2 * p // (steps - 1): p for p in range(steps - 1)}
+    ends = {mark + 1: p for mark, p in begins.items()}
+    rounds = {blocks + 10 * blocks // 12: 1}
 
     def kernel(
         dn, co, gain_ref, mask_ref, w_ref, low_ref, b_hbm, dm_hbm, g0, g1, out, g_all, *rest
     ):
         extra, rest = rest[: 2 * each], rest[2 * each :]
-        around, x_around, d_here, dframed, xframed, g_own, here, level, sent, got, own = rest[:11]
-        ar, halving_sems = rest[11:17], rest[17:]
+        around, x_around, d_here, dframed, xframed, g_own, here, level, addend, sent, got, own, add_sem = rest[:13]
+        ar, halving_sems = rest[13:19], rest[19:]
         plans[0].bind(g0, extra[:each], halving_sems[0], halving_sems[1])
         plans[1].bind(g1, extra[each:], halving_sems[2], halving_sems[3])
         me, d = lax.axis_index("dp"), lax.axis_index("mp")
@@ -930,11 +931,36 @@
         load_x.start()
         load_d.start()
 
-        def pass_on(p):
-            for plan in plans:
-                plan.finish(p)
-            if p == 0:
-                sum_round(0)
+        def halving_loads(p, i):
+            plan, count = plans[i], plans[i].got[p].shape[0]
+            some = pl.ds(0, count)
+            return [
+                pltpu.make_async_copy(plan.part(p, True), addend.at[0, i, some], add_sem.at[0, i]),
+                pltpu.make_async_copy(plan.got[p], addend.at[1, i, some], add_sem.at[1, i]),
+            ]
+
+        def halving_save(p, i, k):
+            plan = plans[i]
+            ways = plan.split(plan.got[p].shape[0], p + 1)
+            target = plan.now[p + 1].at[k // ways[1], k % ways[1]]
+            return pltpu.make_async_copy(addend.at[0, i, k], target, add_sem.at[2 + i, k])
+
+        def halving_begin(p):
+            for i, plan in enumerate(plans):
+                plan.copy(p).wait()
+                for load in halving_loads(p, i):
+                    load.start()
+
+        def halving_end(p):
+            for i, plan in enumerate(plans):
+                for load in halving_loads(p, i):
+                    load.wait()
+                for k in range(plan.got[p].shape[0]):
+                    addend[0, i, k] = (addend[0, i, k].astype(F32) + addend[1, i, k].astype(F32)).astype(BF)
+                    halving_save(p, i, k).start()
+            for i, plan in enumerate(plans):
+                for k in range(plan.got[p].shape[0]):
+                    halving_save(p, i, k).wait()
             if p + 1 < steps:
                 for plan in plans:
                     plan.start(p + 1)
@@ -1056,7 +1082,7 @@
             else:
                 all_of(devices, tell, lambda x: x.wait())
 
-        marks = sorted(set(halving) | set(rounds) | {blocks, 2 * blocks})
+        marks = sorted(set(begins) | set(ends) | set(rounds) | {blocks, 2 * blocks})
         at = 0
         for mark in marks:
             if at < blocks:
@@ -1064,8 +1090,12 @@
             else:
                 lax.fori_loop(at - blocks, mark - blocks, input_block, 0)
             at = mark
-            if mark in halving:
-                pass_on(halving[mark])
+            if mark in ends:
+                halving_end(ends[mark])
+            if mark in begins:
+                halving_begin(begins[mark])
+            if mark == first_due:
+                sum_round(0)
             if mark == blocks:
                 load_d.wait()
 
@@ -1078,7 +1108,9 @@
                     up.wait_recv()
             if mark in rounds:
                 sum_round(rounds[mark])
-        pass_on(steps - 1)
+        sum_round(2)
+        halving_begin(steps - 1)
+        halving_end(steps - 1)
         sum_round(3)
 
         @pl.when(has_up)
@@ -1106,7 +1138,8 @@
             vm((high, cols, c), BF), vm((high, cols, c), BF), vm((rows, cols, c), BF),
             vm((high, cols + 2 * EDGE, LANES), F32), vm((high, cols + 2 * EDGE, LANES), F32),
             vm((devices, small, c), F32), vm((devices, small, c), F32), vm((n, small, c), F32),
-            dma((2,)), dma((2,)), dma((2,)),
+            vm((2, 2, shape[0] // 2) + shape[1:], BF),
+            dma((2,)), dma((2,)), dma((2,)), dma((4, max(2, shape[0] // 2))),
             dma((devices,)), dma((devices,)), dma((n,)), dma((n,)), dma((devices,)), dma((devices,)),
         ]
         + plans[0].semaphores() + plans[1].semaphores(),
@@ -1159,6 +1192,7 @@
     every = n * t
     width = dim // n
     heads = width // HEAD
+    groups = width // LANES
     pairs = devices // 2
     rows = dim // devices
     half = dim // 2
@@ -1308,16 +1342,18 @@
                 src.at[:, pl.ds(pl.multiple_of(d * width, width), width)], dst.at[pl.ds(pl.multiple_of(d * t, t), t)], own_sem.at[k]))
             return out
 
-        def to_tokens(k, src, dst, send, got):
+        def to_tokens(k, src, dst, send, got, group):
             out = []
+            slot = k * groups + group
+            lanes = pl.ds(group * LANES, LANES)
+            there = pl.ds(pl.multiple_of(d * width + group * LANES, LANES), LANES)
             for step in range(1, n):
                 peer = lax.rem(d + step, n)
                 out.append(pltpu.make_async_remote_copy(
-                    src_ref=src.at[pl.ds(pl.multiple_of(peer * t, t), t)],
-                    dst_ref=dst.at[:, pl.ds(pl.multiple_of(d * width, width), width)],
-                    send_sem=send.at[k, step], recv_sem=got.at[k, step], device_id={"mp": peer}, device_id_type=MESH))
+                    src_ref=src.at[pl.ds(pl.multiple_of(peer * t, t), t), lanes], dst_ref=dst.at[:, there],
+                    send_sem=send.at[slot, step], recv_sem=got.at[slot, step], device_id={"mp": peer}, device_id_type=MESH))
             out.append(pltpu.make_async_copy(
-                src.at[pl.ds(pl.multiple_of(d * t, t), t)], dst.at[:, pl.ds(pl.multiple_of(d * width, width), width)], own_sem.at[k]))
+                src.at[pl.ds(pl.multiple_of(d * t, t), t), lanes], dst.at[:, there], own_sem.at[slot]))
             return out
 
         def start(copies):
@@ -1366,8 +1402,8 @@
             forward(lhs[L_FIRST], QUERY + k, 1, put_mixed)
             copies = to_heads(k, mixed.at[k], heads_in.at[k], q_send, q_got)
             start(copies)
-            out_q += copies
-        wait(out_q)
+            out_q.append(copies)
+        wait(out_q[0] + out_q[1])
 
         for h in range(heads):
             lanes = slice(h * HEAD, (h + 1) * HEAD)
@@ -1378,11 +1414,22 @@
                 e = jnp.exp(s - jnp.max(s, -1, keepdims=True))
                 p = (e * (1.0 / jnp.sum(e, -1, keepdims=True))).astype(BF)
                 probs[h, some] = p
-                att_all[some, lanes] = nn(p, heads_in[2, :, lanes]).astype(BF)
                 return 0
             lax.fori_loop(0, n, rows_of, 0)
-        out_a = to_tokens(0, att_all, rhs.at[0, :, r_cols(R_ATT)], a_send, a_got)
-        start(out_a)
+        wait(out_q[2])
+        out_a = []
+        for h in range(heads):
+            lanes = slice(h * HEAD, (h + 1) * HEAD)
+
+            def attend(b, _):
+                some = pl.ds(pl.multiple_of(b * t, t), t)
+                att_all[some, lanes] = nn(probs[h, some], heads_in[2, :, lanes]).astype(BF)
+                return 0
+            lax.fori_loop(0, n, attend, 0)
+            if (h + 1) * HEAD % LANES == 0:
+                copies = to_tokens(0, att_all, rhs.at[0, :, r_cols(R_ATT)], a_send, a_got, h * HEAD // LANES)
+                start(copies)
+                out_a += copies
         wait(out_a)
         r_copy(R_ATT).start()
         backward(lambda at: rhs[0, :, r_cols(R_ATT)], PROJ, 1, resid, True)
@@ -1421,6 +1468,18 @@
         l_copy(L_COT).wait_recv()
         grad(L_COT, R_ACT, 12, 4)
         wait(out_b)
+        out_c = []
+
+        def send_back(k, h):
+            if (h + 1) * HEAD % LANES == 0:
+                copies = to_tokens(k, d_heads.at[k], rhs.at[0, :, r_cols(R_DQ + k)], c_send, c_got, h * HEAD // LANES)
+                start(copies)
+                out_c.extend(copies)
+
+        for h in range(heads):
+            lanes = slice(h * HEAD, (h + 1) * HEAD)
+            d_heads[2, :, lanes] = tn(probs[h], d_att[:, lanes]).astype(BF)
+            send_back(2, h)
         for h in range(heads):
             lanes = slice(h * HEAD, (h + 1) * HEAD)
 
@@ -1434,12 +1493,8 @@
                 return 0
             lax.fori_loop(0, n, rows_of, 0)
             d_heads[1, :, lanes] = tn(d_scores[...], heads_in[0, :, lanes]).astype(BF)
-            d_heads[2, :, lanes] = tn(probs[h], d_att[:, lanes]).astype(BF)
-        out_c = []
-        for k in range(3):
-            copies = to_tokens(k, d_heads.at[k], rhs.at[0, :, r_cols(R_DQ + k)], c_send, c_got)
-            start(copies)
-            out_c += copies
+            send_back(0, h)
+            send_back(1, h)
         l_copy(L_SECOND).wait_recv()
         grad(L_SECOND, R_DUP, 8, 4)
         l_copy(L_DA).wait_recv()
@@ -1501,27 +1556,17 @@
             vm((t, ff), BF), vm((3, t, dim), BF), vm((3, every, width), BF), vm((every, width), BF), vm((every, width), BF),
             vm((1, 8, 128), BF), vm((3, every, width), BF), vm((heads, every, every), BF), vm((every, every), BF),
             vm((2, pairs, rows, TILE), BF), vm((2, half, t), BF),
-            dma((10, 2 * n)), dma((3, n)), dma((3, n)), dma((1, n)), dma((1, n)), dma((1, n)), dma((1, n)), dma((3, n)), dma((3, n)),
-            dma((3,)), dma((8,)), dma((8,)), dma((9,)), dma((9,)), dma((2, 2)),
+            dma((10, 2 * n)), dma((3, n)), dma((3, n)), dma((groups, n)), dma((groups, n)), dma((1, n)), dma((1, n)),
+            dma((3 * groups, n)), dma((3 * groups, n)), dma((3 * groups,)), dma((8,)), dma((8,)), dma((9,)), dma((9,)), dma((2, 2)),
         ],
         compiler_params=pltpu.CompilerParams(collective_id=cid, has_side_effects=True, vmem_limit_bytes=62 * MIB),
         cost_estimate=pl.CostEstimate(flops=14 * 10**9, bytes_accessed=70 * 10**6, transcendentals=10**7),
     )(low, pool_a, pool_b, cot, gain1, gain2, packed.reshape(pairs, 2, n, rows, 16 * width))
-def weight_outputs(own, g_cn_up, g_cn_down, widths, high_rows, others):
+def low_outputs(own, widths, high_rows):
     share = own.shape[0]
     width, wide = widths[0], widths[-1]
-    piece, h = g_cn_up.shape
-
-    def kernel(x, cn_up, cn_down, *rest):
-        sources, rest = rest[: len(others)], rest[len(others) :]
-        gate, high, out, qkv, proj, up, down, o_cn_up, o_cn_down = rest[:9]
-        count = len(others)
-        targets, held, sems = rest[9 : 9 + count], rest[9 + count : -1], rest[-1]
-        loads = [pltpu.make_async_copy(a, b, sems.at[0, i]) for i, (a, b) in enumerate(zip(sources, held))]
-        saves = [pltpu.make_async_copy(a, b, sems.at[1, i]) for i, (a, b) in enumerate(zip(held, targets))]
-        for load in loads:
-            load.start()
-
+
+    def kernel(x, gate, high, out, qkv, proj, up, down):
         def part(i, size=width):
             at = sum(widths[:i])
             return x[:, at : at + size].astype(F32)
@@ -1535,28 +1580,49 @@
         proj[...] = part(7).T
         up[...] = part(8, wide)
         down[...] = part(9, wide).T
-        o_cn_up[...] = cn_up[...].astype(F32)
+
+    local = pl.BlockSpec(memory_space=pltpu.VMEM)
+    shapes = [
+        (share, width), (high_rows, width), (width, share), (3, share, width), (width, share), (share, wide), (wide, share),
+    ]
+    return pl.pallas_call(
+        kernel,
+        out_shape=[jax.ShapeDtypeStruct(s, F32) for s in shapes],
+        in_specs=[local],
+        out_specs=[local] * 7,
+        compiler_params=pltpu.CompilerParams(vmem_limit_bytes=32 * MIB),
+    )(own)
+
+
+def map_outputs(g_up, g_down, others):
+    count = len(others)
+
+    def kernel(up, down, *rest):
+        sources, o_up, o_down = rest[:count], rest[count], rest[count + 1]
+        targets, held, sems = rest[count + 2 : 2 * count + 2], rest[2 * count + 2 : -1], rest[-1]
+        loads = [pltpu.make_async_copy(a, b, sems.at[0, i]) for i, (a, b) in enumerate(zip(sources, held))]
+        saves = [pltpu.make_async_copy(a, b, sems.at[1, i]) for i, (a, b) in enumerate(zip(held, targets))]
+        for load in loads:
+            load.start()
+        o_up[...] = up[...].astype(F32)
+        o_down[...] = down[...].astype(F32)
         for load, save in zip(loads, saves):
             load.wait()
             save.start()
-        o_cn_down[...] = cn_down[...].astype(F32)
         for save in saves:
             save.wait()
 
     whole = pl.BlockSpec(memory_space=pl.ANY)
     local = pl.BlockSpec(memory_space=pltpu.VMEM)
-    shapes = [
-        (share, width), (high_rows, width), (width, share), (3, share, width), (width, share), (share, wide),
-        (wide, share), (piece, h), (piece, h),
-    ]
     return pl.pallas_call(
         kernel,
-        out_shape=[jax.ShapeDtypeStruct(s, F32) for s in shapes + [o.shape for o in others]],
-        in_specs=[local] * 3 + [whole] * len(others),
-        out_specs=[local] * 9 + [whole] * len(others),
-        scratch_shapes=[pltpu.VMEM(o.shape, o.dtype) for o in others] + [pltpu.SemaphoreType.DMA((2, len(others)))],
+        out_shape=[jax.ShapeDtypeStruct(x.shape, F32) for x in (g_up, g_down, *others)],
+        in_specs=[local] * 2 + [whole] * count,
+        out_specs=[local] * 2 + [whole] * count,
+        scratch_shapes=[pltpu.VMEM(o.shape, o.dtype) for o in others] + [pltpu.SemaphoreType.DMA((2, count))],
         compiler_params=pltpu.CompilerParams(vmem_limit_bytes=60 * MIB),
-    )(own, g_cn_up, g_cn_down, *others)
+        cost_estimate=pl.CostEstimate(flops=10**9, bytes_accessed=24 * 10**6, transcendentals=0),
+    )(g_up, g_down, *others)
 
 
 def pack_weights(ad_gate, ad_out, ad_high, w_qkv, w_proj, w_up, w_down, devices):
@@ -1715,12 +1781,11 @@
     d_hr_in = d_hr_in[None]
     g_conv = small_sums[: size * size].reshape(conv_w.shape)
     g_hr_gain, g_ln1, g_ln2 = small_sums[size * size], small_sums[-2, :dims], small_sums[-1, :dims]
-    (
-        g_ad_gate, g_ad_high, g_ad_out, g_qkv, g_proj, g_up, g_down, g_cn_up, g_cn_down,
-        low_out, hr_out, d_low_in, d_hr_in,
-    ) = weight_outputs(
-        low_sums.reshape(share, -1), g_cn_up, g_cn_down, [p.shape[1] for p in pieces], ad_high.shape[0] // devices,
-        (low_out, hr_out, d_low_in, d_hr_in),
+    g_cn_up, g_cn_down, low_out, hr_out, d_low_in, d_hr_in = map_outputs(
+        g_cn_up, g_cn_down, (low_out, hr_out, d_low_in, d_hr_in)
+    )
+    g_ad_gate, g_ad_high, g_ad_out, g_qkv, g_proj, g_up, g_down = low_outputs(
+        low_sums.reshape(share, -1), [p.shape[1] for p in pieces], ad_high.shape[0] // devices
     )
     g_cn_down = g_cn_down.T
     return (

time: 730 us -> 716 us (0.981)
  Pallas kernels: 628 us -> 617 us
    pallas_call x1, Pallas kernels: 111 us -> 101 us  [low_stage(): pl.pallas_call(kernel, out_shape=(tok, tok, tok, tok, one, one, jax.Shape...]
    pallas_call x1, Pallas kernels: 82.7 us -> 75.1 us  [conv_backward(): pl.pallas_call(kernel, out_shape=(jax.ShapeDtypeStruct((rows, cols, c), F...]
  transfers between devices with their start and end apart: 3 -> 3, of which waited for: 2 -> 2; matrix products, arithmetic and copies ran while one was open for 2% -> 2% of each run, Pallas kernels for 40% -> 41%
where the time goes in v11:
time: 716 us; the launch traced here: 710 us
  Pallas kernels  617 us (86%)
  waiting for transfers between devices  52.4 us (7%)
  local copies, waits for them, and re-layouts  20.7 us (3%)
  between operations  14.4 us (2%)
    pallas_call x1, Pallas kernels, big_backward(): pl.pallas_call(kernel, out_shape=(jax.ShapeDtypeStruct((CHUNKS, rows, c),...  220 us
    pallas_call x1, Pallas kernels, big_forward(): pl.pallas_call(kernel, out_shape=(jax.ShapeDtypeStruct((CHUNKS, rows, c),...  178 us
    pallas_call x1, Pallas kernels, low_stage(): pl.pallas_call(kernel, out_shape=(tok, tok, tok, tok, one, one, jax.Shape...  101 us
    pallas_call x1, Pallas kernels, conv_backward(): pl.pallas_call(kernel, out_shape=(jax.ShapeDtypeStruct((rows, cols, c), F...  75.1 us
    all_gather x1, waiting for transfers between devices, per_device(): packed = rows_first(lax.all_gather(packed, 'mp', axis=0, tiled=True))  49.5 us
    pallas_call x1, Pallas kernels, conv_forward(): pl.pallas_call(kernel, out_shape=(jax.ShapeDtypeStruct((rows, cols, c), F...  29.7 us
  transfers between devices with their start and end apart: 3, of which 2 were waited for; matrix products, arithmetic and copies ran while one was open for 2% of the time, Pallas kernels for 41%

profile of v11, /device:TPU:0, one launch (start us, length us, event | category | flops | bytes accessed | tf_op | source)
XLA Modules:
  0.0 709.5 jit_solution(11119850102482202573)
XLA Ops:
  7.3 2.5 shard_map.306
  9.9 0.4 reshape.188.w_ref
  10.4 1.7 bitcast_multiply_fusion.x_ref.res
  12.0 29.7 %shard_map.305 = (f32[12,48,1536]{2,1,0:T(8,128)S(1)}, bf16[18,48,1536]{2,1,0:T(8,128)(2,1)S(1)}) custom-call(bf16[12,48,1536]{2,1,0:T(8,128)(2,1)S(1)} %bitcast_multiply_fusion.x_ref.res, f32[49,1,1536]{2,1,0:T(1,128)S(1)} %reshape.188.w_ref), custom_call_target="tpu_custom_call" | custom-call | tf_op jit(solution)/shard_map/pallas_call | solution.py:874
  41.8 0.4 multiply_reduce_fusion.1
  42.2 0.6 multiply_reduce_fusion
  42.8 0.5 copy-done.5
  43.3 1.2 copy-done
  44.4 1.8 multiply_convert_fusion
  46.2 49.5 %all-gather.3.cloned.1.call-done = bf16[512,4096]{1,0:T(8,128)(2,1)} async-done(((bf16[128,4096]{1,0:T(8,128)(2,1)}), bf16[512,4096]{1,0:T(8,128)(2,1)}) %all-gather.3.cloned.1.call-update) | async-done | bytes 4194320 | tf_op jit(solution)/shard_map/all_gather | solution.py:1733
  95.9 0.9 convert_element_type.67.mask_ref
  96.8 0.1 convert_element_type.65
  96.9 0.2 reshape_squeeze.12
  97.1 0.1 copy.70
  97.2 0.9 reshape.166.low_ref
  98.1 0.1 reduce_sum.29
  98.2 0.8 copy.46.share_ref
  99.0 0.2 reshape_squeeze.13
  99.2 0.1 copy.69
  99.3 0.9 reshape.171.cot_ref
  100.2 0.6 copy.52
  100.8 0.6 copy.53
  101.4 178.4 %shard_map.307 = (f32[6,96,1536]{2,1,0:T(8,128)}, bf16[6,24,1536]{2,1,0:T(8,128)(2,1)}, bf16[4,6,96,1536]{3,2,1,0:T(8,128)(2,1)}, bf16[4,6,96,1536]{3,2,1,0:T(8,...) custom-call(bf16[6,96,1536]{2,1,0:T(8,128)(2,1)} %bitcast.78, ...), custom_call_target="tpu_custom_call" | custom-call | flops 21743271936 | bytes 28311552 | tf_op jit(solution)/shard_map/pallas_call | solution.py:404
  279.8 1.5 reshape_reshape.28
  281.4 0.2 copy.48
  281.6 0.9 reshape.169.pool_a_ref
  282.6 0.2 copy.50
  282.7 0.9 reshape.170.pool_b_ref
  283.7 101.1 %shard_map.308 = (f32[144,1024]{1,0:T(8,128)}, f32[144,1024]{1,0:T(8,128)}, f32[144,1024]{1,0:T(8,128)}, f32[144,1024]{1,0:T(8,128)}, f32[1,1024]{1,0:T(1,128)},...) custom-call(bf16[144,1024]{1,0:T(8,128)(2,1)} %reshape.166.low_ref, bf16[144,1024]{1,0:T(8,128)(2,1)} %reshape.169.pool_a_ref, ...), custom_call_target="tpu_custom_call" | custom-call | flops 14000000000 | bytes 70000000 | tf_op jit(solution)/shard_map/pallas_call | solution.py:1548
  384.7 1.3 reshape.176
  386.1 0.3 copy.55
  386.4 1.3 reshape.175
  387.7 0.3 copy.54
  388.0 0.1 pad_maximum_fusion
  388.1 1.3 reshape_reshape.33.pool_ref
  389.4 220.3 %shard_map.309 = (f32[6,96,1536]{2,1,0:T(8,128)}, bf16[6,96,1536]{2,1,0:T(8,128)(2,1)}, bf16[4,192,1536]{2,1,0:T(8,128)(2,1)}, bf16[4,192,1536]{2,1,0:T(8,128)(2...) custom-call(bf16[12,48,1536]{2,1,0:T(8,128)(2,1)} %bitcast.100, ...), custom_call_target="tpu_custom_call" | custom-call | flops 43486543872 | bytes 28311552 | tf_op jit(solution)/shard_map/pallas_call | solution.py:728
  609.8 0.2 copy.60.mask_ref
  610.0 0.4 copy-done.12
  610.5 75.1 %shard_map.310 = (f32[12,48,1536]{2,1,0:T(8,128)}, f32[8,7,1536]{2,1,0:T(8,128)S(1)}, bf16[2,192,1536]{2,1,0:T(8,128)(2,1)}, bf16[1,192,1536]{2,1,0:T(8,128)(2,1...) custom-call(f32[12,48,1536]{2,1,0:T(8,128)} %bitcast.106, ...), custom_call_target="tpu_custom_call" | custom-call | flops 60000002048 | bytes 100000000 | tf_op jit(solution)/shard_map/pallas_call | solution.py:1127
  685.6 0.8 copy-done.3
  686.4 0.8 slice.30
  687.2 0.1 copy-done.4
  687.4 8.8 %shard_map.311 = (f32[192,1536]{1,0:T(8,128)}, f32[192,1536]{1,0:T(8,128)}, f32[1,144,1024]{2,1,0:T(8,128)}, f32[1,12,48,1536]{3,2,1,0:T(8,128)}, f32[1,144,1024]{2,1,0:T(8,128)}, /*index=5*/f32[1,12,48,1536]{3,2,1,0:T(8,128)}) custom-call(bf16[192,1536]{1,0:T(8,128)(2,1)} %bitcast.69, bf16[192,1536]{1,0:T(8,128)(2,1)} %bitcast.70, ...), custom_call_target="tpu_custom_call" | custom-call | flops 1000000000 | bytes 24000000 | tf_op jit(solution)/shard_map/pallas_call | solution.py:1617
  696.1 0.6 slice_reduce_fusion
  696.8 0.6 fusion
  697.4 2.8 reduce-scatter.2.cloned.1.call-done
  700.2 1.2 copy-done.2
  701.4 1.4 shard_map.312
  (51 shorter events, 0.6 us)
Async XLA Ops:
  7.2 2.6 copy-start.9
  7.2 2.7 copy-start.8
  7.2 3.1 copy-start.10
  7.2 88.5 %all-gather.3.cloned.1.call-start = ((), (), s32[]{:S(2)}) async-start(), calls=%async_computation.1 | async-start | bytes 5242880 | tf_op jit(solution)/shard_map/all_gather | solution.py:1733
  9.8 273.9 %all-gather.5.cloned.1.call-start = ((), (), s32[]{:S(2)}) async-start(), calls=%async_computation.2 | async-start | bytes 37748736 | tf_op jit(solution)/shard_map/all_gather | solution.py:1746
  12.0 30.7 %copy-start.1 = (bf16[12,48,1536]{2,1,0:T(8,128)(2,1)}, bf16[12,48,1536]{2,1,0:T(8,128)(2,1)S(1)}, u32[]{:S(2)}) copy-start(bf16[12,48,1536]{2,1,0:T(8,128)(2,1)S(1)} %bitcast_multiply_fusion.x_ref.res) | copy-start | bytes 5308420
  41.7 1.5 copy-start.5
  41.8 2.7 copy-start
  46.2 50.6 %copy-start.6 = (bf16[1,144,1024]{2,1,0:T(8,128)(2,1)S(1)}, bf16[1,144,1024]{2,1,0:T(8,128)(2,1)}, u32[]{:S(2)}) copy-start(bf16[1,144,1024]{2,1,0:T(8,128)(2,1)} %param.19) | copy-start | bytes 884740
  46.2 52.7 %copy-start.7 = (bf16[1,144,1024]{2,1,0:T(8,128)(2,1)S(1)}, bf16[1,144,1024]{2,1,0:T(8,128)(2,1)}, u32[]{:S(2)}) copy-start(bf16[1,144,1024]{2,1,0:T(8,128)(2,1)} %param.34) | copy-start | bytes 884740
  95.8 4.4 copy-start.13
  95.8 5.0 copy-start.14
  95.8 604.4 %reduce-scatter.2.cloned.1.call-start = ((), (), s32[]{:S(2)}) async-start(), calls=%async_computation.3 | async-start | bytes 5242880 | tf_op jit(solution)/shard_map/reduce_scatter | solution.py:1776
  609.7 0.7 copy-start.12
  609.8 0.7 copy-start.11
  685.6 0.8 copy-start.3
  686.4 1.0 copy-start.4
  700.2 1.2 copy-start.2
Sparse Core Ops, SparseCore 0:
  10.2 85.5 all-gather.2
  97.6 159.8 all-gather.4
  609.9 90.2 reduce-scatter.1

commit v12 on v11

--- a/solution.py
+++ b/solution.py
@@ -375,7 +375,7 @@
                 lanes = slice(b * LANES, (b + 1) * LANES)
                 folded[b] = summed[:, lanes]
                 every = folded[b, pl.ds(0, pairs * half, 2), :] + folded[b, pl.ds(1, pairs * half, 2), :]
-                pooled[j, :, lanes] = (every * share_ref[j]).astype(BF)
+                pooled[j, :, lanes] = every * share_ref[j]
 
         def put(j):
             return pltpu.make_async_copy(partial.at[d, j], out.at[j], load_sem)
@@ -405,7 +405,7 @@
         kernel,
         out_shape=(
             jax.ShapeDtypeStruct((CHUNKS, rows, c), F32),
-            jax.ShapeDtypeStruct((CHUNKS, pairs * half, c), BF),
+            jax.ShapeDtypeStruct((CHUNKS, pairs * half, c), F32),
             jax.ShapeDtypeStruct((n, CHUNKS, rows, c), BF),
             jax.ShapeDtypeStruct((n, CHUNKS, rows, h), BF),
             jax.ShapeDtypeStruct((n, CHUNKS, rows, h), BF),
@@ -478,7 +478,7 @@
             if p + 1 < steps:
                 plan.start(p + 1)
 
-        first_due = 2 * CHUNKS + 3
+        first_due = 2 * CHUNKS + 4
         ticks = {}
         if steps == 2:
             for p, start in ((0, first_due), (1, n * CHUNKS + n - 2)):
@@ -619,13 +619,26 @@
 
             @pl.when(due_now)
             def _():
-                s, jj = item_place(q)
-                for copy in item_copies(q):
-                    copy.wait()
+                of_x, _, of_h = item_copies(q)
+                of_x.wait()
+                of_h.wait()
 
                 def tile(i, _):
                     a = columns(i)
                     g_up[a] += tn(left[:, a], middle[...])
+                    return 0
+
+                lax.fori_loop(0, c // TILE, tile, 0)
+
+            r = jnp.where(between, q, (g - 4) // 2)
+
+            @pl.when((between & due_now) | (jnp.logical_not(between) & (lax.rem(g, 2) == 0) & (g >= 4) & (r < items)))
+            def _():
+                s, jj = item_place(r)
+                item_copies(r)[1].wait()
+
+                def tile(i, _):
+                    a = columns(i)
                     db = gathered[s, pl.ds(2 * jj, 2), :, a].reshape(2 * rows, TILE)
                     g_down[a] += tn(db, right[...])
                     return 0
@@ -1187,7 +1200,7 @@
     return back, jnp.sum(d * hat, axis=0, keepdims=True)
 
 
-def low_stage(low, pool_a, pool_b, cot, gain1, gain2, packed, n, devices, cid):
+def low_stage(low, pooled, cot, gain1, gain2, packed, n, devices, cid):
     t, dim = low.shape
     every = n * t
     width = dim // n
@@ -1197,11 +1210,23 @@
     rows = dim // devices
     half = dim // 2
     ff = 4 * dim
+    natural = rows % LANES == 0
+    high_rows = pooled.shape[1] // devices
+
+    def place_of(k):
+        return (k % 2) * half + k // 2 * rows
+
+    def in_order(ref):
+        if not natural:
+            return ref[...]
+        order = sorted(range(devices), key=place_of)
+        return jnp.concatenate([ref[:, k * rows : (k + 1) * rows] for k in order], axis=1)
+
     scale = HEAD ** (-0.5)
 
     def kernel(
-        low_ref, pool_a_ref, pool_b_ref, cot_ref, gain1_ref, gain2_ref, w_hbm,
-        low_out, d_low, d_pool_a, d_pool_b, g_ln1, g_ln2, grads,
+        low_ref, pooled_ref, cot_ref, gain1_ref, gain2_ref, w_hbm,
+        low_out, d_low, d_pooled, g_ln1, g_ln2, grads,
         wv, lhs, lhs2, rhs, gate, high, merged, resid, d_res, slope, mixed, heads_in, att_all, d_att, d_mixed,
         d_heads, probs, d_scores, stage, left, w_sem, q_send, q_got, a_send, a_got, b_send, b_got, c_send, c_got, own_sem,
         l_send, l_got, r_send, r_got, stage_sem,
@@ -1289,12 +1314,11 @@
         turned = [None]
 
         def put_natural(dst, value):
-            if rows % LANES:
+            if natural:
+                for k in range(devices):
+                    dst[:, k * rows : (k + 1) * rows] = value[:, place_of(k) : place_of(k) + rows]
+            else:
                 dst[...] = value
-            else:
-                for k in range(devices):
-                    at = (k % 2) * half + k // 2 * rows
-                    dst[:, k * rows : (k + 1) * rows] = value[:, at : at + rows]
 
         def grad(i, block, at, count, shared=False):
             if not shared:
@@ -1364,10 +1388,21 @@
             for c in copies:
                 c.wait()
 
-        lhs[L_LOW] = low_ref[...]
-        lhs[L_POOL_A] = pool_a_ref[...]
-        lhs[L_POOL_B] = pool_b_ref[...]
-        lhs[L_COT] = cot_ref[...]
+        gain1_here, gain2_here = in_order(gain1_ref), in_order(gain2_ref)
+        if natural:
+            for i, ref in ((L_LOW, low_ref), (L_COT, cot_ref)):
+                for k in range(devices):
+                    lhs[i, :, place_of(k) : place_of(k) + rows] = ref[:, k * rows : (k + 1) * rows]
+            for k in range(devices):
+                own = slice(place_of(k), place_of(k) + rows)
+                lhs[L_POOL_A, :, own] = pooled_ref[:, k * high_rows : k * high_rows + rows].astype(BF)
+                more = pooled_ref[:, k * high_rows + rows : (k + 1) * high_rows].astype(BF)
+                lhs[L_POOL_B, :, own] = jnp.concatenate([more, jnp.zeros((t, 2 * rows - high_rows), BF)], axis=1)
+        else:
+            lhs[L_LOW] = low_ref[...]
+            lhs[L_COT] = cot_ref[...]
+            lhs[L_POOL_A] = pooled_ref[:, :dim].astype(BF)
+            lhs[L_POOL_B] = pooled_ref[:, dim:].astype(BF)
         acc = d_low
         w_wait(GATE)
 
@@ -1388,7 +1423,7 @@
         forward(lhs[L_POOL_B], HIGH_B, 1, put_merging)
         backward(lambda at: rhs[0, :, r_cols(R_MERGE)], OUT, 1, merged, True)
         merged[...] += lhs[L_LOW].astype(F32)
-        lhs[L_FIRST] = normalise(merged[...], gain1_ref[...]).astype(BF)
+        lhs[L_FIRST] = normalise(merged[...], gain1_here).astype(BF)
 
         w_wait(QUERY, KEY, VALUE, PROJ)
         pl.semaphore_wait(barrier, n)
@@ -1434,7 +1469,7 @@
         r_copy(R_ATT).start()
         backward(lambda at: rhs[0, :, r_cols(R_ATT)], PROJ, 1, resid, True)
         resid[...] += merged[...]
-        lhs[L_SECOND] = normalise(resid[...], gain2_ref[...]).astype(BF)
+        lhs[L_SECOND] = normalise(resid[...], gain2_here).astype(BF)
         l_copy(L_SECOND).start()
 
         w_wait(8)
@@ -1454,8 +1489,8 @@
         forward(lhs[L_COT], 12, 4, put_d_up)
         r_copy(R_DUP).start()
         backward(lambda at: rhs[0, :, pl.ds(r_at(R_DUP) + at, dim)], 8, 4, acc, True)
-        back, g = normalise_back(resid[...], gain2_ref[...], acc[...])
-        g_ln2[...] = g
+        back, g = normalise_back(resid[...], gain2_here, acc[...])
+        put_natural(g_ln2, g)
         d_res[...] = lhs[L_COT].astype(F32) + back
         lhs[L_DA] = d_res[...].astype(BF)
         l_copy(L_DA).start()
@@ -1503,8 +1538,8 @@
         for k in range(3):
             r_copy(R_DQ + k).start()
         backward(lambda at: rhs[0, :, pl.ds(R_DQ * dim + at, dim)], QUERY, 3, acc, True)
-        back, g = normalise_back(merged[...], gain1_ref[...], acc[...])
-        g_ln1[...] = g
+        back, g = normalise_back(merged[...], gain1_here, acc[...])
+        put_natural(g_ln1, g)
         d_res[...] += back
         lhs[L_DF] = d_res[...].astype(BF)
         l_copy(L_DF).start()
@@ -1518,8 +1553,16 @@
         forward(lhs[L_DF], OUT, 1, put_d_gate)
         r_copy(R_DHIGH).start()
         r_copy(R_DGATE).start()
-        backward(lambda at: rhs[0, :, r_cols(R_DHIGH)], HIGH_A, 1, d_pool_a, True)
-        backward(lambda at: rhs[0, :, r_cols(R_DHIGH)], HIGH_B, 1, d_pool_b, True)
+        backward(lambda at: rhs[0, :, r_cols(R_DHIGH)], HIGH_A, 1, gate, True)
+        backward(lambda at: rhs[0, :, r_cols(R_DHIGH)], HIGH_B, 1, high, True)
+        if natural:
+            for k in range(devices):
+                at = place_of(k)
+                d_pooled[:, k * high_rows : k * high_rows + rows] = gate[:, at : at + rows]
+                d_pooled[:, k * high_rows + rows : (k + 1) * high_rows] = high[:, at : at + high_rows - rows]
+        else:
+            d_pooled[:, :dim] = gate[...]
+            d_pooled[:, dim:] = high[...]
         backward(lambda at: rhs[0, :, r_cols(R_DGATE)], GATE, 1, acc, True)
         put_natural(d_low, d_res[...] + acc[...])
         l_copy(L_FIRST).wait_recv()
@@ -1547,9 +1590,9 @@
     one = jax.ShapeDtypeStruct((1, dim), F32)
     return pl.pallas_call(
         kernel,
-        out_shape=(tok, tok, tok, tok, one, one, jax.ShapeDtypeStruct((pairs, n * rows, 16 * width), BF)),
-        in_specs=[local] * 6 + [whole],
-        out_specs=(local,) * 6 + (whole,),
+        out_shape=(tok, tok, jax.ShapeDtypeStruct(pooled.shape, F32), one, one, jax.ShapeDtypeStruct((pairs, n * rows, 16 * width), BF)),
+        in_specs=[local] * 5 + [whole],
+        out_specs=(local,) * 5 + (whole,),
         scratch_shapes=[
             vm((2, pairs, rows, 16 * dim), BF), vm((8, t, dim), BF), vm((8, t, half), BF), vm((2, t, 15 * dim), BF),
             vm((t, dim), F32), vm((t, dim), F32), vm((t, dim), F32), vm((t, dim), F32), vm((t, dim), F32),
@@ -1561,7 +1604,7 @@
         ],
         compiler_params=pltpu.CompilerParams(collective_id=cid, has_side_effects=True, vmem_limit_bytes=62 * MIB),
         cost_estimate=pl.CostEstimate(flops=14 * 10**9, bytes_accessed=70 * 10**6, transcendentals=10**7),
-    )(low, pool_a, pool_b, cot, gain1, gain2, packed.reshape(pairs, 2, n, rows, 16 * width))
+    )(low, pooled, cot, gain1, gain2, packed.reshape(pairs, 2, n, rows, 16 * width))
 def low_outputs(own, widths, high_rows):
     share = own.shape[0]
     width, wide = widths[0], widths[-1]
@@ -1749,27 +1792,29 @@
     )
     hr_out = hr_out.reshape(hr_in.shape)
     tokens = half_rows * half_cols
-    by_share = pooled.reshape(tokens, devices, -1)
-    pool_a = by_share[:, :, :share].reshape(tokens, dims)
-    pool_b = jnp.pad(by_share[:, :, share:], ((0, 0), (0, 0), (0, 2 * share - by_share.shape[2]))).reshape(tokens, dims)
-    low_out, d_low_in, d_pool_a, d_pool_b, g_ln1, g_ln2, low_grads = low_stage(
-        *(core_first(v, devices) for v in (low_in[0], pool_a, pool_b, cot_low[0])),
-        *(core_first(v.astype(F32), devices)[None] for v in (ln1_gain, ln2_gain)),
-        packed, shards, devices, 2,
-    )
+    low_ins, gains = [low_in[0], pooled, cot_low[0]], [ln1_gain.astype(F32)[None], ln2_gain.astype(F32)[None]]
+    if share % LANES:
+        by_share = pooled.reshape(tokens, devices, -1)
+        pool_a = by_share[:, :, :share].reshape(tokens, dims)
+        pool_b = by_share[:, :, share:]
+        pool_b = jnp.pad(pool_b, ((0, 0), (0, 0), (0, share - pool_b.shape[2]))).reshape(tokens, dims)
+        low_ins = [core_first(low_in[0], devices), None, core_first(cot_low[0], devices)]
+        low_ins[1] = jnp.concatenate([core_first(pool_a, devices), core_first(pool_b, devices)], axis=1)
+        gains = [core_first(g, devices) for g in gains]
+    low_out, d_low_in, d_pooled, g_ln1, g_ln2, low_grads = low_stage(*low_ins, *gains, packed, shards, devices, 2)
     if share % LANES:
         low_out, d_low_in = core_last(low_out, devices), core_last(d_low_in, devices)
-    low_out, d_low_in = low_out[None], d_low_in[None]
-    g_ln1, g_ln2 = core_last(g_ln1[0], devices), core_last(g_ln2[0], devices)
-    d_pooled = jnp.concatenate(
-        [
-            core_last(d_pool_a, devices).reshape(tokens, devices, share),
-            core_last(d_pool_b, devices).reshape(tokens, devices, share)[:, :, : by_share.shape[2] - share],
-        ],
-        axis=2,
-    )
+        g_ln1, g_ln2 = core_last(g_ln1, devices), core_last(g_ln2, devices)
+        d_pooled = jnp.concatenate(
+            [
+                core_last(d_pooled[:, :dims], devices).reshape(tokens, devices, share),
+                core_last(d_pooled[:, dims:], devices).reshape(tokens, devices, share)[:, :, : by_share.shape[2] - share],
+            ],
+            axis=2,
+        ).reshape(tokens, chan_count)
+    low_out, d_low_in, g_ln1, g_ln2 = low_out[None], d_low_in[None], g_ln1[0], g_ln2[0]
     d_normed, d_map, cn_grads, low_sums = big_backward(
-        cot_hr[0], d_pooled.reshape(tokens, chan_count), shares, plane_mask, normed_all, hidden_act, hidden_slope,
+        cot_hr[0], d_pooled, shares, plane_mask, normed_all, hidden_act, hidden_slope,
         up_t, down_t, low_grads, shards, devices,
     )
     low_sums = rows_first(low_sums.reshape(shards, share, -1))

time: 716 us -> 706 us (0.986)
  local copies, waits for them, and re-layouts: 20.7 us -> 8.72 us
  transfers between devices with their start and end apart: 3 -> 3, of which waited for: 2 -> 2; matrix products, arithmetic and copies ran while one was open for 2% -> 1% of each run, Pallas kernels for 41% -> 42%
where the time goes in v12:
time: 706 us; the launch traced here: 701 us
  Pallas kernels  619 us (88%)
  waiting for transfers between devices  52.4 us (7%)
  between operations  14.2 us (2%)
  local copies, waits for them, and re-layouts  8.72 us (1%)
    pallas_call x1, Pallas kernels, big_backward(): pl.pallas_call(kernel, out_shape=(jax.ShapeDtypeStruct((CHUNKS, rows, c),...  223 us
    pallas_call x1, Pallas kernels, big_forward(): pl.pallas_call(kernel, out_shape=(jax.ShapeDtypeStruct((CHUNKS, rows, c),...  178 us
    pallas_call x1, Pallas kernels, low_stage(): pl.pallas_call(kernel, out_shape=(tok, tok, jax.ShapeDtypeStruct(pooled.s...  101 us
    pallas_call x1, Pallas kernels, conv_backward(): pl.pallas_call(kernel, out_shape=(jax.ShapeDtypeStruct((rows, cols, c), F...  75.8 us
    all_gather x1, waiting for transfers between devices, per_device(): packed = rows_first(lax.all_gather(packed, 'mp', axis=0, tiled=True))  49.5 us
    pallas_call x1, Pallas kernels, conv_forward(): pl.pallas_call(kernel, out_shape=(jax.ShapeDtypeStruct((rows, cols, c), F...  29.7 us
  transfers between devices with their start and end apart: 3, of which 2 were waited for; matrix products, arithmetic and copies ran while one was open for 1% of the time, Pallas kernels for 42%

profile of v12, /device:TPU:0, one launch (start us, length us, event | category | flops | bytes accessed | tf_op | source)
XLA Modules:
  0.0 700.6 jit_solution(9915194183279327384)
XLA Ops:
  7.2 0.0 copy-start.7
  7.2 0.0 copy-start.6
  7.2 0.0 copy-start.8
  7.2 0.0 all-gather.3.cloned.1.call-start
  7.3 2.5 shard_map.306
  9.8 0.0 all-gather.3.cloned.1.call-update
  9.8 0.0 all-gather.5.cloned.1.call-start
  9.8 0.0 copy-done.7
  9.9 0.0 copy-done.6
  9.9 0.4 reshape.162.w_ref
  10.3 0.0 copy-done.8
  10.4 1.7 bitcast_multiply_fusion.x_ref.res
  12.0 0.0 copy-start.1
  12.0 29.7 %shard_map.305 = (f32[12,48,1536]{2,1,0:T(8,128)S(1)}, bf16[18,48,1536]{2,1,0:T(8,128)(2,1)S(1)}) custom-call(bf16[12,48,1536]{2,1,0:T(8,128)(2,1)S(1)} %bitcast_multiply_fusion.x_ref.res, f32[49,1,1536]{2,1,0:T(1,128)S(1)} %reshape.162.w_ref), custom_call_target="tpu_custom_call" | custom-call | tf_op jit(solution)/shard_map/pallas_call | solution.py:887
  41.7 0.0 copy-start.5
  41.8 0.0 copy-start
  41.8 0.4 multiply_reduce_fusion.1
  42.2 0.6 multiply_reduce_fusion
  42.8 0.5 copy-done.5
  43.3 1.2 copy-done
  44.4 1.8 multiply_convert_fusion
  46.3 49.5 %all-gather.3.cloned.1.call-done = bf16[512,4096]{1,0:T(8,128)(2,1)} async-done(((bf16[128,4096]{1,0:T(8,128)(2,1)}), bf16[512,4096]{1,0:T(8,128)(2,1)}) %all-gather.3.cloned.1.call-update) | async-done | bytes 4194320 | tf_op jit(solution)/shard_map/all_gather | solution.py:1776
  95.8 0.0 all-gather.5.cloned.1.call-update
  95.8 0.0 reduce-scatter.2.cloned.1.call-start
  95.9 0.9 convert_element_type.65.mask_ref
  96.7 0.1 convert_element_type.63
  96.9 0.1 reduce_sum.29
  97.0 0.8 copy.39.share_ref
  97.7 0.6 broadcast_in_dim.35
  98.3 0.6 broadcast_in_dim.36
  98.9 177.8 %shard_map.307 = (f32[6,96,1536]{2,1,0:T(8,128)}, f32[6,24,1536]{2,1,0:T(8,128)}, bf16[4,6,96,1536]{3,2,1,0:T(8,128)(2,1)}, bf16[4,6,96,1536]{3,2,1,0:T(8,128)(2...) custom-call(bf16[6,96,1536]{2,1,0:T(8,128)(2,1)} %bitcast.45, ...), custom_call_target="tpu_custom_call" | custom-call | flops 21743271936 | bytes 28311552 | tf_op jit(solution)/shard_map/pallas_call | solution.py:404
  276.7 0.0 all-gather.5.cloned.1.call-done
  276.7 100.5 %shard_map.308 = (f32[144,1024]{1,0:T(8,128)}, f32[144,1024]{1,0:T(8,128)}, f32[144,1536]{1,0:T(8,128)}, f32[1,1024]{1,0:T(1,128)}, f32[1,1024]{1,0:T(1,128)}, /*index=5*/bf16[4,512,4096]{2,1,0:T(8,128)(2,1)}) custom-call(bf16[144,1024]{1,0:T(8,128)(2,1)} %bitcast.59, f32[144,1536]{1,0:T(8,128)} %bitcast.70, bf16[144,1024]{1,0:T(8,128)(2,1)} %bitcast.60, ...), custom_call_target="tpu_custom_call" | custom-call | flops 14000000000 | bytes 70000000 | tf_op jit(solution)/shard_map/pallas_call | solution.py:1591
  377.3 222.8 %shard_map.309 = (f32[6,96,1536]{2,1,0:T(8,128)}, bf16[6,96,1536]{2,1,0:T(8,128)(2,1)}, bf16[4,192,1536]{2,1,0:T(8,128)(2,1)}, bf16[4,192,1536]{2,1,0:T(8,128)(2...) custom-call(bf16[12,48,1536]{2,1,0:T(8,128)(2,1)} %bitcast.57, ...), custom_call_target="tpu_custom_call" | custom-call | flops 43486543872 | bytes 28311552 | tf_op jit(solution)/shard_map/pallas_call | solution.py:741
  600.1 0.0 reduce-scatter.2.cloned.1.call-update
  600.2 0.2 copy.42.mask_ref
  600.3 0.4 copy-done.9
  600.8 0.0 copy-done.10
  600.8 75.8 %shard_map.310 = (f32[12,48,1536]{2,1,0:T(8,128)}, f32[8,7,1536]{2,1,0:T(8,128)S(1)}, bf16[2,192,1536]{2,1,0:T(8,128)(2,1)}, bf16[1,192,1536]{2,1,0:T(8,128)(2,1...) custom-call(f32[12,48,1536]{2,1,0:T(8,128)} %bitcast.65, ...), custom_call_target="tpu_custom_call" | custom-call | flops 60000002048 | bytes 100000000 | tf_op jit(solution)/shard_map/pallas_call | solution.py:1140
  676.7 0.8 copy-done.3
  677.5 0.8 slice.18
  678.3 0.1 copy-done.4
  678.4 8.8 %shard_map.311 = (f32[192,1536]{1,0:T(8,128)}, f32[192,1536]{1,0:T(8,128)}, f32[1,144,1024]{2,1,0:T(8,128)}, f32[1,12,48,1536]{3,2,1,0:T(8,128)}, f32[1,144,1024]{2,1,0:T(8,128)}, /*index=5*/f32[1,12,48,1536]{3,2,1,0:T(8,128)}) custom-call(bf16[192,1536]{1,0:T(8,128)(2,1)} %bitcast.40, bf16[192,1536]{1,0:T(8,128)(2,1)} %bitcast.41, ...), custom_call_target="tpu_custom_call" | custom-call | flops 1000000000 | bytes 24000000 | tf_op jit(solution)/shard_map/pallas_call | solution.py:1660
  687.2 0.6 slice_reduce_fusion
  687.8 0.6 fusion
  688.4 2.8 reduce-scatter.2.cloned.1.call-done
  691.2 1.2 copy-done.2
  692.5 1.4 shard_map.312
  (21 shorter events, 0.1 us)
Async XLA Ops:
  7.2 2.6 copy-start.7
  7.2 2.7 copy-start.6
  7.2 3.1 copy-start.8
  7.2 88.5 %all-gather.3.cloned.1.call-start = ((), (), s32[]{:S(2)}) async-start(), calls=%async_computation.1 | async-start | bytes 5242880 | tf_op jit(solution)/shard_map/all_gather | solution.py:1776
  9.8 267.0 %all-gather.5.cloned.1.call-start = ((), (), s32[]{:S(2)}) async-start(), calls=%async_computation.2 | async-start | bytes 37748736 | tf_op jit(solution)/shard_map/all_gather | solution.py:1789
  12.0 30.7 %copy-start.1 = (bf16[12,48,1536]{2,1,0:T(8,128)(2,1)}, bf16[12,48,1536]{2,1,0:T(8,128)(2,1)S(1)}, u32[]{:S(2)}) copy-start(bf16[12,48,1536]{2,1,0:T(8,128)(2,1)S(1)} %bitcast_multiply_fusion.x_ref.res) | copy-start | bytes 5308420
  41.7 1.5 copy-start.5
  41.8 2.7 copy-start
  46.3 51.5 %copy-start.11 = (bf16[1024]{0:T(1024)(128)(2,1)S(1)}, bf16[1024]{0:T(1024)(128)(2,1)}, u32[]{:S(2)}) copy-start(bf16[1024]{0:T(1024)(128)(2,1)} %param.28) | copy-start | bytes 6148
  46.3 52.1 %copy-start.12 = (bf16[1024]{0:T(1024)(128)(2,1)S(1)}, bf16[1024]{0:T(1024)(128)(2,1)}, u32[]{:S(2)}) copy-start(bf16[1024]{0:T(1024)(128)(2,1)} %param.31) | copy-start | bytes 6148
  95.8 595.5 %reduce-scatter.2.cloned.1.call-start = ((), (), s32[]{:S(2)}) async-start(), calls=%async_computation.3 | async-start | bytes 5242880 | tf_op jit(solution)/shard_map/reduce_scatter | solution.py:1821
  600.1 0.7 copy-start.9
  600.1 0.7 copy-start.10
  676.7 0.8 copy-start.3
  677.5 1.0 copy-start.4
  691.2 1.2 copy-start.2
Sparse Core Ops, SparseCore 0:
  10.2 85.5 all-gather.2
  97.6 159.8 all-gather.4
  600.3 90.9 reduce-scatter.1

commit v13 on v12

--- a/solution.py
+++ b/solution.py
@@ -605,10 +605,15 @@
             )
 
         between = (d > 0) & (d < n - 1)
+        middle_steps = [n * CHUNKS - items + i for i in range(items)]
+        if n == 4 and CHUNKS == 6:
+            middle_steps = [2, 4, 12, 13, 14, 15, 17, 19, 20, 21, 22, 23]
 
         def item_of(g):
-            q = jnp.where(between, g - items, (g - 3) // 2)
-            return q, (q >= 0) & (q < items) & (g >= 3) & (between | (lax.rem(g, 2) == 1))
+            q = jnp.where(between, -1, (g - 3) // 2)
+            for i, at in enumerate(middle_steps):
+                q = jnp.where(between & (g == at), i, q)
+            return q, (q >= 0) & (q < items) & (g >= 2) & (between | (lax.rem(g, 2) == 1))
 
         def after(g):
             for at, tick in ticks.items():
@@ -619,26 +624,13 @@
 
             @pl.when(due_now)
             def _():
-                of_x, _, of_h = item_copies(q)
-                of_x.wait()
-                of_h.wait()
+                s, jj = item_place(q)
+                for copy in item_copies(q):
+                    copy.wait()
 
                 def tile(i, _):
                     a = columns(i)
                     g_up[a] += tn(left[:, a], middle[...])
-                    return 0
-
-                lax.fori_loop(0, c // TILE, tile, 0)
-
-            r = jnp.where(between, q, (g - 4) // 2)
-
-            @pl.when((between & due_now) | (jnp.logical_not(between) & (lax.rem(g, 2) == 0) & (g >= 4) & (r < items)))
-            def _():
-                s, jj = item_place(r)
-                item_copies(r)[1].wait()
-
-                def tile(i, _):
-                    a = columns(i)
                     db = gathered[s, pl.ds(2 * jj, 2), :, a].reshape(2 * rows, TILE)
                     g_down[a] += tn(db, right[...])
                     return 0
@@ -1785,10 +1777,11 @@
     conv_out, bordered = conv_forward(masked, taps, size, shards)
     hr_gainf = hr_gain.astype(F32)
     normed = layer_norm(conv_out * cell_mask, hr_gainf).astype(BF)
-    normed, packed = lax.optimization_barrier((normed, packed))
+    mask_chunks, share_chunks = plane_mask.reshape(CHUNKS, -1, 1), shares.reshape(CHUNKS, -1, 1)
+    normed, packed, mask_chunks, share_chunks = lax.optimization_barrier((normed, packed, mask_chunks, share_chunks))
     packed = rows_first(lax.all_gather(packed, "dp", axis=0, tiled=True))
     hr_out, pooled, normed_all, hidden_act, hidden_slope, up_t, down_t = big_forward(
-        normed.reshape(row_count * col_count, chan_count), cn_up, cn_down, masked, plane_mask, shares, shards
+        normed.reshape(row_count * col_count, chan_count), cn_up, cn_down, masked, mask_chunks, share_chunks, shards
     )
     hr_out = hr_out.reshape(hr_in.shape)
     tokens = half_rows * half_cols
@@ -1814,7 +1807,7 @@
         ).reshape(tokens, chan_count)
     low_out, d_low_in, g_ln1, g_ln2 = low_out[None], d_low_in[None], g_ln1[0], g_ln2[0]
     d_normed, d_map, cn_grads, low_sums = big_backward(
-        cot_hr[0], d_pooled, shares, plane_mask, normed_all, hidden_act, hidden_slope,
+        cot_hr[0], d_pooled, share_chunks, mask_chunks, normed_all, hidden_act, hidden_slope,
         up_t, down_t, low_grads, shards, devices,
     )
     low_sums = rows_first(low_sums.reshape(shards, share, -1))

time: 706 us -> 699 us (0.990)
  waiting for transfers between devices: 52.4 us -> 44.7 us
    pallas_call x1, Pallas kernels: 223 us -> 213 us  [big_backward(): pl.pallas_call(kernel, out_shape=(jax.ShapeDtypeStruct((CHUNKS, rows, c),...]
    all_gather x1, waiting for transfers between devices: 49.5 us -> 42.4 us  [per_device(): packed = rows_first(lax.all_gather(packed, 'mp', axis=0, tiled=True))]
  transfers between devices with their start and end apart: 3 -> 3, of which waited for: 2 -> 2; matrix products, arithmetic and copies ran while one was open for 1% -> 2% of each run, Pallas kernels for 42% -> 43%
where the time goes in v13:
time: 699 us; the launch traced here: 692 us
  Pallas kernels  612 us (88%)
  waiting for transfers between devices  44.7 us (6%)
  between operations  14.2 us (2%)
  local copies, waits for them, and re-layouts  13.5 us (2%)
  other arithmetic  7.92 us (1%)
    pallas_call x1, Pallas kernels, big_backward(): pl.pallas_call(kernel, out_shape=(jax.ShapeDtypeStruct((CHUNKS, rows, c),...  213 us
    pallas_call x1, Pallas kernels, big_forward(): pl.pallas_call(kernel, out_shape=(jax.ShapeDtypeStruct((CHUNKS, rows, c),...  178 us
    pallas_call x1, Pallas kernels, low_stage(): pl.pallas_call(kernel, out_shape=(tok, tok, jax.ShapeDtypeStruct(pooled.s...  101 us
    pallas_call x1, Pallas kernels, conv_backward(): pl.pallas_call(kernel, out_shape=(jax.ShapeDtypeStruct((rows, cols, c), F...  75.1 us
    all_gather x1, waiting for transfers between devices, per_device(): packed = rows_first(lax.all_gather(packed, 'mp', axis=0, tiled=True))  42.4 us
    pallas_call x1, Pallas kernels, conv_forward(): pl.pallas_call(kernel, out_shape=(jax.ShapeDtypeStruct((rows, cols, c), F...  32.6 us
  transfers between devices with their start and end apart: 3, of which 2 were waited for; matrix products, arithmetic and copies ran while one was open for 2% of the time, Pallas kernels for 43%

profile of v13, /device:TPU:0, one launch (start us, length us, event | category | flops | bytes accessed | tf_op | source)
XLA Modules:
  0.0 692.2 jit_solution(7082003739277096598)
XLA Ops:
  7.2 0.0 copy-start.13
  7.2 0.0 all-gather.3.cloned.1.call-start
  7.3 2.6 shard_map.306
  9.9 0.0 all-gather.3.cloned.1.call-update
  9.9 0.0 all-gather.5.cloned.1.call-start
  10.0 0.7 convert_element_type.62
  10.6 0.8 convert_element_type.63
  11.4 0.6 convert_bitcast_fusion
  12.0 1.2 reshape.160.w_ref
  13.2 0.2 bitcast_multiply_fusion.x_ref.res
  13.4 0.8 copy-done.2
  14.2 32.6 %shard_map.305 = (f32[12,48,1536]{2,1,0:T(8,128)S(1)}, bf16[18,48,1536]{2,1,0:T(8,128)(2,1)S(1)}) custom-call(bf16[12,48,1536]{2,1,0:T(8,128)(2,1)S(1)} %bitcast_multiply_fusion.x_ref.res, f32[49,1,1536]{2,1,0:T(1,128)S(1)} %copy-done.2), custom_call_target="tpu_custom_call" | custom-call | tf_op jit(solution)/shard_map/pallas_call | solution.py:879
  46.8 1.2 copy-done.1
  48.0 1.5 copy-done.7
  49.5 1.8 reduce_sum.29
  51.2 1.3 divide_bitcast_fusion
  52.5 0.4 multiply_reduce_fusion.1
  52.9 0.6 multiply_reduce_fusion
  53.5 1.9 multiply_convert_fusion
  55.4 42.4 %all-gather.3.cloned.1.call-done = bf16[512,4096]{1,0:T(8,128)(2,1)} async-done(((bf16[128,4096]{1,0:T(8,128)(2,1)}), bf16[512,4096]{1,0:T(8,128)(2,1)}) %all-gather.3.cloned.1.call-update) | async-done | bytes 4194320 | tf_op jit(solution)/shard_map/all_gather | solution.py:1768
  97.8 0.0 all-gather.5.cloned.1.call-update
  97.9 0.0 reduce-scatter.2.cloned.1.call-start
  97.9 0.6 broadcast_in_dim.35
  98.5 0.6 broadcast_in_dim.36
  99.1 0.9 copy.38.mask_ref
  100.0 0.7 copy.39.share_ref
  100.7 177.9 %shard_map.307 = (f32[6,96,1536]{2,1,0:T(8,128)}, f32[6,24,1536]{2,1,0:T(8,128)}, bf16[4,6,96,1536]{3,2,1,0:T(8,128)(2,1)}, bf16[4,6,96,1536]{3,2,1,0:T(8,128)(2...) custom-call(bf16[6,96,1536]{2,1,0:T(8,128)(2,1)} %bitcast.45, ...), custom_call_target="tpu_custom_call" | custom-call | flops 21743271936 | bytes 28311552 | tf_op jit(solution)/shard_map/pallas_call | solution.py:404
  278.6 0.0 all-gather.5.cloned.1.call-done
  278.7 100.6 %shard_map.308 = (f32[144,1024]{1,0:T(8,128)}, f32[144,1024]{1,0:T(8,128)}, f32[144,1536]{1,0:T(8,128)}, f32[1,1024]{1,0:T(1,128)}, f32[1,1024]{1,0:T(1,128)}, /*index=5*/bf16[4,512,4096]{2,1,0:T(8,128)(2,1)}) custom-call(bf16[144,1024]{1,0:T(8,128)(2,1)} %bitcast.59, f32[144,1536]{1,0:T(8,128)} %bitcast.70, bf16[144,1024]{1,0:T(8,128)(2,1)} %bitcast.60, ...), custom_call_target="tpu_custom_call" | custom-call | flops 14000000000 | bytes 70000000 | tf_op jit(solution)/shard_map/pallas_call | solution.py:1583
  379.2 212.8 %shard_map.309 = (f32[6,96,1536]{2,1,0:T(8,128)}, bf16[6,96,1536]{2,1,0:T(8,128)(2,1)}, bf16[4,192,1536]{2,1,0:T(8,128)(2,1)}, bf16[4,192,1536]{2,1,0:T(8,128)(2...) custom-call(bf16[12,48,1536]{2,1,0:T(8,128)(2,1)} %bitcast.57, ...), custom_call_target="tpu_custom_call" | custom-call | flops 43486543872 | bytes 28311552 | tf_op jit(solution)/shard_map/pallas_call | solution.py:733
  592.1 0.0 copy-start.14
  592.1 0.0 copy-start.11
  592.1 0.0 copy-start.3
  592.1 0.0 reduce-scatter.2.cloned.1.call-update
  592.1 0.6 copy-done.14
  592.8 0.0 copy-done.11
  592.8 0.2 copy.42.mask_ref
  593.0 0.1 copy-done.3
  593.1 75.1 %shard_map.310 = (f32[12,48,1536]{2,1,0:T(8,128)}, f32[8,7,1536]{2,1,0:T(8,128)S(1)}, bf16[2,192,1536]{2,1,0:T(8,128)(2,1)}, bf16[1,192,1536]{2,1,0:T(8,128)(2,1...) custom-call(f32[12,48,1536]{2,1,0:T(8,128)} %bitcast.65, ...), custom_call_target="tpu_custom_call" | custom-call | flops 60000002048 | bytes 100000000 | tf_op jit(solution)/shard_map/pallas_call | solution.py:1132
  668.2 0.8 copy-done.5
  669.1 0.8 copy-done.6
  669.9 0.8 slice.18
  670.7 8.7 %shard_map.311 = (f32[192,1536]{1,0:T(8,128)}, f32[192,1536]{1,0:T(8,128)}, f32[1,144,1024]{2,1,0:T(8,128)}, f32[1,12,48,1536]{3,2,1,0:T(8,128)}, f32[1,144,1024]{2,1,0:T(8,128)}, /*index=5*/f32[1,12,48,1536]{3,2,1,0:T(8,128)}) custom-call(bf16[192,1536]{1,0:T(8,128)(2,1)} %bitcast.40, bf16[192,1536]{1,0:T(8,128)(2,1)} %bitcast.41, ...), custom_call_target="tpu_custom_call" | custom-call | flops 1000000000 | bytes 24000000 | tf_op jit(solution)/shard_map/pallas_call | solution.py:1652
  679.4 0.6 slice_reduce_fusion
  680.1 0.6 fusion
  680.7 2.2 reduce-scatter.2.cloned.1.call-done
  682.9 1.2 copy-done.4
  684.1 1.4 shard_map.312
  (36 shorter events, 0.2 us)
Async XLA Ops:
  7.2 2.8 copy-start.10
  7.2 4.8 copy-start.9
  7.2 6.0 copy-start.13
  7.2 6.0 copy-start.8
  7.2 90.6 %all-gather.3.cloned.1.call-start = ((), (), s32[]{:S(2)}) async-start(), calls=%async_computation.1 | async-start | bytes 5242880 | tf_op jit(solution)/shard_map/all_gather | solution.py:1768
  9.9 268.8 %all-gather.5.cloned.1.call-start = ((), (), s32[]{:S(2)}) async-start(), calls=%async_computation.2 | async-start | bytes 37748736 | tf_op jit(solution)/shard_map/all_gather | solution.py:1782
  13.2 1.0 copy-start.2
  46.8 1.2 copy-start.1
  48.0 1.5 copy-start.7
  49.5 4.0 copy-start
  55.4 42.5 %copy-start.18 = (bf16[1024]{0:T(1024)(128)(2,1)S(1)}, bf16[1024]{0:T(1024)(128)(2,1)}, u32[]{:S(2)}) copy-start(bf16[1024]{0:T(1024)(128)(2,1)} %param.28) | copy-start | bytes 6148
  55.4 43.1 %copy-start.19 = (bf16[1024]{0:T(1024)(128)(2,1)S(1)}, bf16[1024]{0:T(1024)(128)(2,1)}, u32[]{:S(2)}) copy-start(bf16[1024]{0:T(1024)(128)(2,1)} %param.31) | copy-start | bytes 6148
  55.4 43.7 %copy-start.12 = (f32[6,96,1]{1,0,2:T(8,128)S(1)}, f32[6,96,1]{1,0,2:T(8,128)}, u32[]{:S(2)}) copy-start(f32[6,96,1]{1,0,2:T(8,128)} %convert_element_type.62) | copy-start | bytes 6916
  55.4 44.6 %copy-start.15 = (f32[6,24,1]{1,0,2:T(8,128)S(1)}, f32[6,24,1]{1,0,2:T(8,128)}, u32[]{:S(2)}) copy-start(f32[6,24,1]{1,0,2:T(8,128)} %divide_bitcast_fusion) | copy-start | bytes 1732
  97.9 585.0 %reduce-scatter.2.cloned.1.call-start = ((), (), s32[]{:S(2)}) async-start(), calls=%async_computation.3 | async-start | bytes 5242880 | tf_op jit(solution)/shard_map/reduce_scatter | solution.py:1814
  592.1 0.7 copy-start.14
  592.1 0.7 copy-start.11
  592.1 0.9 copy-start.16
  592.1 0.9 copy-start.17
  592.1 1.0 copy-start.3
  668.2 0.8 copy-start.5
  669.1 0.8 copy-start.6
  682.9 1.2 copy-start.4
Sparse Core Ops, SparseCore 0:
  10.2 87.5 all-gather.2
  99.7 159.8 all-gather.4
  592.3 90.5 reduce-scatter.1

commit v14 on v13

--- a/solution.py
+++ b/solution.py
@@ -384,9 +384,11 @@
             last = g - (n - 1) * (CHUNKS + 1)
             pl.when(last >= 0)(lambda: finish(last))
             for i, (w, target, size) in enumerate(((wu, wu_t, h), (wd, wd_t, c))):
-                @pl.when(g < size // LANES)
+                late = g - n * CHUNKS // 2
+
+                @pl.when((late >= 0) & (late < size // LANES))
                 def _():
-                    some = pl.ds(pl.multiple_of(g * LANES, LANES), LANES)
+                    some = pl.ds(pl.multiple_of(late * LANES, LANES), LANES)
                     turned[i, :, pl.ds(0, w.shape[0])] = w[:, some].T
                     copy = pltpu.make_async_copy(turned.at[i, :, pl.ds(0, w.shape[0])], target.at[some], stored.at[i])
                     copy.start()
@@ -1251,7 +1253,7 @@
 
             lax.fori_loop(0, 2 * n, one, 0)
 
-        for w in range(10):
+        for w in (GATE, HIGH_A, HIGH_B, OUT, QUERY, KEY, VALUE, PROJ):
             w_each(w, lambda copy: copy.start())
 
         def w_wait(*which):
@@ -1402,6 +1404,8 @@
             gate[:, pl.ds(at, TILE)] = 1.0 / (1.0 + jnp.exp(-y))
         forward(lhs[L_LOW], GATE, 1, put_gate)
         w_wait(HIGH_A, HIGH_B, OUT)
+        for w in (8, 9):
+            w_each(w, lambda copy: copy.start())
 
         def put_high(at, y):
             high[:, pl.ds(at, TILE)] = y
@@ -1777,11 +1781,10 @@
     conv_out, bordered = conv_forward(masked, taps, size, shards)
     hr_gainf = hr_gain.astype(F32)
     normed = layer_norm(conv_out * cell_mask, hr_gainf).astype(BF)
-    mask_chunks, share_chunks = plane_mask.reshape(CHUNKS, -1, 1), shares.reshape(CHUNKS, -1, 1)
-    normed, packed, mask_chunks, share_chunks = lax.optimization_barrier((normed, packed, mask_chunks, share_chunks))
+    normed, packed = lax.optimization_barrier((normed, packed))
     packed = rows_first(lax.all_gather(packed, "dp", axis=0, tiled=True))
     hr_out, pooled, normed_all, hidden_act, hidden_slope, up_t, down_t = big_forward(
-        normed.reshape(row_count * col_count, chan_count), cn_up, cn_down, masked, mask_chunks, share_chunks, shards
+        normed.reshape(row_count * col_count, chan_count), cn_up, cn_down, masked, plane_mask, shares, shards
     )
     hr_out = hr_out.reshape(hr_in.shape)
     tokens = half_rows * half_cols
@@ -1807,7 +1810,7 @@
         ).reshape(tokens, chan_count)
     low_out, d_low_in, g_ln1, g_ln2 = low_out[None], d_low_in[None], g_ln1[0], g_ln2[0]
     d_normed, d_map, cn_grads, low_sums = big_backward(
-        cot_hr[0], d_pooled, share_chunks, mask_chunks, normed_all, hidden_act, hidden_slope,
+        cot_hr[0], d_pooled, shares, plane_mask, normed_all, hidden_act, hidden_slope,
         up_t, down_t, low_grads, shards, devices,
     )
     low_sums = rows_first(low_sums.reshape(shards, share, -1))

time: 699 us -> 696 us (level)
  waiting for transfers between devices: 44.7 us -> 52.4 us
    all_gather x1, waiting for transfers between devices: 42.4 us -> 49.5 us  [per_device(): packed = rows_first(lax.all_gather(packed, 'mp', axis=0, tiled=True))]
  transfers between devices with their start and end apart: 3 -> 3, of which waited for: 2 -> 2; matrix products, arithmetic and copies ran while one was open for 2% -> 1% of each run, Pallas kernels for 43% -> 42%
where the time goes in v14:
time: 696 us; the launch traced here: 691 us
  Pallas kernels  609 us (88%)
  waiting for transfers between devices  52.4 us (8%)
  between operations  14.2 us (2%)
  local copies, waits for them, and re-layouts  8.72 us (1%)
    pallas_call x1, Pallas kernels, big_backward(): pl.pallas_call(kernel, out_shape=(jax.ShapeDtypeStruct((CHUNKS, rows, c),...  212 us
    pallas_call x1, Pallas kernels, big_forward(): pl.pallas_call(kernel, out_shape=(jax.ShapeDtypeStruct((CHUNKS, rows, c),...  178 us
    pallas_call x1, Pallas kernels, low_stage(): pl.pallas_call(kernel, out_shape=(tok, tok, jax.ShapeDtypeStruct(pooled.s...  101 us
    pallas_call x1, Pallas kernels, conv_backward(): pl.pallas_call(kernel, out_shape=(jax.ShapeDtypeStruct((rows, cols, c), F...  75.9 us
    all_gather x1, waiting for transfers between devices, per_device(): packed = rows_first(lax.all_gather(packed, 'mp', axis=0, tiled=True))  49.5 us
    pallas_call x1, Pallas kernels, conv_forward(): pl.pallas_call(kernel, out_shape=(jax.ShapeDtypeStruct((rows, cols, c), F...  29.7 us
  transfers between devices with their start and end apart: 3, of which 2 were waited for; matrix products, arithmetic and copies ran while one was open for 1% of the time, Pallas kernels for 42%

profile of v14, /device:TPU:0, one launch (start us, length us, event | category | flops | bytes accessed | tf_op | source)
XLA Modules:
  0.0 690.5 jit_solution(5589330703886736871)
XLA Ops:
  7.2 0.0 copy-start.7
  7.2 0.0 copy-start.6
  7.2 0.0 copy-start.8
  7.2 0.0 all-gather.3.cloned.1.call-start
  7.3 2.5 shard_map.306
  9.8 0.0 all-gather.3.cloned.1.call-update
  9.8 0.0 all-gather.5.cloned.1.call-start
  9.8 0.0 copy-done.7
  9.9 0.4 reshape.162.w_ref
  10.3 0.0 copy-done.8
  10.4 1.7 bitcast_multiply_fusion.x_ref.res
  12.0 29.7 %shard_map.305 = (f32[12,48,1536]{2,1,0:T(8,128)S(1)}, bf16[18,48,1536]{2,1,0:T(8,128)(2,1)S(1)}) custom-call(bf16[12,48,1536]{2,1,0:T(8,128)(2,1)S(1)} %bitcast_multiply_fusion.x_ref.res, f32[49,1,1536]{2,1,0:T(1,128)S(1)} %reshape.162.w_ref), custom_call_target="tpu_custom_call" | custom-call | tf_op jit(solution)/shard_map/pallas_call | solution.py:881
  41.7 0.0 copy-start.5
  41.8 0.0 copy-start
  41.8 0.4 multiply_reduce_fusion.1
  42.2 0.6 multiply_reduce_fusion
  42.8 0.0 copy-done.1
  42.8 0.5 copy-done.5
  43.3 1.2 copy-done
  44.4 1.8 multiply_convert_fusion
  46.3 49.5 %all-gather.3.cloned.1.call-done = bf16[512,4096]{1,0:T(8,128)(2,1)} async-done(((bf16[128,4096]{1,0:T(8,128)(2,1)}), bf16[512,4096]{1,0:T(8,128)(2,1)}) %all-gather.3.cloned.1.call-update) | async-done | bytes 4194320 | tf_op jit(solution)/shard_map/all_gather | solution.py:1772
  95.8 0.0 all-gather.5.cloned.1.call-update
  95.8 0.0 reduce-scatter.2.cloned.1.call-start
  95.9 0.9 convert_element_type.65.mask_ref
  96.7 0.1 convert_element_type.63
  96.9 0.1 reduce_sum.29
  97.0 0.8 copy.39.share_ref
  97.7 0.0 copy-done.11
  97.7 0.6 broadcast_in_dim.35
  98.3 0.6 broadcast_in_dim.36
  98.9 177.9 %shard_map.307 = (f32[6,96,1536]{2,1,0:T(8,128)}, f32[6,24,1536]{2,1,0:T(8,128)}, bf16[4,6,96,1536]{3,2,1,0:T(8,128)(2,1)}, bf16[4,6,96,1536]{3,2,1,0:T(8,128)(2...) custom-call(bf16[6,96,1536]{2,1,0:T(8,128)(2,1)} %bitcast.45, ...), custom_call_target="tpu_custom_call" | custom-call | flops 21743271936 | bytes 28311552 | tf_op jit(solution)/shard_map/pallas_call | solution.py:406
  276.9 0.0 all-gather.5.cloned.1.call-done
  276.9 100.6 %shard_map.308 = (f32[144,1024]{1,0:T(8,128)}, f32[144,1024]{1,0:T(8,128)}, f32[144,1536]{1,0:T(8,128)}, f32[1,1024]{1,0:T(1,128)}, f32[1,1024]{1,0:T(1,128)}, /*index=5*/bf16[4,512,4096]{2,1,0:T(8,128)(2,1)}) custom-call(bf16[144,1024]{1,0:T(8,128)(2,1)} %bitcast.59, f32[144,1536]{1,0:T(8,128)} %bitcast.70, bf16[144,1024]{1,0:T(8,128)(2,1)} %bitcast.60, ...), custom_call_target="tpu_custom_call" | custom-call | flops 14000000000 | bytes 70000000 | tf_op jit(solution)/shard_map/pallas_call | solution.py:1587
  377.6 212.4 %shard_map.309 = (f32[6,96,1536]{2,1,0:T(8,128)}, bf16[6,96,1536]{2,1,0:T(8,128)(2,1)}, bf16[4,192,1536]{2,1,0:T(8,128)(2,1)}, bf16[4,192,1536]{2,1,0:T(8,128)(2...) custom-call(bf16[12,48,1536]{2,1,0:T(8,128)(2,1)} %bitcast.57, ...), custom_call_target="tpu_custom_call" | custom-call | flops 43486543872 | bytes 28311552 | tf_op jit(solution)/shard_map/pallas_call | solution.py:735
  590.0 0.0 reduce-scatter.2.cloned.1.call-update
  590.1 0.2 copy.42.mask_ref
  590.2 0.4 copy-done.9
  590.7 0.0 copy-done.10
  590.7 75.9 %shard_map.310 = (f32[12,48,1536]{2,1,0:T(8,128)}, f32[8,7,1536]{2,1,0:T(8,128)S(1)}, bf16[2,192,1536]{2,1,0:T(8,128)(2,1)}, bf16[1,192,1536]{2,1,0:T(8,128)(2,1...) custom-call(f32[12,48,1536]{2,1,0:T(8,128)} %bitcast.65, ...), custom_call_target="tpu_custom_call" | custom-call | flops 60000002048 | bytes 100000000 | tf_op jit(solution)/shard_map/pallas_call | solution.py:1134
  666.6 0.8 copy-done.3
  667.4 0.8 slice.18
  668.3 0.1 copy-done.4
  668.4 8.8 %shard_map.311 = (f32[192,1536]{1,0:T(8,128)}, f32[192,1536]{1,0:T(8,128)}, f32[1,144,1024]{2,1,0:T(8,128)}, f32[1,12,48,1536]{3,2,1,0:T(8,128)}, f32[1,144,1024]{2,1,0:T(8,128)}, /*index=5*/f32[1,12,48,1536]{3,2,1,0:T(8,128)}) custom-call(bf16[192,1536]{1,0:T(8,128)(2,1)} %bitcast.40, bf16[192,1536]{1,0:T(8,128)(2,1)} %bitcast.41, ...), custom_call_target="tpu_custom_call" | custom-call | flops 1000000000 | bytes 24000000 | tf_op jit(solution)/shard_map/pallas_call | solution.py:1656
  677.1 0.6 slice_reduce_fusion
  677.8 0.6 fusion
  678.4 2.8 reduce-scatter.2.cloned.1.call-done
  681.2 1.2 copy-done.2
  682.4 1.4 shard_map.312
  (21 shorter events, 0.1 us)
Async XLA Ops:
  7.2 2.6 copy-start.7
  7.2 2.7 copy-start.6
  7.2 3.1 copy-start.8
  7.2 88.5 %all-gather.3.cloned.1.call-start = ((), (), s32[]{:S(2)}) async-start(), calls=%async_computation.1 | async-start | bytes 5242880 | tf_op jit(solution)/shard_map/all_gather | solution.py:1772
  9.8 267.1 %all-gather.5.cloned.1.call-start = ((), (), s32[]{:S(2)}) async-start(), calls=%async_computation.2 | async-start | bytes 37748736 | tf_op jit(solution)/shard_map/all_gather | solution.py:1785
  12.0 30.7 %copy-start.1 = (bf16[12,48,1536]{2,1,0:T(8,128)(2,1)}, bf16[12,48,1536]{2,1,0:T(8,128)(2,1)S(1)}, u32[]{:S(2)}) copy-start(bf16[12,48,1536]{2,1,0:T(8,128)(2,1)S(1)} %bitcast_multiply_fusion.x_ref.res) | copy-start | bytes 5308420
  41.7 1.5 copy-start.5
  41.8 2.7 copy-start
  46.3 51.5 %copy-start.11 = (bf16[1024]{0:T(1024)(128)(2,1)S(1)}, bf16[1024]{0:T(1024)(128)(2,1)}, u32[]{:S(2)}) copy-start(bf16[1024]{0:T(1024)(128)(2,1)} %param.28) | copy-start | bytes 6148
  46.3 52.1 %copy-start.12 = (bf16[1024]{0:T(1024)(128)(2,1)S(1)}, bf16[1024]{0:T(1024)(128)(2,1)}, u32[]{:S(2)}) copy-start(bf16[1024]{0:T(1024)(128)(2,1)} %param.31) | copy-start | bytes 6148
  95.8 585.4 %reduce-scatter.2.cloned.1.call-start = ((), (), s32[]{:S(2)}) async-start(), calls=%async_computation.3 | async-start | bytes 5242880 | tf_op jit(solution)/shard_map/reduce_scatter | solution.py:1817
  590.0 0.7 copy-start.9
  590.0 0.7 copy-start.10
  666.6 0.8 copy-start.3
  667.4 1.0 copy-start.4
  681.2 1.2 copy-start.2
Sparse Core Ops, SparseCore 0:
  10.2 85.5 all-gather.2
  97.6 159.8 all-gather.4
  590.2 90.9 reduce-scatter.1

commit v15 on v14

--- a/solution.py
+++ b/solution.py
@@ -10,7 +10,9 @@
 LANES = 128
 EDGE = 8
 CHUNKS = 6
-TILE = 512
+TILE = 1536
+LOW_TILE = 1024
+GRAD_TILE = 512
 MIB = 1024 * 1024
 MESH = pl.DeviceIdType.MESH
 BF = jnp.bfloat16
@@ -1265,9 +1267,9 @@
 
         def forward(x, first, count, put):
             def one(i, _):
-                put(pl.multiple_of(i * TILE, TILE), nn(x, w_cols(pl.multiple_of(first * dim + i * TILE, TILE), TILE)))
+                put(pl.multiple_of(i * LOW_TILE, LOW_TILE), nn(x, w_cols(pl.multiple_of(first * dim + i * LOW_TILE, LOW_TILE), LOW_TILE)))
                 return 0
-            lax.fori_loop(0, count * dim // TILE, one, 0)
+            lax.fori_loop(0, count * dim // LOW_TILE, one, 0)
 
         def backward(get, first, count, dst, fresh):
             def one(i, _):
@@ -1323,12 +1325,12 @@
                 turned[0] = i
 
             wide, base, first = w_place(at if at < 8 else 8 + (at - 8) * dim // ff)
-            piece = min(TILE, wide)
+            piece = min(GRAD_TILE, wide)
 
             def out_copies(slot, k):
                 out = []
-                for q in range(TILE // piece):
-                    z, col = divmod(at * dim - first + k * TILE + q * piece, wide)
+                for q in range(GRAD_TILE // piece):
+                    z, col = divmod(at * dim - first + k * GRAD_TILE + q * piece, wide)
                     out.append(
                         pltpu.make_async_copy(
                             stage.at[slot, :, :, pl.ds(q * piece, piece)],
@@ -1338,13 +1340,13 @@
                     )
                 return out
 
-            for k in range(count * dim // TILE):
+            for k in range(count * dim // GRAD_TILE):
                 slot = len(stored) % 2
                 if len(stored) >= 2:
                     wait(stored[-2])
-                cols = pl.ds(r_at(block) + k * TILE, TILE)
+                cols = pl.ds(r_at(block) + k * GRAD_TILE, GRAD_TILE)
                 y = nn(left[0], rhs[0, :, cols]) + nn(left[1], rhs[1, :, cols])
-                stage[slot] = y.astype(BF).reshape(pairs, rows, TILE)
+                stage[slot] = y.astype(BF).reshape(pairs, rows, GRAD_TILE)
                 stored.append(out_copies(slot, k))
                 start(stored[-1])
 
@@ -1401,21 +1403,21 @@
         w_wait(GATE)
 
         def put_gate(at, y):
-            gate[:, pl.ds(at, TILE)] = 1.0 / (1.0 + jnp.exp(-y))
+            gate[:, pl.ds(at, LOW_TILE)] = 1.0 / (1.0 + jnp.exp(-y))
         forward(lhs[L_LOW], GATE, 1, put_gate)
         w_wait(HIGH_A, HIGH_B, OUT)
         for w in (8, 9):
             w_each(w, lambda copy: copy.start())
 
         def put_high(at, y):
-            high[:, pl.ds(at, TILE)] = y
+            high[:, pl.ds(at, LOW_TILE)] = y
         forward(lhs[L_POOL_A], HIGH_A, 1, put_high)
 
         def put_merging(at, y):
-            cols = pl.ds(at, TILE)
+            cols = pl.ds(at, LOW_TILE)
             total = high[:, cols] + y
             high[:, cols] = total
-            rhs[0, :, pl.ds(R_MERGE * dim + at, TILE)] = (total * gate[:, cols]).astype(BF)
+            rhs[0, :, pl.ds(R_MERGE * dim + at, LOW_TILE)] = (total * gate[:, cols]).astype(BF)
         forward(lhs[L_POOL_B], HIGH_B, 1, put_merging)
         backward(lambda at: rhs[0, :, r_cols(R_MERGE)], OUT, 1, merged, True)
         merged[...] += lhs[L_LOW].astype(F32)
@@ -1429,7 +1431,7 @@
         out_q = []
         for k in range(3):
             def put_mixed(at, y):
-                mixed[k, :, pl.ds(at, TILE)] = y.astype(BF)
+                mixed[k, :, pl.ds(at, LOW_TILE)] = y.astype(BF)
             forward(lhs[L_FIRST], QUERY + k, 1, put_mixed)
             copies = to_heads(k, mixed.at[k], heads_in.at[k], q_send, q_got)
             start(copies)
@@ -1472,8 +1474,8 @@
 
         def put_up(at, y):
             value, rate = gelu_parts(y)
-            rhs[0, :, pl.ds(r_at(R_ACT) + at, TILE)] = value.astype(BF)
-            slope[:, pl.ds(at, TILE)] = rate.astype(BF)
+            rhs[0, :, pl.ds(r_at(R_ACT) + at, LOW_TILE)] = value.astype(BF)
+            slope[:, pl.ds(at, LOW_TILE)] = rate.astype(BF)
         forward(lhs[L_SECOND], 8, 4, put_up)
         r_copy(R_ACT).start()
         w_wait(9)
@@ -1481,7 +1483,7 @@
         put_natural(low_out, resid[...] + acc[...])
 
         def put_d_up(at, y):
-            rhs[0, :, pl.ds(r_at(R_DUP) + at, TILE)] = (y * slope[:, pl.ds(at, TILE)].astype(F32)).astype(BF)
+            rhs[0, :, pl.ds(r_at(R_DUP) + at, LOW_TILE)] = (y * slope[:, pl.ds(at, LOW_TILE)].astype(F32)).astype(BF)
         forward(lhs[L_COT], 12, 4, put_d_up)
         r_copy(R_DUP).start()
         backward(lambda at: rhs[0, :, pl.ds(r_at(R_DUP) + at, dim)], 8, 4, acc, True)
@@ -1492,7 +1494,7 @@
         l_copy(L_DA).start()
 
         def put_d_att(at, y):
-            mixed[0, :, pl.ds(at, TILE)] = y.astype(BF)
+            mixed[0, :, pl.ds(at, LOW_TILE)] = y.astype(BF)
         forward(lhs[L_DA], PROJ, 1, put_d_att)
         out_b = to_heads(0, mixed.at[0], d_att, b_send, b_got)
         start(out_b)
@@ -1541,11 +1543,11 @@
         l_copy(L_DF).start()
 
         def put_d_gate(at, y):
-            cols = pl.ds(at, TILE)
+            cols = pl.ds(at, LOW_TILE)
             gv = gate[:, cols]
             part = y * gv
-            rhs[0, :, pl.ds(R_DHIGH * dim + at, TILE)] = part.astype(BF)
-            rhs[0, :, pl.ds(R_DGATE * dim + at, TILE)] = (part * high[:, cols] * (1.0 - gv)).astype(BF)
+            rhs[0, :, pl.ds(R_DHIGH * dim + at, LOW_TILE)] = part.astype(BF)
+            rhs[0, :, pl.ds(R_DGATE * dim + at, LOW_TILE)] = (part * high[:, cols] * (1.0 - gv)).astype(BF)
         forward(lhs[L_DF], OUT, 1, put_d_gate)
         r_copy(R_DHIGH).start()
         r_copy(R_DGATE).start()
@@ -1594,7 +1596,7 @@
             vm((t, dim), F32), vm((t, dim), F32), vm((t, dim), F32), vm((t, dim), F32), vm((t, dim), F32),
             vm((t, ff), BF), vm((3, t, dim), BF), vm((3, every, width), BF), vm((every, width), BF), vm((every, width), BF),
             vm((1, 8, 128), BF), vm((3, every, width), BF), vm((heads, every, every), BF), vm((every, every), BF),
-            vm((2, pairs, rows, TILE), BF), vm((2, half, t), BF),
+            vm((2, pairs, rows, GRAD_TILE), BF), vm((2, half, t), BF),
             dma((10, 2 * n)), dma((3, n)), dma((3, n)), dma((groups, n)), dma((groups, n)), dma((1, n)), dma((1, n)),
             dma((3 * groups, n)), dma((3 * groups, n)), dma((3 * groups,)), dma((8,)), dma((8,)), dma((9,)), dma((9,)), dma((2, 2)),
         ],

time: 696 us -> 688 us (0.989)
  Pallas kernels: 609 us -> 601 us
    pallas_call x1, Pallas kernels: 212 us -> 201 us  [big_backward(): pl.pallas_call(kernel, out_shape=(jax.ShapeDtypeStruct((CHUNKS, rows, c),...]
  transfers between devices with their start and end apart: 3 -> 3, of which waited for: 2 -> 2; matrix products, arithmetic and copies ran while one was open for 1% -> 2% of each run, Pallas kernels for 42% -> 44%
where the time goes in v15:
time: 688 us; the launch traced here: 682 us
  Pallas kernels  601 us (87%)
  waiting for transfers between devices  52.5 us (8%)
  between operations  14.3 us (2%)
  local copies, waits for them, and re-layouts  8.72 us (1%)
    pallas_call x1, Pallas kernels, big_backward(): pl.pallas_call(kernel, out_shape=(jax.ShapeDtypeStruct((CHUNKS, rows, c),...  201 us
    pallas_call x1, Pallas kernels, big_forward(): pl.pallas_call(kernel, out_shape=(jax.ShapeDtypeStruct((CHUNKS, rows, c),...  178 us
    pallas_call x1, Pallas kernels, low_stage(): pl.pallas_call(kernel, out_shape=(tok, tok, jax.ShapeDtypeStruct(pooled.s...  99.4 us
    pallas_call x1, Pallas kernels, conv_backward(): pl.pallas_call(kernel, out_shape=(jax.ShapeDtypeStruct((rows, cols, c), F...  80.5 us
    all_gather x1, waiting for transfers between devices, per_device(): packed = rows_first(lax.all_gather(packed, 'mp', axis=0, tiled=True))  49.5 us
    pallas_call x1, Pallas kernels, conv_forward(): pl.pallas_call(kernel, out_shape=(jax.ShapeDtypeStruct((rows, cols, c), F...  29.7 us
  transfers between devices with their start and end apart: 3, of which 2 were waited for; matrix products, arithmetic and copies ran while one was open for 2% of the time, Pallas kernels for 44%

profile of v15, /device:TPU:0, one launch (start us, length us, event | category | flops | bytes accessed | tf_op | source)
XLA Modules:
  0.0 682.3 jit_solution(3694597240490583223)
XLA Ops:
  7.2 0.0 copy-start.7
  7.2 0.0 copy-start.6
  7.2 0.0 copy-start.8
  7.2 0.0 all-gather.3.cloned.1.call-start
  7.3 2.5 shard_map.306
  9.8 0.0 all-gather.3.cloned.1.call-update
  9.8 0.0 all-gather.5.cloned.1.call-start
  9.8 0.0 copy-done.7
  9.9 0.0 copy-done.6
  9.9 0.4 reshape.162.w_ref
  10.3 0.0 copy-done.8
  10.4 1.7 bitcast_multiply_fusion.x_ref.res
  12.0 29.7 %shard_map.305 = (f32[12,48,1536]{2,1,0:T(8,128)S(1)}, bf16[18,48,1536]{2,1,0:T(8,128)(2,1)S(1)}) custom-call(bf16[12,48,1536]{2,1,0:T(8,128)(2,1)S(1)} %bitcast_multiply_fusion.x_ref.res, f32[49,1,1536]{2,1,0:T(1,128)S(1)} %reshape.162.w_ref), custom_call_target="tpu_custom_call" | custom-call | tf_op jit(solution)/shard_map/pallas_call | solution.py:883
  41.7 0.0 copy-start.5
  41.8 0.0 copy-start
  41.8 0.4 multiply_reduce_fusion.1
  42.2 0.6 multiply_reduce_fusion
  42.8 0.5 copy-done.5
  43.3 1.2 copy-done
  44.4 1.8 multiply_convert_fusion
  46.3 49.5 %all-gather.3.cloned.1.call-done = bf16[512,4096]{1,0:T(8,128)(2,1)} async-done(((bf16[128,4096]{1,0:T(8,128)(2,1)}), bf16[512,4096]{1,0:T(8,128)(2,1)}) %all-gather.3.cloned.1.call-update) | async-done | bytes 4194320 | tf_op jit(solution)/shard_map/all_gather | solution.py:1774
  95.8 0.0 all-gather.5.cloned.1.call-update
  95.8 0.0 reduce-scatter.2.cloned.1.call-start
  95.9 0.9 convert_element_type.65.mask_ref
  96.7 0.1 convert_element_type.63
  96.9 0.1 reduce_sum.29
  97.0 0.8 copy.39.share_ref
  97.7 0.6 broadcast_in_dim.35
  98.3 0.6 broadcast_in_dim.36
  98.9 178.1 %shard_map.307 = (f32[6,96,1536]{2,1,0:T(8,128)}, f32[6,24,1536]{2,1,0:T(8,128)}, bf16[4,6,96,1536]{3,2,1,0:T(8,128)(2,1)}, bf16[4,6,96,1536]{3,2,1,0:T(8,128)(2...) custom-call(bf16[6,96,1536]{2,1,0:T(8,128)(2,1)} %bitcast.45, ...), custom_call_target="tpu_custom_call" | custom-call | flops 21743271936 | bytes 28311552 | tf_op jit(solution)/shard_map/pallas_call | solution.py:408
  277.0 0.0 all-gather.5.cloned.1.call-done
  277.0 99.4 %shard_map.308 = (f32[144,1024]{1,0:T(8,128)}, f32[144,1024]{1,0:T(8,128)}, f32[144,1536]{1,0:T(8,128)}, f32[1,1024]{1,0:T(1,128)}, f32[1,1024]{1,0:T(1,128)}, /*index=5*/bf16[4,512,4096]{2,1,0:T(8,128)(2,1)}) custom-call(bf16[144,1024]{1,0:T(8,128)(2,1)} %bitcast.59, f32[144,1536]{1,0:T(8,128)} %bitcast.70, bf16[144,1024]{1,0:T(8,128)(2,1)} %bitcast.60, ...), custom_call_target="tpu_custom_call" | custom-call | flops 14000000000 | bytes 70000000 | tf_op jit(solution)/shard_map/pallas_call | solution.py:1589
  376.5 200.5 %shard_map.309 = (f32[6,96,1536]{2,1,0:T(8,128)}, bf16[6,96,1536]{2,1,0:T(8,128)(2,1)}, bf16[4,192,1536]{2,1,0:T(8,128)(2,1)}, bf16[4,192,1536]{2,1,0:T(8,128)(2...) custom-call(bf16[12,48,1536]{2,1,0:T(8,128)(2,1)} %bitcast.57, ...), custom_call_target="tpu_custom_call" | custom-call | flops 43486543872 | bytes 28311552 | tf_op jit(solution)/shard_map/pallas_call | solution.py:737
  577.0 0.0 reduce-scatter.2.cloned.1.call-update
  577.1 0.2 copy.42.mask_ref
  577.3 0.4 copy-done.9
  577.7 0.0 copy-done.10
  577.7 80.5 %shard_map.310 = (f32[12,48,1536]{2,1,0:T(8,128)}, f32[8,7,1536]{2,1,0:T(8,128)S(1)}, bf16[2,192,1536]{2,1,0:T(8,128)(2,1)}, bf16[1,192,1536]{2,1,0:T(8,128)(2,1...) custom-call(f32[12,48,1536]{2,1,0:T(8,128)} %bitcast.65, ...), custom_call_target="tpu_custom_call" | custom-call | flops 60000002048 | bytes 100000000 | tf_op jit(solution)/shard_map/pallas_call | solution.py:1136
  658.2 0.0 copy-start.3
  658.2 0.8 copy-done.3
  659.0 0.8 slice.18
  659.9 0.1 copy-done.4
  660.0 8.8 %shard_map.311 = (f32[192,1536]{1,0:T(8,128)}, f32[192,1536]{1,0:T(8,128)}, f32[1,144,1024]{2,1,0:T(8,128)}, f32[1,12,48,1536]{3,2,1,0:T(8,128)}, f32[1,144,1024]{2,1,0:T(8,128)}, /*index=5*/f32[1,12,48,1536]{3,2,1,0:T(8,128)}) custom-call(bf16[192,1536]{1,0:T(8,128)(2,1)} %bitcast.40, bf16[192,1536]{1,0:T(8,128)(2,1)} %bitcast.41, ...), custom_call_target="tpu_custom_call" | custom-call | flops 1000000000 | bytes 24000000 | tf_op jit(solution)/shard_map/pallas_call | solution.py:1658
  668.8 0.6 slice_reduce_fusion
  669.4 0.6 fusion
  670.0 2.9 reduce-scatter.2.cloned.1.call-done
  672.9 1.2 copy-done.2
  674.1 1.4 shard_map.312
  (21 shorter events, 0.1 us)
Async XLA Ops:
  7.2 2.6 copy-start.7
  7.2 2.7 copy-start.6
  7.2 3.1 copy-start.8
  7.2 88.5 %all-gather.3.cloned.1.call-start = ((), (), s32[]{:S(2)}) async-start(), calls=%async_computation.1 | async-start | bytes 5242880 | tf_op jit(solution)/shard_map/all_gather | solution.py:1774
  9.8 267.2 %all-gather.5.cloned.1.call-start = ((), (), s32[]{:S(2)}) async-start(), calls=%async_computation.2 | async-start | bytes 37748736 | tf_op jit(solution)/shard_map/all_gather | solution.py:1787
  12.0 30.7 %copy-start.1 = (bf16[12,48,1536]{2,1,0:T(8,128)(2,1)}, bf16[12,48,1536]{2,1,0:T(8,128)(2,1)S(1)}, u32[]{:S(2)}) copy-start(bf16[12,48,1536]{2,1,0:T(8,128)(2,1)S(1)} %bitcast_multiply_fusion.x_ref.res) | copy-start | bytes 5308420
  41.7 1.5 copy-start.5
  41.8 2.7 copy-start
  46.3 51.5 %copy-start.11 = (bf16[1024]{0:T(1024)(128)(2,1)S(1)}, bf16[1024]{0:T(1024)(128)(2,1)}, u32[]{:S(2)}) copy-start(bf16[1024]{0:T(1024)(128)(2,1)} %param.28) | copy-start | bytes 6148
  46.3 52.1 %copy-start.12 = (bf16[1024]{0:T(1024)(128)(2,1)S(1)}, bf16[1024]{0:T(1024)(128)(2,1)}, u32[]{:S(2)}) copy-start(bf16[1024]{0:T(1024)(128)(2,1)} %param.31) | copy-start | bytes 6148
  95.8 577.1 %reduce-scatter.2.cloned.1.call-start = ((), (), s32[]{:S(2)}) async-start(), calls=%async_computation.3 | async-start | bytes 5242880 | tf_op jit(solution)/shard_map/reduce_scatter | solution.py:1819
  577.0 0.7 copy-start.9
  577.0 0.7 copy-start.10
  658.2 0.8 copy-start.3
  659.0 1.0 copy-start.4
  672.9 1.2 copy-start.2
Sparse Core Ops, SparseCore 0:
  10.2 85.5 all-gather.2
  97.6 159.7 all-gather.4
  577.2 95.6 reduce-scatter.1

commit v16 on v15

--- a/solution.py
+++ b/solution.py
@@ -614,10 +614,10 @@
             middle_steps = [2, 4, 12, 13, 14, 15, 17, 19, 20, 21, 22, 23]
 
         def item_of(g):
-            q = jnp.where(between, -1, (g - 3) // 2)
+            q = jnp.where(between, -1, (g - 2) // 2)
             for i, at in enumerate(middle_steps):
                 q = jnp.where(between & (g == at), i, q)
-            return q, (q >= 0) & (q < items) & (g >= 2) & (between | (lax.rem(g, 2) == 1))
+            return q, (q >= 0) & (q < items) & (g >= 2) & (between | (lax.rem(g, 2) == 0))
 
         def after(g):
             for at, tick in ticks.items():
@@ -641,12 +641,12 @@
 
                 lax.fori_loop(0, c // TILE, tile, 0)
 
-            @pl.when(g == 2 * items + 2)
+            @pl.when(g == 2 * items + 1)
             def _():
                 give(g_up, left, out_up, stored.at[2])
                 swaps[0].start()
 
-            @pl.when(g == 2 * items + 3)
+            @pl.when(g == 2 * items + 2)
             def _():
                 give(g_down, right, out_down, stored.at[3])
                 swaps[1].start()
@@ -1786,7 +1786,7 @@
     normed, packed = lax.optimization_barrier((normed, packed))
     packed = rows_first(lax.all_gather(packed, "dp", axis=0, tiled=True))
     hr_out, pooled, normed_all, hidden_act, hidden_slope, up_t, down_t = big_forward(
-        normed.reshape(row_count * col_count, chan_count), cn_up, cn_down, masked, plane_mask, shares, shards
+        normed.reshape(row_count * col_count, chan_count), cn_up, cn_down, masked, cell_mask, shares, shards
     )
     hr_out = hr_out.reshape(hr_in.shape)
     tokens = half_rows * half_cols
@@ -1812,7 +1812,7 @@
         ).reshape(tokens, chan_count)
     low_out, d_low_in, g_ln1, g_ln2 = low_out[None], d_low_in[None], g_ln1[0], g_ln2[0]
     d_normed, d_map, cn_grads, low_sums = big_backward(
-        cot_hr[0], d_pooled, shares, plane_mask, normed_all, hidden_act, hidden_slope,
+        cot_hr[0], d_pooled, shares, cell_mask, normed_all, hidden_act, hidden_slope,
         up_t, down_t, low_grads, shards, devices,
     )
     low_sums = rows_first(low_sums.reshape(shards, share, -1))

time: 688 us -> 682 us (level)
  no operation moved by 1% of the time
where the time goes in v16:
time: 682 us; the launch traced here: 677 us
  Pallas kernels  596 us (87%)
  waiting for transfers between devices  52.3 us (8%)
  between operations  14.3 us (2%)
  local copies, waits for them, and re-layouts  8.72 us (1%)
    pallas_call x1, Pallas kernels, big_backward(): pl.pallas_call(kernel, out_shape=(jax.ShapeDtypeStruct((CHUNKS, rows, c),...  195 us
    pallas_call x1, Pallas kernels, big_forward(): pl.pallas_call(kernel, out_shape=(jax.ShapeDtypeStruct((CHUNKS, rows, c),...  178 us
    pallas_call x1, Pallas kernels, low_stage(): pl.pallas_call(kernel, out_shape=(tok, tok, jax.ShapeDtypeStruct(pooled.s...  99.4 us
    pallas_call x1, Pallas kernels, conv_backward(): pl.pallas_call(kernel, out_shape=(jax.ShapeDtypeStruct((rows, cols, c), F...  80.8 us
    all_gather x1, waiting for transfers between devices, per_device(): packed = rows_first(lax.all_gather(packed, 'mp', axis=0, tiled=True))  49.5 us
    pallas_call x1, Pallas kernels, conv_forward(): pl.pallas_call(kernel, out_shape=(jax.ShapeDtypeStruct((rows, cols, c), F...  29.7 us
  transfers between devices with their start and end apart: 3, of which 2 were waited for; matrix products, arithmetic and copies ran while one was open for 2% of the time, Pallas kernels for 44%

profile of v16, /device:TPU:0, one launch (start us, length us, event | category | flops | bytes accessed | tf_op | source)
XLA Modules:
  0.0 676.7 jit_solution(11815815502027352101)
XLA Ops:
  7.2 0.0 copy-start.7
  7.2 0.0 copy-start.6
  7.2 0.0 copy-start.8
  7.2 0.0 all-gather.3.cloned.1.call-start
  7.3 2.5 shard_map.306
  9.8 0.0 all-gather.3.cloned.1.call-update
  9.8 0.0 all-gather.5.cloned.1.call-start
  9.9 0.4 reshape.160.w_ref
  10.3 0.0 copy-done.8
  10.4 1.7 bitcast_multiply_fusion.x_ref.res
  12.0 29.7 %shard_map.305 = (f32[12,48,1536]{2,1,0:T(8,128)S(1)}, bf16[18,48,1536]{2,1,0:T(8,128)(2,1)S(1)}) custom-call(bf16[12,48,1536]{2,1,0:T(8,128)(2,1)S(1)} %bitcast_multiply_fusion.x_ref.res, f32[49,1,1536]{2,1,0:T(1,128)S(1)} %reshape.160.w_ref), custom_call_target="tpu_custom_call" | custom-call | tf_op jit(solution)/shard_map/pallas_call | solution.py:883
  41.7 0.0 copy-start.5
  41.8 0.0 copy-start
  41.8 0.4 multiply_reduce_fusion.1
  42.2 0.6 multiply_reduce_fusion
  42.8 0.0 copy-done.1
  42.8 0.5 copy-done.5
  43.3 1.2 copy-done
  44.4 1.8 multiply_convert_fusion
  46.3 49.5 %all-gather.3.cloned.1.call-done = bf16[512,4096]{1,0:T(8,128)(2,1)} async-done(((bf16[128,4096]{1,0:T(8,128)(2,1)}), bf16[512,4096]{1,0:T(8,128)(2,1)}) %all-gather.3.cloned.1.call-update) | async-done | bytes 4194320 | tf_op jit(solution)/shard_map/all_gather | solution.py:1774
  95.8 0.0 all-gather.5.cloned.1.call-update
  95.8 0.0 reduce-scatter.2.cloned.1.call-start
  95.9 0.9 convert_element_type.65.mask_ref
  96.7 0.1 convert_element_type.63
  96.9 0.1 reduce_sum.29
  97.0 0.8 copy.39.share_ref
  97.7 0.0 copy-done.11
  97.7 0.6 broadcast_in_dim.35
  98.3 0.6 broadcast_in_dim.36
  98.9 178.1 %shard_map.307 = (f32[6,96,1536]{2,1,0:T(8,128)}, f32[6,24,1536]{2,1,0:T(8,128)}, bf16[4,6,96,1536]{3,2,1,0:T(8,128)(2,1)}, bf16[4,6,96,1536]{3,2,1,0:T(8,128)(2...) custom-call(bf16[6,96,1536]{2,1,0:T(8,128)(2,1)} %bitcast.45, ...), custom_call_target="tpu_custom_call" | custom-call | flops 21743271936 | bytes 28311552 | tf_op jit(solution)/shard_map/pallas_call | solution.py:408
  277.0 0.0 all-gather.5.cloned.1.call-done
  277.0 99.4 %shard_map.308 = (f32[144,1024]{1,0:T(8,128)}, f32[144,1024]{1,0:T(8,128)}, f32[144,1536]{1,0:T(8,128)}, f32[1,1024]{1,0:T(1,128)}, f32[1,1024]{1,0:T(1,128)}, /*index=5*/bf16[4,512,4096]{2,1,0:T(8,128)(2,1)}) custom-call(bf16[144,1024]{1,0:T(8,128)(2,1)} %bitcast.59, f32[144,1536]{1,0:T(8,128)} %bitcast.70, bf16[144,1024]{1,0:T(8,128)(2,1)} %bitcast.60, ...), custom_call_target="tpu_custom_call" | custom-call | flops 14000000000 | bytes 70000000 | tf_op jit(solution)/shard_map/pallas_call | solution.py:1589
  376.5 195.0 %shard_map.309 = (f32[6,96,1536]{2,1,0:T(8,128)}, bf16[6,96,1536]{2,1,0:T(8,128)(2,1)}, bf16[4,192,1536]{2,1,0:T(8,128)(2,1)}, bf16[4,192,1536]{2,1,0:T(8,128)(2...) custom-call(bf16[12,48,1536]{2,1,0:T(8,128)(2,1)} %bitcast.57, ...), custom_call_target="tpu_custom_call" | custom-call | flops 43486543872 | bytes 28311552 | tf_op jit(solution)/shard_map/pallas_call | solution.py:737
  571.4 0.0 copy-start.9
  571.5 0.0 reduce-scatter.2.cloned.1.call-update
  571.5 0.2 copy.42.mask_ref
  571.7 0.4 copy-done.9
  572.1 0.0 copy-done.10
  572.1 80.8 %shard_map.310 = (f32[12,48,1536]{2,1,0:T(8,128)}, f32[8,7,1536]{2,1,0:T(8,128)S(1)}, bf16[2,192,1536]{2,1,0:T(8,128)(2,1)}, bf16[1,192,1536]{2,1,0:T(8,128)(2,1...) custom-call(f32[12,48,1536]{2,1,0:T(8,128)} %bitcast.65, ...), custom_call_target="tpu_custom_call" | custom-call | flops 60000002048 | bytes 100000000 | tf_op jit(solution)/shard_map/pallas_call | solution.py:1136
  652.9 0.8 copy-done.3
  653.7 0.8 slice.18
  654.6 0.1 copy-done.4
  654.7 8.7 %shard_map.311 = (f32[192,1536]{1,0:T(8,128)}, f32[192,1536]{1,0:T(8,128)}, f32[1,144,1024]{2,1,0:T(8,128)}, f32[1,12,48,1536]{3,2,1,0:T(8,128)}, f32[1,144,1024]{2,1,0:T(8,128)}, /*index=5*/f32[1,12,48,1536]{3,2,1,0:T(8,128)}) custom-call(bf16[192,1536]{1,0:T(8,128)(2,1)} %bitcast.40, bf16[192,1536]{1,0:T(8,128)(2,1)} %bitcast.41, ...), custom_call_target="tpu_custom_call" | custom-call | flops 1000000000 | bytes 24000000 | tf_op jit(solution)/shard_map/pallas_call | solution.py:1658
  663.4 0.6 slice_reduce_fusion
  664.0 0.6 fusion
  664.7 2.7 reduce-scatter.2.cloned.1.call-done
  667.3 1.2 copy-done.2
  668.6 1.4 shard_map.312
  (21 shorter events, 0.1 us)
Async XLA Ops:
  7.2 2.6 copy-start.7
  7.2 2.7 copy-start.6
  7.2 3.1 copy-start.8
  7.2 88.5 %all-gather.3.cloned.1.call-start = ((), (), s32[]{:S(2)}) async-start(), calls=%async_computation.1 | async-start | bytes 5242880 | tf_op jit(solution)/shard_map/all_gather | solution.py:1774
  9.8 267.2 %all-gather.5.cloned.1.call-start = ((), (), s32[]{:S(2)}) async-start(), calls=%async_computation.2 | async-start | bytes 37748736 | tf_op jit(solution)/shard_map/all_gather | solution.py:1787
  12.0 30.7 %copy-start.1 = (bf16[12,48,1536]{2,1,0:T(8,128)(2,1)}, bf16[12,48,1536]{2,1,0:T(8,128)(2,1)S(1)}, u32[]{:S(2)}) copy-start(bf16[12,48,1536]{2,1,0:T(8,128)(2,1)S(1)} %bitcast_multiply_fusion.x_ref.res) | copy-start | bytes 5308420
  41.7 1.5 copy-start.5
  41.8 2.7 copy-start
  46.3 51.5 %copy-start.11 = (bf16[1024]{0:T(1024)(128)(2,1)S(1)}, bf16[1024]{0:T(1024)(128)(2,1)}, u32[]{:S(2)}) copy-start(bf16[1024]{0:T(1024)(128)(2,1)} %param.28) | copy-start | bytes 6148
  46.3 52.1 %copy-start.12 = (bf16[1024]{0:T(1024)(128)(2,1)S(1)}, bf16[1024]{0:T(1024)(128)(2,1)}, u32[]{:S(2)}) copy-start(bf16[1024]{0:T(1024)(128)(2,1)} %param.31) | copy-start | bytes 6148
  95.8 571.5 %reduce-scatter.2.cloned.1.call-start = ((), (), s32[]{:S(2)}) async-start(), calls=%async_computation.3 | async-start | bytes 5242880 | tf_op jit(solution)/shard_map/reduce_scatter | solution.py:1819
  571.4 0.7 copy-start.9
  571.4 0.7 copy-start.10
  652.9 0.8 copy-start.3
  653.7 1.0 copy-start.4
  667.3 1.2 copy-start.2
Sparse Core Ops, SparseCore 0:
  10.2 85.5 all-gather.2
  97.6 159.7 all-gather.4
  571.6 95.6 reduce-scatter.1

commit v17 on v16

--- a/solution.py
+++ b/solution.py
@@ -651,6 +651,10 @@
                 give(g_down, right, out_down, stored.at[3])
                 swaps[1].start()
 
+            @pl.when(g == 2 * items + 3)
+            def _():
+                keep_sums(0)
+
         core = dp_bit(0)
 
         def result(j):
@@ -674,8 +678,9 @@
 
             lax.fori_loop(0, devices // 2, one, 0)
 
-        def keep_sums():
-            sets = ((g_up, left, got_up, g_up_out, 2), (g_down, right, got_down, g_down_out, 3))
+        def keep_sums(which):
+            swaps[which].wait()
+            sets = (((g_up, left, got_up, g_up_out, 2), (g_down, right, got_down, g_down_out, 3))[which],)
 
             def loads(i):
                 return [
@@ -727,9 +732,7 @@
         if not ticks:
             for plan in plans:
                 pass_on(steps - 1, plan)
-        for swap in swaps:
-            swap.wait()
-        keep_sums()
+        keep_sums(1)
 
     whole = pl.BlockSpec(memory_space=pl.ANY)
     local = pl.BlockSpec(memory_space=pltpu.VMEM)

time: 682 us -> 689 us (1.010)
    pallas_call x1, Pallas kernels: 195 us -> 202 us  [big_backward(): pl.pallas_call(kernel, out_shape=(jax.ShapeDtypeStruct((CHUNKS, rows, c),...]
  transfers between devices with their start and end apart: 3 -> 3, of which waited for: 2 -> 2; matrix products, arithmetic and copies ran while one was open for 2% -> 2% of each run, Pallas kernels for 44% -> 43%
where the time goes in v17:
time: 689 us; the launch traced here: 684 us
  Pallas kernels  601 us (87%)
  waiting for transfers between devices  53.7 us (8%)
  between operations  14.3 us (2%)
  local copies, waits for them, and re-layouts  8.72 us (1%)
    pallas_call x1, Pallas kernels, big_backward(): pl.pallas_call(kernel, out_shape=(jax.ShapeDtypeStruct((CHUNKS, rows, c),...  202 us
    pallas_call x1, Pallas kernels, big_forward(): pl.pallas_call(kernel, out_shape=(jax.ShapeDtypeStruct((CHUNKS, rows, c),...  178 us
    pallas_call x1, Pallas kernels, low_stage(): pl.pallas_call(kernel, out_shape=(tok, tok, jax.ShapeDtypeStruct(pooled.s...  99.4 us
    pallas_call x1, Pallas kernels, conv_backward(): pl.pallas_call(kernel, out_shape=(jax.ShapeDtypeStruct((rows, cols, c), F...  79.3 us
    all_gather x1, waiting for transfers between devices, per_device(): packed = rows_first(lax.all_gather(packed, 'mp', axis=0, tiled=True))  49.5 us
    pallas_call x1, Pallas kernels, conv_forward(): pl.pallas_call(kernel, out_shape=(jax.ShapeDtypeStruct((rows, cols, c), F...  29.7 us
  transfers between devices with their start and end apart: 3, of which 2 were waited for; matrix products, arithmetic and copies ran while one was open for 2% of the time, Pallas kernels for 43%

profile of v17, /device:TPU:0, one launch (start us, length us, event | category | flops | bytes accessed | tf_op | source)
XLA Modules:
  0.0 683.8 jit_solution(4960671688882275489)
XLA Ops:
  7.2 0.0 copy-start.7
  7.2 0.0 copy-start.6
  7.2 0.0 copy-start.8
  7.2 0.0 all-gather.3.cloned.1.call-start
  7.3 2.5 shard_map.306
  9.8 0.0 all-gather.3.cloned.1.call-update
  9.8 0.0 all-gather.5.cloned.1.call-start
  9.8 0.0 copy-done.7
  9.9 0.0 copy-done.6
  9.9 0.4 reshape.160.w_ref
  10.3 0.0 copy-done.8
  10.4 1.7 bitcast_multiply_fusion.x_ref.res
  12.0 0.0 copy-start.1
  12.0 29.7 %shard_map.305 = (f32[12,48,1536]{2,1,0:T(8,128)S(1)}, bf16[18,48,1536]{2,1,0:T(8,128)(2,1)S(1)}) custom-call(bf16[12,48,1536]{2,1,0:T(8,128)(2,1)S(1)} %bitcast_multiply_fusion.x_ref.res, f32[49,1,1536]{2,1,0:T(1,128)S(1)} %reshape.160.w_ref), custom_call_target="tpu_custom_call" | custom-call | tf_op jit(solution)/shard_map/pallas_call | solution.py:886
  41.7 0.0 copy-start.5
  41.8 0.0 copy-start
  41.8 0.4 multiply_reduce_fusion.1
  42.2 0.6 multiply_reduce_fusion
  42.8 0.5 copy-done.5
  43.3 1.2 copy-done
  44.4 1.8 multiply_convert_fusion
  46.3 49.5 %all-gather.3.cloned.1.call-done = bf16[512,4096]{1,0:T(8,128)(2,1)} async-done(((bf16[128,4096]{1,0:T(8,128)(2,1)}), bf16[512,4096]{1,0:T(8,128)(2,1)}) %all-gather.3.cloned.1.call-update) | async-done | bytes 4194320 | tf_op jit(solution)/shard_map/all_gather | solution.py:1777
  95.8 0.0 all-gather.5.cloned.1.call-update
  95.8 0.0 reduce-scatter.2.cloned.1.call-start
  95.9 0.9 convert_element_type.65.mask_ref
  96.7 0.1 convert_element_type.63
  96.9 0.1 reduce_sum.29
  97.0 0.8 copy.39.share_ref
  97.7 0.6 broadcast_in_dim.35
  98.3 0.6 broadcast_in_dim.36
  98.9 178.1 %shard_map.307 = (f32[6,96,1536]{2,1,0:T(8,128)}, f32[6,24,1536]{2,1,0:T(8,128)}, bf16[4,6,96,1536]{3,2,1,0:T(8,128)(2,1)}, bf16[4,6,96,1536]{3,2,1,0:T(8,128)(2...) custom-call(bf16[6,96,1536]{2,1,0:T(8,128)(2,1)} %bitcast.45, ...), custom_call_target="tpu_custom_call" | custom-call | flops 21743271936 | bytes 28311552 | tf_op jit(solution)/shard_map/pallas_call | solution.py:408
  277.0 0.0 all-gather.5.cloned.1.call-done
  277.0 99.4 %shard_map.308 = (f32[144,1024]{1,0:T(8,128)}, f32[144,1024]{1,0:T(8,128)}, f32[144,1536]{1,0:T(8,128)}, f32[1,1024]{1,0:T(1,128)}, f32[1,1024]{1,0:T(1,128)}, /*index=5*/bf16[4,512,4096]{2,1,0:T(8,128)(2,1)}) custom-call(bf16[144,1024]{1,0:T(8,128)(2,1)} %bitcast.59, f32[144,1536]{1,0:T(8,128)} %bitcast.70, bf16[144,1024]{1,0:T(8,128)(2,1)} %bitcast.60, ...), custom_call_target="tpu_custom_call" | custom-call | flops 14000000000 | bytes 70000000 | tf_op jit(solution)/shard_map/pallas_call | solution.py:1592
  376.5 202.1 %shard_map.309 = (f32[6,96,1536]{2,1,0:T(8,128)}, bf16[6,96,1536]{2,1,0:T(8,128)(2,1)}, bf16[4,192,1536]{2,1,0:T(8,128)(2,1)}, bf16[4,192,1536]{2,1,0:T(8,128)(2...) custom-call(bf16[12,48,1536]{2,1,0:T(8,128)(2,1)} %bitcast.57, ...), custom_call_target="tpu_custom_call" | custom-call | flops 43486543872 | bytes 28311552 | tf_op jit(solution)/shard_map/pallas_call | solution.py:740
  578.6 0.0 reduce-scatter.2.cloned.1.call-update
  578.6 0.2 copy.42.mask_ref
  578.8 0.4 copy-done.9
  579.2 0.0 copy-done.10
  579.3 79.3 %shard_map.310 = (f32[12,48,1536]{2,1,0:T(8,128)}, f32[8,7,1536]{2,1,0:T(8,128)S(1)}, bf16[2,192,1536]{2,1,0:T(8,128)(2,1)}, bf16[1,192,1536]{2,1,0:T(8,128)(2,1...) custom-call(f32[12,48,1536]{2,1,0:T(8,128)} %bitcast.65, ...), custom_call_target="tpu_custom_call" | custom-call | flops 60000002048 | bytes 100000000 | tf_op jit(solution)/shard_map/pallas_call | solution.py:1139
  658.6 0.8 copy-done.3
  659.4 0.8 slice.18
  660.2 0.1 copy-done.4
  660.3 8.8 %shard_map.311 = (f32[192,1536]{1,0:T(8,128)}, f32[192,1536]{1,0:T(8,128)}, f32[1,144,1024]{2,1,0:T(8,128)}, f32[1,12,48,1536]{3,2,1,0:T(8,128)}, f32[1,144,1024]{2,1,0:T(8,128)}, /*index=5*/f32[1,12,48,1536]{3,2,1,0:T(8,128)}) custom-call(bf16[192,1536]{1,0:T(8,128)(2,1)} %bitcast.40, bf16[192,1536]{1,0:T(8,128)(2,1)} %bitcast.41, ...), custom_call_target="tpu_custom_call" | custom-call | flops 1000000000 | bytes 24000000 | tf_op jit(solution)/shard_map/pallas_call | solution.py:1661
  669.1 0.6 slice_reduce_fusion
  669.7 0.6 fusion
  670.3 4.1 reduce-scatter.2.cloned.1.call-done
  674.5 1.2 copy-done.2
  675.7 1.4 shard_map.312
  (21 shorter events, 0.1 us)
Async XLA Ops:
  7.2 2.6 copy-start.7
  7.2 2.7 copy-start.6
  7.2 3.1 copy-start.8
  7.2 88.5 %all-gather.3.cloned.1.call-start = ((), (), s32[]{:S(2)}) async-start(), calls=%async_computation.1 | async-start | bytes 5242880 | tf_op jit(solution)/shard_map/all_gather | solution.py:1777
  9.8 267.2 %all-gather.5.cloned.1.call-start = ((), (), s32[]{:S(2)}) async-start(), calls=%async_computation.2 | async-start | bytes 37748736 | tf_op jit(solution)/shard_map/all_gather | solution.py:1790
  12.0 30.7 %copy-start.1 = (bf16[12,48,1536]{2,1,0:T(8,128)(2,1)}, bf16[12,48,1536]{2,1,0:T(8,128)(2,1)S(1)}, u32[]{:S(2)}) copy-start(bf16[12,48,1536]{2,1,0:T(8,128)(2,1)S(1)} %bitcast_multiply_fusion.x_ref.res) | copy-start | bytes 5308420
  41.7 1.5 copy-start.5
  41.8 2.7 copy-start
  46.3 51.5 %copy-start.11 = (bf16[1024]{0:T(1024)(128)(2,1)S(1)}, bf16[1024]{0:T(1024)(128)(2,1)}, u32[]{:S(2)}) copy-start(bf16[1024]{0:T(1024)(128)(2,1)} %param.28) | copy-start | bytes 6148
  46.3 52.1 %copy-start.12 = (bf16[1024]{0:T(1024)(128)(2,1)S(1)}, bf16[1024]{0:T(1024)(128)(2,1)}, u32[]{:S(2)}) copy-start(bf16[1024]{0:T(1024)(128)(2,1)} %param.31) | copy-start | bytes 6148
  95.8 578.7 %reduce-scatter.2.cloned.1.call-start = ((), (), s32[]{:S(2)}) async-start(), calls=%async_computation.3 | async-start | bytes 5242880 | tf_op jit(solution)/shard_map/reduce_scatter | solution.py:1822
  578.6 0.7 copy-start.9
  578.6 0.7 copy-start.10
  658.5 0.8 copy-start.3
  659.4 1.0 copy-start.4
  674.5 1.2 copy-start.2
Sparse Core Ops, SparseCore 0:
  10.2 85.5 all-gather.2
  97.6 159.7 all-gather.4
  578.7 95.6 reduce-scatter.1
